TPU v7x, 512 devices: a whole 4x4x16 slice. The times are simulated.
512 devices in a mesh: expert: 32 (over x_lo, z), tensor: 16 (over y, x_hi, core).
Axes of the slice: x: 4 (x_hi: 2, x_lo: 2; x = x_hi * 2 + x_lo), y: 4, z: 16, core: 2. Of those that a mesh axis runs over, the one named last changes fastest.
Arguments:
- tokens: bfloat16 [1536, 5120], P('expert', 'tensor'), may hold values from -6 to 6
- expert_ids: int32 [1536, 6], P('expert'), may hold values from 0 to 31, all different within a row; in each aligned block of 48 rows (0 to 47, 48 to 95, ...) at most 18 rows name the same one
- route_weights: float32 [1536, 6], P('expert'), may hold values from 0.05 to 0.6
- routed_gate: bfloat16 [32, 1536, 5120], P('expert', 'tensor'), may hold values from -0.078125 to 0.078125
- routed_up: bfloat16 [32, 1536, 5120], P('expert', 'tensor'), may hold values from -0.078125 to 0.078125
- routed_down: bfloat16 [32, 1536, 5120], P('expert', None, 'tensor'), may hold values from -0.15625 to 0.15625
- shared_gate: bfloat16 [5120, 3072], P('expert', 'tensor'), may hold values from -0.078125 to 0.078125
- shared_up: bfloat16 [5120, 3072], P('expert', 'tensor'), may hold values from -0.078125 to 0.078125
- shared_down: bfloat16 [3072, 5120], P('tensor', 'expert'), may hold values from -0.21875 to 0.21875
- norm_gain: float32 [5120], replicated, may hold values from 0.25 to 1.75
- proj_weight: bfloat16 [2112, 5120], P('tensor'), may hold values from -0.078125 to 0.078125
Outputs:
- stream: bfloat16 [1536, 5120], P('expert', 'tensor')
- projected: bfloat16 [1536, 2112], P('expert', 'tensor')
Inputs may be any that keep to these rules, and one draw needn't show every extreme that they name: `expert_ids`: in each aligned block of 48 tokens (those of one index of expert) no expert is chosen by more than 18 tokens, and some expert is chosen by exactly 18; a token's 6 experts differ.
All inputs are finite; a program needn't handle non-finite values.
Results may differ from a plain program's by a relative error of at most 0.019.
Values may be sent and summed in bfloat16 or wider, within the bound.
No kernel may reach another device: no remote copies, remote signals or barrier semaphores. Data moves between devices by JAX's collectives and lax.ppermute only.
A program may use at most 128 MiB of HBM per device.

v0:
```python
import jax
import jax.numpy as jnp
from jax import lax
from jax.sharding import PartitionSpec as P


def swiglu(gate, up):
    return (jax.nn.silu(gate) * up).astype(jnp.bfloat16)


def dot_rows(left, right):
    return lax.dot_general(
        left, right, (((1,), (1,)), ((), ())), preferred_element_type=jnp.float32
    )


def per_device(
    tokens,
    expert_ids,
    route_weights,
    routed_gate,
    routed_up,
    routed_down,
    shared_gate,
    shared_up,
    shared_down,
    norm_gain,
    proj_weight,
):
    tok_rows = tokens.shape[0]
    local_width = tokens.shape[1]
    top = expert_ids.shape[1]
    experts = lax.axis_size("expert")
    capacity = min(tok_rows, 2 * tok_rows * top // experts)
    features = lax.all_gather(tokens, "tensor", axis=1, tiled=True)
    flat_ids = expert_ids.reshape(-1)
    onehot = (flat_ids[:, None] == jnp.arange(experts, dtype=jnp.int32)[None, :]).astype(jnp.int32)
    slots = jnp.sum((jnp.cumsum(onehot, axis=0) - onehot) * onehot, axis=1)
    target = flat_ids * capacity + slots
    owners = jnp.repeat(jnp.arange(tok_rows, dtype=jnp.int32), top)
    sources = jnp.full((experts * capacity,), tok_rows, jnp.int32).at[target].set(owners)
    gate_w = routed_gate[0]
    up_w = routed_up[0]
    down_w = routed_down[0]
    padded = jnp.concatenate([features, jnp.zeros((1, features.shape[1]), features.dtype)], axis=0)
    outgoing = padded[sources].reshape(experts, capacity, features.shape[1])
    arrived = lax.all_to_all(outgoing, "expert", split_axis=0, concat_axis=0, tiled=True)
    count = arrived.shape[1]
    rows = arrived.reshape(-1, arrived.shape[2])
    hidden = swiglu(dot_rows(rows, gate_w), dot_rows(rows, up_w))
    hidden_all = lax.all_gather(hidden, "tensor", axis=1, tiled=True)
    result = jnp.dot(hidden_all, down_w, preferred_element_type=jnp.float32).astype(jnp.bfloat16)
    result = result.reshape(experts, count, result.shape[1])
    returned = lax.all_to_all(result, "expert", split_axis=0, concat_axis=0, tiled=True)
    flat_back = returned.reshape(experts * capacity, returned.shape[2])
    picked = flat_back[target].reshape(tok_rows, top, returned.shape[2]).astype(jnp.float32)
    routed = jnp.sum(picked * route_weights[:, :, None], axis=1)
    gate_sum = jnp.dot(
        features,
        lax.all_gather(shared_gate, "expert", axis=0, tiled=True),
        preferred_element_type=jnp.float32,
    )
    up_sum = jnp.dot(
        features,
        lax.all_gather(shared_up, "expert", axis=0, tiled=True),
        preferred_element_type=jnp.float32,
    )
    shared_hidden = swiglu(gate_sum, up_sum)
    shared_terms = jnp.dot(
        shared_hidden,
        lax.all_gather(shared_down, "expert", axis=1, tiled=True),
        preferred_element_type=jnp.float32,
    )
    rank = lax.axis_index("tensor")
    shared_full = lax.psum(shared_terms.astype(jnp.bfloat16), "tensor").astype(jnp.float32)
    shared_mine = lax.dynamic_slice_in_dim(shared_full, rank * local_width, local_width, 1)
    stream = (tokens.astype(jnp.float32) + shared_mine + routed).astype(jnp.bfloat16)
    stream_all = lax.all_gather(stream, "tensor", axis=1, tiled=True)
    values = stream_all.astype(jnp.float32)
    scale = lax.rsqrt(jnp.mean(values * values, axis=1, keepdims=True) + 1e-06)
    normed = (values * scale * norm_gain[None, :]).astype(jnp.bfloat16)
    projected = dot_rows(normed, proj_weight).astype(jnp.bfloat16)
    return (stream, projected)


def solution(mesh):
    in_specs = (
        P("expert", "tensor"),
        P("expert", None),
        P("expert", None),
        P("expert", "tensor", None),
        P("expert", "tensor", None),
        P("expert", None, "tensor"),
        P("expert", "tensor"),
        P("expert", "tensor"),
        P("tensor", "expert"),
        P(),
        P("tensor", None),
    )
    out_specs = (P("expert", "tensor"), P("expert", "tensor"))
    return jax.shard_map(
        per_device, mesh=mesh, in_specs=in_specs, out_specs=out_specs, check_vma=False
    )
```

profile of v0, /device:TPU:1, one launch (start us, length us, event | category | flops | bytes accessed | tf_op | source)
XLA Modules:
  0.0 1078.1 jit_solution(14754052590517255412)
XLA Ops:
  7.2 0.0 copy-start
  7.2 0.0 all-gather.13.cloned.1.call-start
  7.2 0.9 copy.26
  8.1 0.7 broadcast_multiply_fusion
  8.8 0.1 eq.22
  8.9 0.9 reduce-window.6
  9.8 0.2 slice_reduce_fusion
  10.1 0.1 bitcast_bitcast_fusion
  10.2 0.1 copy.25
  10.3 0.1 mul.68
  10.4 0.1 reshape.102
  10.6 2.9 scatter_custom_fusion
  13.5 29.4 %all-gather = bf16[16,320,48]{1,2,0:T(8,128)(2,1)S(1)} all-gather(bf16[1,320,48]{1,2,0:T(8,128)(2,1)} %bitcast.43), channel_id=1, replica_groups=mesh['expert'=32,'tensor'=16] {'tensor'}, dimensions={0}, use_global_device_ids=true | all-gather | bytes 522240 | tf_op jit(solution)/shard_map/all_gather | solution.py:35
  43.0 0.1 copy.24
  43.1 0.4 reshape.108
  43.6 6.0 gather_fusion
  49.6 8.5 reshape.76
  58.1 359.3 %all_to_all.10 = bf16[32,18,5120]{2,1,0:T(8,128)(2,1)} all-to-all(bf16[32,18,5120]{2,1,0:T(8,128)(2,1)} %reshape.76), channel_id=1, replica_groups=mesh['expert'=32,'tensor'=16] {'expert'}, dimensions={0} | all-to-all | bytes 11796480 | tf_op jit(solution)/shard_map/all_to_all | solution.py:47
  417.4 0.0 copy-start.2
  417.4 8.8 reshape.77
  426.2 0.0 copy-done.2
  426.2 0.0 copy-start.1
  426.2 4.8 fusion.4
  431.0 0.0 copy-done.1
  431.0 0.0 copy-done.6
  431.1 2.6 fusion
  433.7 0.0 all-gather.13.cloned.1.call-update
  433.7 0.0 all-gather.7.cloned.1.call-start
  433.8 0.7 all-gather.7.cloned.1.call-update
  434.5 0.0 all-gather.11.cloned.1.call-start
  434.5 0.7 all-gather.11.cloned.1.call-update
  435.2 0.0 all-gather.9.cloned.1.call-start
  435.3 0.5 all-gather.9.cloned.1.call-update
  435.8 51.4 %all-gather.13.cloned.1.call-done = bf16[576,1536]{0,1:T(8,128)(2,1)} async-done(((bf16[576,96]{0,1:T(8,128)(2,1)}), bf16[576,1536]{0,1:T(8,128)(2,1)}) %all-gather.13.cloned.1.call-update) | async-done | bytes 1769488 | tf_op jit(solution)/shard_map/all_gather | solution.py:51
  487.2 2.8 convolution_convert_fusion.1
  490.0 0.2 copy.29
  490.2 1.0 reshape.78
  491.3 12.3 %all-to-all-start.1 = ((bf16[32,18,320]{2,1,0:T(8,128)(2,1)}), bf16[32,18,320]{2,1,0:T(8,128)(2,1)S(1)}, u32[]{:S(2)}, u32[]{:S(2)}) async-start(bf16[32,18,320]{2,1,0:T(8,128)(2,1)} %reshape.78), calls=%async_computation.1 | async-start | bytes 1179648 | tf_op jit(solution)/shard_map/all_to_all | solution.py:54
  503.6 0.2 all-reduce.4.cloned.1.call-start
  503.8 112.2 %all-gather.7.cloned.1.call-done = bf16[5120,192]{1,0:T(8,128)(2,1)} async-done(((bf16[160,192]{1,0:T(8,128)(2,1)}), bf16[5120,192]{1,0:T(8,128)(2,1)}) %all-gather.7.cloned.1.call-update) | async-done | bytes 1966096 | tf_op jit(solution)/shard_map/all_gather | solution.py:60
  616.0 2.3 fusion.20
  618.3 0.0 copy-start.5
  618.3 122.3 %all-gather.11.cloned.1.call-done = bf16[192,5120]{0,1:T(8,128)(2,1)} async-done(((bf16[192,160]{0,1:T(8,128)(2,1)}), bf16[192,5120]{0,1:T(8,128)(2,1)}) %all-gather.11.cloned.1.call-update) | async-done | bytes 1966096 | tf_op jit(solution)/shard_map/all_gather | solution.py:71
  740.6 130.1 %all-gather.9.cloned.1.call-done = bf16[5120,192]{1,0:T(8,128)(2,1)} async-done(((bf16[160,192]{1,0:T(8,128)(2,1)}), bf16[5120,192]{1,0:T(8,128)(2,1)}) %all-gather.9.cloned.1.call-update) | async-done | bytes 1966096 | tf_op jit(solution)/shard_map/all_gather | solution.py:65
  870.7 5.2 convolution_convert_fusion
  875.9 0.0 all-reduce.4.cloned.1.call-update
  875.9 0.0 copy-done.5
  875.9 0.1 copy.30
  876.0 0.0 all-to-all-done.1
  876.1 0.2 reshape.79
  876.3 2.0 gather_fusion.1
  878.3 0.1 reshape.81
  878.4 0.2 multiply_reduce_fusion.1
  878.6 161.6 %all-reduce.4.cloned.1.call-done = bf16[48,5120]{1,0:T(8,128)(2,1)} async-done(((bf16[48,5120]{1,0:T(8,128)(2,1)}), bf16[48,5120]{1,0:T(8,128)(2,1)}) %all-reduce.4.cloned.1.call-update) | async-done | bytes 491536 | tf_op jit(solution)/shard_map/psum | solution.py:75
  1040.3 0.0 copy-done.3
  1040.3 0.9 add_convert_fusion
  1041.2 0.0 copy-start.4
  1041.2 27.8 %all-gather.1 = bf16[16,320,48]{1,2,0:T(8,128)(2,1)S(1)} all-gather(bf16[1,320,48]{1,2,0:T(8,128)(2,1)S(1)} %bitcast.44), channel_id=1, replica_groups=mesh['expert'=32,'tensor'=16] {'tensor'}, dimensions={0}, use_global_device_ids=true | all-gather | bytes 522240 | tf_op jit(solution)/shard_map/all_gather | solution.py:78
  1068.9 0.0 copy-done.4
  1068.9 0.1 copy.31
  1069.1 0.3 reshape.111
  1069.4 0.2 multiply_reduce_fusion
  1069.6 0.0 copy-done
  1069.6 2.0 convolution_convert_fusion.2
  (13 shorter events, 0.2 us)
Async XLA Ops:
  7.2 1062.5 %copy-start = (bf16[132,5120]{1,0:T(8,128)(2,1)S(1)}, bf16[132,5120]{1,0:T(8,128)(2,1)}, u32[]{:S(2)}) copy-start(bf16[132,5120]{1,0:T(8,128)(2,1)} %param.21) | copy-start | bytes 4055044
  7.2 480.0 %all-gather.13.cloned.1.call-start = ((), (), s32[]{:S(2)}) async-start(), calls=%async_computation.6 | async-start | bytes 2088960 | tf_op jit(solution)/shard_map/all_gather | solution.py:51
  417.4 8.8 copy-start.2
  426.2 4.8 copy-start.1
  426.2 4.8 copy-start.6
  433.7 182.3 %all-gather.7.cloned.1.call-start = ((), (), s32[]{:S(2)}) async-start(), calls=%async_computation.2 | async-start | bytes 2703360 | tf_op jit(solution)/shard_map/all_gather | solution.py:60
  434.5 306.1 %all-gather.11.cloned.1.call-start = ((), (), s32[]{:S(2)}) async-start(), calls=%async_computation.4 | async-start | bytes 2703360 | tf_op jit(solution)/shard_map/all_gather | solution.py:71
  435.2 435.5 %all-gather.9.cloned.1.call-start = ((), (), s32[]{:S(2)}) async-start(), calls=%async_computation.3 | async-start | bytes 2703360 | tf_op jit(solution)/shard_map/all_gather | solution.py:65
  491.3 384.8 %all-to-all-start.1 = ((bf16[32,18,320]{2,1,0:T(8,128)(2,1)}), bf16[32,18,320]{2,1,0:T(8,128)(2,1)S(1)}, u32[]{:S(2)}, u32[]{:S(2)}) async-start(bf16[32,18,320]{2,1,0:T(8,128)(2,1)} %reshape.78), calls=%async_computation.1 | async-start | bytes 1179648 | tf_op jit(solution)/shard_map/all_to_all | solution.py:54
  503.6 536.7 %all-reduce.4.cloned.1.call-start = ((), (), s32[]{:S(2)}) async-start(), calls=%async_computation.5 | async-start | bytes 983040 | tf_op jit(solution)/shard_map/psum | solution.py:75
  618.3 257.7 %copy-start.5 = (f32[48,6]{0,1:T(8,128)S(1)}, f32[48,6]{0,1:T(8,128)}, u32[]{:S(2)}) copy-start(f32[48,6]{0,1:T(8,128)} %param.13) | copy-start | bytes 3460
  875.9 164.4 %copy-start.3 = (bf16[48,320]{1,0:T(8,128)(2,1)S(1)}, bf16[48,320]{1,0:T(8,128)(2,1)}, u32[]{:S(2)}) copy-start(bf16[48,320]{1,0:T(8,128)(2,1)} %param.11) | copy-start | bytes 92164
  1041.2 27.8 %copy-start.4 = (bf16[48,320]{1,0:T(8,128)(2,1)}, bf16[48,320]{1,0:T(8,128)(2,1)S(1)}, u32[]{:S(2)}) copy-start(bf16[48,320]{1,0:T(8,128)(2,1)S(1)} %add_convert_fusion) | copy-start | bytes 92164
Sparse Core Ops, SparseCore 0:
  433.8 53.3 all-gather.12
  489.3 126.6 all-gather.6
  618.1 122.4 all-gather.10
  742.5 128.1 all-gather.8
  876.1 164.1 all-reduce.3
where the time goes:
time: 1080 us
  waiting for transfers between devices  580 us (54%)
  blocking collectives  416 us (39%)
  local copies, waits for them, and re-layouts  32.6 us (3%)
  matrix products  19.7 us (2%)
  between operations  14 us (1%)
  starting transfers between devices  12.7 us (1%)
    all_to_all x1, blocking collectives, per_device(): lax.all_to_all(outgoing, 'expert', split_axis=0, concat_axis=0, tiled=True)  359 us
    psum x1, waiting for transfers between devices, per_device(): lax.psum(shared_terms.astype(jnp.bfloat16), 'tensor').astype(jnp.float32)  162 us
    all_gather x1, waiting for transfers between devices, per_device(): lax.all_gather(shared_up, 'expert', axis=0, tiled=True)  130 us
    all_gather x1, waiting for transfers between devices, per_device(): lax.all_gather(shared_down, 'expert', axis=1, tiled=True)  122 us
    all_gather x1, waiting for transfers between devices, per_device(): lax.all_gather(shared_gate, 'expert', axis=0, tiled=True)  112 us
    all_gather x1, waiting for transfers between devices, per_device(): hidden_all = lax.all_gather(hidden, 'tensor', axis=1, tiled=True)  51.4 us
    all_gather x1, blocking collectives, per_device(): features = lax.all_gather(tokens, 'tensor', axis=1, tiled=True)  29.4 us
    all_gather x1, blocking collectives, per_device(): stream_all = lax.all_gather(stream, 'tensor', axis=1, tiled=True)  27.8 us
  transfers between devices with their start and end apart: 6, of which 5 were waited for; matrix products, arithmetic and copies ran while one was open for 1% of the time, Pallas kernels for 0%

commit v1 on v0

v1 whole, which is shorter than its diff:
```python
import jax
import jax.numpy as jnp
from jax import lax
from jax.sharding import PartitionSpec as P

ROWS = 16
CHIPS = 8
LANES = [[x * ROWS + z for z in range(ROWS)] for x in range(2)]
SIDES = [[2 * chip + core for chip in range(CHIPS)] for core in range(2)]


def dot(left, right, over_left, over_right):
    return lax.dot_general(
        left, right, (((over_left,), (over_right,)), ((), ())), preferred_element_type=jnp.float32
    )


def exchange(parts, axis, groups=None):
    return lax.all_to_all(
        parts, axis, split_axis=0, concat_axis=0, tiled=True, axis_index_groups=groups
    )


def gather_halves(block):
    mine = exchange(jnp.broadcast_to(block[None], (CHIPS,) + block.shape), "tensor", SIDES)
    theirs = lax.ppermute(mine, "tensor", [(i, i ^ 1) for i in range(2 * CHIPS)])
    return mine, theirs


def per_device(
    tokens,
    expert_ids,
    route_weights,
    routed_gate,
    routed_up,
    routed_down,
    shared_gate,
    shared_up,
    shared_down,
    norm_gain,
    proj_weight,
):
    tok, width = tokens.shape
    top = expert_ids.shape[1]
    experts = lax.axis_size("expert")
    cap = min(tok, 2 * tok * top // experts)
    slots = experts * cap
    bf16, f32 = jnp.bfloat16, jnp.float32
    side = lax.axis_index("tensor") % 2
    column = lax.axis_index("expert") // ROWS

    own = jnp.concatenate([shared_gate, shared_up, shared_down.T], axis=1)
    other = lax.ppermute(own, "expert", [(i, (i + ROWS) % (2 * ROWS)) for i in range(2 * ROWS)])
    pair = jnp.where(column == 0, jnp.stack([own, other]), jnp.stack([other, own]))
    gathered = lax.all_gather(pair, "expert", axis=0, axis_index_groups=LANES)

    match = expert_ids[:, :, None] == jnp.arange(experts, dtype=jnp.int32)[None, None, :]
    named = jnp.any(match, axis=1)
    weight = jnp.sum(jnp.where(match, route_weights[:, :, None], 0.0), axis=1)
    earlier = jnp.tril(jnp.ones((tok, tok), f32), -1)
    slot = jnp.dot(earlier, named.astype(f32)).astype(jnp.int32)
    chosen = named[:, :, None] & (
        slot[:, :, None] == jnp.arange(cap, dtype=jnp.int32)[None, None, :]
    )
    chosen = chosen.reshape(tok, slots)
    outgoing = dot(chosen.astype(bf16), tokens, 0, 0).astype(bf16)
    arrived = exchange(outgoing.reshape(experts, cap, width), "expert")
    rows = jnp.concatenate([arrived.reshape(slots, width), tokens], axis=0)

    def by_side(array, axis):
        size = array.shape[axis] // (2 * CHIPS)
        pieces = [lax.slice_in_dim(array, k * size, (k + 1) * size, axis=axis) for k in range(2 * CHIPS)]
        even, odd = (jnp.concatenate(pieces[k::2], axis=axis) for k in range(2))
        return jnp.where(side == 0, even, odd), jnp.where(side == 0, odd, even)

    gate_up = jnp.concatenate([routed_gate[0], routed_up[0]], axis=0)
    hid = routed_gate.shape[1]
    in_mine, in_theirs = by_side(gate_up, 1)
    out_mine, out_theirs = by_side(routed_down[0], 0)

    mine, theirs = gather_halves(rows.T)
    total = slots + tok
    both = dot(in_mine, mine.reshape(-1, total), 1, 0) + dot(in_theirs, theirs.reshape(-1, total), 1, 0)
    hidden = (jax.nn.silu(both[:hid, :slots]) * both[hid:, :slots]).astype(bf16)
    hidden_mine, hidden_theirs = gather_halves(hidden)
    result = dot(hidden_mine.reshape(-1, slots), out_mine, 0, 0) + dot(
        hidden_theirs.reshape(-1, slots), out_theirs, 0, 0
    )
    returned = exchange(result.astype(bf16).reshape(experts, cap, width), "expert")
    scaled = jnp.where(chosen, jnp.repeat(weight, cap, axis=1), 0.0)
    high = lax.reduce_precision(scaled, 8, 7)
    split = jnp.concatenate([high, scaled - high], axis=0).astype(bf16)
    terms = dot(split, returned.reshape(slots, width), 1, 0)
    routed = terms[:tok] + terms[tok:]

    half_mine, half_theirs = mine[:, :, slots:], theirs[:, :, slots:]
    even = jnp.where(side == 0, half_mine, half_theirs)
    odd = jnp.where(side == 0, half_theirs, half_mine)
    features = jnp.stack([even, odd], axis=1).reshape(2, ROWS, -1, tok)
    features = jnp.swapaxes(features, 0, 1).reshape(-1, tok)
    table = gathered.reshape(-1, gathered.shape[-1])
    inner = shared_gate.shape[1]
    sums = dot(features, table[:, : 2 * inner], 0, 0)
    shared_hidden = (jax.nn.silu(sums[:, :inner]) * sums[:, inner:]).astype(bf16)
    partial = dot(shared_hidden, table[:, 2 * inner :], 1, 1).astype(bf16)
    partial = partial.reshape(tok, ROWS, 2, -1)
    partial = jnp.transpose(partial, (2, 1, 0, 3)).reshape(2 * CHIPS, 2, tok, -1)
    partial = jnp.concatenate([partial[:, 0], partial[:, 1]], axis=2)
    shared = jnp.sum(exchange(partial, "tensor").astype(f32), axis=0)

    stream = (tokens.astype(f32) + shared + routed).astype(bf16)
    spread = exchange(jnp.broadcast_to(stream[None], (2 * CHIPS,) + stream.shape), "tensor")
    values = jnp.swapaxes(spread, 0, 1).reshape(tok, -1).astype(f32)
    scale = lax.rsqrt(jnp.mean(values * values, axis=1, keepdims=True) + 1e-06)
    normed = (values * scale * norm_gain[None, :]).astype(bf16)
    projected = dot(normed, proj_weight, 1, 1).astype(bf16)
    return (stream, projected)


def solution(mesh):
    in_specs = (
        P("expert", "tensor"),
        P("expert", None),
        P("expert", None),
        P("expert", "tensor", None),
        P("expert", "tensor", None),
        P("expert", None, "tensor"),
        P("expert", "tensor"),
        P("expert", "tensor"),
        P("tensor", "expert"),
        P(),
        P("tensor", None),
    )
    out_specs = (P("expert", "tensor"), P("expert", "tensor"))
    return jax.shard_map(
        per_device, mesh=mesh, in_specs=in_specs, out_specs=out_specs, check_vma=False
    )
```

time: 1080 us -> 255 us (0.24)
  waiting for transfers between devices: 580 us -> 29.3 us
  blocking collectives: 416 us -> 133 us
  starting transfers between devices: 12.7 us -> 25.9 us
    all_gather x4 -> x1, waiting for transfers between devices: 416 us -> 0.02 us  [per_device(): gathered = lax.all_gather(pair, 'expert', axis=0, axis_index_groups=LANES)]
    all_to_all x1 -> x4, blocking collectives: 359 us -> 133 us  [exchange(): lax.all_to_all(parts, axis, split_axis=0, concat_axis=0, tiled=True, axis...]
    psum x1 -> x0, waiting for transfers between devices: 162 us -> none  [per_device(): lax.psum(shared_terms.astype(jnp.bfloat16), 'tensor').astype(jnp.float32)]
    all_gather x2 -> x0, blocking collectives: 57.2 us -> none  [the longest x1 29.4 us: per_device(): features = lax.all_gather(tokens, 'tensor', axis=1, tiled=True)]
    all_to_all x1 -> x2, waiting for transfers between devices: 0.01 us -> 28.1 us  [exchange(): lax.all_to_all(parts, axis, split_axis=0, concat_axis=0, tiled=True, axis...]
    ppermute x0 -> x3, starting transfers between devices: none -> 14.3 us  [the longest x2 10.4 us: gather_halves(): lax.ppermute(mine, 'tensor', [(i, i ^ 1) for i in range(2 * CHIPS)])]
    reshape x5 -> x9, local copies, waits for them, and re-layouts: 18.7 us -> 4.97 us  [the longest x2 1.35 us: per_device(): partial = partial.reshape(tok, ROWS, 2, -1)]
  transfers between devices with their start and end apart: 6 -> 6, of which waited for: 5 -> 3; matrix products, arithmetic and copies ran while one was open for 1% -> 17% of each run, Pallas kernels for 0% -> 0%
where the time goes in v1:
time: 255 us; the launch traced here: 253 us
  blocking collectives  133 us (52%)
  waiting for transfers between devices  29.3 us (11%)
  starting transfers between devices  25.9 us (10%)
  local copies, waits for them, and re-layouts  22.5 us (9%)
  matrix products  17.8 us (7%)
  between operations  14.6 us (6%)
  other arithmetic  10.4 us (4%)
    all_to_all x4, blocking collectives, exchange(): lax.all_to_all(parts, axis, split_axis=0, concat_axis=0, tiled=True, axis...  133 us
    all_to_all x2, waiting for transfers between devices, exchange(): lax.all_to_all(parts, axis, split_axis=0, concat_axis=0, tiled=True, axis...  28.1 us
    dot_general x9, matrix products, dot(): lax.dot_general(left, right, (((over_left,), (over_right,)), ((), ())), p...  17.6 us
    all_to_all x2, starting transfers between devices, exchange(): lax.all_to_all(parts, axis, split_axis=0, concat_axis=0, tiled=True, axis...  11.5 us
    ppermute x2, starting transfers between devices, gather_halves(): lax.ppermute(mine, 'tensor', [(i, i ^ 1) for i in range(2 * CHIPS)])  10.4 us
    concatenate x4, local copies, waits for them, and re-layouts, by_side(): even, odd = (jnp.concatenate(pieces[k::2], axis=axis) for k in range(2))  7.96 us
  transfers between devices with their start and end apart: 6, of which 3 were waited for; matrix products, arithmetic and copies ran while one was open for 17% of the time, Pallas kernels for 0%

profile of v1, /device:TPU:1, one launch (start us, length us, event | category | flops | bytes accessed | tf_op | source)
XLA Modules:
  0.0 253.2 jit_solution(7509496442934745222)
XLA Ops:
  7.2 1.2 pad_maximum_fusion.2
  8.4 3.9 %collective-permute-start.1 = (bf16[160,576]{1,0:T(8,128)(2,1)S(1)}, bf16[160,576]{1,0:T(8,128)(2,1)S(1)}, u32[]{:S(2)}, u32[]{:S(2)}) collective-permute-start(bf16[160,576]{1,0:T(8,128)(2,1)S(1)} %pad_maximum_fusion.2), channel_id=1, source_target_pairs={{0,256},{16,272},{32,288},{48,304},{64,320},{80,336},{96,352},{112... | collective-permute-start | bytes 552968 | tf_op jit(solution)/shard_map/ppermute | solution.py:53
  12.4 1.1 fusion.62
  13.5 0.7 fusion.38
  14.2 0.2 convolution_convert_fusion.3
  14.4 1.1 collective-permute-done.1
  15.5 0.8 maximum_select_fusion
  16.7 0.1 eq.53
  16.8 0.8 reduce-precision_convert_fusion
  17.6 0.6 copy-done.7
  18.2 0.3 convolution_convert_fusion.1
  18.5 0.2 copy.48
  18.8 0.2 reshape.144
  19.0 54.3 %all_to_all.30 = bf16[32,18,320]{2,1,0:T(8,128)(2,1)S(1)} all-to-all(bf16[32,18,320]{2,1,0:T(8,128)(2,1)S(1)} %reshape.144), channel_id=1, replica_groups=mesh['expert'=32,'tensor'=16] {'expert'}, dimensions={0} | all-to-all | bytes 737280 | tf_op jit(solution)/shard_map/all_to_all | solution.py:19
  73.3 0.2 reshape.145
  73.6 0.2 copy.49
  73.8 0.3 broadcast_in_dim.32
  74.1 42.8 %all_to_all.31 = bf16[8,320,624]{2,1,0:T(8,128)(2,1)} all-to-all(bf16[8,320,624]{2,1,0:T(8,128)(2,1)S(1)} %broadcast_in_dim.32), channel_id=1, replica_groups={{0,2,4,6,8,10,12,14},{1,3,5,7,9,11,13,15},{16,18,20,22,24,26,28,30},{17..., dimensions={0} | all-to-all | bytes 6389760 | tf_op jit(solution)/shard_map/all_to_all | solution.py:19
  116.9 7.7 %collective-permute-start = (bf16[8,320,624]{2,1,0:T(8,128)(2,1)}, bf16[8,320,624]{2,1,0:T(8,128)(2,1)}, u32[]{:S(2)}, u32[]{:S(2)}) collective-permute-start(bf16[8,320,624]{2,1,0:T(8,128)(2,1)} %all_to_all.31), channel_id=1, source_target_pairs={{0,1},{1,0},{2,3},{3,2},{4,5},{5,4},{6,7},{7,6},{8,9},{9,8},{10,11... | collective-permute-start | bytes 9584648 | tf_op jit(solution)/shard_map/ppermute | solution.py:26
  124.6 1.1 pad_maximum_fusion.3
  125.7 3.2 %concatenate.47 = bf16[192,2560]{1,0:T(8,128)(2,1)} concatenate(bf16[192,320]{1,0:T(8,128)(2,1)} %get-tuple-element.5, bf16[192,320]{1,0:T(8,128)(2,1)} %get-tuple-element.6, bf16[192,320]{1,0:T(8,128)(2,1)} %get-tuple-element.7, bf16[192,320]{1,0:T(8,128)(2,1)} %get-tuple-element.8, bf16[192,320]{1,0:T(8,128)(2,1)} %get-tuple-element.9, bf16[192,320]{1,0:T(8,128)(2,1)} %get-tuple-element.10, ...), dimensions={1} | concatenate | bytes 1966080 | tf_op jit(solution)/shard_map/concatenate | solution.py:73
  129.0 1.4 fusion.19
  130.4 2.3 concatenate.48
  132.7 2.9 %fusion.6 = f32[192,624]{1,0:T(8,128)S(1)} fusion(bf16[2560,624]{1,0:T(8,128)(2,1)} %bitcast.15, bf16[192,2560]{1,0:T(8,128)(2,1)S(1)} %copy-done.6, bf16[192,2560]{1,0:T(8,128)(2,1)S(1)} %concatenate.48, pred[]{:T(512)S(6)} %eq.46), kind=kOutput, calls=%fused_computation.46 | convolution fusion | flops 613908480 | bytes 5640193 | tf_op jit(solution)/shard_map/dot_general | solution.py:13
  135.6 2.9 %convolution_add_fusion.1 = f32[192,624]{1,0:T(8,128)S(1)} fusion(f32[192,624]{1,0:T(8,128)S(1)} %fusion.6, bf16[2560,624]{1,0:T(8,128)(2,1)} %bitcast.16, bf16[192,2560]{1,0:T(8,128)(2,1)S(1)} %concatenate.48, bf16[192,2560]{1,0:T(8,128)(2,1)S(1)} %copy-done.6, pred[]{:T(512)S(6)} %eq.46), kind=kOutput, calls=%fused_computation.39 | convolution fusion | flops 614028288 | bytes 6119425 | tf_op jit(solution)/shard_map/dot_general | solution.py:13
  138.6 0.1 broadcast_in_dim.59
  138.7 19.2 %all_to_all.32 = bf16[8,96,576]{2,1,0:T(8,128)(2,1)S(1)} all-to-all(bf16[8,96,576]{2,1,0:T(8,128)(2,1)S(1)} %broadcast_in_dim.59), channel_id=1, replica_groups={{0,2,4,6,8,10,12,14},{1,3,5,7,9,11,13,15},{16,18,20,22,24,26,28,30},{17..., dimensions={0} | all-to-all | bytes 1769472 | tf_op jit(solution)/shard_map/all_to_all | solution.py:19
  157.8 2.7 %collective-permute-start.2 = (bf16[8,96,576]{2,1,0:T(8,128)(2,1)S(1)}, bf16[8,96,576]{2,1,0:T(8,128)(2,1)}, u32[]{:S(2)}, u32[]{:S(2)}) collective-permute-start(bf16[8,96,576]{2,1,0:T(8,128)(2,1)S(1)} %all_to_all.32), channel_id=1, source_target_pairs={{0,1},{1,0},{2,3},{3,2},{4,5},{5,4},{6,7},{7,6},{8,9},{9,8},{10,11... | collective-permute-start | bytes 2654216 | tf_op jit(solution)/shard_map/ppermute | solution.py:26
  160.6 1.2 slice_bitcast_fusion.2
  161.8 1.2 concatenate.49
  163.0 1.3 concatenate.50
  164.2 0.6 fusion.13
  164.9 1.8 fusion.3
  166.7 0.2 copy.56
  166.9 1.0 reshape.156
  167.9 7.1 %all-to-all-start.4 = ((bf16[32,18,320]{2,1,0:T(8,128)(2,1)}), bf16[32,18,320]{2,1,0:T(8,128)(2,1)S(1)}, u32[]{:S(2)}, u32[]{:S(2)}) async-start(bf16[32,18,320]{2,1,0:T(8,128)(2,1)} %reshape.156), calls=%async_computation.4 | async-start | bytes 1179648 | tf_op jit(solution)/shard_map/all_to_all | solution.py:19
  175.0 1.3 slice.240
  176.3 0.3 copy.58
  176.6 1.3 slice.241
  178.0 0.3 copy.59
  178.3 0.1 pad_maximum_fusion
  178.4 0.5 copy.52
  178.9 0.8 reshape.146
  179.7 0.8 copy.53
  180.5 1.2 reshape.147
  181.7 2.8 %fusion = f32[48,384]{1,0:T(8,128)S(1)} fusion(bf16[5120,48]{0,1:T(8,128)(2,1)S(1)} %reshape.147, bf16[5120,576]{1,0:T(8,128)(2,1)} %bitcast.88), kind=kOutput, calls=%fused_computation.31 | convolution fusion | flops 188743680 | bytes 4497408 | tf_op jit(solution)/shard_map/dot_general | solution.py:13
  184.5 2.6 %convolution_convert_fusion = bf16[48,5120]{1,0:T(8,128)(2,1)S(1)} fusion(bf16[5120,576]{1,0:T(8,128)(2,1)} %bitcast.89, f32[48,384]{1,0:T(8,128)S(1)} %fusion), kind=kOutput, calls=%fused_computation | convolution fusion | flops 94672896 | bytes 3211264 | tf_op jit(solution)/shard_map/dot_general | solution.py:13
  187.2 0.9 reshape.149
  188.1 0.4 copy.54
  188.6 1.0 pad_maximum_fusion.1
  189.7 18.3 %all-to-all-done.4 = bf16[32,18,320]{2,1,0:T(8,128)(2,1)S(1)} async-done(((bf16[32,18,320]{2,1,0:T(8,128)(2,1)}), bf16[32,18,320]{2,1,0:T(8,128)(2,1)S(1)}, u32[]{:S(2)}, u32[]{:S(2)}) %all-to-all-start.4) | async-done | bytes 368672 | tf_op jit(solution)/shard_map/all_to_all | solution.py:19
  208.0 4.4 %all-to-all-start.2 = ((bf16[16,48,320]{2,1,0:T(8,128)(2,1)}), bf16[16,48,320]{2,1,0:T(8,128)(2,1)S(1)}, u32[]{:S(2)}, u32[]{:S(2)}) async-start(bf16[16,48,320]{2,1,0:T(8,128)(2,1)} %pad_maximum_fusion.1), calls=%async_computation.2 | async-start | bytes 1179648 | tf_op jit(solution)/shard_map/all_to_all | solution.py:19
  212.4 0.7 fusion.17
  213.1 0.2 reshape.157
  213.4 1.3 fusion.34
  214.7 9.8 %all-to-all-done.2 = bf16[16,48,320]{2,1,0:T(8,128)(2,1)S(1)} async-done(((bf16[16,48,320]{2,1,0:T(8,128)(2,1)}), bf16[16,48,320]{2,1,0:T(8,128)(2,1)S(1)}, u32[]{:S(2)}, u32[]{:S(2)}) %all-to-all-start.2) | async-done | bytes 491552 | tf_op jit(solution)/shard_map/all_to_all | solution.py:19
  224.5 0.1 convert_reduce_fusion
  224.6 0.8 fusion.40
  225.4 16.4 %all_to_all.33 = bf16[16,48,320]{2,1,0:T(8,128)(2,1)S(1)} all-to-all(bf16[16,48,320]{2,1,0:T(8,128)(2,1)S(1)} %broadcast_in_dim.60), channel_id=1, replica_groups=mesh['expert'=32,'tensor'=16] {'tensor'}, dimensions={0} | all-to-all | bytes 983040 | tf_op jit(solution)/shard_map/all_to_all | solution.py:19
  241.8 0.1 convert_bitcast_fusion
  241.9 0.4 copy.57
  242.3 1.3 reshape.158
  243.6 0.2 fusion.4
  243.9 2.4 convolution_convert_fusion.2
  (49 shorter events, 0.7 us)
Async XLA Ops:
  7.2 236.7 %copy-start = (bf16[132,5120]{1,0:T(8,128)(2,1)S(1)}, bf16[132,5120]{1,0:T(8,128)(2,1)}, u32[]{:S(2)}) copy-start(bf16[132,5120]{1,0:T(8,128)(2,1)} %param.21) | copy-start | bytes 4055044
  7.2 9.2 %copy-start.13 = (s32[48,6]{0,1:T(8,128)S(1)}, s32[48,6]{0,1:T(8,128)}, u32[]{:S(2)}) copy-start(s32[48,6]{0,1:T(8,128)} %param.12) | copy-start | bytes 3460
  7.2 9.2 %copy-start.14 = (f32[48,6]{0,1:T(8,128)S(1)}, f32[48,6]{0,1:T(8,128)}, u32[]{:S(2)}) copy-start(f32[48,6]{0,1:T(8,128)} %param.13) | copy-start | bytes 3460
  7.2 174.5 %all-gather.2.cloned.1.call-start = ((), (), s32[]{:S(2)}) async-start(), calls=%async_computation.6 | async-start | bytes 6963200 | tf_op jit(solution)/shard_map/all_gather | solution.py:55
  8.4 7.1 %collective-permute-start.1 = (bf16[160,576]{1,0:T(8,128)(2,1)S(1)}, bf16[160,576]{1,0:T(8,128)(2,1)S(1)}, u32[]{:S(2)}, u32[]{:S(2)}) collective-permute-start(bf16[160,576]{1,0:T(8,128)(2,1)S(1)} %pad_maximum_fusion.2), channel_id=1, source_target_pairs={{0,256},{16,272},{32,288},{48,304},{64,320},{80,336},{96,352},{112... | collective-permute-start | bytes 552968 | tf_op jit(solution)/shard_map/ppermute | solution.py:53
  16.3 1.9 copy-start.10
  16.5 2.5 copy-start.3
  17.6 0.6 copy-start.7
  74.1 50.5 %copy-start.1 = (bf16[1,96,5120]{2,1,0:T(8,128)(2,1)S(1)}, bf16[1,96,5120]{2,1,0:T(8,128)(2,1)}, u32[]{:S(2)}) copy-start(bf16[1,96,5120]{2,1,0:T(8,128)(2,1)} %param.15) | copy-start | bytes 2949124
  74.1 50.5 %copy-start.2 = (bf16[1,96,5120]{2,1,0:T(8,128)(2,1)S(1)}, bf16[1,96,5120]{2,1,0:T(8,128)(2,1)}, u32[]{:S(2)}) copy-start(bf16[1,96,5120]{2,1,0:T(8,128)(2,1)} %param.14) | copy-start | bytes 2949124
  116.9 18.7 %collective-permute-start = (bf16[8,320,624]{2,1,0:T(8,128)(2,1)}, bf16[8,320,624]{2,1,0:T(8,128)(2,1)}, u32[]{:S(2)}, u32[]{:S(2)}) collective-permute-start(bf16[8,320,624]{2,1,0:T(8,128)(2,1)} %all_to_all.31), channel_id=1, source_target_pairs={{0,1},{1,0},{2,3},{3,2},{4,5},{5,4},{6,7},{7,6},{8,9},{9,8},{10,11... | collective-permute-start | bytes 9584648 | tf_op jit(solution)/shard_map/ppermute | solution.py:26
  130.4 2.3 copy-start.6
  138.5 22.1 %copy-start.5 = (bf16[1,1536,320]{1,2,0:T(8,128)(2,1)S(1)}, bf16[1,1536,320]{1,2,0:T(8,128)(2,1)}, u32[]{:S(2)}) copy-start(bf16[1,1536,320]{1,2,0:T(8,128)(2,1)} %param.16) | copy-start | bytes 2949124
  157.8 7.0 %collective-permute-start.2 = (bf16[8,96,576]{2,1,0:T(8,128)(2,1)S(1)}, bf16[8,96,576]{2,1,0:T(8,128)(2,1)}, u32[]{:S(2)}, u32[]{:S(2)}) collective-permute-start(bf16[8,96,576]{2,1,0:T(8,128)(2,1)S(1)} %all_to_all.32), channel_id=1, source_target_pairs={{0,1},{1,0},{2,3},{3,2},{4,5},{5,4},{6,7},{7,6},{8,9},{9,8},{10,11... | collective-permute-start | bytes 2654216 | tf_op jit(solution)/shard_map/ppermute | solution.py:26
  167.9 40.1 %all-to-all-start.4 = ((bf16[32,18,320]{2,1,0:T(8,128)(2,1)}), bf16[32,18,320]{2,1,0:T(8,128)(2,1)S(1)}, u32[]{:S(2)}, u32[]{:S(2)}) async-start(bf16[32,18,320]{2,1,0:T(8,128)(2,1)} %reshape.156), calls=%async_computation.4 | async-start | bytes 1179648 | tf_op jit(solution)/shard_map/all_to_all | solution.py:19
  188.5 23.9 %copy-start.4 = (f32[48,576]{0,1:T(8,128)S(1)}, f32[48,576]{0,1:T(8,128)}, u32[]{:S(2)}) copy-start(f32[48,576]{0,1:T(8,128)} %copy-done.3) | copy-start | bytes 331780
  188.5 23.9 %copy-start.8 = (pred[48,576]{0,1:T(32,128)(4,1)S(1)}, pred[48,576]{0,1:T(32,128)(4,1)}, u32[]{:S(2)}) copy-start(pred[48,576]{0,1:T(32,128)(4,1)} %copy-done.7) | copy-start | bytes 82948
  188.6 24.8 %copy-start.9 = (bf16[48,576]{0,1:T(8,128)(2,1)S(1)}, bf16[48,576]{0,1:T(8,128)(2,1)}, u32[]{:S(2)}) copy-start(bf16[48,576]{0,1:T(8,128)(2,1)} %get-tuple-element.2) | copy-start | bytes 165892
  208.0 16.5 %all-to-all-start.2 = ((bf16[16,48,320]{2,1,0:T(8,128)(2,1)}), bf16[16,48,320]{2,1,0:T(8,128)(2,1)S(1)}, u32[]{:S(2)}, u32[]{:S(2)}) async-start(bf16[16,48,320]{2,1,0:T(8,128)(2,1)} %pad_maximum_fusion.1), calls=%async_computation.2 | async-start | bytes 1179648 | tf_op jit(solution)/shard_map/all_to_all | solution.py:19
  225.4 16.9 %copy-start.11 = (bf16[48,320]{1,0:T(8,128)(2,1)}, bf16[48,320]{1,0:T(8,128)(2,1)S(1)}, u32[]{:S(2)}) copy-start(bf16[48,320]{1,0:T(8,128)(2,1)S(1)} %fusion.40) | copy-start | bytes 92164
  242.3 1.6 copy-start.12
Sparse Core Ops, SparseCore 0:
  16.5 114.4 all-gather.1

commit v2 on v1

--- a/solution.py
+++ b/solution.py
@@ -1,9 +1,11 @@
 import jax
 import jax.numpy as jnp
+import numpy as np
 from jax import lax
 from jax.sharding import PartitionSpec as P
 
 ROWS = 16
+PACK = 48
 CHIPS = 8
 LANES = [[x * ROWS + z for z in range(ROWS)] for x in range(2)]
 SIDES = [[2 * chip + core for chip in range(CHIPS)] for core in range(2)]
@@ -27,6 +29,19 @@
     return mine, theirs
 
 
+def packed(rows):
+    half = rows.shape[1] // 2
+    tail = jnp.concatenate([rows[:, :half, 256:], rows[:, half:, 256:]], axis=2)
+    flat = jnp.concatenate([rows[:, :, :128], rows[:, :, 128:256], tail], axis=1)
+    return jnp.pad(flat, ((0, 0), (0, PACK - flat.shape[1]), (0, 0)))
+
+
+def unpacked(flat, cap):
+    tail = flat[:, 2 * cap : 2 * cap + cap // 2]
+    tail = jnp.concatenate([tail[:, :, :64], tail[:, :, 64:]], axis=1)
+    return jnp.concatenate([flat[:, :cap], flat[:, cap : 2 * cap], tail], axis=2)
+
+
 def per_device(
     tokens,
     expert_ids,
@@ -46,26 +61,42 @@
     cap = min(tok, 2 * tok * top // experts)
     slots = experts * cap
     bf16, f32 = jnp.bfloat16, jnp.float32
-    side = lax.axis_index("tensor") % 2
-    column = lax.axis_index("expert") // ROWS
-
-    own = jnp.concatenate([shared_gate, shared_up, shared_down.T], axis=1)
-    other = lax.ppermute(own, "expert", [(i, (i + ROWS) % (2 * ROWS)) for i in range(2 * ROWS)])
-    pair = jnp.where(column == 0, jnp.stack([own, other]), jnp.stack([other, own]))
-    gathered = lax.all_gather(pair, "expert", axis=0, axis_index_groups=LANES)
+    rank = lax.axis_index("tensor")
+    side, across, ring = rank & 1, (rank >> 1) & 1, rank >> 2
+    column = lax.axis_index("expert") >> 4
 
     match = expert_ids[:, :, None] == jnp.arange(experts, dtype=jnp.int32)[None, None, :]
     named = jnp.any(match, axis=1)
     weight = jnp.sum(jnp.where(match, route_weights[:, :, None], 0.0), axis=1)
-    earlier = jnp.tril(jnp.ones((tok, tok), f32), -1)
-    slot = jnp.dot(earlier, named.astype(f32)).astype(jnp.int32)
-    chosen = named[:, :, None] & (
-        slot[:, :, None] == jnp.arange(cap, dtype=jnp.int32)[None, None, :]
+    earlier = jnp.tril(jnp.ones((tok, tok), bf16), -1)
+    slot = jnp.where(named, jnp.dot(earlier, named.astype(bf16), preferred_element_type=f32), -2.0)
+    place = np.arange(experts * PACK)
+    row = place % PACK
+    spread = jnp.asarray(place[None, :] // PACK == np.arange(experts)[:, None], bf16)
+    tail = (row >= 2 * cap) & (row < 2 * cap + cap // 2)
+    held = np.stack(
+        [
+            np.where(row < cap, row, -1),
+            np.where((row >= cap) & (row < 2 * cap), row - cap, -1),
+            np.where(tail, row - 2 * cap, -1),
+            np.where(tail, row - 2 * cap + cap // 2, -1),
+        ]
     )
-    chosen = chosen.reshape(tok, slots)
-    outgoing = dot(chosen.astype(bf16), tokens, 0, 0).astype(bf16)
-    arrived = exchange(outgoing.reshape(experts, cap, width), "expert")
-    rows = jnp.concatenate([arrived.reshape(slots, width), tokens], axis=0)
+    wide = jnp.dot(slot.astype(bf16), spread, preferred_element_type=f32).astype(bf16)
+    chosen = wide[None] == jnp.asarray(held, bf16)[:, None, :]
+    chosen = chosen.reshape(4 * tok, -1)
+    blank = jnp.zeros((tok, 64), bf16)
+    lanes = jnp.concatenate(
+        [
+            tokens[:, :128],
+            tokens[:, 128:256],
+            jnp.concatenate([tokens[:, 256:], blank], axis=1),
+            jnp.concatenate([blank, tokens[:, 256:]], axis=1),
+        ],
+        axis=0,
+    )
+    outgoing = dot(chosen.astype(bf16), lanes, 0, 0).astype(bf16)
+    arrived = exchange(outgoing.reshape(experts, PACK, 128), "expert")
 
     def by_side(array, axis):
         size = array.shape[axis] // (2 * CHIPS)
@@ -78,6 +109,16 @@
     in_mine, in_theirs = by_side(gate_up, 1)
     out_mine, out_theirs = by_side(routed_down[0], 0)
 
+    own = jnp.concatenate([shared_gate, shared_up, shared_down.T], axis=1)
+    other = lax.ppermute(own, "expert", [(i, (i + ROWS) % (2 * ROWS)) for i in range(2 * ROWS)])
+    pair = jnp.where(column == 0, jnp.stack([own, other]), jnp.stack([other, own]))
+    arrived, pair, in_mine, in_theirs, out_mine, out_theirs = lax.optimization_barrier(
+        (arrived, pair, in_mine, in_theirs, out_mine, out_theirs)
+    )
+    gathered = lax.all_gather(pair, "expert", axis=0, axis_index_groups=LANES)
+
+    rows = unpacked(arrived, cap).reshape(slots, width)
+    rows = jnp.concatenate([rows, tokens], axis=0)
     mine, theirs = gather_halves(rows.T)
     total = slots + tok
     both = dot(in_mine, mine.reshape(-1, total), 1, 0) + dot(in_theirs, theirs.reshape(-1, total), 1, 0)
@@ -86,13 +127,7 @@
     result = dot(hidden_mine.reshape(-1, slots), out_mine, 0, 0) + dot(
         hidden_theirs.reshape(-1, slots), out_theirs, 0, 0
     )
-    returned = exchange(result.astype(bf16).reshape(experts, cap, width), "expert")
-    scaled = jnp.where(chosen, jnp.repeat(weight, cap, axis=1), 0.0)
-    high = lax.reduce_precision(scaled, 8, 7)
-    split = jnp.concatenate([high, scaled - high], axis=0).astype(bf16)
-    terms = dot(split, returned.reshape(slots, width), 1, 0)
-    routed = terms[:tok] + terms[tok:]
-
+    returned = exchange(packed(result.astype(bf16).reshape(experts, cap, width)), "expert")
     half_mine, half_theirs = mine[:, :, slots:], theirs[:, :, slots:]
     even = jnp.where(side == 0, half_mine, half_theirs)
     odd = jnp.where(side == 0, half_theirs, half_mine)
@@ -106,11 +141,37 @@
     partial = partial.reshape(tok, ROWS, 2, -1)
     partial = jnp.transpose(partial, (2, 1, 0, 3)).reshape(2 * CHIPS, 2, tok, -1)
     partial = jnp.concatenate([partial[:, 0], partial[:, 1]], axis=2)
-    shared = jnp.sum(exchange(partial, "tensor").astype(f32), axis=0)
+
+    def halve(blocks, mine_is_odd, flip):
+        twos = blocks.reshape((-1, 2) + blocks.shape[1:])
+        keep = jnp.where(mine_is_odd == 0, twos[:, 0], twos[:, 1])
+        give = jnp.where(mine_is_odd == 0, twos[:, 1], twos[:, 0])
+        got = lax.ppermute(give, "tensor", [(i, i ^ flip) for i in range(2 * CHIPS)])
+        return keep.astype(f32) + got.astype(f32)
+
+    partial = halve(partial, side, 1).astype(bf16)
+    partial = halve(partial, across, 2)
+    shared = lax.dynamic_index_in_dim(partial, ring, 0, keepdims=False)
+    for step in range(1, 4):
+        give = lax.dynamic_index_in_dim(partial.astype(bf16), (ring + step) & 3, 0, keepdims=False)
+        got = lax.ppermute(
+            give, "tensor", [(i, (i + 4 * step) % (2 * CHIPS)) for i in range(2 * CHIPS)]
+        )
+        shared = shared + got.astype(f32)
+
+    returned, shared = lax.optimization_barrier((returned, shared))
+    high = lax.reduce_precision(weight, 8, 7)
+    parts = jnp.concatenate([high, weight - high], axis=0).astype(bf16)
+    parts = jnp.dot(parts, spread, preferred_element_type=f32).astype(bf16).reshape(2, 1, tok, -1)
+    scaled = jnp.where(chosen.reshape(1, 4, tok, -1), parts, jnp.zeros((), bf16))
+    terms = dot(scaled.reshape(8 * tok, -1), returned.reshape(-1, 128), 1, 0)
+    terms = terms.reshape(2, 4, tok, 128)
+    terms = terms[0] + terms[1]
+    routed = jnp.concatenate([terms[0], terms[1], terms[2, :, :64] + terms[3, :, 64:]], axis=1)
 
     stream = (tokens.astype(f32) + shared + routed).astype(bf16)
-    spread = exchange(jnp.broadcast_to(stream[None], (2 * CHIPS,) + stream.shape), "tensor")
-    values = jnp.swapaxes(spread, 0, 1).reshape(tok, -1).astype(f32)
+    copies = exchange(jnp.broadcast_to(stream[None], (2 * CHIPS,) + stream.shape), "tensor")
+    values = jnp.swapaxes(copies, 0, 1).reshape(tok, -1).astype(f32)
     scale = lax.rsqrt(jnp.mean(values * values, axis=1, keepdims=True) + 1e-06)
     normed = (values * scale * norm_gain[None, :]).astype(bf16)
     projected = dot(normed, proj_weight, 1, 1).astype(bf16)

time: 255 us -> 243 us (0.953)
  blocking collectives: 133 us -> 60.4 us
  starting transfers between devices: 25.9 us -> 55.4 us
  local copies, waits for them, and re-layouts: 22.5 us -> 37.6 us
  other arithmetic: 10.4 us -> 20.7 us
  waiting for transfers between devices: 29.3 us -> 34.3 us
    all_to_all x4 -> x2, blocking collectives: 133 us -> 60.4 us  [exchange(): lax.all_to_all(parts, axis, split_axis=0, concat_axis=0, tiled=True, axis...]
    all_to_all x2 -> x3, starting transfers between devices: 11.5 us -> 30.7 us  [exchange(): lax.all_to_all(parts, axis, split_axis=0, concat_axis=0, tiled=True, axis...]
    ppermute x0 -> x5, starting transfers between devices: none -> 11.7 us  [the longest x3 7.2 us: per_device(): lax.ppermute(give, 'tensor', [(i, (i + 4 * step) % (2 * CHIPS)) for i in...]
    ppermute x0 -> x5, waiting for transfers between devices: none -> 10.3 us  [the longest x2 6.19 us: halve(): lax.ppermute(give, 'tensor', [(i, i ^ flip) for i in range(2 * CHIPS)])]
    all_to_all x2 -> x3, waiting for transfers between devices: 28.1 us -> 19.5 us  [exchange(): lax.all_to_all(parts, axis, split_axis=0, concat_axis=0, tiled=True, axis...]
    slice x0 -> x8, local copies, waits for them, and re-layouts: none -> 5.34 us  [the longest x1 1.38 us: per_device(): tokens[:, :128]]
    ppermute x2, waiting for transfers between devices: 0.01 us -> 4.5 us  [gather_halves(): lax.ppermute(mine, 'tensor', [(i, i ^ 1) for i in range(2 * CHIPS)])]
    select_n x0 -> x5, other arithmetic: none -> 3.89 us  [the longest x2 2.73 us: by_side(): return (jnp.where(side == 0, even, odd), jnp.where(side == 0, odd, even))]
  transfers between devices with their start and end apart: 6 -> 12, of which waited for: 3 -> 7; matrix products, arithmetic and copies ran while one was open for 17% -> 23% of each run, Pallas kernels for 0% -> 0%
where the time goes in v2:
time: 243 us; the launch traced here: 241 us
  blocking collectives  60.4 us (25%)
  starting transfers between devices  55.4 us (23%)
  local copies, waits for them, and re-layouts  37.6 us (15%)
  waiting for transfers between devices  34.3 us (14%)
  other arithmetic  20.7 us (9%)
  matrix products  18 us (7%)
  between operations  14.7 us (6%)
    all_to_all x2, blocking collectives, exchange(): lax.all_to_all(parts, axis, split_axis=0, concat_axis=0, tiled=True, axis...  60.4 us
    all_to_all x3, starting transfers between devices, exchange(): lax.all_to_all(parts, axis, split_axis=0, concat_axis=0, tiled=True, axis...  30.7 us
    all_to_all x3, waiting for transfers between devices, exchange(): lax.all_to_all(parts, axis, split_axis=0, concat_axis=0, tiled=True, axis...  19.5 us
    dot_general x9, matrix products, dot(): lax.dot_general(left, right, (((over_left,), (over_right,)), ((), ())), p...  15.7 us
    ppermute x2, starting transfers between devices, gather_halves(): lax.ppermute(mine, 'tensor', [(i, i ^ 1) for i in range(2 * CHIPS)])  9.93 us
    concatenate x4, local copies, waits for them, and re-layouts, by_side(): even, odd = (jnp.concatenate(pieces[k::2], axis=axis) for k in range(2))  9.11 us
    ppermute x3, starting transfers between devices, per_device(): lax.ppermute(give, 'tensor', [(i, (i + 4 * step) % (2 * CHIPS)) for i in...  7.2 us
    ppermute x2, waiting for transfers between devices, halve(): lax.ppermute(give, 'tensor', [(i, i ^ flip) for i in range(2 * CHIPS)])  6.19 us
  transfers between devices with their start and end apart: 12, of which 7 were waited for; matrix products, arithmetic and copies ran while one was open for 23% of the time, Pallas kernels for 0%

profile of v2, /device:TPU:1, one launch (start us, length us, event | category | flops | bytes accessed | tf_op | source)
XLA Modules:
  0.0 241.2 jit_solution(14677904423415500374)
XLA Ops:
  8.1 1.4 fusion.92
  10.2 1.3 convolution_convert_fusion.3
  11.5 0.9 broadcast_compare_fusion
  13.1 2.1 convolution_convert_fusion.1
  15.2 17.1 %all-to-all-start = ((bf16[32,48,128]{2,1,0:T(8,128)(2,1)}), bf16[32,48,128]{2,1,0:T(8,128)(2,1)}, u32[]{:S(2)}, u32[]{:S(2)}) async-start(bf16[32,48,128]{2,1,0:T(8,128)(2,1)} %bitcast.164), calls=%async_computation | async-start | bytes 786432 | tf_op jit(solution)/shard_map/all_to_all | solution.py:21
  32.3 1.7 pad_maximum_fusion.2
  34.0 3.1 %collective-permute-start = (bf16[160,576]{1,0:T(8,128)(2,1)}, bf16[160,576]{1,0:T(8,128)(2,1)}, u32[]{:S(2)}, u32[]{:S(2)}) collective-permute-start(bf16[160,576]{1,0:T(8,128)(2,1)} %pad_maximum_fusion.2), channel_id=1, source_target_pairs={{0,256},{16,272},{32,288},{48,304},{64,320},{80,336},{96,352},{112... | collective-permute-start | bytes 552968 | tf_op jit(solution)/shard_map/ppermute | solution.py:113
  37.1 1.4 fusion.20
  38.5 1.1 pad_maximum_fusion.3
  39.7 3.3 %concatenate.63 = bf16[192,2560]{1,0:T(8,128)(2,1)} concatenate(bf16[192,320]{1,0:T(8,128)(2,1)} %get-tuple-element.32, bf16[192,320]{1,0:T(8,128)(2,1)} %get-tuple-element.33, bf16[192,320]{1,0:T(8,128)(2,1)} %get-tuple-element.34, bf16[192,320]{1,0:T(8,128)(2,1)} %get-tuple-element.35, bf16[192,320]{1,0:T(8,128)(2,1)} %get-tuple-element.36, ...), dimensions={1} | concatenate | bytes 1966080 | tf_op jit(solution)/shard_map/concatenate | solution.py:104
  43.1 2.8 %concatenate.62 = bf16[192,2560]{1,0:T(8,128)(2,1)} concatenate(bf16[192,320]{1,0:T(8,128)(2,1)S(1)} %get-tuple-element.23, bf16[192,320]{1,0:T(8,128)(2,1)S(1)} %copy-done.12, bf16[192,320]{1,0:T(8,128)(2,1)S(1)} %copy-done.13, bf16[192,320]{1,0:T(8,128)(2,1)S(1)} %copy-done.14, bf16[192,320]{1,0:T(8,128)(2,1)S(1)} %copy-done.15, bf16[192,320]{1,0:T(8,128)(2,1)S(1)} %copy-done.16, ...), dimensions={1} | concatenate | bytes 1966080 | tf_op jit(solution)/shard_map/concatenate | solution.py:104
  45.9 1.0 slice_bitcast_fusion
  46.9 1.9 concatenate.65
  48.7 1.1 concatenate.64
  49.9 1.7 broadcast_select_fusion.1
  51.6 1.0 broadcast_select_fusion.3
  52.7 1.0 fusion.112
  53.7 1.9 maximum_select_fusion
  55.6 1.7 all-to-all-done
  57.3 1.1 fusion.90
  58.4 1.1 fusion.89
  59.5 1.0 maximum_maximum_fusion
  60.5 2.1 reshape.130
  62.6 1.8 maximum_bitcast_fusion
  64.4 2.0 copy.69
  66.4 1.3 broadcast_in_dim.74
  67.7 43.6 %all_to_all.25 = bf16[8,320,624]{2,1,0:T(8,128)(2,1)S(1)} all-to-all(bf16[8,320,624]{2,1,0:T(8,128)(2,1)S(1)} %broadcast_in_dim.74), channel_id=1, replica_groups={{0,2,4,6,8,10,12,14},{1,3,5,7,9,11,13,15},{16,18,20,22,24,26,28,30},{17..., dimensions={0} | all-to-all | bytes 6389760 | tf_op jit(solution)/shard_map/all_to_all | solution.py:21
  111.3 6.6 %collective-permute-start.1 = (bf16[8,320,624]{2,1,0:T(8,128)(2,1)S(1)}, bf16[8,320,624]{2,1,0:T(8,128)(2,1)S(1)}, u32[]{:S(2)}, u32[]{:S(2)}) collective-permute-start(bf16[8,320,624]{2,1,0:T(8,128)(2,1)S(1)} %all_to_all.25), channel_id=1, source_target_pairs={{0,1},{1,0},{2,3},{3,2},{4,5},{5,4},{6,7},{7,6},{8,9},{9,8},{10,11... | collective-permute-start | bytes 9584648 | tf_op jit(solution)/shard_map/ppermute | solution.py:28
  117.9 0.9 fusion.93
  118.8 4.5 %collective-permute-done.1 = bf16[8,320,624]{2,1,0:T(8,128)(2,1)S(1)} collective-permute-done((bf16[8,320,624]{2,1,0:T(8,128)(2,1)S(1)}, bf16[8,320,624]{2,1,0:T(8,128)(2,1)S(1)}, u32[]{:S(2)}, u32[]{:S(2)}) %collective-permute-start.1) | collective-permute-done | bytes 3194912 | tf_op jit(solution)/shard_map/ppermute | solution.py:28
  123.3 0.9 convolution_add_fusion.1
  125.2 1.0 broadcast_in_dim.75
  126.2 3.6 %all-to-all-start.2 = ((bf16[8,96,576]{2,1,0:T(8,128)(2,1)}), bf16[8,96,576]{2,1,0:T(8,128)(2,1)S(1)}, u32[]{:S(2)}, u32[]{:S(2)}) async-start(bf16[8,96,576]{2,1,0:T(8,128)(2,1)} %broadcast_in_dim.75), calls=%async_computation.2 | async-start | bytes 1966080 | tf_op jit(solution)/shard_map/all_to_all | solution.py:21
  129.9 16.1 %all-to-all-done.2 = bf16[8,96,576]{2,1,0:T(8,128)(2,1)S(1)} async-done(((bf16[8,96,576]{2,1,0:T(8,128)(2,1)}), bf16[8,96,576]{2,1,0:T(8,128)(2,1)S(1)}, u32[]{:S(2)}, u32[]{:S(2)}) %all-to-all-start.2) | async-done | bytes 884768 | tf_op jit(solution)/shard_map/all_to_all | solution.py:21
  146.0 3.3 %collective-permute-start.2 = (bf16[8,96,576]{2,1,0:T(8,128)(2,1)S(1)}, bf16[8,96,576]{2,1,0:T(8,128)(2,1)}, u32[]{:S(2)}, u32[]{:S(2)}) collective-permute-start(bf16[8,96,576]{2,1,0:T(8,128)(2,1)S(1)} %all-to-all-done.2), channel_id=1, source_target_pairs={{0,1},{1,0},{2,3},{3,2},{4,5},{5,4},{6,7},{7,6},{8,9},{9,8},{10,11... | collective-permute-start | bytes 2654216 | tf_op jit(solution)/shard_map/ppermute | solution.py:28
  149.9 1.3 slice.364
  151.6 1.3 slice.365
  152.9 1.0 copy.86
  153.9 1.0 select_bitcast_fusion.1
  155.5 1.7 reshape.136
  157.2 1.9 copy.74
  159.1 1.9 reshape.137
  161.1 1.6 fusion.95
  162.7 1.8 fusion.3
  165.7 2.8 %fusion = f32[48,384]{1,0:T(8,128)S(1)} fusion(bf16[5120,48]{0,1:T(8,128)(2,1)S(1)} %copy-done.18, bf16[5120,576]{1,0:T(8,128)(2,1)} %bitcast.162), kind=kOutput, calls=%fused_computation.31 | convolution fusion | flops 188743680 | bytes 4497408 | tf_op jit(solution)/shard_map/dot_general | solution.py:15
  168.5 2.6 %convolution_convert_fusion = bf16[48,5120]{1,0:T(8,128)(2,1)S(1)} fusion(bf16[5120,576]{1,0:T(8,128)(2,1)} %bitcast.163, f32[48,384]{1,0:T(8,128)S(1)} %fusion), kind=kOutput, calls=%fused_computation | convolution fusion | flops 94672896 | bytes 3211264 | tf_op jit(solution)/shard_map/dot_general | solution.py:15
  171.1 0.9 reshape.139
  172.5 1.0 fusion.16
  173.5 2.0 collective-permute-start.3
  175.6 1.0 fusion.14
  176.6 10.0 %all-to-all-start.3 = ((bf16[32,48,128]{2,1,0:T(8,128)(2,1)}), bf16[32,48,128]{2,1,0:T(8,128)(2,1)S(1)}, u32[]{:S(2)}, u32[]{:S(2)}) async-start(bf16[32,48,128]{2,1,0:T(8,128)(2,1)} %fusion.14), calls=%async_computation.3 | async-start | bytes 786432 | tf_op jit(solution)/shard_map/all_to_all | solution.py:21
  186.7 1.2 fusion.10
  187.9 2.4 %collective-permute-start.4 = (bf16[4,48,320]{2,1,0:T(8,128)(2,1)S(1)}, bf16[4,48,320]{2,1,0:T(8,128)(2,1)S(1)}, u32[]{:S(2)}, u32[]{:S(2)}) collective-permute-start(bf16[4,48,320]{2,1,0:T(8,128)(2,1)S(1)} %fusion.35), channel_id=1, source_target_pairs={{0,2},{1,3},{2,0},{3,1},{4,6},{5,7},{6,4},{7,5},{8,10},{9,11},{10,... | collective-permute-start | bytes 368648 | tf_op jit(solution)/shard_map/ppermute | solution.py:149
  190.3 1.0 convolution_convert_fusion.2
  191.4 6.2 %collective-permute-done.4 = bf16[4,48,320]{2,1,0:T(8,128)(2,1)S(1)} collective-permute-done((bf16[4,48,320]{2,1,0:T(8,128)(2,1)S(1)}, bf16[4,48,320]{2,1,0:T(8,128)(2,1)S(1)}, u32[]{:S(2)}, u32[]{:S(2)}) %collective-permute-start.4) | collective-permute-done | bytes 122912 | tf_op jit(solution)/shard_map/ppermute | solution.py:149
  198.3 2.5 %collective-permute-start.7 = (bf16[48,320]{1,0:T(8,128)(2,1)}, bf16[48,320]{1,0:T(8,128)(2,1)}, u32[]{:S(2)}, u32[]{:S(2)}) collective-permute-start(bf16[48,320]{1,0:T(8,128)(2,1)} %get-tuple-element.69), channel_id=1, source_target_pairs={{0,12},{1,13},{2,14},{3,15},{4,0},{5,1},{6,2},{7,3},{8,4},{9,5},{1... | collective-permute-start | bytes 92168 | tf_op jit(solution)/shard_map/ppermute | solution.py:157
  200.8 1.9 collective-permute-start.6
  202.7 2.8 %collective-permute-start.5 = (bf16[48,320]{1,0:T(8,128)(2,1)}, bf16[48,320]{1,0:T(8,128)(2,1)}, u32[]{:S(2)}, u32[]{:S(2)}) collective-permute-start(bf16[48,320]{1,0:T(8,128)(2,1)} %get-tuple-element.68), channel_id=1, source_target_pairs={{0,4},{1,5},{2,6},{3,7},{4,8},{5,9},{6,10},{7,11},{8,12},{9,13},{1... | collective-permute-start | bytes 92168 | tf_op jit(solution)/shard_map/ppermute | solution.py:157
  205.7 1.8 collective-permute-done.6
  207.5 2.3 collective-permute-done.5
  210.6 1.7 all-to-all-done.3
  213.0 16.8 %all_to_all.26 = bf16[16,48,320]{2,1,0:T(8,128)(2,1)S(1)} all-to-all(bf16[16,48,320]{2,1,0:T(8,128)(2,1)S(1)} %broadcast_in_dim.82), channel_id=1, replica_groups=mesh['expert'=32,'tensor'=16] {'tensor'}, dimensions={0} | all-to-all | bytes 983040 | tf_op jit(solution)/shard_map/all_to_all | solution.py:21
  230.3 1.3 reshape.145
  231.9 2.4 %convolution_convert_fusion.4 = bf16[48,132]{1,0:T(8,128)(2,1)} fusion(bf16[132,5120]{1,0:T(8,128)(2,1)S(1)} %copy-done, f32[48,5120]{1,0:T(8,128)} %reshape.145, f32[5120]{0:T(1024)S(1)} %copy-done.27, f32[48]{0:T(128)S(1)} %add_rsqrt_fusion), kind=kOutput, calls=%fused_computation.44 | convolution fusion | flops 65624256 | bytes 2368064 | tf_op jit(solution)/shard_map/dot_general | solution.py:15
  (97 shorter events, 9.7 us)
Async XLA Ops:
  7.2 224.7 %copy-start = (bf16[132,5120]{1,0:T(8,128)(2,1)S(1)}, bf16[132,5120]{1,0:T(8,128)(2,1)}, u32[]{:S(2)}) copy-start(bf16[132,5120]{1,0:T(8,128)(2,1)} %param.23) | copy-start | bytes 4055044
  7.2 29.9 %copy-start.3 = (bf16[1,96,5120]{2,1,0:T(8,128)(2,1)S(1)}, bf16[1,96,5120]{2,1,0:T(8,128)(2,1)}, u32[]{:S(2)}) copy-start(bf16[1,96,5120]{2,1,0:T(8,128)(2,1)} %param.16) | copy-start | bytes 2949124
  7.2 29.9 %copy-start.4 = (bf16[1,96,5120]{2,1,0:T(8,128)(2,1)S(1)}, bf16[1,96,5120]{2,1,0:T(8,128)(2,1)}, u32[]{:S(2)}) copy-start(bf16[1,96,5120]{2,1,0:T(8,128)(2,1)} %param.17) | copy-start | bytes 2949124
  12.4 0.7 copy-start.9
  12.4 19.9 %copy-start.22 = (bf16[192,160]{0,1:T(8,128)(2,1)S(1)}, bf16[192,160]{0,1:T(8,128)(2,1)}, u32[]{:S(2)}) copy-start(bf16[192,160]{0,1:T(8,128)(2,1)} %param.21) | copy-start | bytes 184324
  12.4 19.9 %copy-start.24 = (bf16[160,192]{1,0:T(8,128)(2,1)S(1)}, bf16[160,192]{1,0:T(8,128)(2,1)}, u32[]{:S(2)}) copy-start(bf16[160,192]{1,0:T(8,128)(2,1)} %param.20) | copy-start | bytes 184324
  15.2 42.1 %all-to-all-start = ((bf16[32,48,128]{2,1,0:T(8,128)(2,1)}), bf16[32,48,128]{2,1,0:T(8,128)(2,1)}, u32[]{:S(2)}, u32[]{:S(2)}) async-start(bf16[32,48,128]{2,1,0:T(8,128)(2,1)} %bitcast.164), calls=%async_computation | async-start | bytes 786432 | tf_op jit(solution)/shard_map/all_to_all | solution.py:21
  32.3 133.4 %all-gather.3.cloned.1.call-start = ((), (), s32[]{:S(2)}) async-start(), calls=%async_computation.5 | async-start | bytes 6963200 | tf_op jit(solution)/shard_map/all_gather | solution.py:118
  34.0 19.6 %collective-permute-start = (bf16[160,576]{1,0:T(8,128)(2,1)}, bf16[160,576]{1,0:T(8,128)(2,1)}, u32[]{:S(2)}, u32[]{:S(2)}) collective-permute-start(bf16[160,576]{1,0:T(8,128)(2,1)} %pad_maximum_fusion.2), channel_id=1, source_target_pairs={{0,256},{16,272},{32,288},{48,304},{64,320},{80,336},{96,352},{112... | collective-permute-start | bytes 552968 | tf_op jit(solution)/shard_map/ppermute | solution.py:113
  39.6 3.4 %copy-start.12 = (bf16[192,320]{1,0:T(8,128)(2,1)S(1)}, bf16[192,320]{1,0:T(8,128)(2,1)}, u32[]{:S(2)}) copy-start(bf16[192,320]{1,0:T(8,128)(2,1)} %get-tuple-element.24) | copy-start | bytes 368644
  39.6 3.4 %copy-start.13 = (bf16[192,320]{1,0:T(8,128)(2,1)S(1)}, bf16[192,320]{1,0:T(8,128)(2,1)}, u32[]{:S(2)}) copy-start(bf16[192,320]{1,0:T(8,128)(2,1)} %get-tuple-element.25) | copy-start | bytes 368644
  39.6 3.4 %copy-start.14 = (bf16[192,320]{1,0:T(8,128)(2,1)S(1)}, bf16[192,320]{1,0:T(8,128)(2,1)}, u32[]{:S(2)}) copy-start(bf16[192,320]{1,0:T(8,128)(2,1)} %get-tuple-element.26) | copy-start | bytes 368644
  39.6 3.4 %copy-start.15 = (bf16[192,320]{1,0:T(8,128)(2,1)S(1)}, bf16[192,320]{1,0:T(8,128)(2,1)}, u32[]{:S(2)}) copy-start(bf16[192,320]{1,0:T(8,128)(2,1)} %get-tuple-element.27) | copy-start | bytes 368644
  39.6 3.4 %copy-start.16 = (bf16[192,320]{1,0:T(8,128)(2,1)S(1)}, bf16[192,320]{1,0:T(8,128)(2,1)}, u32[]{:S(2)}) copy-start(bf16[192,320]{1,0:T(8,128)(2,1)} %get-tuple-element.28) | copy-start | bytes 368644
  39.6 3.4 %copy-start.17 = (bf16[192,320]{1,0:T(8,128)(2,1)S(1)}, bf16[192,320]{1,0:T(8,128)(2,1)}, u32[]{:S(2)}) copy-start(bf16[192,320]{1,0:T(8,128)(2,1)} %get-tuple-element.29) | copy-start | bytes 368644
  39.7 6.2 %copy-start.8 = (bf16[1,1536,320]{1,2,0:T(8,128)(2,1)S(1)}, bf16[1,1536,320]{1,2,0:T(8,128)(2,1)}, u32[]{:S(2)}) copy-start(bf16[1,1536,320]{1,2,0:T(8,128)(2,1)} %param.18) | copy-start | bytes 2949124
  49.9 1.7 copy-start.6
  49.9 1.8 copy-start.7
  51.6 1.0 copy-start.23
  51.6 1.0 copy-start.25
  57.3 5.3 %copy-start.20 = (bf16[48,320]{1,0:T(8,128)(2,1)S(1)}, bf16[48,320]{1,0:T(8,128)(2,1)}, u32[]{:S(2)}) copy-start(bf16[48,320]{1,0:T(8,128)(2,1)} %param.13) | copy-start | bytes 92164
  111.3 7.6 %copy-start.1 = (bf16[8,320,624]{2,1,0:T(8,128)(2,1)}, bf16[8,320,624]{2,1,0:T(8,128)(2,1)S(1)}, u32[]{:S(2)}) copy-start(bf16[8,320,624]{2,1,0:T(8,128)(2,1)S(1)} %all_to_all.25) | copy-start | bytes 9584644
  111.3 12.1 %collective-permute-start.1 = (bf16[8,320,624]{2,1,0:T(8,128)(2,1)S(1)}, bf16[8,320,624]{2,1,0:T(8,128)(2,1)S(1)}, u32[]{:S(2)}, u32[]{:S(2)}) collective-permute-start(bf16[8,320,624]{2,1,0:T(8,128)(2,1)S(1)} %all_to_all.25), channel_id=1, source_target_pairs={{0,1},{1,0},{2,3},{3,2},{4,5},{5,4},{6,7},{7,6},{8,9},{9,8},{10,11... | collective-permute-start | bytes 9584648 | tf_op jit(solution)/shard_map/ppermute | solution.py:28
  123.3 1.8 copy-start.2
  125.1 4.7 %copy-start.28 = (s32[48,6]{0,1:T(8,128)S(1)}, s32[48,6]{0,1:T(8,128)}, u32[]{:S(2)}) copy-start(s32[48,6]{0,1:T(8,128)} %param.14) | copy-start | bytes 3460
  125.1 4.7 %copy-start.29 = (f32[48,6]{0,1:T(8,128)S(1)}, f32[48,6]{0,1:T(8,128)}, u32[]{:S(2)}) copy-start(f32[48,6]{0,1:T(8,128)} %param.15) | copy-start | bytes 3460
  126.2 19.7 %all-to-all-start.2 = ((bf16[8,96,576]{2,1,0:T(8,128)(2,1)}), bf16[8,96,576]{2,1,0:T(8,128)(2,1)S(1)}, u32[]{:S(2)}, u32[]{:S(2)}) async-start(bf16[8,96,576]{2,1,0:T(8,128)(2,1)} %broadcast_in_dim.75), calls=%async_computation.2 | async-start | bytes 1966080 | tf_op jit(solution)/shard_map/all_to_all | solution.py:21
  146.0 16.7 %collective-permute-start.2 = (bf16[8,96,576]{2,1,0:T(8,128)(2,1)S(1)}, bf16[8,96,576]{2,1,0:T(8,128)(2,1)}, u32[]{:S(2)}, u32[]{:S(2)}) collective-permute-start(bf16[8,96,576]{2,1,0:T(8,128)(2,1)S(1)} %all-to-all-done.2), channel_id=1, source_target_pairs={{0,1},{1,0},{2,3},{3,2},{4,5},{5,4},{6,7},{7,6},{8,9},{9,8},{10,11... | collective-permute-start | bytes 2654216 | tf_op jit(solution)/shard_map/ppermute | solution.py:28
  161.1 1.7 copy-start.5
  164.5 1.2 copy-start.18
  172.4 3.1 %copy-start.11 = (bf16[32,18,128]{2,1,0:T(8,128)(2,1)S(1)}, bf16[32,18,128]{2,1,0:T(8,128)(2,1)}, u32[]{:S(2)}) copy-start(bf16[32,18,128]{2,1,0:T(8,128)(2,1)} %get-tuple-element.61) | copy-start | bytes 442372
  173.5 16.8 %copy-start.19 = (bf16[32,1536]{1,0:T(8,128)(2,1)S(1)}, bf16[32,1536]{1,0:T(8,128)(2,1)}, u32[]{:S(2)}) copy-start(bf16[32,1536]{1,0:T(8,128)(2,1)} %constant.62.clone) | copy-start | bytes 294916
  173.5 13.2 %collective-permute-start.3 = (bf16[8,48,320]{2,1,0:T(8,128)(2,1)}, bf16[8,48,320]{2,1,0:T(8,128)(2,1)}, u32[]{:S(2)}, u32[]{:S(2)}) collective-permute-start(bf16[8,48,320]{2,1,0:T(8,128)(2,1)} %fusion.16), channel_id=1, source_target_pairs={{0,1},{1,0},{2,3},{3,2},{4,5},{5,4},{6,7},{7,6},{8,9},{9,8},{10,11... | collective-permute-start | bytes 737288 | tf_op jit(solution)/shard_map/ppermute | solution.py:149
  176.6 28.9 %copy-start.10 = (pred[4,48,1536]{2,1,0:T(8,128)(4,1)S(1)}, pred[4,48,1536]{2,1,0:T(8,128)(4,1)}, u32[]{:S(2)}) copy-start(pred[4,48,1536]{2,1,0:T(8,128)(4,1)} %copy-done.9) | copy-start | bytes 884740
  176.6 35.7 %all-to-all-start.3 = ((bf16[32,48,128]{2,1,0:T(8,128)(2,1)}), bf16[32,48,128]{2,1,0:T(8,128)(2,1)S(1)}, u32[]{:S(2)}, u32[]{:S(2)}) async-start(bf16[32,48,128]{2,1,0:T(8,128)(2,1)} %fusion.14), calls=%async_computation.3 | async-start | bytes 786432 | tf_op jit(solution)/shard_map/all_to_all | solution.py:21
  187.9 9.7 %collective-permute-start.4 = (bf16[4,48,320]{2,1,0:T(8,128)(2,1)S(1)}, bf16[4,48,320]{2,1,0:T(8,128)(2,1)S(1)}, u32[]{:S(2)}, u32[]{:S(2)}) collective-permute-start(bf16[4,48,320]{2,1,0:T(8,128)(2,1)S(1)} %fusion.35), channel_id=1, source_target_pairs={{0,2},{1,3},{2,0},{3,1},{4,6},{5,7},{6,4},{7,5},{8,10},{9,11},{10,... | collective-permute-start | bytes 368648 | tf_op jit(solution)/shard_map/ppermute | solution.py:149
  198.3 7.4 %collective-permute-start.7 = (bf16[48,320]{1,0:T(8,128)(2,1)}, bf16[48,320]{1,0:T(8,128)(2,1)}, u32[]{:S(2)}, u32[]{:S(2)}) collective-permute-start(bf16[48,320]{1,0:T(8,128)(2,1)} %get-tuple-element.69), channel_id=1, source_target_pairs={{0,12},{1,13},{2,14},{3,15},{4,0},{5,1},{6,2},{7,3},{8,4},{9,5},{1... | collective-permute-start | bytes 92168 | tf_op jit(solution)/shard_map/ppermute | solution.py:157
  200.8 6.7 %collective-permute-start.6 = (bf16[48,320]{1,0:T(8,128)(2,1)}, bf16[48,320]{1,0:T(8,128)(2,1)}, u32[]{:S(2)}, u32[]{:S(2)}) collective-permute-start(bf16[48,320]{1,0:T(8,128)(2,1)} %get-tuple-element.70), channel_id=1, source_target_pairs={{0,8},{1,9},{2,10},{3,11},{4,12},{5,13},{6,14},{7,15},{8,0},{9,1},... | collective-permute-start | bytes 92168 | tf_op jit(solution)/shard_map/ppermute | solution.py:157
  202.7 7.1 %collective-permute-start.5 = (bf16[48,320]{1,0:T(8,128)(2,1)}, bf16[48,320]{1,0:T(8,128)(2,1)}, u32[]{:S(2)}, u32[]{:S(2)}) collective-permute-start(bf16[48,320]{1,0:T(8,128)(2,1)} %get-tuple-element.68), channel_id=1, source_target_pairs={{0,4},{1,5},{2,6},{3,7},{4,8},{5,9},{6,10},{7,11},{8,12},{9,13},{1... | collective-permute-start | bytes 92168 | tf_op jit(solution)/shard_map/ppermute | solution.py:157
  205.7 7.2 %copy-start.21 = (bf16[48,320]{1,0:T(8,128)(2,1)S(1)}, bf16[48,320]{1,0:T(8,128)(2,1)}, u32[]{:S(2)}) copy-start(bf16[48,320]{1,0:T(8,128)(2,1)} %param.13) | copy-start | bytes 92164
  212.9 17.4 %copy-start.26 = (bf16[48,320]{1,0:T(8,128)(2,1)}, bf16[48,320]{1,0:T(8,128)(2,1)S(1)}, u32[]{:S(2)}) copy-start(bf16[48,320]{1,0:T(8,128)(2,1)S(1)} %fusion.41) | copy-start | bytes 92164
  230.3 1.6 copy-start.27
Sparse Core Ops, SparseCore 0:
  57.4 86.7 all-gather.2

commit v3 on v1

v3 whole, which is shorter than its diff:
```python
import jax
import jax.numpy as jnp
import numpy as np
from jax import lax
from jax.experimental import pallas as pl
from jax.experimental.pallas import tpu as pltpu
from jax.sharding import PartitionSpec as P

ROWS = 16
CHIPS = 8
LANES = [[x * ROWS + z for z in range(ROWS)] for x in range(2)]
SIDES = [[2 * chip + core for chip in range(CHIPS)] for core in range(2)]


def dot(left, right, over_left, over_right):
    return lax.dot_general(
        left, right, (((over_left,), (over_right,)), ((), ())), preferred_element_type=jnp.float32
    )


def exchange(parts, axis, groups=None):
    return lax.all_to_all(
        parts, axis, split_axis=0, concat_axis=0, tiled=True, axis_index_groups=groups
    )


def gather_halves(block):
    mine = exchange(jnp.broadcast_to(block[None], (CHIPS,) + block.shape), "tensor", SIDES)
    theirs = lax.ppermute(mine, "tensor", [(i, i ^ 1) for i in range(2 * CHIPS)])
    return mine, theirs


def shared_kernel(side_ref, mine_ref, theirs_ref, table_ref, keep_ref, give_ref):
    side = side_ref[0]
    inner = table_ref.shape[3] // 3
    size = table_ref.shape[2]
    start = mine_ref.shape[2] // 2

    def weights(chip, half):
        first = 2 * (2 * (chip % 4) + half)
        return table_ref.at[pl.ds(first, 2), chip // 4]

    sums = jnp.zeros((mine_ref.shape[2], 2 * inner), jnp.float32)
    for chip in range(CHIPS):
        for ref, half in ((mine_ref, side), (theirs_ref, 1 - side)):
            block = weights(chip, half)[:, :, : 2 * inner].reshape(2 * size, 2 * inner)
            sums = sums + dot(ref[chip], block, 0, 0)
    sums = sums[start : start + keep_ref.shape[1]]
    gate, up = sums[:, :inner], sums[:, inner:]
    hidden = (gate * (1.0 / (1.0 + jnp.exp(-gate))) * up).astype(jnp.bfloat16)
    for chip in range(CHIPS):
        for ref, half in ((keep_ref, side), (give_ref, 1 - side)):
            block = weights(chip, half)[:, :, 2 * inner :].reshape(2 * size, inner)
            ref[chip] = dot(hidden, block, 1, 1).astype(ref.dtype)


def shared_partial(side, mine, theirs, table, tok):
    width = mine.shape[1]
    out = jax.ShapeDtypeStruct((CHIPS, tok, width), jnp.bfloat16)
    last = pl.BlockSpec((CHIPS, width, 128), lambda i: (0, 0, 4))
    whole = pl.BlockSpec(out.shape, lambda i: (0, 0, 0))
    return pl.pallas_call(
        shared_kernel,
        out_shape=(out, out),
        grid=(1,),
        in_specs=[
            pl.BlockSpec(memory_space=pltpu.SMEM),
            last,
            last,
            pl.BlockSpec(table.shape, lambda i: (0, 0, 0, 0), pipeline_mode=pl.Buffered(1)),
        ],
        out_specs=(whole, whole),
        compiler_params=pltpu.CompilerParams(vmem_limit_bytes=32 * 2**20),
        cost_estimate=pl.CostEstimate(flops=1000, bytes_accessed=1000, transcendentals=0),
    )(side.reshape(1), mine, theirs, table)


def per_device(
    tokens,
    expert_ids,
    route_weights,
    routed_gate,
    routed_up,
    routed_down,
    shared_gate,
    shared_up,
    shared_down,
    norm_gain,
    proj_weight,
):
    tok, width = tokens.shape
    top = expert_ids.shape[1]
    experts = lax.axis_size("expert")
    cap = min(tok, 2 * tok * top // experts)
    slots = experts * cap
    bf16, f32 = jnp.bfloat16, jnp.float32
    rank = lax.axis_index("tensor")
    side, across, ring = rank & 1, (rank >> 1) & 1, rank >> 2
    column = lax.axis_index("expert") >> 4

    match = expert_ids[:, :, None] == jnp.arange(experts, dtype=jnp.int32)[None, None, :]
    named = jnp.any(match, axis=1)
    weight = jnp.sum(jnp.where(match, route_weights[:, :, None], 0.0), axis=1)
    earlier = jnp.tril(jnp.ones((tok, tok), bf16), -1)
    slot = jnp.where(named, jnp.dot(earlier, named.astype(bf16), preferred_element_type=f32), -2.0)
    place = np.arange(slots)
    spread = jnp.asarray(place[None, :] // cap == np.arange(experts)[:, None], bf16)
    wide = jnp.dot(slot.astype(bf16), spread, preferred_element_type=f32)
    chosen = wide == jnp.asarray(place % cap, f32)[None, :]
    outgoing = dot(chosen.astype(bf16), tokens, 0, 0).astype(bf16)
    arrived = exchange(outgoing.reshape(experts, cap, width), "expert")

    def by_side(array, axis):
        size = array.shape[axis] // (2 * CHIPS)
        pieces = [lax.slice_in_dim(array, k * size, (k + 1) * size, axis=axis) for k in range(2 * CHIPS)]
        even, odd = (jnp.concatenate(pieces[k::2], axis=axis) for k in range(2))
        return jnp.where(side == 0, even, odd), jnp.where(side == 0, odd, even)

    gate_up = jnp.concatenate([routed_gate[0], routed_up[0]], axis=0)
    hid = routed_gate.shape[1]
    in_mine, in_theirs = by_side(gate_up, 1)
    out_mine, out_theirs = by_side(routed_down[0], 0)

    own = jnp.concatenate([shared_gate, shared_up, shared_down.T], axis=1)
    other = lax.ppermute(own, "expert", [(i, (i + ROWS) % (2 * ROWS)) for i in range(2 * ROWS)])
    pair = jnp.where(column == 0, jnp.stack([own, other]), jnp.stack([other, own]))
    arrived, pair, in_mine, in_theirs, out_mine, out_theirs = lax.optimization_barrier(
        (arrived, pair, in_mine, in_theirs, out_mine, out_theirs)
    )
    gathered = lax.all_gather(pair, "expert", axis=0, axis_index_groups=LANES)

    rows = jnp.concatenate([arrived.reshape(slots, width), tokens], axis=0)
    mine, theirs = gather_halves(rows.T)
    total = slots + tok
    both = dot(in_mine, mine.reshape(-1, total), 1, 0) + dot(in_theirs, theirs.reshape(-1, total), 1, 0)
    hidden = (jax.nn.silu(both[:hid, :slots]) * both[hid:, :slots]).astype(bf16)
    hidden_mine, hidden_theirs = gather_halves(hidden)
    result = dot(hidden_mine.reshape(-1, slots), out_mine, 0, 0) + dot(
        hidden_theirs.reshape(-1, slots), out_theirs, 0, 0
    )
    returned = exchange(result.astype(bf16).reshape(experts, cap, width), "expert")
    keep, give = shared_partial(side, mine, theirs, gathered, tok)

    got = lax.ppermute(give, "tensor", [(i, i ^ 1) for i in range(2 * CHIPS)])
    partial = (keep.astype(f32) + got.astype(f32)).astype(bf16)
    partial = partial.reshape((-1, 2) + partial.shape[1:])
    keep = jnp.where(across == 0, partial[:, 0], partial[:, 1])
    give = jnp.where(across == 0, partial[:, 1], partial[:, 0])
    got = lax.ppermute(give, "tensor", [(i, i ^ 2) for i in range(2 * CHIPS)])
    partial = keep.astype(f32) + got.astype(f32)
    shared = lax.dynamic_index_in_dim(partial, ring, 0, keepdims=False)
    for step in range(1, 4):
        give = lax.dynamic_index_in_dim(partial.astype(bf16), (ring + step) & 3, 0, keepdims=False)
        got = lax.ppermute(
            give, "tensor", [(i, (i + 4 * step) % (2 * CHIPS)) for i in range(2 * CHIPS)]
        )
        shared = shared + got.astype(f32)

    returned, shared = lax.optimization_barrier((returned, shared))
    high = lax.reduce_precision(weight, 8, 7)
    parts = jnp.concatenate([high, weight - high], axis=0).astype(bf16)
    parts = jnp.dot(parts, spread, preferred_element_type=f32).astype(bf16).reshape(2, tok, -1)
    scaled = jnp.where(chosen[None], parts, jnp.zeros((), bf16)).reshape(2 * tok, -1)
    terms = dot(scaled, returned.reshape(slots, width), 1, 0)
    routed = terms[:tok] + terms[tok:]

    stream = (tokens.astype(f32) + shared + routed).astype(bf16)
    copies = exchange(jnp.broadcast_to(stream[None], (2 * CHIPS,) + stream.shape), "tensor")
    values = jnp.swapaxes(copies, 0, 1).reshape(tok, -1).astype(f32)
    scale = lax.rsqrt(jnp.mean(values * values, axis=1, keepdims=True) + 1e-06)
    normed = (values * scale * norm_gain[None, :]).astype(bf16)
    projected = dot(normed, proj_weight, 1, 1).astype(bf16)
    return (stream, projected)


def solution(mesh):
    in_specs = (
        P("expert", "tensor"),
        P("expert", None),
        P("expert", None),
        P("expert", "tensor", None),
        P("expert", "tensor", None),
        P("expert", None, "tensor"),
        P("expert", "tensor"),
        P("expert", "tensor"),
        P("tensor", "expert"),
        P(),
        P("tensor", None),
    )
    out_specs = (P("expert", "tensor"), P("expert", "tensor"))
    return jax.shard_map(
        per_device, mesh=mesh, in_specs=in_specs, out_specs=out_specs, check_vma=False
    )
```

time: 255 us -> 236 us (0.925)
  blocking collectives: 133 us -> 83.2 us
  starting transfers between devices: 25.9 us -> 49.4 us
  matrix products: 17.8 us -> 10.3 us
  local copies, waits for them, and re-layouts: 22.5 us -> 29 us
  waiting for transfers between devices: 29.3 us -> 32.5 us
  other arithmetic: 10.4 us -> 13.1 us
    all_to_all x4 -> x3, blocking collectives: 133 us -> 83.2 us  [exchange(): lax.all_to_all(parts, axis, split_axis=0, concat_axis=0, tiled=True, axis...]
    ppermute x0 -> x5, starting transfers between devices: none -> 15 us  [the longest x3 9.6 us: per_device(): lax.ppermute(give, 'tensor', [(i, (i + 4 * step) % (2 * CHIPS)) for i in...]
    all_to_all x2, starting transfers between devices: 11.5 us -> 23.1 us  [exchange(): lax.all_to_all(parts, axis, split_axis=0, concat_axis=0, tiled=True, axis...]
    dot_general x9 -> x7, matrix products: 17.6 us -> 9.12 us  [dot(): lax.dot_general(left, right, (((over_left,), (over_right,)), ((), ())), p...]
    all_to_all x2, waiting for transfers between devices: 28.1 us -> 20 us  [exchange(): lax.all_to_all(parts, axis, split_axis=0, concat_axis=0, tiled=True, axis...]
    ppermute x0 -> x5, waiting for transfers between devices: none -> 7.98 us  [the longest x1 4.46 us: per_device(): got = lax.ppermute(give, 'tensor', [(i, i ^ 2) for i in range(2 * CHIPS)])]
    unnamed x32 -> x80, local copies, waits for them, and re-layouts: 1.28 us -> 7.79 us
    ppermute x2, waiting for transfers between devices: 0.01 us -> 4.5 us  [gather_halves(): lax.ppermute(mine, 'tensor', [(i, i ^ 1) for i in range(2 * CHIPS)])]
  transfers between devices with their start and end apart: 6 -> 11, of which waited for: 3 -> 6; matrix products, arithmetic and copies ran while one was open for 17% -> 15% of each run, Pallas kernels for 0% -> 1%
where the time goes in v3:
time: 236 us; the launch traced here: 235 us
  blocking collectives  83.2 us (35%)
  starting transfers between devices  49.4 us (21%)
  waiting for transfers between devices  32.5 us (14%)
  local copies, waits for them, and re-layouts  29 us (12%)
  between operations  14.7 us (6%)
  other arithmetic  13.1 us (6%)
  matrix products  10.3 us (4%)
  Pallas kernels  2.37 us (1%)
    all_to_all x3, blocking collectives, exchange(): lax.all_to_all(parts, axis, split_axis=0, concat_axis=0, tiled=True, axis...  83.2 us
    all_to_all x2, starting transfers between devices, exchange(): lax.all_to_all(parts, axis, split_axis=0, concat_axis=0, tiled=True, axis...  23.1 us
    all_to_all x2, waiting for transfers between devices, exchange(): lax.all_to_all(parts, axis, split_axis=0, concat_axis=0, tiled=True, axis...  20 us
    ppermute x3, starting transfers between devices, per_device(): lax.ppermute(give, 'tensor', [(i, (i + 4 * step) % (2 * CHIPS)) for i in...  9.6 us
    dot_general x7, matrix products, dot(): lax.dot_general(left, right, (((over_left,), (over_right,)), ((), ())), p...  9.12 us
    concatenate x4, local copies, waits for them, and re-layouts, by_side(): even, odd = (jnp.concatenate(pieces[k::2], axis=axis) for k in range(2))  8.24 us
    ppermute x2, starting transfers between devices, gather_halves(): lax.ppermute(mine, 'tensor', [(i, i ^ 1) for i in range(2 * CHIPS)])  8.19 us
    unnamed x80, local copies, waits for them, and re-layouts  7.79 us
  transfers between devices with their start and end apart: 11, of which 6 were waited for; matrix products, arithmetic and copies ran while one was open for 15% of the time, Pallas kernels for 1%

profile of v3, /device:TPU:1, one launch (start us, length us, event | category | flops | bytes accessed | tf_op | source)
XLA Modules:
  0.0 234.5 jit_solution(12419977436775371478)
XLA Ops:
  7.2 0.8 fusion.25
  8.0 1.2 convolution_compare_fusion
  9.2 1.1 convolution_convert_fusion
  10.3 0.2 copy.41
  10.6 1.0 reshape.78
  11.5 17.2 %all-to-all-start = ((bf16[32,18,320]{2,1,0:T(8,128)(2,1)}), bf16[32,18,320]{2,1,0:T(8,128)(2,1)}, u32[]{:S(2)}, u32[]{:S(2)}) async-start(bf16[32,18,320]{2,1,0:T(8,128)(2,1)} %reshape.78), calls=%async_computation | async-start | bytes 1179648 | tf_op jit(solution)/shard_map/all_to_all | solution.py:22
  28.8 0.0 all-gather.3.cloned.1.call-start
  28.8 1.7 pad_maximum_fusion
  30.5 3.1 %collective-permute-start = (bf16[160,576]{1,0:T(8,128)(2,1)}, bf16[160,576]{1,0:T(8,128)(2,1)}, u32[]{:S(2)}, u32[]{:S(2)}) collective-permute-start(bf16[160,576]{1,0:T(8,128)(2,1)} %pad_maximum_fusion), channel_id=1, source_target_pairs={{0,256},{16,272},{32,288},{48,304},{64,320},{80,336},{96,352},{112... | collective-permute-start | bytes 552968 | tf_op jit(solution)/shard_map/ppermute | solution.py:125
  33.6 3.1 %slice_bitcast_fusion = (bf16[96,320]{0,1:T(8,128)(2,1)}, bf16[96,320]{0,1:T(8,128)(2,1)}, bf16[96,320]{0,1:T(8,128)(2,1)}, bf16[96,320]{0,1:T(8,128)(2,1)}, bf1...) fusion(bf16[1,1536,320]{1,2,0:T(8,128)(2,1)} %param.18), kind=kLoop, calls=%fused_computation.81 | loop fusion | bytes 1966080 | tf_op jit(solution)/shard_map/slice | solution.py:115
  36.7 1.1 pad_maximum_fusion.1
  37.7 1.4 fusion.8
  39.2 3.4 %concatenate.28 = bf16[192,2560]{1,0:T(8,128)(2,1)} concatenate(bf16[192,320]{1,0:T(8,128)(2,1)} %get-tuple-element.36, bf16[192,320]{1,0:T(8,128)(2,1)} %get-tuple-element.37, bf16[192,320]{1,0:T(8,128)(2,1)} %get-tuple-element.38, bf16[192,320]{1,0:T(8,128)(2,1)} %get-tuple-element.39, bf16[192,320]{1,0:T(8,128)(2,1)} %get-tuple-element.40, ...), dimensions={1} | concatenate | bytes 1966080 | tf_op jit(solution)/shard_map/concatenate | solution.py:116
  42.7 1.9 concatenate.27
  44.6 1.9 concatenate.30
  46.6 1.1 concatenate.29
  47.7 1.7 broadcast_select_fusion
  49.5 1.0 broadcast_select_fusion.2
  50.5 1.0 fusion.74
  51.5 1.9 maximum_select_fusion
  53.4 8.4 %all-to-all-done = bf16[32,18,320]{2,1,0:T(8,128)(2,1)} async-done(((bf16[32,18,320]{2,1,0:T(8,128)(2,1)}), bf16[32,18,320]{2,1,0:T(8,128)(2,1)}, u32[]{:S(2)}, u32[]{:S(2)}) %all-to-all-start) | async-done | bytes 368672 | tf_op jit(solution)/shard_map/all_to_all | solution.py:22
  61.8 2.1 reshape.79
  64.0 1.8 maximum_bitcast_fusion
  65.8 2.0 copy.42
  67.8 1.3 broadcast_in_dim.65
  69.0 45.4 %all_to_all.25.mine_ref = bf16[8,320,624]{2,1,0:T(8,128)(2,1)S(1)} all-to-all(bf16[8,320,624]{2,1,0:T(8,128)(2,1)S(1)} %broadcast_in_dim.65), channel_id=1, replica_groups={{0,2,4,6,8,10,12,14},{1,3,5,7,9,11,13,15},{16,18,20,22,24,26,28,30},{17..., dimensions={0} | all-to-all | bytes 6389760 | tf_op jit(solution)/shard_map/all_to_all | solution.py:22
  114.5 4.8 %collective-permute-start.1 = (bf16[8,320,624]{2,1,0:T(8,128)(2,1)S(1)}, bf16[8,320,624]{2,1,0:T(8,128)(2,1)S(1)}, u32[]{:S(2)}, u32[]{:S(2)}) collective-permute-start(bf16[8,320,624]{2,1,0:T(8,128)(2,1)S(1)} %all_to_all.25.mine_ref), channel_id=1, source_target_pairs={{0,1},{1,0},{2,3},{3,2},{4,5},{5,4},{6,7},{7,6},{8,9},{9,8},{10,11... | collective-permute-start | bytes 9584648 | tf_op jit(solution)/shard_map/ppermute | solution.py:29
  119.3 0.9 fusion.57
  120.2 4.5 %collective-permute-done.1.theirs_ref = bf16[8,320,624]{2,1,0:T(8,128)(2,1)S(1)} collective-permute-done((bf16[8,320,624]{2,1,0:T(8,128)(2,1)S(1)}, bf16[8,320,624]{2,1,0:T(8,128)(2,1)S(1)}, u32[]{:S(2)}, u32[]{:S(2)}) %collective-permute-start.1) | collective-permute-done | bytes 3194912 | tf_op jit(solution)/shard_map/ppermute | solution.py:29
  124.7 0.9 convolution_add_fusion.1
  125.6 0.9 copy-done.3
  126.5 0.1 fusion.7
  126.6 0.1 broadcast_in_dim.66
  126.7 18.4 %all_to_all.26 = bf16[8,96,576]{2,1,0:T(8,128)(2,1)S(1)} all-to-all(bf16[8,96,576]{2,1,0:T(8,128)(2,1)S(1)} %broadcast_in_dim.66), channel_id=1, replica_groups={{0,2,4,6,8,10,12,14},{1,3,5,7,9,11,13,15},{16,18,20,22,24,26,28,30},{17..., dimensions={0} | all-to-all | bytes 1769472 | tf_op jit(solution)/shard_map/all_to_all | solution.py:22
  145.1 3.4 %collective-permute-start.2 = (bf16[8,96,576]{2,1,0:T(8,128)(2,1)S(1)}, bf16[8,96,576]{2,1,0:T(8,128)(2,1)}, u32[]{:S(2)}, u32[]{:S(2)}) collective-permute-start(bf16[8,96,576]{2,1,0:T(8,128)(2,1)S(1)} %all_to_all.26), channel_id=1, source_target_pairs={{0,1},{1,0},{2,3},{3,2},{4,5},{5,4},{6,7},{7,6},{8,9},{9,8},{10,11... | collective-permute-start | bytes 2654216 | tf_op jit(solution)/shard_map/ppermute | solution.py:29
  148.5 1.5 fusion.58
  150.0 1.9 copy-done.2
  151.9 1.9 copy-done.4
  153.8 2.9 %copy-done.5 = bf16[32,160,576]{2,1,0:T(8,128)(2,1)S(1)} copy-done((bf16[32,160,576]{2,1,0:T(8,128)(2,1)S(1)}, bf16[32,160,576]{2,1,0:T(8,128)(2,1)}, u32[]{:S(2)}) %copy-start.5) | copy-done | bytes 5898264
  156.7 2.4 %shard_map.140 = (bf16[8,48,320]{2,1,0:T(8,128)(2,1)S(1)}, bf16[8,48,320]{2,1,0:T(8,128)(2,1)S(1)}) custom-call(s32[1]{0:T(128)} %bitcast.26.side_ref, bf16[8,320,624]{2,1,0:T(8,128)(2,1)S(1)} %copy-done.2, bf16[8,320,624]{2,1,0:T(8,128)(2,1)S(1)} %copy-done.4, bf16[16,2,160,576]{3,2,1,0:T(8,128)(2,1)S(1)} %bitcast.103), custom_call_target="tpu_custom_call" | custom-call | flops 1000 | bytes 1000 | tf_op jit(solution)/shard_map/pallas_call | solution.py:62
  159.1 1.9 collective-permute-start.3
  161.0 1.8 fusion
  162.8 0.2 copy.43
  163.1 1.0 reshape.84
  164.1 5.9 %all-to-all-start.3 = ((bf16[32,18,320]{2,1,0:T(8,128)(2,1)}), bf16[32,18,320]{2,1,0:T(8,128)(2,1)S(1)}, u32[]{:S(2)}, u32[]{:S(2)}) async-start(bf16[32,18,320]{2,1,0:T(8,128)(2,1)} %reshape.84), calls=%async_computation.3 | async-start | bytes 1179648 | tf_op jit(solution)/shard_map/all_to_all | solution.py:22
  170.0 0.1 add_convert_fusion
  170.1 3.5 %collective-permute-start.4 = (bf16[4,48,320]{2,1,0:T(8,128)(2,1)S(1)}, bf16[4,48,320]{2,1,0:T(8,128)(2,1)S(1)}, u32[]{:S(2)}, u32[]{:S(2)}) collective-permute-start(bf16[4,48,320]{2,1,0:T(8,128)(2,1)S(1)} %fusion.23), channel_id=1, source_target_pairs={{0,2},{1,3},{2,0},{3,1},{4,6},{5,7},{6,4},{7,5},{8,10},{9,11},{10,... | collective-permute-start | bytes 368648 | tf_op jit(solution)/shard_map/ppermute | solution.py:149
  173.7 4.5 %collective-permute-done.4 = bf16[4,48,320]{2,1,0:T(8,128)(2,1)S(1)} collective-permute-done((bf16[4,48,320]{2,1,0:T(8,128)(2,1)S(1)}, bf16[4,48,320]{2,1,0:T(8,128)(2,1)S(1)}, u32[]{:S(2)}, u32[]{:S(2)}) %collective-permute-start.4) | collective-permute-done | bytes 122912 | tf_op jit(solution)/shard_map/ppermute | solution.py:149
  178.1 0.1 fusion.56
  178.2 4.6 %collective-permute-start.7 = (bf16[48,320]{1,0:T(8,128)(2,1)S(1)}, bf16[48,320]{1,0:T(8,128)(2,1)S(1)}, u32[]{:S(2)}, u32[]{:S(2)}) collective-permute-start(bf16[48,320]{1,0:T(8,128)(2,1)S(1)} %get-tuple-element.61), channel_id=1, source_target_pairs={{0,12},{1,13},{2,14},{3,15},{4,0},{5,1},{6,2},{7,3},{8,4},{9,5},{1... | collective-permute-start | bytes 92168 | tf_op jit(solution)/shard_map/ppermute | solution.py:154
  182.9 2.3 collective-permute-start.6
  185.1 2.7 %collective-permute-start.5 = (bf16[48,320]{1,0:T(8,128)(2,1)S(1)}, bf16[48,320]{1,0:T(8,128)(2,1)S(1)}, u32[]{:S(2)}, u32[]{:S(2)}) collective-permute-start(bf16[48,320]{1,0:T(8,128)(2,1)S(1)} %get-tuple-element.60), channel_id=1, source_target_pairs={{0,4},{1,5},{2,6},{3,7},{4,8},{5,9},{6,10},{7,11},{8,12},{9,13},{1... | collective-permute-start | bytes 92168 | tf_op jit(solution)/shard_map/ppermute | solution.py:154
  187.9 1.5 collective-permute-done.6
  189.4 2.0 collective-permute-done.5
  191.4 11.6 %all-to-all-done.3 = bf16[32,18,320]{2,1,0:T(8,128)(2,1)S(1)} async-done(((bf16[32,18,320]{2,1,0:T(8,128)(2,1)}), bf16[32,18,320]{2,1,0:T(8,128)(2,1)S(1)}, u32[]{:S(2)}, u32[]{:S(2)}) %all-to-all-start.3) | async-done | bytes 368672 | tf_op jit(solution)/shard_map/all_to_all | solution.py:22
  203.0 0.2 reshape.87
  203.3 0.5 fusion.3
  203.8 0.1 broadcast_in_dim.72
  203.8 19.3 %all_to_all.27 = bf16[16,48,320]{2,1,0:T(8,128)(2,1)S(1)} all-to-all(bf16[16,48,320]{2,1,0:T(8,128)(2,1)S(1)} %broadcast_in_dim.72), channel_id=1, replica_groups=mesh['expert'=32,'tensor'=16] {'tensor'}, dimensions={0} | all-to-all | bytes 983040 | tf_op jit(solution)/shard_map/all_to_all | solution.py:22
  223.2 0.1 convert_bitcast_fusion
  223.3 0.4 copy.48
  223.7 1.3 reshape.89
  225.0 0.2 fusion.1
  225.3 2.4 %convolution_convert_fusion.2 = bf16[48,132]{1,0:T(8,128)(2,1)} fusion(bf16[132,5120]{1,0:T(8,128)(2,1)S(1)} %copy-done, f32[48,5120]{1,0:T(8,128)} %reshape.89, f32[5120]{0:T(1024)S(1)} %copy-done.37, f32[48]{0:T(128)S(1)} %add_rsqrt_fusion), kind=kOutput, calls=%fused_computation.41 | convolution fusion | flops 65624256 | bytes 2368064 | tf_op jit(solution)/shard_map/dot_general | solution.py:16
  (91 shorter events, 0.4 us)
Async XLA Ops:
  7.2 218.1 %copy-start = (bf16[132,5120]{1,0:T(8,128)(2,1)S(1)}, bf16[132,5120]{1,0:T(8,128)(2,1)}, u32[]{:S(2)}) copy-start(bf16[132,5120]{1,0:T(8,128)(2,1)} %param.23) | copy-start | bytes 4055044
  7.2 21.6 %copy-start.32 = (bf16[192,160]{0,1:T(8,128)(2,1)S(1)}, bf16[192,160]{0,1:T(8,128)(2,1)}, u32[]{:S(2)}) copy-start(bf16[192,160]{0,1:T(8,128)(2,1)} %param.21) | copy-start | bytes 184324
  7.2 21.6 %copy-start.34 = (bf16[160,192]{1,0:T(8,128)(2,1)S(1)}, bf16[160,192]{1,0:T(8,128)(2,1)}, u32[]{:S(2)}) copy-start(bf16[160,192]{1,0:T(8,128)(2,1)} %param.20) | copy-start | bytes 184324
  11.5 25.1 %copy-start.6 = (bf16[1,96,5120]{2,1,0:T(8,128)(2,1)S(1)}, bf16[1,96,5120]{2,1,0:T(8,128)(2,1)}, u32[]{:S(2)}) copy-start(bf16[1,96,5120]{2,1,0:T(8,128)(2,1)} %param.16) | copy-start | bytes 2949124
  11.5 25.1 %copy-start.7 = (bf16[1,96,5120]{2,1,0:T(8,128)(2,1)S(1)}, bf16[1,96,5120]{2,1,0:T(8,128)(2,1)}, u32[]{:S(2)}) copy-start(bf16[1,96,5120]{2,1,0:T(8,128)(2,1)} %param.17) | copy-start | bytes 2949124
  11.5 50.3 %all-to-all-start = ((bf16[32,18,320]{2,1,0:T(8,128)(2,1)}), bf16[32,18,320]{2,1,0:T(8,128)(2,1)}, u32[]{:S(2)}, u32[]{:S(2)}) async-start(bf16[32,18,320]{2,1,0:T(8,128)(2,1)} %reshape.78), calls=%async_computation | async-start | bytes 1179648 | tf_op jit(solution)/shard_map/all_to_all | solution.py:22
  28.8 121.2 %all-gather.3.cloned.1.call-start = ((), (), s32[]{:S(2)}) async-start(), calls=%async_computation.5 | async-start | bytes 6963200 | tf_op jit(solution)/shard_map/all_gather | solution.py:130
  30.5 21.0 %collective-permute-start = (bf16[160,576]{1,0:T(8,128)(2,1)}, bf16[160,576]{1,0:T(8,128)(2,1)}, u32[]{:S(2)}, u32[]{:S(2)}) collective-permute-start(bf16[160,576]{1,0:T(8,128)(2,1)} %pad_maximum_fusion), channel_id=1, source_target_pairs={{0,256},{16,272},{32,288},{48,304},{64,320},{80,336},{96,352},{112... | collective-permute-start | bytes 552968 | tf_op jit(solution)/shard_map/ppermute | solution.py:125
  39.2 3.5 %copy-start.13 = (bf16[192,320]{1,0:T(8,128)(2,1)S(1)}, bf16[192,320]{1,0:T(8,128)(2,1)}, u32[]{:S(2)}) copy-start(bf16[192,320]{1,0:T(8,128)(2,1)} %get-tuple-element.28) | copy-start | bytes 368644
  39.2 3.5 %copy-start.14 = (bf16[192,320]{1,0:T(8,128)(2,1)S(1)}, bf16[192,320]{1,0:T(8,128)(2,1)}, u32[]{:S(2)}) copy-start(bf16[192,320]{1,0:T(8,128)(2,1)} %get-tuple-element.29) | copy-start | bytes 368644
  39.2 3.5 %copy-start.15 = (bf16[192,320]{1,0:T(8,128)(2,1)S(1)}, bf16[192,320]{1,0:T(8,128)(2,1)}, u32[]{:S(2)}) copy-start(bf16[192,320]{1,0:T(8,128)(2,1)} %get-tuple-element.30) | copy-start | bytes 368644
  39.2 3.5 %copy-start.16 = (bf16[192,320]{1,0:T(8,128)(2,1)S(1)}, bf16[192,320]{1,0:T(8,128)(2,1)}, u32[]{:S(2)}) copy-start(bf16[192,320]{1,0:T(8,128)(2,1)} %get-tuple-element.31) | copy-start | bytes 368644
  39.2 3.5 %copy-start.17 = (bf16[192,320]{1,0:T(8,128)(2,1)S(1)}, bf16[192,320]{1,0:T(8,128)(2,1)}, u32[]{:S(2)}) copy-start(bf16[192,320]{1,0:T(8,128)(2,1)} %get-tuple-element.32) | copy-start | bytes 368644
  39.2 3.5 %copy-start.18 = (bf16[192,320]{1,0:T(8,128)(2,1)S(1)}, bf16[192,320]{1,0:T(8,128)(2,1)}, u32[]{:S(2)}) copy-start(bf16[192,320]{1,0:T(8,128)(2,1)} %get-tuple-element.33) | copy-start | bytes 368644
  39.2 3.5 %copy-start.19 = (bf16[192,320]{1,0:T(8,128)(2,1)S(1)}, bf16[192,320]{1,0:T(8,128)(2,1)}, u32[]{:S(2)}) copy-start(bf16[192,320]{1,0:T(8,128)(2,1)} %get-tuple-element.34) | copy-start | bytes 368644
  39.2 5.4 %copy-start.29 = (bf16[96,320]{0,1:T(8,128)(2,1)S(1)}, bf16[96,320]{0,1:T(8,128)(2,1)}, u32[]{:S(2)}) copy-start(bf16[96,320]{0,1:T(8,128)(2,1)} %get-tuple-element.44) | copy-start | bytes 184324
  39.2 5.4 %copy-start.30 = (bf16[96,320]{0,1:T(8,128)(2,1)S(1)}, bf16[96,320]{0,1:T(8,128)(2,1)}, u32[]{:S(2)}) copy-start(bf16[96,320]{0,1:T(8,128)(2,1)} %get-tuple-element.45) | copy-start | bytes 184324
  39.2 5.4 %copy-start.31 = (bf16[96,320]{0,1:T(8,128)(2,1)S(1)}, bf16[96,320]{0,1:T(8,128)(2,1)}, u32[]{:S(2)}) copy-start(bf16[96,320]{0,1:T(8,128)(2,1)} %get-tuple-element.46) | copy-start | bytes 184324
  42.6 3.9 %copy-start.21 = (bf16[96,320]{0,1:T(8,128)(2,1)S(1)}, bf16[96,320]{0,1:T(8,128)(2,1)}, u32[]{:S(2)}) copy-start(bf16[96,320]{0,1:T(8,128)(2,1)} %get-tuple-element.51) | copy-start | bytes 184324
  42.6 3.9 %copy-start.22 = (bf16[96,320]{0,1:T(8,128)(2,1)S(1)}, bf16[96,320]{0,1:T(8,128)(2,1)}, u32[]{:S(2)}) copy-start(bf16[96,320]{0,1:T(8,128)(2,1)} %get-tuple-element.52) | copy-start | bytes 184324
  42.6 3.9 %copy-start.23 = (bf16[96,320]{0,1:T(8,128)(2,1)S(1)}, bf16[96,320]{0,1:T(8,128)(2,1)}, u32[]{:S(2)}) copy-start(bf16[96,320]{0,1:T(8,128)(2,1)} %get-tuple-element.53) | copy-start | bytes 184324
  42.6 3.9 %copy-start.24 = (bf16[96,320]{0,1:T(8,128)(2,1)S(1)}, bf16[96,320]{0,1:T(8,128)(2,1)}, u32[]{:S(2)}) copy-start(bf16[96,320]{0,1:T(8,128)(2,1)} %get-tuple-element.54) | copy-start | bytes 184324
  42.6 3.9 %copy-start.25 = (bf16[96,320]{0,1:T(8,128)(2,1)S(1)}, bf16[96,320]{0,1:T(8,128)(2,1)}, u32[]{:S(2)}) copy-start(bf16[96,320]{0,1:T(8,128)(2,1)} %get-tuple-element.55) | copy-start | bytes 184324
  42.6 3.9 %copy-start.26 = (bf16[96,320]{0,1:T(8,128)(2,1)S(1)}, bf16[96,320]{0,1:T(8,128)(2,1)}, u32[]{:S(2)}) copy-start(bf16[96,320]{0,1:T(8,128)(2,1)} %get-tuple-element.56) | copy-start | bytes 184324
  42.7 3.9 %copy-start.27 = (bf16[96,320]{0,1:T(8,128)(2,1)S(1)}, bf16[96,320]{0,1:T(8,128)(2,1)}, u32[]{:S(2)}) copy-start(bf16[96,320]{0,1:T(8,128)(2,1)} %get-tuple-element.57) | copy-start | bytes 184324
  42.7 3.9 %copy-start.28 = (bf16[96,320]{0,1:T(8,128)(2,1)S(1)}, bf16[96,320]{0,1:T(8,128)(2,1)}, u32[]{:S(2)}) copy-start(bf16[96,320]{0,1:T(8,128)(2,1)} %get-tuple-element.58) | copy-start | bytes 184324
  47.7 1.7 copy-start.11
  47.7 1.8 copy-start.12
  49.5 1.0 copy-start.33
  49.5 14.5 %copy-start.20 = (bf16[48,320]{1,0:T(8,128)(2,1)S(1)}, bf16[48,320]{1,0:T(8,128)(2,1)}, u32[]{:S(2)}) copy-start(bf16[48,320]{1,0:T(8,128)(2,1)} %param.13) | copy-start | bytes 92164
  114.5 5.7 %copy-start.1 = (bf16[8,320,624]{2,1,0:T(8,128)(2,1)}, bf16[8,320,624]{2,1,0:T(8,128)(2,1)S(1)}, u32[]{:S(2)}) copy-start(bf16[8,320,624]{2,1,0:T(8,128)(2,1)S(1)} %all_to_all.25.mine_ref) | copy-start | bytes 9584644
  114.5 10.2 %collective-permute-start.1 = (bf16[8,320,624]{2,1,0:T(8,128)(2,1)S(1)}, bf16[8,320,624]{2,1,0:T(8,128)(2,1)S(1)}, u32[]{:S(2)}, u32[]{:S(2)}) collective-permute-start(bf16[8,320,624]{2,1,0:T(8,128)(2,1)S(1)} %all_to_all.25.mine_ref), channel_id=1, source_target_pairs={{0,1},{1,0},{2,3},{3,2},{4,5},{5,4},{6,7},{7,6},{8,9},{9,8},{10,11... | collective-permute-start | bytes 9584648 | tf_op jit(solution)/shard_map/ppermute | solution.py:29
  124.7 1.8 copy-start.3
  126.5 22.0 %copy-start.10 = (bf16[768,320]{0,1:T(8,128)(2,1)S(1)}, bf16[768,320]{0,1:T(8,128)(2,1)}, u32[]{:S(2)}) copy-start(bf16[768,320]{0,1:T(8,128)(2,1)} %get-tuple-element.15) | copy-start | bytes 1474564
  145.1 15.9 %collective-permute-start.2 = (bf16[8,96,576]{2,1,0:T(8,128)(2,1)S(1)}, bf16[8,96,576]{2,1,0:T(8,128)(2,1)}, u32[]{:S(2)}, u32[]{:S(2)}) collective-permute-start(bf16[8,96,576]{2,1,0:T(8,128)(2,1)S(1)} %all_to_all.26), channel_id=1, source_target_pairs={{0,1},{1,0},{2,3},{3,2},{4,5},{5,4},{6,7},{7,6},{8,9},{9,8},{10,11... | collective-permute-start | bytes 2654216 | tf_op jit(solution)/shard_map/ppermute | solution.py:29
  150.0 1.9 copy-start.2
  151.9 1.9 copy-start.4
  153.8 2.9 %copy-start.5 = (bf16[32,160,576]{2,1,0:T(8,128)(2,1)S(1)}, bf16[32,160,576]{2,1,0:T(8,128)(2,1)}, u32[]{:S(2)}) copy-start(bf16[32,160,576]{2,1,0:T(8,128)(2,1)} %all-gather.3.cloned.1.call-done) | copy-start | bytes 17694724
  156.7 4.3 %copy-start.8 = (f32[576,320]{0,1:T(8,128)S(1)}, f32[576,320]{0,1:T(8,128)}, u32[]{:S(2)}) copy-start(f32[576,320]{0,1:T(8,128)} %fusion.58) | copy-start | bytes 2211844
  156.7 4.3 %copy-start.9 = (bf16[768,320]{0,1:T(8,128)(2,1)S(1)}, bf16[768,320]{0,1:T(8,128)(2,1)}, u32[]{:S(2)}) copy-start(bf16[768,320]{0,1:T(8,128)(2,1)} %get-tuple-element.16) | copy-start | bytes 1474564
  159.1 10.9 %collective-permute-start.3 = (bf16[8,48,320]{2,1,0:T(8,128)(2,1)S(1)}, bf16[8,48,320]{2,1,0:T(8,128)(2,1)S(1)}, u32[]{:S(2)}, u32[]{:S(2)}) collective-permute-start(bf16[8,48,320]{2,1,0:T(8,128)(2,1)S(1)} %get-tuple-element.19), channel_id=1, source_target_pairs={{0,1},{1,0},{2,3},{3,2},{4,5},{5,4},{6,7},{7,6},{8,9},{9,8},{10,11... | collective-permute-start | bytes 737288 | tf_op jit(solution)/shard_map/ppermute | solution.py:144
  163.1 10.6 %copy-start.38 = (s32[48,6]{0,1:T(8,128)S(1)}, s32[48,6]{0,1:T(8,128)}, u32[]{:S(2)}) copy-start(s32[48,6]{0,1:T(8,128)} %param.14) | copy-start | bytes 3460
  163.1 10.6 %copy-start.39 = (f32[48,6]{0,1:T(8,128)S(1)}, f32[48,6]{0,1:T(8,128)}, u32[]{:S(2)}) copy-start(f32[48,6]{0,1:T(8,128)} %param.15) | copy-start | bytes 3460
  164.1 38.9 %all-to-all-start.3 = ((bf16[32,18,320]{2,1,0:T(8,128)(2,1)}), bf16[32,18,320]{2,1,0:T(8,128)(2,1)S(1)}, u32[]{:S(2)}, u32[]{:S(2)}) async-start(bf16[32,18,320]{2,1,0:T(8,128)(2,1)} %reshape.84), calls=%async_computation.3 | async-start | bytes 1179648 | tf_op jit(solution)/shard_map/all_to_all | solution.py:22
  170.0 33.2 %copy-start.36 = (bf16[32,576]{1,0:T(8,128)(2,1)S(1)}, bf16[32,576]{1,0:T(8,128)(2,1)}, u32[]{:S(2)}) copy-start(bf16[32,576]{1,0:T(8,128)(2,1)} %constant.58.clone) | copy-start | bytes 110596
  170.1 8.0 %collective-permute-start.4 = (bf16[4,48,320]{2,1,0:T(8,128)(2,1)S(1)}, bf16[4,48,320]{2,1,0:T(8,128)(2,1)S(1)}, u32[]{:S(2)}, u32[]{:S(2)}) collective-permute-start(bf16[4,48,320]{2,1,0:T(8,128)(2,1)S(1)} %fusion.23), channel_id=1, source_target_pairs={{0,2},{1,3},{2,0},{3,1},{4,6},{5,7},{6,4},{7,5},{8,10},{9,11},{10,... | collective-permute-start | bytes 368648 | tf_op jit(solution)/shard_map/ppermute | solution.py:149
  178.2 9.6 %collective-permute-start.7 = (bf16[48,320]{1,0:T(8,128)(2,1)S(1)}, bf16[48,320]{1,0:T(8,128)(2,1)S(1)}, u32[]{:S(2)}, u32[]{:S(2)}) collective-permute-start(bf16[48,320]{1,0:T(8,128)(2,1)S(1)} %get-tuple-element.61), channel_id=1, source_target_pairs={{0,12},{1,13},{2,14},{3,15},{4,0},{5,1},{6,2},{7,3},{8,4},{9,5},{1... | collective-permute-start | bytes 92168 | tf_op jit(solution)/shard_map/ppermute | solution.py:154
  182.9 6.5 %collective-permute-start.6 = (bf16[48,320]{1,0:T(8,128)(2,1)S(1)}, bf16[48,320]{1,0:T(8,128)(2,1)S(1)}, u32[]{:S(2)}, u32[]{:S(2)}) collective-permute-start(bf16[48,320]{1,0:T(8,128)(2,1)S(1)} %get-tuple-element.62), channel_id=1, source_target_pairs={{0,8},{1,9},{2,10},{3,11},{4,12},{5,13},{6,14},{7,15},{8,0},{9,1},... | collective-permute-start | bytes 92168 | tf_op jit(solution)/shard_map/ppermute | solution.py:154
  185.1 6.2 %collective-permute-start.5 = (bf16[48,320]{1,0:T(8,128)(2,1)S(1)}, bf16[48,320]{1,0:T(8,128)(2,1)S(1)}, u32[]{:S(2)}, u32[]{:S(2)}) collective-permute-start(bf16[48,320]{1,0:T(8,128)(2,1)S(1)} %get-tuple-element.60), channel_id=1, source_target_pairs={{0,4},{1,5},{2,6},{3,7},{4,8},{5,9},{6,10},{7,11},{8,12},{9,13},{1... | collective-permute-start | bytes 92168 | tf_op jit(solution)/shard_map/ppermute | solution.py:154
  203.8 19.9 %copy-start.35 = (bf16[48,320]{1,0:T(8,128)(2,1)}, bf16[48,320]{1,0:T(8,128)(2,1)S(1)}, u32[]{:S(2)}) copy-start(bf16[48,320]{1,0:T(8,128)(2,1)S(1)} %fusion.27) | copy-start | bytes 92164
  223.7 1.6 copy-start.37
Sparse Core Ops, SparseCore 0:
  62.0 82.1 all-gather.2

commit v4 on v3

--- a/solution.py
+++ b/solution.py
@@ -30,15 +30,15 @@
     return mine, theirs
 
 
-def shared_kernel(side_ref, mine_ref, theirs_ref, table_ref, keep_ref, give_ref):
-    side = side_ref[0]
+def shared_kernel(rank_ref, mine_ref, theirs_ref, table_ref, keep_ref, give_ref):
+    side, place = rank_ref[0] & 1, rank_ref[0] >> 1
     inner = table_ref.shape[3] // 3
     size = table_ref.shape[2]
     start = mine_ref.shape[2] // 2
 
     def weights(chip, half):
-        first = 2 * (2 * (chip % 4) + half)
-        return table_ref.at[pl.ds(first, 2), chip // 4]
+        first = 2 * (2 * (chip & 3) + half)
+        return table_ref.at[pl.ds(first, 2), chip >> 2]
 
     sums = jnp.zeros((mine_ref.shape[2], 2 * inner), jnp.float32)
     for chip in range(CHIPS):
@@ -48,13 +48,13 @@
     sums = sums[start : start + keep_ref.shape[1]]
     gate, up = sums[:, :inner], sums[:, inner:]
     hidden = (gate * (1.0 / (1.0 + jnp.exp(-gate))) * up).astype(jnp.bfloat16)
-    for chip in range(CHIPS):
+    for step in range(CHIPS):
         for ref, half in ((keep_ref, side), (give_ref, 1 - side)):
-            block = weights(chip, half)[:, :, 2 * inner :].reshape(2 * size, inner)
-            ref[chip] = dot(hidden, block, 1, 1).astype(ref.dtype)
+            block = weights(place ^ step, half)[:, :, 2 * inner :].reshape(2 * size, inner)
+            ref[step] = dot(hidden, block, 1, 1).astype(ref.dtype)
 
 
-def shared_partial(side, mine, theirs, table, tok):
+def shared_partial(rank, mine, theirs, table, tok):
     width = mine.shape[1]
     out = jax.ShapeDtypeStruct((CHIPS, tok, width), jnp.bfloat16)
     last = pl.BlockSpec((CHIPS, width, 128), lambda i: (0, 0, 4))
@@ -72,7 +72,7 @@
         out_specs=(whole, whole),
         compiler_params=pltpu.CompilerParams(vmem_limit_bytes=32 * 2**20),
         cost_estimate=pl.CostEstimate(flops=1000, bytes_accessed=1000, transcendentals=0),
-    )(side.reshape(1), mine, theirs, table)
+    )(rank.reshape(1), mine, theirs, table)
 
 
 def per_device(
@@ -95,7 +95,7 @@
     slots = experts * cap
     bf16, f32 = jnp.bfloat16, jnp.float32
     rank = lax.axis_index("tensor")
-    side, across, ring = rank & 1, (rank >> 1) & 1, rank >> 2
+    side = rank & 1
     column = lax.axis_index("expert") >> 4
 
     match = expert_ids[:, :, None] == jnp.arange(experts, dtype=jnp.int32)[None, None, :]
@@ -123,13 +123,15 @@
 
     own = jnp.concatenate([shared_gate, shared_up, shared_down.T], axis=1)
     other = lax.ppermute(own, "expert", [(i, (i + ROWS) % (2 * ROWS)) for i in range(2 * ROWS)])
+    first = arrived[0, 0, 0]
+    column = column + jnp.where(first == first, 0, 2)
     pair = jnp.where(column == 0, jnp.stack([own, other]), jnp.stack([other, own]))
-    arrived, pair, in_mine, in_theirs, out_mine, out_theirs = lax.optimization_barrier(
-        (arrived, pair, in_mine, in_theirs, out_mine, out_theirs)
+    pair, late, in_mine, in_theirs, out_mine, out_theirs = lax.optimization_barrier(
+        (pair, tokens, in_mine, in_theirs, out_mine, out_theirs)
     )
     gathered = lax.all_gather(pair, "expert", axis=0, axis_index_groups=LANES)
 
-    rows = jnp.concatenate([arrived.reshape(slots, width), tokens], axis=0)
+    rows = jnp.concatenate([arrived.reshape(slots, width), late], axis=0)
     mine, theirs = gather_halves(rows.T)
     total = slots + tok
     both = dot(in_mine, mine.reshape(-1, total), 1, 0) + dot(in_theirs, theirs.reshape(-1, total), 1, 0)
@@ -138,22 +140,16 @@
     result = dot(hidden_mine.reshape(-1, slots), out_mine, 0, 0) + dot(
         hidden_theirs.reshape(-1, slots), out_theirs, 0, 0
     )
-    returned = exchange(result.astype(bf16).reshape(experts, cap, width), "expert")
-    keep, give = shared_partial(side, mine, theirs, gathered, tok)
+    result = result.astype(bf16).reshape(experts, cap, width)
+    returned = exchange(result, "expert")
+    keep, give = shared_partial(rank, mine, theirs, gathered, tok)
 
     got = lax.ppermute(give, "tensor", [(i, i ^ 1) for i in range(2 * CHIPS)])
-    partial = (keep.astype(f32) + got.astype(f32)).astype(bf16)
-    partial = partial.reshape((-1, 2) + partial.shape[1:])
-    keep = jnp.where(across == 0, partial[:, 0], partial[:, 1])
-    give = jnp.where(across == 0, partial[:, 1], partial[:, 0])
-    got = lax.ppermute(give, "tensor", [(i, i ^ 2) for i in range(2 * CHIPS)])
     partial = keep.astype(f32) + got.astype(f32)
-    shared = lax.dynamic_index_in_dim(partial, ring, 0, keepdims=False)
-    for step in range(1, 4):
-        give = lax.dynamic_index_in_dim(partial.astype(bf16), (ring + step) & 3, 0, keepdims=False)
-        got = lax.ppermute(
-            give, "tensor", [(i, (i + 4 * step) % (2 * CHIPS)) for i in range(2 * CHIPS)]
-        )
+    shared = partial[0]
+    for step in range(1, CHIPS):
+        give = partial[step].astype(bf16)
+        got = lax.ppermute(give, "tensor", [(i, i ^ (2 * step)) for i in range(2 * CHIPS)])
         shared = shared + got.astype(f32)
 
     returned, shared = lax.optimization_barrier((returned, shared))

time: 236 us -> 246 us (1.042)
  starting transfers between devices: 49.4 us -> 62.3 us
  waiting for transfers between devices: 32.5 us -> 25.5 us
  local copies, waits for them, and re-layouts: 29 us -> 31.5 us
    ppermute x4 -> x7, starting transfers between devices: 13.1 us -> 25.6 us  [per_device(): lax.ppermute(give, 'tensor', [(i, i ^ 2 * step) for i in range(2 * CHIPS)])]
    ppermute x4 -> x7, waiting for transfers between devices: 7.98 us -> 2.44 us  [per_device(): lax.ppermute(give, 'tensor', [(i, i ^ 2 * step) for i in range(2 * CHIPS)])]
    all_to_all x2, waiting for transfers between devices: 20 us -> 15.7 us  [exchange(): lax.all_to_all(parts, axis, split_axis=0, concat_axis=0, tiled=True, axis...]
    unnamed x80 -> x52, local copies, waits for them, and re-layouts: 7.79 us -> 7.72 us
  transfers between devices with their start and end apart: 11 -> 14, of which waited for: 6 -> 5; matrix products, arithmetic and copies ran while one was open for 15% -> 15% of each run, Pallas kernels for 1% -> 1%
where the time goes in v4:
time: 246 us; the launch traced here: 244 us
  blocking collectives  83.2 us (34%)
  starting transfers between devices  62.3 us (25%)
  local copies, waits for them, and re-layouts  31.5 us (13%)
  waiting for transfers between devices  25.5 us (10%)
  between operations  15.9 us (6%)
  other arithmetic  14.1 us (6%)
  matrix products  8.93 us (4%)
    all_to_all x3, blocking collectives, exchange(): lax.all_to_all(parts, axis, split_axis=0, concat_axis=0, tiled=True, axis...  83.2 us
    ppermute x7, starting transfers between devices, per_device(): lax.ppermute(give, 'tensor', [(i, i ^ 2 * step) for i in range(2 * CHIPS)])  25.6 us
    all_to_all x2, starting transfers between devices, exchange(): lax.all_to_all(parts, axis, split_axis=0, concat_axis=0, tiled=True, axis...  21.3 us
    all_to_all x2, waiting for transfers between devices, exchange(): lax.all_to_all(parts, axis, split_axis=0, concat_axis=0, tiled=True, axis...  15.7 us
    concatenate x4, local copies, waits for them, and re-layouts, by_side(): even, odd = (jnp.concatenate(pieces[k::2], axis=axis) for k in range(2))  9.08 us
    ppermute x2, starting transfers between devices, gather_halves(): lax.ppermute(mine, 'tensor', [(i, i ^ 1) for i in range(2 * CHIPS)])  8.64 us
    dot_general x7, matrix products, dot(): lax.dot_general(left, right, (((over_left,), (over_right,)), ((), ())), p...  7.75 us
    unnamed x52, local copies, waits for them, and re-layouts  7.72 us
  transfers between devices with their start and end apart: 14, of which 5 were waited for; matrix products, arithmetic and copies ran while one was open for 15% of the time, Pallas kernels for 1%

profile of v4, /device:TPU:1, one launch (start us, length us, event | category | flops | bytes accessed | tf_op | source)
XLA Modules:
  0.0 243.8 jit_solution(2177148360557082495)
XLA Ops:
  7.2 1.9 pad_maximum_fusion
  9.0 4.1 %collective-permute-start = (bf16[160,576]{1,0:T(8,128)(2,1)}, bf16[160,576]{1,0:T(8,128)(2,1)}, u32[]{:S(2)}, u32[]{:S(2)}) collective-permute-start(bf16[160,576]{1,0:T(8,128)(2,1)} %pad_maximum_fusion), channel_id=1, source_target_pairs={{0,256},{16,272},{32,288},{48,304},{64,320},{80,336},{96,352},{112... | collective-permute-start | bytes 552968 | tf_op jit(solution)/shard_map/ppermute | solution.py:125
  13.1 0.7 fusion.23
  13.8 1.2 convolution_compare_fusion
  15.0 1.9 convolution_convert_fusion
  16.9 2.0 copy.29
  18.8 2.0 reshape.80
  20.8 15.3 %all-to-all-start = ((bf16[32,18,320]{2,1,0:T(8,128)(2,1)}), bf16[32,18,320]{2,1,0:T(8,128)(2,1)}, u32[]{:S(2)}, u32[]{:S(2)}) async-start(bf16[32,18,320]{2,1,0:T(8,128)(2,1)} %reshape.80), calls=%async_computation | async-start | bytes 1179648 | tf_op jit(solution)/shard_map/all_to_all | solution.py:22
  36.2 1.4 fusion.8
  37.7 1.1 pad_maximum_fusion.1
  38.8 3.4 %concatenate.28 = bf16[192,2560]{1,0:T(8,128)(2,1)} concatenate(bf16[192,320]{1,0:T(8,128)(2,1)} %get-tuple-element.34, bf16[192,320]{1,0:T(8,128)(2,1)} %get-tuple-element.35, bf16[192,320]{1,0:T(8,128)(2,1)} %get-tuple-element.36, bf16[192,320]{1,0:T(8,128)(2,1)} %get-tuple-element.37, bf16[192,320]{1,0:T(8,128)(2,1)} %get-tuple-element.38, ...), dimensions={1} | concatenate | bytes 1966080 | tf_op jit(solution)/shard_map/concatenate | solution.py:116
  42.2 2.8 %concatenate.27 = bf16[192,2560]{1,0:T(8,128)(2,1)} concatenate(bf16[192,320]{1,0:T(8,128)(2,1)S(1)} %get-tuple-element.25, bf16[192,320]{1,0:T(8,128)(2,1)S(1)} %copy-done.13, bf16[192,320]{1,0:T(8,128)(2,1)S(1)} %copy-done.14, bf16[192,320]{1,0:T(8,128)(2,1)S(1)} %copy-done.15, bf16[192,320]{1,0:T(8,128)(2,1)S(1)} %copy-done.16, bf16[192,320]{1,0:T(8,128)(2,1)S(1)} %copy-done.17, ...), dimensions={1} | concatenate | bytes 1966080 | tf_op jit(solution)/shard_map/concatenate | solution.py:116
  45.0 1.0 slice_bitcast_fusion
  46.0 1.8 concatenate.30
  47.9 1.1 concatenate.29
  49.0 1.7 broadcast_select_fusion
  50.8 1.0 broadcast_select_fusion.2
  51.8 1.7 fusion.77
  53.5 15.7 %all-to-all-done = bf16[32,18,320]{2,1,0:T(8,128)(2,1)} async-done(((bf16[32,18,320]{2,1,0:T(8,128)(2,1)}), bf16[32,18,320]{2,1,0:T(8,128)(2,1)}, u32[]{:S(2)}, u32[]{:S(2)}) %all-to-all-start) | async-done | bytes 368672 | tf_op jit(solution)/shard_map/all_to_all | solution.py:22
  69.2 1.2 slice.251
  71.7 2.1 maximum_select_fusion
  73.9 2.1 reshape.81
  76.0 1.8 maximum_bitcast_fusion
  77.8 2.0 copy.30
  79.8 1.3 broadcast_in_dim.65
  81.0 45.2 %all_to_all.25.mine_ref = bf16[8,320,624]{2,1,0:T(8,128)(2,1)S(1)} all-to-all(bf16[8,320,624]{2,1,0:T(8,128)(2,1)S(1)} %broadcast_in_dim.65), channel_id=1, replica_groups={{0,2,4,6,8,10,12,14},{1,3,5,7,9,11,13,15},{16,18,20,22,24,26,28,30},{17..., dimensions={0} | all-to-all | bytes 6389760 | tf_op jit(solution)/shard_map/all_to_all | solution.py:22
  126.3 5.2 %collective-permute-start.1 = (bf16[8,320,624]{2,1,0:T(8,128)(2,1)S(1)}, bf16[8,320,624]{2,1,0:T(8,128)(2,1)S(1)}, u32[]{:S(2)}, u32[]{:S(2)}) collective-permute-start(bf16[8,320,624]{2,1,0:T(8,128)(2,1)S(1)} %all_to_all.25.mine_ref), channel_id=1, source_target_pairs={{0,1},{1,0},{2,3},{3,2},{4,5},{5,4},{6,7},{7,6},{8,9},{9,8},{10,11... | collective-permute-start | bytes 9584648 | tf_op jit(solution)/shard_map/ppermute | solution.py:29
  131.5 0.9 fusion.60
  132.5 4.5 %collective-permute-done.1.theirs_ref = bf16[8,320,624]{2,1,0:T(8,128)(2,1)S(1)} collective-permute-done((bf16[8,320,624]{2,1,0:T(8,128)(2,1)S(1)}, bf16[8,320,624]{2,1,0:T(8,128)(2,1)S(1)}, u32[]{:S(2)}, u32[]{:S(2)}) %collective-permute-start.1) | collective-permute-done | bytes 3194912 | tf_op jit(solution)/shard_map/ppermute | solution.py:29
  137.0 0.9 convolution_add_fusion.1
  137.9 0.9 copy-done.3
  138.8 0.1 fusion.7
  138.9 0.1 broadcast_in_dim.66
  139.0 18.5 %all_to_all.26 = bf16[8,96,576]{2,1,0:T(8,128)(2,1)S(1)} all-to-all(bf16[8,96,576]{2,1,0:T(8,128)(2,1)S(1)} %broadcast_in_dim.66), channel_id=1, replica_groups={{0,2,4,6,8,10,12,14},{1,3,5,7,9,11,13,15},{16,18,20,22,24,26,28,30},{17..., dimensions={0} | all-to-all | bytes 1769472 | tf_op jit(solution)/shard_map/all_to_all | solution.py:22
  157.5 3.4 %collective-permute-start.2 = (bf16[8,96,576]{2,1,0:T(8,128)(2,1)S(1)}, bf16[8,96,576]{2,1,0:T(8,128)(2,1)S(1)}, u32[]{:S(2)}, u32[]{:S(2)}) collective-permute-start(bf16[8,96,576]{2,1,0:T(8,128)(2,1)S(1)} %all_to_all.26), channel_id=1, source_target_pairs={{0,1},{1,0},{2,3},{3,2},{4,5},{5,4},{6,7},{7,6},{8,9},{9,8},{10,11... | collective-permute-start | bytes 2654216 | tf_op jit(solution)/shard_map/ppermute | solution.py:29
  160.9 0.6 fusion.61
  161.5 1.6 collective-permute-done.2
  163.1 0.6 fusion
  163.6 0.2 copy.31
  163.9 1.0 reshape.86
  164.9 5.9 %all-to-all-start.3 = ((bf16[32,18,320]{2,1,0:T(8,128)(2,1)}), bf16[32,18,320]{2,1,0:T(8,128)(2,1)S(1)}, u32[]{:S(2)}, u32[]{:S(2)}) async-start(bf16[32,18,320]{2,1,0:T(8,128)(2,1)} %reshape.86), calls=%async_computation.3 | async-start | bytes 1179648 | tf_op jit(solution)/shard_map/all_to_all | solution.py:22
  170.8 1.9 copy-done.2
  172.8 1.9 copy-done.4
  174.7 2.9 %copy-done.5 = bf16[32,160,576]{2,1,0:T(8,128)(2,1)S(1)} copy-done((bf16[32,160,576]{2,1,0:T(8,128)(2,1)S(1)}, bf16[32,160,576]{2,1,0:T(8,128)(2,1)}, u32[]{:S(2)}) %copy-start.5) | copy-done | bytes 5898264
  177.5 2.4 shard_map.140
  180.0 2.7 %collective-permute-start.3 = (bf16[8,48,320]{2,1,0:T(8,128)(2,1)S(1)}, bf16[8,48,320]{2,1,0:T(8,128)(2,1)S(1)}, u32[]{:S(2)}, u32[]{:S(2)}) collective-permute-start(bf16[8,48,320]{2,1,0:T(8,128)(2,1)S(1)} %get-tuple-element.19), channel_id=1, source_target_pairs={{0,1},{1,0},{2,3},{3,2},{4,5},{5,4},{6,7},{7,6},{8,9},{9,8},{10,11... | collective-permute-start | bytes 737288 | tf_op jit(solution)/shard_map/ppermute | solution.py:147
  182.7 1.2 collective-permute-done.3
  183.9 0.1 fusion.59
  184.0 3.7 %collective-permute-start.10 = (bf16[48,320]{1,0:T(8,128)(2,1)S(1)}, bf16[48,320]{1,0:T(8,128)(2,1)S(1)}, u32[]{:S(2)}, u32[]{:S(2)}) collective-permute-start(bf16[48,320]{1,0:T(8,128)(2,1)S(1)} %get-tuple-element.61), channel_id=1, source_target_pairs={{0,14},{1,15},{2,12},{3,13},{4,10},{5,11},{6,8},{7,9},{8,6},{9,7},... | collective-permute-start | bytes 92168 | tf_op jit(solution)/shard_map/ppermute | solution.py:152
  187.6 3.7 %collective-permute-start.9 = (bf16[48,320]{1,0:T(8,128)(2,1)S(1)}, bf16[48,320]{1,0:T(8,128)(2,1)S(1)}, u32[]{:S(2)}, u32[]{:S(2)}) collective-permute-start(bf16[48,320]{1,0:T(8,128)(2,1)S(1)} %get-tuple-element.62), channel_id=1, source_target_pairs={{0,12},{1,13},{2,14},{3,15},{4,8},{5,9},{6,10},{7,11},{8,4},{9,5},... | collective-permute-start | bytes 92168 | tf_op jit(solution)/shard_map/ppermute | solution.py:152
  191.4 3.1 %collective-permute-start.8 = (bf16[48,320]{1,0:T(8,128)(2,1)S(1)}, bf16[48,320]{1,0:T(8,128)(2,1)S(1)}, u32[]{:S(2)}, u32[]{:S(2)}) collective-permute-start(bf16[48,320]{1,0:T(8,128)(2,1)S(1)} %get-tuple-element.63), channel_id=1, source_target_pairs={{0,10},{1,11},{2,8},{3,9},{4,14},{5,15},{6,12},{7,13},{8,2},{9,3},... | collective-permute-start | bytes 92168 | tf_op jit(solution)/shard_map/ppermute | solution.py:152
  194.5 5.2 %collective-permute-start.7 = (bf16[48,320]{1,0:T(8,128)(2,1)S(1)}, bf16[48,320]{1,0:T(8,128)(2,1)S(1)}, u32[]{:S(2)}, u32[]{:S(2)}) collective-permute-start(bf16[48,320]{1,0:T(8,128)(2,1)S(1)} %get-tuple-element.64), channel_id=1, source_target_pairs={{0,8},{1,9},{2,10},{3,11},{4,12},{5,13},{6,14},{7,15},{8,0},{9,1},... | collective-permute-start | bytes 92168 | tf_op jit(solution)/shard_map/ppermute | solution.py:152
  199.7 1.9 collective-permute-start.6
  201.7 4.2 %collective-permute-start.5 = (bf16[48,320]{1,0:T(8,128)(2,1)S(1)}, bf16[48,320]{1,0:T(8,128)(2,1)S(1)}, u32[]{:S(2)}, u32[]{:S(2)}) collective-permute-start(bf16[48,320]{1,0:T(8,128)(2,1)S(1)} %get-tuple-element.66), channel_id=1, source_target_pairs={{0,4},{1,5},{2,6},{3,7},{4,0},{5,1},{6,2},{7,3},{8,12},{9,13},{10,... | collective-permute-start | bytes 92168 | tf_op jit(solution)/shard_map/ppermute | solution.py:152
  205.9 3.7 %collective-permute-start.4 = (bf16[48,320]{1,0:T(8,128)(2,1)S(1)}, bf16[48,320]{1,0:T(8,128)(2,1)S(1)}, u32[]{:S(2)}, u32[]{:S(2)}) collective-permute-start(bf16[48,320]{1,0:T(8,128)(2,1)S(1)} %get-tuple-element.60), channel_id=1, source_target_pairs={{0,2},{1,3},{2,0},{3,1},{4,6},{5,7},{6,4},{7,5},{8,10},{9,11},{10,... | collective-permute-start | bytes 92168 | tf_op jit(solution)/shard_map/ppermute | solution.py:152
  209.7 2.4 collective-permute-done.4
  212.2 0.2 reshape.88
  212.5 0.5 fusion.3
  213.0 19.5 %all_to_all.27 = bf16[16,48,320]{2,1,0:T(8,128)(2,1)S(1)} all-to-all(bf16[16,48,320]{2,1,0:T(8,128)(2,1)S(1)} %broadcast_in_dim.72), channel_id=1, replica_groups=mesh['expert'=32,'tensor'=16] {'tensor'}, dimensions={0} | all-to-all | bytes 983040 | tf_op jit(solution)/shard_map/all_to_all | solution.py:22
  232.5 0.1 convert_bitcast_fusion
  232.6 0.4 copy.32
  233.0 1.3 reshape.89
  234.3 0.2 fusion.1
  234.6 2.4 convolution_convert_fusion.2
  (68 shorter events, 0.5 us)
Async XLA Ops:
  7.2 227.4 %copy-start = (bf16[132,5120]{1,0:T(8,128)(2,1)S(1)}, bf16[132,5120]{1,0:T(8,128)(2,1)}, u32[]{:S(2)}) copy-start(bf16[132,5120]{1,0:T(8,128)(2,1)} %param.23) | copy-start | bytes 4055044
  9.0 27.2 %copy-start.6 = (bf16[1,96,5120]{2,1,0:T(8,128)(2,1)S(1)}, bf16[1,96,5120]{2,1,0:T(8,128)(2,1)}, u32[]{:S(2)}) copy-start(bf16[1,96,5120]{2,1,0:T(8,128)(2,1)} %param.16) | copy-start | bytes 2949124
  9.0 27.2 %copy-start.7 = (bf16[1,96,5120]{2,1,0:T(8,128)(2,1)S(1)}, bf16[1,96,5120]{2,1,0:T(8,128)(2,1)}, u32[]{:S(2)}) copy-start(bf16[1,96,5120]{2,1,0:T(8,128)(2,1)} %param.17) | copy-start | bytes 2949124
  9.0 62.7 %collective-permute-start = (bf16[160,576]{1,0:T(8,128)(2,1)}, bf16[160,576]{1,0:T(8,128)(2,1)}, u32[]{:S(2)}, u32[]{:S(2)}) collective-permute-start(bf16[160,576]{1,0:T(8,128)(2,1)} %pad_maximum_fusion), channel_id=1, source_target_pairs={{0,256},{16,272},{32,288},{48,304},{64,320},{80,336},{96,352},{112... | collective-permute-start | bytes 552968 | tf_op jit(solution)/shard_map/ppermute | solution.py:125
  20.8 48.4 %all-to-all-start = ((bf16[32,18,320]{2,1,0:T(8,128)(2,1)}), bf16[32,18,320]{2,1,0:T(8,128)(2,1)}, u32[]{:S(2)}, u32[]{:S(2)}) async-start(bf16[32,18,320]{2,1,0:T(8,128)(2,1)} %reshape.80), calls=%async_computation | async-start | bytes 1179648 | tf_op jit(solution)/shard_map/all_to_all | solution.py:22
  36.2 134.7 %all-gather.3.cloned.1.call-start = ((), (), s32[]{:S(2)}) async-start(), calls=%async_computation.5 | async-start | bytes 6963200 | tf_op jit(solution)/shard_map/all_gather | solution.py:132
  38.8 3.4 %copy-start.13 = (bf16[192,320]{1,0:T(8,128)(2,1)S(1)}, bf16[192,320]{1,0:T(8,128)(2,1)}, u32[]{:S(2)}) copy-start(bf16[192,320]{1,0:T(8,128)(2,1)} %get-tuple-element.26) | copy-start | bytes 368644
  38.8 3.4 %copy-start.14 = (bf16[192,320]{1,0:T(8,128)(2,1)S(1)}, bf16[192,320]{1,0:T(8,128)(2,1)}, u32[]{:S(2)}) copy-start(bf16[192,320]{1,0:T(8,128)(2,1)} %get-tuple-element.27) | copy-start | bytes 368644
  38.8 3.4 %copy-start.15 = (bf16[192,320]{1,0:T(8,128)(2,1)S(1)}, bf16[192,320]{1,0:T(8,128)(2,1)}, u32[]{:S(2)}) copy-start(bf16[192,320]{1,0:T(8,128)(2,1)} %get-tuple-element.28) | copy-start | bytes 368644
  38.8 3.4 %copy-start.16 = (bf16[192,320]{1,0:T(8,128)(2,1)S(1)}, bf16[192,320]{1,0:T(8,128)(2,1)}, u32[]{:S(2)}) copy-start(bf16[192,320]{1,0:T(8,128)(2,1)} %get-tuple-element.29) | copy-start | bytes 368644
  38.8 3.4 %copy-start.17 = (bf16[192,320]{1,0:T(8,128)(2,1)S(1)}, bf16[192,320]{1,0:T(8,128)(2,1)}, u32[]{:S(2)}) copy-start(bf16[192,320]{1,0:T(8,128)(2,1)} %get-tuple-element.30) | copy-start | bytes 368644
  38.8 3.4 %copy-start.18 = (bf16[192,320]{1,0:T(8,128)(2,1)S(1)}, bf16[192,320]{1,0:T(8,128)(2,1)}, u32[]{:S(2)}) copy-start(bf16[192,320]{1,0:T(8,128)(2,1)} %get-tuple-element.31) | copy-start | bytes 368644
  38.8 6.2 %copy-start.12 = (bf16[1,1536,320]{1,2,0:T(8,128)(2,1)S(1)}, bf16[1,1536,320]{1,2,0:T(8,128)(2,1)}, u32[]{:S(2)}) copy-start(bf16[1,1536,320]{1,2,0:T(8,128)(2,1)} %param.18) | copy-start | bytes 2949124
  49.0 1.7 copy-start.10
  49.0 1.8 copy-start.11
  50.7 1.0 copy-start.20
  50.8 25.2 %copy-start.19 = (bf16[48,320]{1,0:T(8,128)(2,1)S(1)}, bf16[48,320]{1,0:T(8,128)(2,1)}, u32[]{:S(2)}) copy-start(bf16[48,320]{1,0:T(8,128)(2,1)} %param.13) | copy-start | bytes 92164
  126.3 6.2 %copy-start.1 = (bf16[8,320,624]{2,1,0:T(8,128)(2,1)}, bf16[8,320,624]{2,1,0:T(8,128)(2,1)S(1)}, u32[]{:S(2)}) copy-start(bf16[8,320,624]{2,1,0:T(8,128)(2,1)S(1)} %all_to_all.25.mine_ref) | copy-start | bytes 9584644
  126.3 10.7 %collective-permute-start.1 = (bf16[8,320,624]{2,1,0:T(8,128)(2,1)S(1)}, bf16[8,320,624]{2,1,0:T(8,128)(2,1)S(1)}, u32[]{:S(2)}, u32[]{:S(2)}) collective-permute-start(bf16[8,320,624]{2,1,0:T(8,128)(2,1)S(1)} %all_to_all.25.mine_ref), channel_id=1, source_target_pairs={{0,1},{1,0},{2,3},{3,2},{4,5},{5,4},{6,7},{7,6},{8,9},{9,8},{10,11... | collective-permute-start | bytes 9584648 | tf_op jit(solution)/shard_map/ppermute | solution.py:29
  137.0 1.8 copy-start.3
  138.8 22.1 %copy-start.9 = (bf16[768,320]{0,1:T(8,128)(2,1)S(1)}, bf16[768,320]{0,1:T(8,128)(2,1)}, u32[]{:S(2)}) copy-start(bf16[768,320]{0,1:T(8,128)(2,1)} %get-tuple-element.15) | copy-start | bytes 1474564
  138.9 24.1 %copy-start.8 = (bf16[768,320]{0,1:T(8,128)(2,1)S(1)}, bf16[768,320]{0,1:T(8,128)(2,1)}, u32[]{:S(2)}) copy-start(bf16[768,320]{0,1:T(8,128)(2,1)} %get-tuple-element.16) | copy-start | bytes 1474564
  157.5 5.6 %collective-permute-start.2 = (bf16[8,96,576]{2,1,0:T(8,128)(2,1)S(1)}, bf16[8,96,576]{2,1,0:T(8,128)(2,1)S(1)}, u32[]{:S(2)}, u32[]{:S(2)}) collective-permute-start(bf16[8,96,576]{2,1,0:T(8,128)(2,1)S(1)} %all_to_all.26), channel_id=1, source_target_pairs={{0,1},{1,0},{2,3},{3,2},{4,5},{5,4},{6,7},{7,6},{8,9},{9,8},{10,11... | collective-permute-start | bytes 2654216 | tf_op jit(solution)/shard_map/ppermute | solution.py:29
  164.9 47.3 %all-to-all-start.3 = ((bf16[32,18,320]{2,1,0:T(8,128)(2,1)}), bf16[32,18,320]{2,1,0:T(8,128)(2,1)S(1)}, u32[]{:S(2)}, u32[]{:S(2)}) async-start(bf16[32,18,320]{2,1,0:T(8,128)(2,1)} %reshape.86), calls=%async_computation.3 | async-start | bytes 1179648 | tf_op jit(solution)/shard_map/all_to_all | solution.py:22
  170.8 1.9 copy-start.2
  172.8 1.9 copy-start.4
  174.7 2.9 %copy-start.5 = (bf16[32,160,576]{2,1,0:T(8,128)(2,1)S(1)}, bf16[32,160,576]{2,1,0:T(8,128)(2,1)}, u32[]{:S(2)}) copy-start(bf16[32,160,576]{2,1,0:T(8,128)(2,1)} %all-gather.3.cloned.1.call-done) | copy-start | bytes 17694724
  179.9 11.4 %copy-start.24 = (s32[48,6]{0,1:T(8,128)S(1)}, s32[48,6]{0,1:T(8,128)}, u32[]{:S(2)}) copy-start(s32[48,6]{0,1:T(8,128)} %param.14) | copy-start | bytes 3460
  179.9 11.4 %copy-start.25 = (f32[48,6]{0,1:T(8,128)S(1)}, f32[48,6]{0,1:T(8,128)}, u32[]{:S(2)}) copy-start(f32[48,6]{0,1:T(8,128)} %param.15) | copy-start | bytes 3460
  180.0 32.5 %copy-start.22 = (bf16[32,576]{1,0:T(8,128)(2,1)S(1)}, bf16[32,576]{1,0:T(8,128)(2,1)}, u32[]{:S(2)}) copy-start(bf16[32,576]{1,0:T(8,128)(2,1)} %constant.47.clone) | copy-start | bytes 110596
  180.0 3.9 %collective-permute-start.3 = (bf16[8,48,320]{2,1,0:T(8,128)(2,1)S(1)}, bf16[8,48,320]{2,1,0:T(8,128)(2,1)S(1)}, u32[]{:S(2)}, u32[]{:S(2)}) collective-permute-start(bf16[8,48,320]{2,1,0:T(8,128)(2,1)S(1)} %get-tuple-element.19), channel_id=1, source_target_pairs={{0,1},{1,0},{2,3},{3,2},{4,5},{5,4},{6,7},{7,6},{8,9},{9,8},{10,11... | collective-permute-start | bytes 737288 | tf_op jit(solution)/shard_map/ppermute | solution.py:147
  184.0 17.7 %collective-permute-start.10 = (bf16[48,320]{1,0:T(8,128)(2,1)S(1)}, bf16[48,320]{1,0:T(8,128)(2,1)S(1)}, u32[]{:S(2)}, u32[]{:S(2)}) collective-permute-start(bf16[48,320]{1,0:T(8,128)(2,1)S(1)} %get-tuple-element.61), channel_id=1, source_target_pairs={{0,14},{1,15},{2,12},{3,13},{4,10},{5,11},{6,8},{7,9},{8,6},{9,7},... | collective-permute-start | bytes 92168 | tf_op jit(solution)/shard_map/ppermute | solution.py:152
  187.6 18.3 %collective-permute-start.9 = (bf16[48,320]{1,0:T(8,128)(2,1)S(1)}, bf16[48,320]{1,0:T(8,128)(2,1)S(1)}, u32[]{:S(2)}, u32[]{:S(2)}) collective-permute-start(bf16[48,320]{1,0:T(8,128)(2,1)S(1)} %get-tuple-element.62), channel_id=1, source_target_pairs={{0,12},{1,13},{2,14},{3,15},{4,8},{5,9},{6,10},{7,11},{8,4},{9,5},... | collective-permute-start | bytes 92168 | tf_op jit(solution)/shard_map/ppermute | solution.py:152
  191.4 18.3 %collective-permute-start.8 = (bf16[48,320]{1,0:T(8,128)(2,1)S(1)}, bf16[48,320]{1,0:T(8,128)(2,1)S(1)}, u32[]{:S(2)}, u32[]{:S(2)}) collective-permute-start(bf16[48,320]{1,0:T(8,128)(2,1)S(1)} %get-tuple-element.63), channel_id=1, source_target_pairs={{0,10},{1,11},{2,8},{3,9},{4,14},{5,15},{6,12},{7,13},{8,2},{9,3},... | collective-permute-start | bytes 92168 | tf_op jit(solution)/shard_map/ppermute | solution.py:152
  194.5 15.2 %collective-permute-start.7 = (bf16[48,320]{1,0:T(8,128)(2,1)S(1)}, bf16[48,320]{1,0:T(8,128)(2,1)S(1)}, u32[]{:S(2)}, u32[]{:S(2)}) collective-permute-start(bf16[48,320]{1,0:T(8,128)(2,1)S(1)} %get-tuple-element.64), channel_id=1, source_target_pairs={{0,8},{1,9},{2,10},{3,11},{4,12},{5,13},{6,14},{7,15},{8,0},{9,1},... | collective-permute-start | bytes 92168 | tf_op jit(solution)/shard_map/ppermute | solution.py:152
  199.7 10.0 %collective-permute-start.6 = (bf16[48,320]{1,0:T(8,128)(2,1)S(1)}, bf16[48,320]{1,0:T(8,128)(2,1)S(1)}, u32[]{:S(2)}, u32[]{:S(2)}) collective-permute-start(bf16[48,320]{1,0:T(8,128)(2,1)S(1)} %get-tuple-element.65), channel_id=1, source_target_pairs={{0,6},{1,7},{2,4},{3,5},{4,2},{5,3},{6,0},{7,1},{8,14},{9,15},{10,... | collective-permute-start | bytes 92168 | tf_op jit(solution)/shard_map/ppermute | solution.py:152
  201.7 8.0 %collective-permute-start.5 = (bf16[48,320]{1,0:T(8,128)(2,1)S(1)}, bf16[48,320]{1,0:T(8,128)(2,1)S(1)}, u32[]{:S(2)}, u32[]{:S(2)}) collective-permute-start(bf16[48,320]{1,0:T(8,128)(2,1)S(1)} %get-tuple-element.66), channel_id=1, source_target_pairs={{0,4},{1,5},{2,6},{3,7},{4,0},{5,1},{6,2},{7,3},{8,12},{9,13},{10,... | collective-permute-start | bytes 92168 | tf_op jit(solution)/shard_map/ppermute | solution.py:152
  205.9 6.2 %collective-permute-start.4 = (bf16[48,320]{1,0:T(8,128)(2,1)S(1)}, bf16[48,320]{1,0:T(8,128)(2,1)S(1)}, u32[]{:S(2)}, u32[]{:S(2)}) collective-permute-start(bf16[48,320]{1,0:T(8,128)(2,1)S(1)} %get-tuple-element.60), channel_id=1, source_target_pairs={{0,2},{1,3},{2,0},{3,1},{4,6},{5,7},{6,4},{7,5},{8,10},{9,11},{10,... | collective-permute-start | bytes 92168 | tf_op jit(solution)/shard_map/ppermute | solution.py:152
  212.9 20.0 %copy-start.21 = (bf16[48,320]{1,0:T(8,128)(2,1)}, bf16[48,320]{1,0:T(8,128)(2,1)S(1)}, u32[]{:S(2)}) copy-start(bf16[48,320]{1,0:T(8,128)(2,1)S(1)} %fusion.25) | copy-start | bytes 92164
  233.0 1.6 copy-start.23
Sparse Core Ops, SparseCore 0:
  74.0 82.3 all-gather.2

commit v5 on v4

--- a/solution.py
+++ b/solution.py
@@ -70,7 +70,7 @@
             pl.BlockSpec(table.shape, lambda i: (0, 0, 0, 0), pipeline_mode=pl.Buffered(1)),
         ],
         out_specs=(whole, whole),
-        compiler_params=pltpu.CompilerParams(vmem_limit_bytes=32 * 2**20),
+        compiler_params=pltpu.CompilerParams(vmem_limit_bytes=56 * 2**20),
         cost_estimate=pl.CostEstimate(flops=1000, bytes_accessed=1000, transcendentals=0),
     )(rank.reshape(1), mine, theirs, table)
 
@@ -116,18 +116,18 @@
         even, odd = (jnp.concatenate(pieces[k::2], axis=axis) for k in range(2))
         return jnp.where(side == 0, even, odd), jnp.where(side == 0, odd, even)
 
+    hid = routed_gate.shape[1]
     gate_up = jnp.concatenate([routed_gate[0], routed_up[0]], axis=0)
-    hid = routed_gate.shape[1]
     in_mine, in_theirs = by_side(gate_up, 1)
     out_mine, out_theirs = by_side(routed_down[0], 0)
 
     own = jnp.concatenate([shared_gate, shared_up, shared_down.T], axis=1)
     other = lax.ppermute(own, "expert", [(i, (i + ROWS) % (2 * ROWS)) for i in range(2 * ROWS)])
-    first = arrived[0, 0, 0]
+    first = outgoing[0, 0]
     column = column + jnp.where(first == first, 0, 2)
     pair = jnp.where(column == 0, jnp.stack([own, other]), jnp.stack([other, own]))
-    pair, late, in_mine, in_theirs, out_mine, out_theirs = lax.optimization_barrier(
-        (pair, tokens, in_mine, in_theirs, out_mine, out_theirs)
+    late, in_mine, in_theirs, out_mine, out_theirs = lax.optimization_barrier(
+        (tokens, in_mine, in_theirs, out_mine, out_theirs)
     )
     gathered = lax.all_gather(pair, "expert", axis=0, axis_index_groups=LANES)
 

time: 246 us -> 244 us (level)
  local copies, waits for them, and re-layouts: 31.5 us -> 20.7 us
  waiting for transfers between devices: 25.5 us -> 33.8 us
  Pallas kernels: 2.38 us -> 6.33 us
    all_to_all x2, waiting for transfers between devices: 15.7 us -> 23.9 us  [exchange(): lax.all_to_all(parts, axis, split_axis=0, concat_axis=0, tiled=True, axis...]
    unnamed x52 -> x34, local copies, waits for them, and re-layouts: 7.72 us -> 1.58 us
    pallas_call x1, Pallas kernels: 2.38 us -> 6.33 us  [shared_partial(): pl.pallas_call(shared_kernel, out_shape=(out, out), grid=(1,), in_specs=[...]
  transfers between devices with their start and end apart: 14 -> 14, of which waited for: 5 -> 5; matrix products, arithmetic and copies ran while one was open for 15% -> 13% of each run, Pallas kernels for 1% -> 3%
where the time goes in v5:
time: 244 us; the launch traced here: 242 us
  blocking collectives  82.7 us (34%)
  starting transfers between devices  61.9 us (25%)
  waiting for transfers between devices  33.8 us (14%)
  local copies, waits for them, and re-layouts  20.7 us (8%)
  between operations  15.9 us (7%)
  other arithmetic  12.5 us (5%)
  matrix products  8.16 us (3%)
  Pallas kernels  6.33 us (3%)
    all_to_all x3, blocking collectives, exchange(): lax.all_to_all(parts, axis, split_axis=0, concat_axis=0, tiled=True, axis...  82.7 us
    ppermute x7, starting transfers between devices, per_device(): lax.ppermute(give, 'tensor', [(i, i ^ 2 * step) for i in range(2 * CHIPS)])  25.6 us
    all_to_all x2, waiting for transfers between devices, exchange(): lax.all_to_all(parts, axis, split_axis=0, concat_axis=0, tiled=True, axis...  23.9 us
    all_to_all x2, starting transfers between devices, exchange(): lax.all_to_all(parts, axis, split_axis=0, concat_axis=0, tiled=True, axis...  20.3 us
    ppermute x2, starting transfers between devices, gather_halves(): lax.ppermute(mine, 'tensor', [(i, i ^ 1) for i in range(2 * CHIPS)])  9.37 us
    concatenate x4, local copies, waits for them, and re-layouts, by_side(): even, odd = (jnp.concatenate(pieces[k::2], axis=axis) for k in range(2))  8.12 us
    dot_general x7, matrix products, dot(): lax.dot_general(left, right, (((over_left,), (over_right,)), ((), ())), p...  6.98 us
    pallas_call x1, Pallas kernels, shared_partial(): pl.pallas_call(shared_kernel, out_shape=(out, out), grid=(1,), in_specs=[...  6.33 us
  transfers between devices with their start and end apart: 14, of which 5 were waited for; matrix products, arithmetic and copies ran while one was open for 13% of the time, Pallas kernels for 3%

profile of v5, /device:TPU:1, one launch (start us, length us, event | category | flops | bytes accessed | tf_op | source)
XLA Modules:
  0.0 242.1 jit_solution(4448401516551235725)
XLA Ops:
  7.2 0.0 all-gather.2.cloned.1.call-start
  7.2 1.2 pad_maximum_fusion
  8.4 3.9 %collective-permute-start.2 = (bf16[160,576]{1,0:T(8,128)(2,1)S(1)}, bf16[160,576]{1,0:T(8,128)(2,1)S(1)}, u32[]{:S(2)}, u32[]{:S(2)}) collective-permute-start(bf16[160,576]{1,0:T(8,128)(2,1)S(1)} %pad_maximum_fusion), channel_id=1, source_target_pairs={{0,256},{16,272},{32,288},{48,304},{64,320},{80,336},{96,352},{112... | collective-permute-start | bytes 552968 | tf_op jit(solution)/shard_map/ppermute | solution.py:125
  12.4 0.7 fusion.23
  13.1 1.2 convolution_compare_fusion
  14.3 1.1 convolution_convert_fusion
  15.4 0.6 slice.283
  17.2 1.1 fusion.77
  18.3 0.7 copy-done.11
  19.0 2.1 maximum_select_fusion
  21.1 2.0 copy.29
  23.1 2.0 reshape.139
  25.0 15.3 %all-to-all-start = ((bf16[32,18,320]{2,1,0:T(8,128)(2,1)}), bf16[32,18,320]{2,1,0:T(8,128)(2,1)}, u32[]{:S(2)}, u32[]{:S(2)}) async-start(bf16[32,18,320]{2,1,0:T(8,128)(2,1)} %reshape.139), calls=%async_computation | async-start | bytes 1179648 | tf_op jit(solution)/shard_map/all_to_all | solution.py:22
  40.4 1.2 pad_maximum_fusion.1
  41.6 1.4 fusion.8
  42.9 2.4 concatenate.41
  45.3 3.2 %concatenate.40 = bf16[192,2560]{1,0:T(8,128)(2,1)} concatenate(bf16[192,320]{1,0:T(8,128)(2,1)S(1)} %get-tuple-element.23, bf16[192,320]{1,0:T(8,128)(2,1)} %get-tuple-element.24, bf16[192,320]{1,0:T(8,128)(2,1)} %get-tuple-element.25, bf16[192,320]{1,0:T(8,128)(2,1)} %get-tuple-element.26, bf16[192,320]{1,0:T(8,128)(2,1)} %get-tuple-element.27, ...), dimensions={1} | concatenate | bytes 1966080 | tf_op jit(solution)/shard_map/concatenate | solution.py:116
  48.5 1.5 slice_bitcast_fusion
  50.0 1.3 concatenate.43
  51.3 1.3 concatenate.42
  52.5 1.0 broadcast_select_fusion.2
  53.6 2.3 broadcast_select_fusion
  55.8 23.9 %all-to-all-done = bf16[32,18,320]{2,1,0:T(8,128)(2,1)} async-done(((bf16[32,18,320]{2,1,0:T(8,128)(2,1)}), bf16[32,18,320]{2,1,0:T(8,128)(2,1)}, u32[]{:S(2)}, u32[]{:S(2)}) %all-to-all-start) | async-done | bytes 368672 | tf_op jit(solution)/shard_map/all_to_all | solution.py:22
  79.7 1.3 reshape.140
  81.0 0.1 maximum_bitcast_fusion
  81.1 0.2 copy.30
  81.3 0.3 broadcast_in_dim.65
  81.6 44.8 %all_to_all.25.mine_ref = bf16[8,320,624]{2,1,0:T(8,128)(2,1)S(1)} all-to-all(bf16[8,320,624]{2,1,0:T(8,128)(2,1)S(1)} %broadcast_in_dim.65), channel_id=1, replica_groups={{0,2,4,6,8,10,12,14},{1,3,5,7,9,11,13,15},{16,18,20,22,24,26,28,30},{17..., dimensions={0} | all-to-all | bytes 6389760 | tf_op jit(solution)/shard_map/all_to_all | solution.py:22
  126.4 5.9 %collective-permute-start = (bf16[8,320,624]{2,1,0:T(8,128)(2,1)S(1)}, bf16[8,320,624]{2,1,0:T(8,128)(2,1)S(1)}, u32[]{:S(2)}, u32[]{:S(2)}) collective-permute-start(bf16[8,320,624]{2,1,0:T(8,128)(2,1)S(1)} %all_to_all.25.mine_ref), channel_id=1, source_target_pairs={{0,1},{1,0},{2,3},{3,2},{4,5},{5,4},{6,7},{7,6},{8,9},{9,8},{10,11... | collective-permute-start | bytes 9584648 | tf_op jit(solution)/shard_map/ppermute | solution.py:29
  132.3 0.9 fusion.60
  133.3 4.5 %collective-permute-done.theirs_ref = bf16[8,320,624]{2,1,0:T(8,128)(2,1)S(1)} collective-permute-done((bf16[8,320,624]{2,1,0:T(8,128)(2,1)S(1)}, bf16[8,320,624]{2,1,0:T(8,128)(2,1)S(1)}, u32[]{:S(2)}, u32[]{:S(2)}) %collective-permute-start) | collective-permute-done | bytes 3194912 | tf_op jit(solution)/shard_map/ppermute | solution.py:29
  137.8 0.9 convolution_add_fusion.1
  138.7 0.8 copy-done.2
  139.6 0.1 fusion.7
  139.6 0.1 broadcast_in_dim.66
  139.7 18.5 %all_to_all.26 = bf16[8,96,576]{2,1,0:T(8,128)(2,1)S(1)} all-to-all(bf16[8,96,576]{2,1,0:T(8,128)(2,1)S(1)} %broadcast_in_dim.66), channel_id=1, replica_groups={{0,2,4,6,8,10,12,14},{1,3,5,7,9,11,13,15},{16,18,20,22,24,26,28,30},{17..., dimensions={0} | all-to-all | bytes 1769472 | tf_op jit(solution)/shard_map/all_to_all | solution.py:22
  158.2 3.4 %collective-permute-start.1 = (bf16[8,96,576]{2,1,0:T(8,128)(2,1)S(1)}, bf16[8,96,576]{2,1,0:T(8,128)(2,1)S(1)}, u32[]{:S(2)}, u32[]{:S(2)}) collective-permute-start(bf16[8,96,576]{2,1,0:T(8,128)(2,1)S(1)} %all_to_all.26), channel_id=1, source_target_pairs={{0,1},{1,0},{2,3},{3,2},{4,5},{5,4},{6,7},{7,6},{8,9},{9,8},{10,11... | collective-permute-start | bytes 2654216 | tf_op jit(solution)/shard_map/ppermute | solution.py:29
  161.7 0.6 fusion.61
  162.2 1.6 collective-permute-done.1
  163.8 0.6 fusion
  164.4 0.2 copy.31
  164.7 1.0 reshape.145
  165.6 5.0 %all-to-all-start.3 = ((bf16[32,18,320]{2,1,0:T(8,128)(2,1)}), bf16[32,18,320]{2,1,0:T(8,128)(2,1)S(1)}, u32[]{:S(2)}, u32[]{:S(2)}) async-start(bf16[32,18,320]{2,1,0:T(8,128)(2,1)} %reshape.145), calls=%async_computation.3 | async-start | bytes 1179648 | tf_op jit(solution)/shard_map/all_to_all | solution.py:22
  170.7 6.3 %shard_map.140 = (bf16[8,48,320]{2,1,0:T(8,128)(2,1)}, bf16[8,48,320]{2,1,0:T(8,128)(2,1)}) custom-call(s32[1]{0:T(128)} %bitcast.23.rank_ref, bf16[8,320,624]{2,1,0:T(8,128)(2,1)} %copy-done.1, bf16[8,320,624]{2,1,0:T(8,128)(2,1)} %copy-done.2, bf16[16,2,160,576]{3,2,1,0:T(8,128)(2,1)} %all-gather.2.cloned.1.call-done.table_ref), custom_call_target="tpu_custom_call" | custom-call | flops 1000 | bytes 1000 | tf_op jit(solution)/shard_map/pallas_call | solution.py:62
  177.0 2.7 %collective-permute-start.3 = (bf16[8,48,320]{2,1,0:T(8,128)(2,1)}, bf16[8,48,320]{2,1,0:T(8,128)(2,1)S(1)}, u32[]{:S(2)}, u32[]{:S(2)}) collective-permute-start(bf16[8,48,320]{2,1,0:T(8,128)(2,1)} %get-tuple-element.17), channel_id=1, source_target_pairs={{0,1},{1,0},{2,3},{3,2},{4,5},{5,4},{6,7},{7,6},{8,9},{9,8},{10,11... | collective-permute-start | bytes 737288 | tf_op jit(solution)/shard_map/ppermute | solution.py:147
  179.7 1.4 collective-permute-done.3
  181.1 1.0 fusion.59
  182.2 3.7 %collective-permute-start.10 = (bf16[48,320]{1,0:T(8,128)(2,1)S(1)}, bf16[48,320]{1,0:T(8,128)(2,1)S(1)}, u32[]{:S(2)}, u32[]{:S(2)}) collective-permute-start(bf16[48,320]{1,0:T(8,128)(2,1)S(1)} %get-tuple-element.59), channel_id=1, source_target_pairs={{0,14},{1,15},{2,12},{3,13},{4,10},{5,11},{6,8},{7,9},{8,6},{9,7},... | collective-permute-start | bytes 92168 | tf_op jit(solution)/shard_map/ppermute | solution.py:152
  185.8 3.7 %collective-permute-start.9 = (bf16[48,320]{1,0:T(8,128)(2,1)S(1)}, bf16[48,320]{1,0:T(8,128)(2,1)S(1)}, u32[]{:S(2)}, u32[]{:S(2)}) collective-permute-start(bf16[48,320]{1,0:T(8,128)(2,1)S(1)} %get-tuple-element.60), channel_id=1, source_target_pairs={{0,12},{1,13},{2,14},{3,15},{4,8},{5,9},{6,10},{7,11},{8,4},{9,5},... | collective-permute-start | bytes 92168 | tf_op jit(solution)/shard_map/ppermute | solution.py:152
  189.6 3.1 %collective-permute-start.8 = (bf16[48,320]{1,0:T(8,128)(2,1)S(1)}, bf16[48,320]{1,0:T(8,128)(2,1)S(1)}, u32[]{:S(2)}, u32[]{:S(2)}) collective-permute-start(bf16[48,320]{1,0:T(8,128)(2,1)S(1)} %get-tuple-element.61), channel_id=1, source_target_pairs={{0,10},{1,11},{2,8},{3,9},{4,14},{5,15},{6,12},{7,13},{8,2},{9,3},... | collective-permute-start | bytes 92168 | tf_op jit(solution)/shard_map/ppermute | solution.py:152
  192.7 5.2 %collective-permute-start.7 = (bf16[48,320]{1,0:T(8,128)(2,1)S(1)}, bf16[48,320]{1,0:T(8,128)(2,1)S(1)}, u32[]{:S(2)}, u32[]{:S(2)}) collective-permute-start(bf16[48,320]{1,0:T(8,128)(2,1)S(1)} %get-tuple-element.62), channel_id=1, source_target_pairs={{0,8},{1,9},{2,10},{3,11},{4,12},{5,13},{6,14},{7,15},{8,0},{9,1},... | collective-permute-start | bytes 92168 | tf_op jit(solution)/shard_map/ppermute | solution.py:152
  197.9 1.9 collective-permute-start.6
  199.9 4.2 %collective-permute-start.5 = (bf16[48,320]{1,0:T(8,128)(2,1)S(1)}, bf16[48,320]{1,0:T(8,128)(2,1)S(1)}, u32[]{:S(2)}, u32[]{:S(2)}) collective-permute-start(bf16[48,320]{1,0:T(8,128)(2,1)S(1)} %get-tuple-element.64), channel_id=1, source_target_pairs={{0,4},{1,5},{2,6},{3,7},{4,0},{5,1},{6,2},{7,3},{8,12},{9,13},{10,... | collective-permute-start | bytes 92168 | tf_op jit(solution)/shard_map/ppermute | solution.py:152
  204.1 3.7 %collective-permute-start.4 = (bf16[48,320]{1,0:T(8,128)(2,1)S(1)}, bf16[48,320]{1,0:T(8,128)(2,1)S(1)}, u32[]{:S(2)}, u32[]{:S(2)}) collective-permute-start(bf16[48,320]{1,0:T(8,128)(2,1)S(1)} %get-tuple-element.58), channel_id=1, source_target_pairs={{0,2},{1,3},{2,0},{3,1},{4,6},{5,7},{6,4},{7,5},{8,10},{9,11},{10,... | collective-permute-start | bytes 92168 | tf_op jit(solution)/shard_map/ppermute | solution.py:152
  207.9 2.4 collective-permute-done.4
  210.4 0.2 reshape.147
  210.7 0.5 fusion.3
  211.2 0.1 broadcast_in_dim.72
  211.2 19.5 %all_to_all.27 = bf16[16,48,320]{2,1,0:T(8,128)(2,1)S(1)} all-to-all(bf16[16,48,320]{2,1,0:T(8,128)(2,1)S(1)} %broadcast_in_dim.72), channel_id=1, replica_groups=mesh['expert'=32,'tensor'=16] {'tensor'}, dimensions={0} | all-to-all | bytes 983040 | tf_op jit(solution)/shard_map/all_to_all | solution.py:22
  230.7 0.1 convert_bitcast_fusion
  230.8 0.4 copy.32
  231.2 1.3 reshape.148
  232.5 0.2 fusion.1
  232.8 2.4 %convolution_convert_fusion.2 = bf16[48,132]{1,0:T(8,128)(2,1)} fusion(bf16[132,5120]{1,0:T(8,128)(2,1)S(1)} %copy-done, f32[48,5120]{1,0:T(8,128)} %reshape.148, f32[5120]{0:T(1024)S(1)} %copy-done.14, f32[48]{0:T(128)S(1)} %add_rsqrt_fusion), kind=kOutput, calls=%fused_computation.41 | convolution fusion | flops 65624256 | bytes 2368064 | tf_op jit(solution)/shard_map/dot_general | solution.py:16
  (50 shorter events, 0.3 us)
Async XLA Ops:
  7.2 225.6 %copy-start = (bf16[132,5120]{1,0:T(8,128)(2,1)S(1)}, bf16[132,5120]{1,0:T(8,128)(2,1)}, u32[]{:S(2)}) copy-start(bf16[132,5120]{1,0:T(8,128)(2,1)} %param.23) | copy-start | bytes 4055044
  7.2 163.5 %all-gather.2.cloned.1.call-start = ((), (), s32[]{:S(2)}) async-start(), calls=%async_computation.5 | async-start | bytes 6963200 | tf_op jit(solution)/shard_map/all_gather | solution.py:132
  8.4 9.9 %collective-permute-start.2 = (bf16[160,576]{1,0:T(8,128)(2,1)S(1)}, bf16[160,576]{1,0:T(8,128)(2,1)S(1)}, u32[]{:S(2)}, u32[]{:S(2)}) collective-permute-start(bf16[160,576]{1,0:T(8,128)(2,1)S(1)} %pad_maximum_fusion), channel_id=1, source_target_pairs={{0,256},{16,272},{32,288},{48,304},{64,320},{80,336},{96,352},{112... | collective-permute-start | bytes 552968 | tf_op jit(solution)/shard_map/ppermute | solution.py:125
  15.4 3.0 %copy-start.9 = (bf16[576,320]{0,1:T(8,128)(2,1)}, bf16[576,320]{0,1:T(8,128)(2,1)S(1)}, u32[]{:S(2)}) copy-start(bf16[576,320]{0,1:T(8,128)(2,1)S(1)} %convolution_convert_fusion) | copy-start | bytes 1105924
  18.3 0.7 copy-start.11
  19.0 21.4 %copy-start.3 = (bf16[1,96,5120]{2,1,0:T(8,128)(2,1)S(1)}, bf16[1,96,5120]{2,1,0:T(8,128)(2,1)}, u32[]{:S(2)}) copy-start(bf16[1,96,5120]{2,1,0:T(8,128)(2,1)} %param.16) | copy-start | bytes 2949124
  19.0 21.4 %copy-start.4 = (bf16[1,96,5120]{2,1,0:T(8,128)(2,1)S(1)}, bf16[1,96,5120]{2,1,0:T(8,128)(2,1)}, u32[]{:S(2)}) copy-start(bf16[1,96,5120]{2,1,0:T(8,128)(2,1)} %param.17) | copy-start | bytes 2949124
  25.0 54.7 %all-to-all-start = ((bf16[32,18,320]{2,1,0:T(8,128)(2,1)}), bf16[32,18,320]{2,1,0:T(8,128)(2,1)}, u32[]{:S(2)}, u32[]{:S(2)}) async-start(bf16[32,18,320]{2,1,0:T(8,128)(2,1)} %reshape.139), calls=%async_computation | async-start | bytes 1179648 | tf_op jit(solution)/shard_map/all_to_all | solution.py:22
  42.9 5.6 %copy-start.8 = (bf16[1,1536,320]{1,2,0:T(8,128)(2,1)S(1)}, bf16[1,1536,320]{1,2,0:T(8,128)(2,1)}, u32[]{:S(2)}) copy-start(bf16[1,1536,320]{1,2,0:T(8,128)(2,1)} %param.18) | copy-start | bytes 2949124
  53.6 27.5 %copy-start.10 = (bf16[48,320]{1,0:T(8,128)(2,1)S(1)}, bf16[48,320]{1,0:T(8,128)(2,1)}, u32[]{:S(2)}) copy-start(bf16[48,320]{1,0:T(8,128)(2,1)} %param.13) | copy-start | bytes 92164
  81.6 50.7 %copy-start.5 = (bf16[192,2560]{1,0:T(8,128)(2,1)S(1)}, bf16[192,2560]{1,0:T(8,128)(2,1)}, u32[]{:S(2)}) copy-start(bf16[192,2560]{1,0:T(8,128)(2,1)} %get-tuple-element.11) | copy-start | bytes 2949124
  126.4 6.9 %copy-start.1 = (bf16[8,320,624]{2,1,0:T(8,128)(2,1)}, bf16[8,320,624]{2,1,0:T(8,128)(2,1)S(1)}, u32[]{:S(2)}) copy-start(bf16[8,320,624]{2,1,0:T(8,128)(2,1)S(1)} %all_to_all.25.mine_ref) | copy-start | bytes 9584644
  126.4 11.4 %collective-permute-start = (bf16[8,320,624]{2,1,0:T(8,128)(2,1)S(1)}, bf16[8,320,624]{2,1,0:T(8,128)(2,1)S(1)}, u32[]{:S(2)}, u32[]{:S(2)}) collective-permute-start(bf16[8,320,624]{2,1,0:T(8,128)(2,1)S(1)} %all_to_all.25.mine_ref), channel_id=1, source_target_pairs={{0,1},{1,0},{2,3},{3,2},{4,5},{5,4},{6,7},{7,6},{8,9},{9,8},{10,11... | collective-permute-start | bytes 9584648 | tf_op jit(solution)/shard_map/ppermute | solution.py:29
  137.8 1.8 copy-start.2
  139.6 22.1 %copy-start.7 = (bf16[768,320]{0,1:T(8,128)(2,1)S(1)}, bf16[768,320]{0,1:T(8,128)(2,1)}, u32[]{:S(2)}) copy-start(bf16[768,320]{0,1:T(8,128)(2,1)} %get-tuple-element.14) | copy-start | bytes 1474564
  139.7 24.1 %copy-start.6 = (bf16[768,320]{0,1:T(8,128)(2,1)S(1)}, bf16[768,320]{0,1:T(8,128)(2,1)}, u32[]{:S(2)}) copy-start(bf16[768,320]{0,1:T(8,128)(2,1)} %get-tuple-element.15) | copy-start | bytes 1474564
  158.2 5.6 %collective-permute-start.1 = (bf16[8,96,576]{2,1,0:T(8,128)(2,1)S(1)}, bf16[8,96,576]{2,1,0:T(8,128)(2,1)S(1)}, u32[]{:S(2)}, u32[]{:S(2)}) collective-permute-start(bf16[8,96,576]{2,1,0:T(8,128)(2,1)S(1)} %all_to_all.26), channel_id=1, source_target_pairs={{0,1},{1,0},{2,3},{3,2},{4,5},{5,4},{6,7},{7,6},{8,9},{9,8},{10,11... | collective-permute-start | bytes 2654216 | tf_op jit(solution)/shard_map/ppermute | solution.py:29
  165.6 44.8 %all-to-all-start.3 = ((bf16[32,18,320]{2,1,0:T(8,128)(2,1)}), bf16[32,18,320]{2,1,0:T(8,128)(2,1)S(1)}, u32[]{:S(2)}, u32[]{:S(2)}) async-start(bf16[32,18,320]{2,1,0:T(8,128)(2,1)} %reshape.145), calls=%async_computation.3 | async-start | bytes 1179648 | tf_op jit(solution)/shard_map/all_to_all | solution.py:22
  177.0 12.6 %copy-start.15 = (s32[48,6]{0,1:T(8,128)S(1)}, s32[48,6]{0,1:T(8,128)}, u32[]{:S(2)}) copy-start(s32[48,6]{0,1:T(8,128)} %param.14) | copy-start | bytes 3460
  177.0 12.6 %copy-start.16 = (f32[48,6]{0,1:T(8,128)S(1)}, f32[48,6]{0,1:T(8,128)}, u32[]{:S(2)}) copy-start(f32[48,6]{0,1:T(8,128)} %param.15) | copy-start | bytes 3460
  177.0 33.6 %copy-start.13 = (bf16[32,576]{1,0:T(8,128)(2,1)S(1)}, bf16[32,576]{1,0:T(8,128)(2,1)}, u32[]{:S(2)}) copy-start(bf16[32,576]{1,0:T(8,128)(2,1)} %constant.47.clone) | copy-start | bytes 110596
  177.0 4.1 %collective-permute-start.3 = (bf16[8,48,320]{2,1,0:T(8,128)(2,1)}, bf16[8,48,320]{2,1,0:T(8,128)(2,1)S(1)}, u32[]{:S(2)}, u32[]{:S(2)}) collective-permute-start(bf16[8,48,320]{2,1,0:T(8,128)(2,1)} %get-tuple-element.17), channel_id=1, source_target_pairs={{0,1},{1,0},{2,3},{3,2},{4,5},{5,4},{6,7},{7,6},{8,9},{9,8},{10,11... | collective-permute-start | bytes 737288 | tf_op jit(solution)/shard_map/ppermute | solution.py:147
  182.2 17.7 %collective-permute-start.10 = (bf16[48,320]{1,0:T(8,128)(2,1)S(1)}, bf16[48,320]{1,0:T(8,128)(2,1)S(1)}, u32[]{:S(2)}, u32[]{:S(2)}) collective-permute-start(bf16[48,320]{1,0:T(8,128)(2,1)S(1)} %get-tuple-element.59), channel_id=1, source_target_pairs={{0,14},{1,15},{2,12},{3,13},{4,10},{5,11},{6,8},{7,9},{8,6},{9,7},... | collective-permute-start | bytes 92168 | tf_op jit(solution)/shard_map/ppermute | solution.py:152
  185.8 18.3 %collective-permute-start.9 = (bf16[48,320]{1,0:T(8,128)(2,1)S(1)}, bf16[48,320]{1,0:T(8,128)(2,1)S(1)}, u32[]{:S(2)}, u32[]{:S(2)}) collective-permute-start(bf16[48,320]{1,0:T(8,128)(2,1)S(1)} %get-tuple-element.60), channel_id=1, source_target_pairs={{0,12},{1,13},{2,14},{3,15},{4,8},{5,9},{6,10},{7,11},{8,4},{9,5},... | collective-permute-start | bytes 92168 | tf_op jit(solution)/shard_map/ppermute | solution.py:152
  189.6 18.3 %collective-permute-start.8 = (bf16[48,320]{1,0:T(8,128)(2,1)S(1)}, bf16[48,320]{1,0:T(8,128)(2,1)S(1)}, u32[]{:S(2)}, u32[]{:S(2)}) collective-permute-start(bf16[48,320]{1,0:T(8,128)(2,1)S(1)} %get-tuple-element.61), channel_id=1, source_target_pairs={{0,10},{1,11},{2,8},{3,9},{4,14},{5,15},{6,12},{7,13},{8,2},{9,3},... | collective-permute-start | bytes 92168 | tf_op jit(solution)/shard_map/ppermute | solution.py:152
  192.7 15.2 %collective-permute-start.7 = (bf16[48,320]{1,0:T(8,128)(2,1)S(1)}, bf16[48,320]{1,0:T(8,128)(2,1)S(1)}, u32[]{:S(2)}, u32[]{:S(2)}) collective-permute-start(bf16[48,320]{1,0:T(8,128)(2,1)S(1)} %get-tuple-element.62), channel_id=1, source_target_pairs={{0,8},{1,9},{2,10},{3,11},{4,12},{5,13},{6,14},{7,15},{8,0},{9,1},... | collective-permute-start | bytes 92168 | tf_op jit(solution)/shard_map/ppermute | solution.py:152
  197.9 10.0 %collective-permute-start.6 = (bf16[48,320]{1,0:T(8,128)(2,1)S(1)}, bf16[48,320]{1,0:T(8,128)(2,1)S(1)}, u32[]{:S(2)}, u32[]{:S(2)}) collective-permute-start(bf16[48,320]{1,0:T(8,128)(2,1)S(1)} %get-tuple-element.63), channel_id=1, source_target_pairs={{0,6},{1,7},{2,4},{3,5},{4,2},{5,3},{6,0},{7,1},{8,14},{9,15},{10,... | collective-permute-start | bytes 92168 | tf_op jit(solution)/shard_map/ppermute | solution.py:152
  199.9 8.0 %collective-permute-start.5 = (bf16[48,320]{1,0:T(8,128)(2,1)S(1)}, bf16[48,320]{1,0:T(8,128)(2,1)S(1)}, u32[]{:S(2)}, u32[]{:S(2)}) collective-permute-start(bf16[48,320]{1,0:T(8,128)(2,1)S(1)} %get-tuple-element.64), channel_id=1, source_target_pairs={{0,4},{1,5},{2,6},{3,7},{4,0},{5,1},{6,2},{7,3},{8,12},{9,13},{10,... | collective-permute-start | bytes 92168 | tf_op jit(solution)/shard_map/ppermute | solution.py:152
  204.1 6.2 %collective-permute-start.4 = (bf16[48,320]{1,0:T(8,128)(2,1)S(1)}, bf16[48,320]{1,0:T(8,128)(2,1)S(1)}, u32[]{:S(2)}, u32[]{:S(2)}) collective-permute-start(bf16[48,320]{1,0:T(8,128)(2,1)S(1)} %get-tuple-element.58), channel_id=1, source_target_pairs={{0,2},{1,3},{2,0},{3,1},{4,6},{5,7},{6,4},{7,5},{8,10},{9,11},{10,... | collective-permute-start | bytes 92168 | tf_op jit(solution)/shard_map/ppermute | solution.py:152
  211.2 20.0 %copy-start.12 = (bf16[48,320]{1,0:T(8,128)(2,1)}, bf16[48,320]{1,0:T(8,128)(2,1)S(1)}, u32[]{:S(2)}) copy-start(bf16[48,320]{1,0:T(8,128)(2,1)S(1)} %fusion.25) | copy-start | bytes 92164
  231.2 1.6 copy-start.14
Sparse Core Ops, SparseCore 0:
  21.2 113.6 all-gather.1

commit v6 on v5

--- a/solution.py
+++ b/solution.py
@@ -30,38 +30,36 @@
     return mine, theirs
 
 
-def shared_kernel(rank_ref, mine_ref, theirs_ref, table_ref, keep_ref, give_ref):
-    side, place = rank_ref[0] & 1, rank_ref[0] >> 1
+def shared_kernel(rank_ref, mine_ref, theirs_ref, table_ref, out_ref):
+    rank = rank_ref[0]
     inner = table_ref.shape[3] // 3
     size = table_ref.shape[2]
     start = mine_ref.shape[2] // 2
 
-    def weights(chip, half):
-        first = 2 * (2 * (chip & 3) + half)
-        return table_ref.at[pl.ds(first, 2), chip >> 2]
+    def weights(device):
+        return table_ref.at[pl.ds(2 * (device & 7), 2), device >> 3]
 
     sums = jnp.zeros((mine_ref.shape[2], 2 * inner), jnp.float32)
     for chip in range(CHIPS):
-        for ref, half in ((mine_ref, side), (theirs_ref, 1 - side)):
-            block = weights(chip, half)[:, :, : 2 * inner].reshape(2 * size, 2 * inner)
+        for ref, core in ((mine_ref, rank & 1), (theirs_ref, 1 - (rank & 1))):
+            block = weights(2 * chip + core)[:, :, : 2 * inner].reshape(2 * size, 2 * inner)
             sums = sums + dot(ref[chip], block, 0, 0)
-    sums = sums[start : start + keep_ref.shape[1]]
+    sums = sums[start : start + out_ref.shape[2]]
     gate, up = sums[:, :inner], sums[:, inner:]
     hidden = (gate * (1.0 / (1.0 + jnp.exp(-gate))) * up).astype(jnp.bfloat16)
-    for step in range(CHIPS):
-        for ref, half in ((keep_ref, side), (give_ref, 1 - side)):
-            block = weights(place ^ step, half)[:, :, 2 * inner :].reshape(2 * size, inner)
-            ref[step] = dot(hidden, block, 1, 1).astype(ref.dtype)
+    for near in range(4):
+        for far in range(4):
+            block = weights(rank ^ (near + 4 * far))[:, :, 2 * inner :].reshape(2 * size, inner)
+            out_ref[near, far] = dot(hidden, block, 1, 1).astype(out_ref.dtype)
 
 
 def shared_partial(rank, mine, theirs, table, tok):
     width = mine.shape[1]
-    out = jax.ShapeDtypeStruct((CHIPS, tok, width), jnp.bfloat16)
+    out = jax.ShapeDtypeStruct((4, 4, tok, width), jnp.bfloat16)
     last = pl.BlockSpec((CHIPS, width, 128), lambda i: (0, 0, 4))
-    whole = pl.BlockSpec(out.shape, lambda i: (0, 0, 0))
     return pl.pallas_call(
         shared_kernel,
-        out_shape=(out, out),
+        out_shape=out,
         grid=(1,),
         in_specs=[
             pl.BlockSpec(memory_space=pltpu.SMEM),
@@ -69,7 +67,7 @@
             last,
             pl.BlockSpec(table.shape, lambda i: (0, 0, 0, 0), pipeline_mode=pl.Buffered(1)),
         ],
-        out_specs=(whole, whole),
+        out_specs=pl.BlockSpec(out.shape, lambda i: (0, 0, 0, 0)),
         compiler_params=pltpu.CompilerParams(vmem_limit_bytes=56 * 2**20),
         cost_estimate=pl.CostEstimate(flops=1000, bytes_accessed=1000, transcendentals=0),
     )(rank.reshape(1), mine, theirs, table)
@@ -123,15 +121,13 @@
 
     own = jnp.concatenate([shared_gate, shared_up, shared_down.T], axis=1)
     other = lax.ppermute(own, "expert", [(i, (i + ROWS) % (2 * ROWS)) for i in range(2 * ROWS)])
-    first = outgoing[0, 0]
-    column = column + jnp.where(first == first, 0, 2)
     pair = jnp.where(column == 0, jnp.stack([own, other]), jnp.stack([other, own]))
-    late, in_mine, in_theirs, out_mine, out_theirs = lax.optimization_barrier(
-        (tokens, in_mine, in_theirs, out_mine, out_theirs)
+    arrived, pair, in_mine, in_theirs, out_mine, out_theirs = lax.optimization_barrier(
+        (arrived, pair, in_mine, in_theirs, out_mine, out_theirs)
     )
     gathered = lax.all_gather(pair, "expert", axis=0, axis_index_groups=LANES)
 
-    rows = jnp.concatenate([arrived.reshape(slots, width), late], axis=0)
+    rows = jnp.concatenate([arrived.reshape(slots, width), tokens], axis=0)
     mine, theirs = gather_halves(rows.T)
     total = slots + tok
     both = dot(in_mine, mine.reshape(-1, total), 1, 0) + dot(in_theirs, theirs.reshape(-1, total), 1, 0)
@@ -142,15 +138,16 @@
     )
     result = result.astype(bf16).reshape(experts, cap, width)
     returned = exchange(result, "expert")
-    keep, give = shared_partial(rank, mine, theirs, gathered, tok)
+    partial = shared_partial(rank, mine, theirs, gathered, tok)
 
-    got = lax.ppermute(give, "tensor", [(i, i ^ 1) for i in range(2 * CHIPS)])
-    partial = keep.astype(f32) + got.astype(f32)
-    shared = partial[0]
-    for step in range(1, CHIPS):
-        give = partial[step].astype(bf16)
-        got = lax.ppermute(give, "tensor", [(i, i ^ (2 * step)) for i in range(2 * CHIPS)])
-        shared = shared + got.astype(f32)
+    def summed(parts, stride):
+        total = parts[0].astype(f32)
+        for k in range(1, 4):
+            perm = [(i, i ^ (k * stride)) for i in range(2 * CHIPS)]
+            total = total + lax.ppermute(parts[k], "tensor", perm).astype(f32)
+        return total
+
+    shared = summed(summed(partial, 1).astype(bf16), 4)
 
     returned, shared = lax.optimization_barrier((returned, shared))
     high = lax.reduce_precision(weight, 8, 7)

time: 244 us -> 225 us (0.922)
  waiting for transfers between devices: 33.8 us -> 21.3 us
  starting transfers between devices: 61.9 us -> 52.8 us
  local copies, waits for them, and re-layouts: 20.7 us -> 23.4 us
    all_to_all x2, waiting for transfers between devices: 23.9 us -> 8.36 us  [exchange(): lax.all_to_all(parts, axis, split_axis=0, concat_axis=0, tiled=True, axis...]
    ppermute x8 -> x6, starting transfers between devices: 28.3 us -> 18.3 us  [summed(): total = total + lax.ppermute(parts[k], 'tensor', perm).astype(f32)]
    ppermute x8 -> x6, waiting for transfers between devices: 3.82 us -> 6.81 us  [summed(): total = total + lax.ppermute(parts[k], 'tensor', perm).astype(f32)]
    all_to_all x2, starting transfers between devices: 20.3 us -> 23.1 us  [exchange(): lax.all_to_all(parts, axis, split_axis=0, concat_axis=0, tiled=True, axis...]
  transfers between devices with their start and end apart: 14 -> 12, of which waited for: 5 -> 6; matrix products, arithmetic and copies ran while one was open for 13% -> 16% of each run, Pallas kernels for 3% -> 3%
where the time goes in v6:
time: 225 us; the launch traced here: 224 us
  blocking collectives  82.8 us (37%)
  starting transfers between devices  52.8 us (23%)
  local copies, waits for them, and re-layouts  23.4 us (10%)
  waiting for transfers between devices  21.3 us (9%)
  between operations  14.7 us (7%)
  other arithmetic  14 us (6%)
  matrix products  8.15 us (4%)
  Pallas kernels  6.43 us (3%)
    all_to_all x3, blocking collectives, exchange(): lax.all_to_all(parts, axis, split_axis=0, concat_axis=0, tiled=True, axis...  82.8 us
    all_to_all x2, starting transfers between devices, exchange(): lax.all_to_all(parts, axis, split_axis=0, concat_axis=0, tiled=True, axis...  23.1 us
    ppermute x6, starting transfers between devices, summed(): total = total + lax.ppermute(parts[k], 'tensor', perm).astype(f32)  18.3 us
    all_to_all x2, waiting for transfers between devices, exchange(): lax.all_to_all(parts, axis, split_axis=0, concat_axis=0, tiled=True, axis...  8.36 us
    concatenate x4, local copies, waits for them, and re-layouts, by_side(): even, odd = (jnp.concatenate(pieces[k::2], axis=axis) for k in range(2))  8.26 us
    ppermute x2, starting transfers between devices, gather_halves(): lax.ppermute(mine, 'tensor', [(i, i ^ 1) for i in range(2 * CHIPS)])  8.19 us
    dot_general x7, matrix products, dot(): lax.dot_general(left, right, (((over_left,), (over_right,)), ((), ())), p...  6.97 us
    ppermute x6, waiting for transfers between devices, summed(): total = total + lax.ppermute(parts[k], 'tensor', perm).astype(f32)  6.81 us
  transfers between devices with their start and end apart: 12, of which 6 were waited for; matrix products, arithmetic and copies ran while one was open for 16% of the time, Pallas kernels for 3%

profile of v6, /device:TPU:1, one launch (start us, length us, event | category | flops | bytes accessed | tf_op | source)
XLA Modules:
  0.0 223.5 jit_solution(7128607288341430237)
XLA Ops:
  7.2 0.8 fusion.26
  8.0 1.2 convolution_compare_fusion
  9.2 1.1 convolution_convert_fusion
  10.3 0.2 copy.29
  10.6 1.0 reshape.73
  11.6 17.2 %all-to-all-start = ((bf16[32,18,320]{2,1,0:T(8,128)(2,1)}), bf16[32,18,320]{2,1,0:T(8,128)(2,1)}, u32[]{:S(2)}, u32[]{:S(2)}) async-start(bf16[32,18,320]{2,1,0:T(8,128)(2,1)} %reshape.73), calls=%async_computation | async-start | bytes 1179648 | tf_op jit(solution)/shard_map/all_to_all | solution.py:22
  28.8 0.0 all-gather.3.cloned.1.call-start
  28.8 1.7 pad_maximum_fusion
  30.5 3.1 %collective-permute-start = (bf16[160,576]{1,0:T(8,128)(2,1)}, bf16[160,576]{1,0:T(8,128)(2,1)}, u32[]{:S(2)}, u32[]{:S(2)}) collective-permute-start(bf16[160,576]{1,0:T(8,128)(2,1)} %pad_maximum_fusion), channel_id=1, source_target_pairs={{0,256},{16,272},{32,288},{48,304},{64,320},{80,336},{96,352},{112... | collective-permute-start | bytes 552968 | tf_op jit(solution)/shard_map/ppermute | solution.py:123
  33.6 3.1 %slice_bitcast_fusion.4 = (bf16[96,320]{0,1:T(8,128)(2,1)}, bf16[96,320]{0,1:T(8,128)(2,1)}, bf16[96,320]{0,1:T(8,128)(2,1)}, bf16[96,320]{0,1:T(8,128)(2,1)}, b...) fusion(bf16[1,1536,320]{1,2,0:T(8,128)(2,1)} %param.18), kind=kLoop, calls=%fused_computation.83 | loop fusion | bytes 1966080 | tf_op jit(solution)/shard_map/slice | solution.py:113
  36.7 1.1 pad_maximum_fusion.1
  37.8 1.4 fusion.11
  39.3 3.4 %concatenate.28 = bf16[192,2560]{1,0:T(8,128)(2,1)} concatenate(bf16[192,320]{1,0:T(8,128)(2,1)} %get-tuple-element.30, bf16[192,320]{1,0:T(8,128)(2,1)} %get-tuple-element.31, bf16[192,320]{1,0:T(8,128)(2,1)} %get-tuple-element.32, bf16[192,320]{1,0:T(8,128)(2,1)} %get-tuple-element.33, bf16[192,320]{1,0:T(8,128)(2,1)} %get-tuple-element.34, ...), dimensions={1} | concatenate | bytes 1966080 | tf_op jit(solution)/shard_map/concatenate | solution.py:114
  42.8 1.9 concatenate.27
  44.7 1.9 concatenate.30
  46.7 1.1 concatenate.29
  47.8 1.7 broadcast_select_fusion
  49.5 0.0 copy-done.8
  49.5 1.0 broadcast_select_fusion.2
  50.5 1.0 fusion.74
  51.6 1.9 maximum_select_fusion
  53.5 8.4 %all-to-all-done = bf16[32,18,320]{2,1,0:T(8,128)(2,1)} async-done(((bf16[32,18,320]{2,1,0:T(8,128)(2,1)}), bf16[32,18,320]{2,1,0:T(8,128)(2,1)}, u32[]{:S(2)}, u32[]{:S(2)}) %all-to-all-start) | async-done | bytes 368672 | tf_op jit(solution)/shard_map/all_to_all | solution.py:22
  61.9 2.1 reshape.74
  64.0 1.8 maximum_bitcast_fusion
  65.8 2.0 copy.30
  67.8 1.3 broadcast_in_dim.65
  69.0 45.4 %all_to_all.25.mine_ref = bf16[8,320,624]{2,1,0:T(8,128)(2,1)S(1)} all-to-all(bf16[8,320,624]{2,1,0:T(8,128)(2,1)S(1)} %broadcast_in_dim.65), channel_id=1, replica_groups={{0,2,4,6,8,10,12,14},{1,3,5,7,9,11,13,15},{16,18,20,22,24,26,28,30},{17..., dimensions={0} | all-to-all | bytes 6389760 | tf_op jit(solution)/shard_map/all_to_all | solution.py:22
  114.5 4.8 %collective-permute-start.1 = (bf16[8,320,624]{2,1,0:T(8,128)(2,1)S(1)}, bf16[8,320,624]{2,1,0:T(8,128)(2,1)S(1)}, u32[]{:S(2)}, u32[]{:S(2)}) collective-permute-start(bf16[8,320,624]{2,1,0:T(8,128)(2,1)S(1)} %all_to_all.25.mine_ref), channel_id=1, source_target_pairs={{0,1},{1,0},{2,3},{3,2},{4,5},{5,4},{6,7},{7,6},{8,9},{9,8},{10,11... | collective-permute-start | bytes 9584648 | tf_op jit(solution)/shard_map/ppermute | solution.py:29
  119.2 0.9 fusion.57
  120.2 4.5 %collective-permute-done.1.theirs_ref = bf16[8,320,624]{2,1,0:T(8,128)(2,1)S(1)} collective-permute-done((bf16[8,320,624]{2,1,0:T(8,128)(2,1)S(1)}, bf16[8,320,624]{2,1,0:T(8,128)(2,1)S(1)}, u32[]{:S(2)}, u32[]{:S(2)}) %collective-permute-start.1) | collective-permute-done | bytes 3194912 | tf_op jit(solution)/shard_map/ppermute | solution.py:29
  124.7 0.9 convolution_add_fusion.1
  125.6 0.9 copy-done.2
  126.5 0.1 fusion.10
  126.6 0.1 broadcast_in_dim.66
  126.7 18.5 %all_to_all.26 = bf16[8,96,576]{2,1,0:T(8,128)(2,1)S(1)} all-to-all(bf16[8,96,576]{2,1,0:T(8,128)(2,1)S(1)} %broadcast_in_dim.66), channel_id=1, replica_groups={{0,2,4,6,8,10,12,14},{1,3,5,7,9,11,13,15},{16,18,20,22,24,26,28,30},{17..., dimensions={0} | all-to-all | bytes 1769472 | tf_op jit(solution)/shard_map/all_to_all | solution.py:22
  145.2 3.4 %collective-permute-start.2 = (bf16[8,96,576]{2,1,0:T(8,128)(2,1)S(1)}, bf16[8,96,576]{2,1,0:T(8,128)(2,1)S(1)}, u32[]{:S(2)}, u32[]{:S(2)}) collective-permute-start(bf16[8,96,576]{2,1,0:T(8,128)(2,1)S(1)} %all_to_all.26), channel_id=1, source_target_pairs={{0,1},{1,0},{2,3},{3,2},{4,5},{5,4},{6,7},{7,6},{8,9},{9,8},{10,11... | collective-permute-start | bytes 2654216 | tf_op jit(solution)/shard_map/ppermute | solution.py:29
  148.6 0.6 fusion.58
  149.2 1.6 collective-permute-done.2
  150.8 0.6 fusion
  151.3 0.2 copy.31
  151.6 1.0 reshape.79
  152.6 5.9 %all-to-all-start.3 = ((bf16[32,18,320]{2,1,0:T(8,128)(2,1)}), bf16[32,18,320]{2,1,0:T(8,128)(2,1)S(1)}, u32[]{:S(2)}, u32[]{:S(2)}) async-start(bf16[32,18,320]{2,1,0:T(8,128)(2,1)} %reshape.79), calls=%async_computation.3 | async-start | bytes 1179648 | tf_op jit(solution)/shard_map/all_to_all | solution.py:22
  158.5 0.0 all-gather.3.cloned.1.call-done
  158.6 6.4 %shard_map.140 = bf16[4,4,48,320]{3,2,1,0:T(8,128)(2,1)} custom-call(s32[1]{0:T(128)} %bitcast.26.rank_ref, bf16[8,320,624]{2,1,0:T(8,128)(2,1)} %copy-done.1, bf16[8,320,624]{2,1,0:T(8,128)(2,1)} %copy-done.2, bf16[16,2,160,576]{3,2,1,0:T(8,128)(2,1)} %bitcast.88), custom_call_target="tpu_custom_call" | custom-call | flops 1000 | bytes 1000 | tf_op jit(solution)/shard_map/pallas_call | solution.py:60
  165.0 1.1 slice_bitcast_fusion.2
  166.1 3.6 %collective-permute-start.5 = (bf16[4,48,320]{2,1,0:T(8,128)(2,1)S(1)}, bf16[4,48,320]{2,1,0:T(8,128)(2,1)S(1)}, u32[]{:S(2)}, u32[]{:S(2)}) collective-permute-start(bf16[4,48,320]{2,1,0:T(8,128)(2,1)S(1)} %get-tuple-element.55), channel_id=1, source_target_pairs={{0,3},{1,2},{2,1},{3,0},{4,7},{5,6},{6,5},{7,4},{8,11},{9,10},{10,... | collective-permute-start | bytes 368648 | tf_op jit(solution)/shard_map/ppermute | solution.py:147
  169.7 3.7 %collective-permute-start.4 = (bf16[4,48,320]{2,1,0:T(8,128)(2,1)S(1)}, bf16[4,48,320]{2,1,0:T(8,128)(2,1)S(1)}, u32[]{:S(2)}, u32[]{:S(2)}) collective-permute-start(bf16[4,48,320]{2,1,0:T(8,128)(2,1)S(1)} %get-tuple-element.56), channel_id=1, source_target_pairs={{0,2},{1,3},{2,0},{3,1},{4,6},{5,7},{6,4},{7,5},{8,10},{9,11},{10,... | collective-permute-start | bytes 368648 | tf_op jit(solution)/shard_map/ppermute | solution.py:147
  173.5 2.0 collective-permute-start.3
  175.6 1.6 collective-permute-done.5
  177.1 3.9 %collective-permute-done.4 = bf16[4,48,320]{2,1,0:T(8,128)(2,1)S(1)} collective-permute-done((bf16[4,48,320]{2,1,0:T(8,128)(2,1)S(1)}, bf16[4,48,320]{2,1,0:T(8,128)(2,1)S(1)}, u32[]{:S(2)}, u32[]{:S(2)}) %collective-permute-start.4) | collective-permute-done | bytes 122912 | tf_op jit(solution)/shard_map/ppermute | solution.py:147
  181.1 1.0 fusion.9
  182.1 2.4 %collective-permute-start.8 = (bf16[48,320]{1,0:T(8,128)(2,1)S(1)}, bf16[48,320]{1,0:T(8,128)(2,1)S(1)}, u32[]{:S(2)}, u32[]{:S(2)}) collective-permute-start(bf16[48,320]{1,0:T(8,128)(2,1)S(1)} %get-tuple-element.58), channel_id=1, source_target_pairs={{0,12},{1,13},{2,14},{3,15},{4,8},{5,9},{6,10},{7,11},{8,4},{9,5},... | collective-permute-start | bytes 92168 | tf_op jit(solution)/shard_map/ppermute | solution.py:147
  184.4 3.1 %collective-permute-start.7 = (bf16[48,320]{1,0:T(8,128)(2,1)S(1)}, bf16[48,320]{1,0:T(8,128)(2,1)S(1)}, u32[]{:S(2)}, u32[]{:S(2)}) collective-permute-start(bf16[48,320]{1,0:T(8,128)(2,1)S(1)} %get-tuple-element.59), channel_id=1, source_target_pairs={{0,8},{1,9},{2,10},{3,11},{4,12},{5,13},{6,14},{7,15},{8,0},{9,1},... | collective-permute-start | bytes 92168 | tf_op jit(solution)/shard_map/ppermute | solution.py:147
  187.6 3.5 %collective-permute-start.6 = (bf16[48,320]{1,0:T(8,128)(2,1)S(1)}, bf16[48,320]{1,0:T(8,128)(2,1)S(1)}, u32[]{:S(2)}, u32[]{:S(2)}) collective-permute-start(bf16[48,320]{1,0:T(8,128)(2,1)S(1)} %get-tuple-element.57), channel_id=1, source_target_pairs={{0,4},{1,5},{2,6},{3,7},{4,0},{5,1},{6,2},{7,3},{8,12},{9,13},{10,... | collective-permute-start | bytes 92168 | tf_op jit(solution)/shard_map/ppermute | solution.py:147
  191.1 1.3 collective-permute-done.6
  192.4 0.2 reshape.81
  192.7 0.5 fusion.3
  193.2 0.1 broadcast_in_dim.72
  193.3 18.9 %all_to_all.27 = bf16[16,48,320]{2,1,0:T(8,128)(2,1)S(1)} all-to-all(bf16[16,48,320]{2,1,0:T(8,128)(2,1)S(1)} %broadcast_in_dim.72), channel_id=1, replica_groups=mesh['expert'=32,'tensor'=16] {'tensor'}, dimensions={0} | all-to-all | bytes 983040 | tf_op jit(solution)/shard_map/all_to_all | solution.py:22
  212.2 0.1 convert_bitcast_fusion
  212.2 0.4 copy.32
  212.7 1.3 reshape.84
  214.0 0.2 fusion.1
  214.3 2.4 %convolution_convert_fusion.2 = bf16[48,132]{1,0:T(8,128)(2,1)} fusion(bf16[132,5120]{1,0:T(8,128)(2,1)S(1)} %copy-done, f32[48,5120]{1,0:T(8,128)} %reshape.84, f32[5120]{0:T(1024)S(1)} %copy-done.33, f32[48]{0:T(128)S(1)} %add_rsqrt_fusion), kind=kOutput, calls=%fused_computation.41 | convolution fusion | flops 65624256 | bytes 2368064 | tf_op jit(solution)/shard_map/dot_general | solution.py:16
  (84 shorter events, 0.3 us)
Async XLA Ops:
  7.2 207.1 %copy-start = (bf16[132,5120]{1,0:T(8,128)(2,1)S(1)}, bf16[132,5120]{1,0:T(8,128)(2,1)}, u32[]{:S(2)}) copy-start(bf16[132,5120]{1,0:T(8,128)(2,1)} %param.23) | copy-start | bytes 4055044
  7.2 21.6 %copy-start.28 = (bf16[192,160]{0,1:T(8,128)(2,1)S(1)}, bf16[192,160]{0,1:T(8,128)(2,1)}, u32[]{:S(2)}) copy-start(bf16[192,160]{0,1:T(8,128)(2,1)} %param.21) | copy-start | bytes 184324
  7.2 21.6 %copy-start.30 = (bf16[160,192]{1,0:T(8,128)(2,1)S(1)}, bf16[160,192]{1,0:T(8,128)(2,1)}, u32[]{:S(2)}) copy-start(bf16[160,192]{1,0:T(8,128)(2,1)} %param.20) | copy-start | bytes 184324
  11.6 25.1 %copy-start.3 = (bf16[1,96,5120]{2,1,0:T(8,128)(2,1)S(1)}, bf16[1,96,5120]{2,1,0:T(8,128)(2,1)}, u32[]{:S(2)}) copy-start(bf16[1,96,5120]{2,1,0:T(8,128)(2,1)} %param.16) | copy-start | bytes 2949124
  11.6 25.1 %copy-start.4 = (bf16[1,96,5120]{2,1,0:T(8,128)(2,1)S(1)}, bf16[1,96,5120]{2,1,0:T(8,128)(2,1)}, u32[]{:S(2)}) copy-start(bf16[1,96,5120]{2,1,0:T(8,128)(2,1)} %param.17) | copy-start | bytes 2949124
  11.6 50.3 %all-to-all-start = ((bf16[32,18,320]{2,1,0:T(8,128)(2,1)}), bf16[32,18,320]{2,1,0:T(8,128)(2,1)}, u32[]{:S(2)}, u32[]{:S(2)}) async-start(bf16[32,18,320]{2,1,0:T(8,128)(2,1)} %reshape.73), calls=%async_computation | async-start | bytes 1179648 | tf_op jit(solution)/shard_map/all_to_all | solution.py:22
  28.8 129.8 %all-gather.3.cloned.1.call-start = ((), (), s32[]{:S(2)}) async-start(), calls=%async_computation.5 | async-start | bytes 6963200 | tf_op jit(solution)/shard_map/all_gather | solution.py:128
  30.5 21.1 %collective-permute-start = (bf16[160,576]{1,0:T(8,128)(2,1)}, bf16[160,576]{1,0:T(8,128)(2,1)}, u32[]{:S(2)}, u32[]{:S(2)}) collective-permute-start(bf16[160,576]{1,0:T(8,128)(2,1)} %pad_maximum_fusion), channel_id=1, source_target_pairs={{0,256},{16,272},{32,288},{48,304},{64,320},{80,336},{96,352},{112... | collective-permute-start | bytes 552968 | tf_op jit(solution)/shard_map/ppermute | solution.py:123
  39.2 3.5 %copy-start.9 = (bf16[192,320]{1,0:T(8,128)(2,1)S(1)}, bf16[192,320]{1,0:T(8,128)(2,1)}, u32[]{:S(2)}) copy-start(bf16[192,320]{1,0:T(8,128)(2,1)} %get-tuple-element.22) | copy-start | bytes 368644
  39.2 3.5 %copy-start.10 = (bf16[192,320]{1,0:T(8,128)(2,1)S(1)}, bf16[192,320]{1,0:T(8,128)(2,1)}, u32[]{:S(2)}) copy-start(bf16[192,320]{1,0:T(8,128)(2,1)} %get-tuple-element.23) | copy-start | bytes 368644
  39.2 3.5 %copy-start.11 = (bf16[192,320]{1,0:T(8,128)(2,1)S(1)}, bf16[192,320]{1,0:T(8,128)(2,1)}, u32[]{:S(2)}) copy-start(bf16[192,320]{1,0:T(8,128)(2,1)} %get-tuple-element.24) | copy-start | bytes 368644
  39.2 3.5 %copy-start.12 = (bf16[192,320]{1,0:T(8,128)(2,1)S(1)}, bf16[192,320]{1,0:T(8,128)(2,1)}, u32[]{:S(2)}) copy-start(bf16[192,320]{1,0:T(8,128)(2,1)} %get-tuple-element.25) | copy-start | bytes 368644
  39.2 3.5 %copy-start.13 = (bf16[192,320]{1,0:T(8,128)(2,1)S(1)}, bf16[192,320]{1,0:T(8,128)(2,1)}, u32[]{:S(2)}) copy-start(bf16[192,320]{1,0:T(8,128)(2,1)} %get-tuple-element.26) | copy-start | bytes 368644
  39.2 3.5 %copy-start.14 = (bf16[192,320]{1,0:T(8,128)(2,1)S(1)}, bf16[192,320]{1,0:T(8,128)(2,1)}, u32[]{:S(2)}) copy-start(bf16[192,320]{1,0:T(8,128)(2,1)} %get-tuple-element.27) | copy-start | bytes 368644
  39.2 3.5 %copy-start.15 = (bf16[192,320]{1,0:T(8,128)(2,1)S(1)}, bf16[192,320]{1,0:T(8,128)(2,1)}, u32[]{:S(2)}) copy-start(bf16[192,320]{1,0:T(8,128)(2,1)} %get-tuple-element.28) | copy-start | bytes 368644
  39.3 5.4 %copy-start.25 = (bf16[96,320]{0,1:T(8,128)(2,1)S(1)}, bf16[96,320]{0,1:T(8,128)(2,1)}, u32[]{:S(2)}) copy-start(bf16[96,320]{0,1:T(8,128)(2,1)} %get-tuple-element.38) | copy-start | bytes 184324
  39.3 5.4 %copy-start.26 = (bf16[96,320]{0,1:T(8,128)(2,1)S(1)}, bf16[96,320]{0,1:T(8,128)(2,1)}, u32[]{:S(2)}) copy-start(bf16[96,320]{0,1:T(8,128)(2,1)} %get-tuple-element.39) | copy-start | bytes 184324
  39.3 5.4 %copy-start.27 = (bf16[96,320]{0,1:T(8,128)(2,1)S(1)}, bf16[96,320]{0,1:T(8,128)(2,1)}, u32[]{:S(2)}) copy-start(bf16[96,320]{0,1:T(8,128)(2,1)} %get-tuple-element.40) | copy-start | bytes 184324
  42.6 4.0 %copy-start.17 = (bf16[96,320]{0,1:T(8,128)(2,1)S(1)}, bf16[96,320]{0,1:T(8,128)(2,1)}, u32[]{:S(2)}) copy-start(bf16[96,320]{0,1:T(8,128)(2,1)} %get-tuple-element.45) | copy-start | bytes 184324
  42.6 4.0 %copy-start.18 = (bf16[96,320]{0,1:T(8,128)(2,1)S(1)}, bf16[96,320]{0,1:T(8,128)(2,1)}, u32[]{:S(2)}) copy-start(bf16[96,320]{0,1:T(8,128)(2,1)} %get-tuple-element.46) | copy-start | bytes 184324
  42.7 4.0 %copy-start.19 = (bf16[96,320]{0,1:T(8,128)(2,1)S(1)}, bf16[96,320]{0,1:T(8,128)(2,1)}, u32[]{:S(2)}) copy-start(bf16[96,320]{0,1:T(8,128)(2,1)} %get-tuple-element.47) | copy-start | bytes 184324
  42.7 4.0 %copy-start.20 = (bf16[96,320]{0,1:T(8,128)(2,1)S(1)}, bf16[96,320]{0,1:T(8,128)(2,1)}, u32[]{:S(2)}) copy-start(bf16[96,320]{0,1:T(8,128)(2,1)} %get-tuple-element.48) | copy-start | bytes 184324
  42.7 4.0 %copy-start.21 = (bf16[96,320]{0,1:T(8,128)(2,1)S(1)}, bf16[96,320]{0,1:T(8,128)(2,1)}, u32[]{:S(2)}) copy-start(bf16[96,320]{0,1:T(8,128)(2,1)} %get-tuple-element.49) | copy-start | bytes 184324
  42.7 4.0 %copy-start.22 = (bf16[96,320]{0,1:T(8,128)(2,1)S(1)}, bf16[96,320]{0,1:T(8,128)(2,1)}, u32[]{:S(2)}) copy-start(bf16[96,320]{0,1:T(8,128)(2,1)} %get-tuple-element.50) | copy-start | bytes 184324
  42.7 4.0 %copy-start.23 = (bf16[96,320]{0,1:T(8,128)(2,1)S(1)}, bf16[96,320]{0,1:T(8,128)(2,1)}, u32[]{:S(2)}) copy-start(bf16[96,320]{0,1:T(8,128)(2,1)} %get-tuple-element.51) | copy-start | bytes 184324
  42.7 4.0 %copy-start.24 = (bf16[96,320]{0,1:T(8,128)(2,1)S(1)}, bf16[96,320]{0,1:T(8,128)(2,1)}, u32[]{:S(2)}) copy-start(bf16[96,320]{0,1:T(8,128)(2,1)} %get-tuple-element.52) | copy-start | bytes 184324
  47.8 1.7 copy-start.7
  47.8 1.8 copy-start.8
  49.5 1.0 copy-start.29
  49.5 14.4 %copy-start.16 = (bf16[48,320]{1,0:T(8,128)(2,1)S(1)}, bf16[48,320]{1,0:T(8,128)(2,1)}, u32[]{:S(2)}) copy-start(bf16[48,320]{1,0:T(8,128)(2,1)} %param.13) | copy-start | bytes 92164
  114.5 5.7 %copy-start.1 = (bf16[8,320,624]{2,1,0:T(8,128)(2,1)}, bf16[8,320,624]{2,1,0:T(8,128)(2,1)S(1)}, u32[]{:S(2)}) copy-start(bf16[8,320,624]{2,1,0:T(8,128)(2,1)S(1)} %all_to_all.25.mine_ref) | copy-start | bytes 9584644
  114.5 10.2 %collective-permute-start.1 = (bf16[8,320,624]{2,1,0:T(8,128)(2,1)S(1)}, bf16[8,320,624]{2,1,0:T(8,128)(2,1)S(1)}, u32[]{:S(2)}, u32[]{:S(2)}) collective-permute-start(bf16[8,320,624]{2,1,0:T(8,128)(2,1)S(1)} %all_to_all.25.mine_ref), channel_id=1, source_target_pairs={{0,1},{1,0},{2,3},{3,2},{4,5},{5,4},{6,7},{7,6},{8,9},{9,8},{10,11... | collective-permute-start | bytes 9584648 | tf_op jit(solution)/shard_map/ppermute | solution.py:29
  124.7 1.8 copy-start.2
  126.5 22.1 %copy-start.6 = (bf16[768,320]{0,1:T(8,128)(2,1)S(1)}, bf16[768,320]{0,1:T(8,128)(2,1)}, u32[]{:S(2)}) copy-start(bf16[768,320]{0,1:T(8,128)(2,1)} %get-tuple-element.13) | copy-start | bytes 1474564
  126.7 24.1 %copy-start.5 = (bf16[768,320]{0,1:T(8,128)(2,1)S(1)}, bf16[768,320]{0,1:T(8,128)(2,1)}, u32[]{:S(2)}) copy-start(bf16[768,320]{0,1:T(8,128)(2,1)} %get-tuple-element.14) | copy-start | bytes 1474564
  145.2 5.6 %collective-permute-start.2 = (bf16[8,96,576]{2,1,0:T(8,128)(2,1)S(1)}, bf16[8,96,576]{2,1,0:T(8,128)(2,1)S(1)}, u32[]{:S(2)}, u32[]{:S(2)}) collective-permute-start(bf16[8,96,576]{2,1,0:T(8,128)(2,1)S(1)} %all_to_all.26), channel_id=1, source_target_pairs={{0,1},{1,0},{2,3},{3,2},{4,5},{5,4},{6,7},{7,6},{8,9},{9,8},{10,11... | collective-permute-start | bytes 2654216 | tf_op jit(solution)/shard_map/ppermute | solution.py:29
  152.6 39.9 %all-to-all-start.3 = ((bf16[32,18,320]{2,1,0:T(8,128)(2,1)}), bf16[32,18,320]{2,1,0:T(8,128)(2,1)S(1)}, u32[]{:S(2)}, u32[]{:S(2)}) async-start(bf16[32,18,320]{2,1,0:T(8,128)(2,1)} %reshape.79), calls=%async_computation.3 | async-start | bytes 1179648 | tf_op jit(solution)/shard_map/all_to_all | solution.py:22
  158.6 17.0 %copy-start.34 = (s32[48,6]{0,1:T(8,128)S(1)}, s32[48,6]{0,1:T(8,128)}, u32[]{:S(2)}) copy-start(s32[48,6]{0,1:T(8,128)} %param.14) | copy-start | bytes 3460
  158.6 17.0 %copy-start.35 = (f32[48,6]{0,1:T(8,128)S(1)}, f32[48,6]{0,1:T(8,128)}, u32[]{:S(2)}) copy-start(f32[48,6]{0,1:T(8,128)} %param.15) | copy-start | bytes 3460
  165.0 27.7 %copy-start.32 = (bf16[32,576]{1,0:T(8,128)(2,1)S(1)}, bf16[32,576]{1,0:T(8,128)(2,1)}, u32[]{:S(2)}) copy-start(bf16[32,576]{1,0:T(8,128)(2,1)} %constant.42.clone) | copy-start | bytes 110596
  166.1 11.0 %collective-permute-start.5 = (bf16[4,48,320]{2,1,0:T(8,128)(2,1)S(1)}, bf16[4,48,320]{2,1,0:T(8,128)(2,1)S(1)}, u32[]{:S(2)}, u32[]{:S(2)}) collective-permute-start(bf16[4,48,320]{2,1,0:T(8,128)(2,1)S(1)} %get-tuple-element.55), channel_id=1, source_target_pairs={{0,3},{1,2},{2,1},{3,0},{4,7},{5,6},{6,5},{7,4},{8,11},{9,10},{10,... | collective-permute-start | bytes 368648 | tf_op jit(solution)/shard_map/ppermute | solution.py:147
  169.7 11.3 %collective-permute-start.4 = (bf16[4,48,320]{2,1,0:T(8,128)(2,1)S(1)}, bf16[4,48,320]{2,1,0:T(8,128)(2,1)S(1)}, u32[]{:S(2)}, u32[]{:S(2)}) collective-permute-start(bf16[4,48,320]{2,1,0:T(8,128)(2,1)S(1)} %get-tuple-element.56), channel_id=1, source_target_pairs={{0,2},{1,3},{2,0},{3,1},{4,6},{5,7},{6,4},{7,5},{8,10},{9,11},{10,... | collective-permute-start | bytes 368648 | tf_op jit(solution)/shard_map/ppermute | solution.py:147
  173.5 7.6 %collective-permute-start.3 = (bf16[4,48,320]{2,1,0:T(8,128)(2,1)S(1)}, bf16[4,48,320]{2,1,0:T(8,128)(2,1)S(1)}, u32[]{:S(2)}, u32[]{:S(2)}) collective-permute-start(bf16[4,48,320]{2,1,0:T(8,128)(2,1)S(1)} %get-tuple-element.54), channel_id=1, source_target_pairs={{0,1},{1,0},{2,3},{3,2},{4,5},{5,4},{6,7},{7,6},{8,9},{9,8},{10,11... | collective-permute-start | bytes 368648 | tf_op jit(solution)/shard_map/ppermute | solution.py:147
  182.1 9.0 %collective-permute-start.8 = (bf16[48,320]{1,0:T(8,128)(2,1)S(1)}, bf16[48,320]{1,0:T(8,128)(2,1)S(1)}, u32[]{:S(2)}, u32[]{:S(2)}) collective-permute-start(bf16[48,320]{1,0:T(8,128)(2,1)S(1)} %get-tuple-element.58), channel_id=1, source_target_pairs={{0,12},{1,13},{2,14},{3,15},{4,8},{5,9},{6,10},{7,11},{8,4},{9,5},... | collective-permute-start | bytes 92168 | tf_op jit(solution)/shard_map/ppermute | solution.py:147
  184.4 6.7 %collective-permute-start.7 = (bf16[48,320]{1,0:T(8,128)(2,1)S(1)}, bf16[48,320]{1,0:T(8,128)(2,1)S(1)}, u32[]{:S(2)}, u32[]{:S(2)}) collective-permute-start(bf16[48,320]{1,0:T(8,128)(2,1)S(1)} %get-tuple-element.59), channel_id=1, source_target_pairs={{0,8},{1,9},{2,10},{3,11},{4,12},{5,13},{6,14},{7,15},{8,0},{9,1},... | collective-permute-start | bytes 92168 | tf_op jit(solution)/shard_map/ppermute | solution.py:147
  187.6 4.9 %collective-permute-start.6 = (bf16[48,320]{1,0:T(8,128)(2,1)S(1)}, bf16[48,320]{1,0:T(8,128)(2,1)S(1)}, u32[]{:S(2)}, u32[]{:S(2)}) collective-permute-start(bf16[48,320]{1,0:T(8,128)(2,1)S(1)} %get-tuple-element.57), channel_id=1, source_target_pairs={{0,4},{1,5},{2,6},{3,7},{4,0},{5,1},{6,2},{7,3},{8,12},{9,13},{10,... | collective-permute-start | bytes 92168 | tf_op jit(solution)/shard_map/ppermute | solution.py:147
  193.2 19.4 %copy-start.31 = (bf16[48,320]{1,0:T(8,128)(2,1)}, bf16[48,320]{1,0:T(8,128)(2,1)S(1)}, u32[]{:S(2)}) copy-start(bf16[48,320]{1,0:T(8,128)(2,1)S(1)} %fusion.28) | copy-start | bytes 92164
  212.6 1.6 copy-start.33
Sparse Core Ops, SparseCore 0:
  62.0 81.7 all-gather.2

commit v7 on v6

--- a/solution.py
+++ b/solution.py
@@ -10,6 +10,7 @@
 CHIPS = 8
 LANES = [[x * ROWS + z for z in range(ROWS)] for x in range(2)]
 SIDES = [[2 * chip + core for chip in range(CHIPS)] for core in range(2)]
+RINGS = [[4 * y + near for y in range(4)] for near in range(4)]
 
 
 def dot(left, right, over_left, over_right):
@@ -24,27 +25,35 @@
     )
 
 
-def gather_halves(block):
-    mine = exchange(jnp.broadcast_to(block[None], (CHIPS,) + block.shape), "tensor", SIDES)
+def gather_halves(block, groups, held=None):
+    spread = jnp.broadcast_to(block[None], (len(groups[0]),) + block.shape)
+    mine = exchange(spread, "tensor", groups)
+    if held is not None:
+        mine, held = lax.optimization_barrier((mine, held))
     theirs = lax.ppermute(mine, "tensor", [(i, i ^ 1) for i in range(2 * CHIPS)])
-    return mine, theirs
-
-
-def shared_kernel(rank_ref, mine_ref, theirs_ref, table_ref, out_ref):
+    return mine, theirs, held
+
+
+def shared_kernel(rank_ref, mine_ref, far_mine_ref, theirs_ref, far_theirs_ref, table_ref, out_ref):
     rank = rank_ref[0]
     inner = table_ref.shape[3] // 3
     size = table_ref.shape[2]
-    start = mine_ref.shape[2] // 2
+    tok = out_ref.shape[2]
 
     def weights(device):
         return table_ref.at[pl.ds(2 * (device & 7), 2), device >> 3]
 
-    sums = jnp.zeros((mine_ref.shape[2], 2 * inner), jnp.float32)
-    for chip in range(CHIPS):
-        for ref, core in ((mine_ref, rank & 1), (theirs_ref, 1 - (rank & 1))):
-            block = weights(2 * chip + core)[:, :, : 2 * inner].reshape(2 * size, 2 * inner)
-            sums = sums + dot(ref[chip], block, 0, 0)
-    sums = sums[start : start + out_ref.shape[2]]
+    def product(refs, across):
+        total = jnp.zeros((mine_ref.shape[2], 2 * inner), jnp.float32)
+        for y in range(4):
+            for core in range(2):
+                device = 4 * y + (((rank & 3) ^ (2 * across)) ^ core)
+                block = weights(device)[:, :, : 2 * inner].reshape(2 * size, 2 * inner)
+                total = total + dot(refs[core][y], block, 0, 0)
+        return total
+
+    sums = product((mine_ref, theirs_ref), 0)[64 : 64 + tok]
+    sums = sums + product((far_mine_ref, far_theirs_ref), 1)[:tok]
     gate, up = sums[:, :inner], sums[:, inner:]
     hidden = (gate * (1.0 / (1.0 + jnp.exp(-gate))) * up).astype(jnp.bfloat16)
     for near in range(4):
@@ -56,21 +65,24 @@
 def shared_partial(rank, mine, theirs, table, tok):
     width = mine.shape[1]
     out = jax.ShapeDtypeStruct((4, 4, tok, width), jnp.bfloat16)
-    last = pl.BlockSpec((CHIPS, width, 128), lambda i: (0, 0, 4))
+    near = pl.BlockSpec((4, width, 128), lambda i: (0, 0, 4))
+    far = pl.BlockSpec((4, width, 128), lambda i: (0, 0, 5))
     return pl.pallas_call(
         shared_kernel,
         out_shape=out,
         grid=(1,),
         in_specs=[
             pl.BlockSpec(memory_space=pltpu.SMEM),
-            last,
-            last,
+            near,
+            far,
+            near,
+            far,
             pl.BlockSpec(table.shape, lambda i: (0, 0, 0, 0), pipeline_mode=pl.Buffered(1)),
         ],
         out_specs=pl.BlockSpec(out.shape, lambda i: (0, 0, 0, 0)),
         compiler_params=pltpu.CompilerParams(vmem_limit_bytes=56 * 2**20),
         cost_estimate=pl.CostEstimate(flops=1000, bytes_accessed=1000, transcendentals=0),
-    )(rank.reshape(1), mine, theirs, table)
+    )(rank.reshape(1), mine, mine, theirs, theirs, table)
 
 
 def per_device(
@@ -116,23 +128,41 @@
 
     hid = routed_gate.shape[1]
     gate_up = jnp.concatenate([routed_gate[0], routed_up[0]], axis=0)
-    in_mine, in_theirs = by_side(gate_up, 1)
+    near = [jnp.concatenate([gate_up[:, k * width : (k + 1) * width] for k in range(low, 16, 4)], axis=1) for low in range(4)]
+
+    def columns(flip):
+        low = (rank & 3) ^ flip
+        return jnp.where(low < 2, jnp.where(low == 0, near[0], near[1]), jnp.where(low == 2, near[2], near[3]))
+
+    in_mine, in_theirs = columns(0), columns(1)
+    give = jnp.concatenate([columns(2), columns(3)], axis=1)
     out_mine, out_theirs = by_side(routed_down[0], 0)
 
     own = jnp.concatenate([shared_gate, shared_up, shared_down.T], axis=1)
     other = lax.ppermute(own, "expert", [(i, (i + ROWS) % (2 * ROWS)) for i in range(2 * ROWS)])
     pair = jnp.where(column == 0, jnp.stack([own, other]), jnp.stack([other, own]))
-    arrived, pair, in_mine, in_theirs, out_mine, out_theirs = lax.optimization_barrier(
-        (arrived, pair, in_mine, in_theirs, out_mine, out_theirs)
-    )
+    beside = lax.ppermute(tokens, "tensor", [(i, i ^ 2) for i in range(2 * CHIPS)])
+    across = [(i, i ^ 2) for i in range(2 * CHIPS)]
+    far_gate = lax.ppermute(give[:hid], "tensor", across)
+    arrived, beside, pair, in_mine, in_theirs, give, far_gate, out_mine, out_theirs = lax.optimization_barrier(
+        (arrived, beside, pair, in_mine, in_theirs, give, far_gate, out_mine, out_theirs)
+    )
+    far_up = lax.ppermute(give[hid:], "tensor", across)
     gathered = lax.all_gather(pair, "expert", axis=0, axis_index_groups=LANES)
 
-    rows = jnp.concatenate([arrived.reshape(slots, width), tokens], axis=0)
-    mine, theirs = gather_halves(rows.T)
-    total = slots + tok
-    both = dot(in_mine, mine.reshape(-1, total), 1, 0) + dot(in_theirs, theirs.reshape(-1, total), 1, 0)
-    hidden = (jax.nn.silu(both[:hid, :slots]) * both[hid:, :slots]).astype(bf16)
-    hidden_mine, hidden_theirs = gather_halves(hidden)
+    blank = jnp.zeros((16, width), bf16)
+    rows = jnp.concatenate([arrived.reshape(slots, width), tokens, blank, beside], axis=0)
+    mine, theirs, far_up = gather_halves(rows.T, RINGS, far_up)
+    far = jnp.concatenate([far_gate, far_up], axis=0)
+    total = rows.shape[0]
+    left, right = mine.reshape(-1, total), theirs.reshape(-1, total)
+    middle = left.shape[0]
+    send = dot(far[:, :middle], left, 1, 0) + dot(far[:, middle:], right, 1, 0)
+    got = lax.ppermute(send[:, :slots].astype(bf16), "tensor", [(i, i ^ 2) for i in range(2 * CHIPS)])
+    both = dot(in_mine, left, 1, 0) + dot(in_theirs, right, 1, 0)
+    both = both[:, :slots] + got.astype(f32)
+    hidden = (jax.nn.silu(both[:hid]) * both[hid:]).astype(bf16)
+    hidden_mine, hidden_theirs, _ = gather_halves(hidden, SIDES)
     result = dot(hidden_mine.reshape(-1, slots), out_mine, 0, 0) + dot(
         hidden_theirs.reshape(-1, slots), out_theirs, 0, 0
     )

time: 225 us -> 227 us (level)
  blocking collectives: 82.8 us -> 36.7 us
  starting transfers between devices: 52.8 us -> 77.4 us
  waiting for transfers between devices: 21.3 us -> 40.1 us
    all_to_all x3 -> x2, blocking collectives: 82.8 us -> 36.7 us  [exchange(): lax.all_to_all(parts, axis, split_axis=0, concat_axis=0, tiled=True, axis...]
    ppermute x0 -> x4, waiting for transfers between devices: none -> 23.6 us  [the longest x1 10.7 us: per_device(): far_up = lax.ppermute(give[hid:], 'tensor', across)]
    ppermute x0 -> x4, starting transfers between devices: none -> 15.5 us  [the longest x1 5.62 us: per_device(): lax.ppermute(tokens, 'tensor', [(i, i ^ 2) for i in range(2 * CHIPS)])]
    all_to_all x2 -> x3, starting transfers between devices: 23.1 us -> 31 us  [exchange(): lax.all_to_all(parts, axis, split_axis=0, concat_axis=0, tiled=True, axis...]
    concatenate x0 -> x6, local copies, waits for them, and re-layouts: none -> 6.92 us  [the longest x4 5.78 us: per_device(): jnp.concatenate([gate_up[:, k * width:(k + 1) * width] for k in range(low...]
    concatenate x4 -> x2, local copies, waits for them, and re-layouts: 8.26 us -> 2.56 us  [by_side(): even, odd = (jnp.concatenate(pieces[k::2], axis=axis) for k in range(2))]
    ppermute x2, waiting for transfers between devices: 6.1 us -> 2.17 us  [gather_halves(): lax.ppermute(mine, 'tensor', [(i, i ^ 1) for i in range(2 * CHIPS)])]
    select_n x0 -> x1, other arithmetic: none -> 2.36 us  [columns(): jnp.where(low < 2, jnp.where(low == 0, near[0], near[1]), jnp.where(low =...]
  transfers between devices with their start and end apart: 12 -> 17, of which waited for: 6 -> 9; matrix products, arithmetic and copies ran while one was open for 16% -> 20% of each run, Pallas kernels for 3% -> 3%
where the time goes in v7:
time: 227 us; the launch traced here: 225 us
  starting transfers between devices  77.4 us (34%)
  waiting for transfers between devices  40.1 us (18%)
  blocking collectives  36.7 us (16%)
  local copies, waits for them, and re-layouts  24.5 us (11%)
  between operations  14.8 us (7%)
  other arithmetic  14.6 us (6%)
  matrix products  10.4 us (5%)
  Pallas kernels  6.41 us (3%)
    all_to_all x2, blocking collectives, exchange(): lax.all_to_all(parts, axis, split_axis=0, concat_axis=0, tiled=True, axis...  36.7 us
    all_to_all x3, starting transfers between devices, exchange(): lax.all_to_all(parts, axis, split_axis=0, concat_axis=0, tiled=True, axis...  31 us
    ppermute x6, starting transfers between devices, summed(): total = total + lax.ppermute(parts[k], 'tensor', perm).astype(f32)  18.5 us
    ppermute x1, waiting for transfers between devices, per_device(): far_up = lax.ppermute(give[hid:], 'tensor', across)  10.7 us
    ppermute x2, starting transfers between devices, gather_halves(): lax.ppermute(mine, 'tensor', [(i, i ^ 1) for i in range(2 * CHIPS)])  9.29 us
    dot_general x9, matrix products, dot(): lax.dot_general(left, right, (((over_left,), (over_right,)), ((), ())), p...  9.26 us
    all_to_all x3, waiting for transfers between devices, exchange(): lax.all_to_all(parts, axis, split_axis=0, concat_axis=0, tiled=True, axis...  7.68 us
    ppermute x1, waiting for transfers between devices, per_device(): lax.ppermute(send[:, :slots].astype(bf16), 'tensor', [(i, i ^ 2) for i in...  7.28 us
  transfers between devices with their start and end apart: 17, of which 9 were waited for; matrix products, arithmetic and copies ran while one was open for 20% of the time, Pallas kernels for 3%

profile of v7, /device:TPU:1, one launch (start us, length us, event | category | flops | bytes accessed | tf_op | source)
XLA Modules:
  0.0 225.0 jit_solution(12974791506582719763)
XLA Ops:
  7.2 5.6 %collective-permute-start = (bf16[48,320]{1,0:T(8,128)(2,1)}, bf16[48,320]{1,0:T(8,128)(2,1)}, u32[]{:S(2)}, u32[]{:S(2)}) collective-permute-start(bf16[48,320]{1,0:T(8,128)(2,1)} %param.13), channel_id=1, source_target_pairs={{0,2},{1,3},{2,0},{3,1},{4,6},{5,7},{6,4},{7,5},{8,10},{9,11},{10,... | collective-permute-start | bytes 92168 | tf_op jit(solution)/shard_map/ppermute | solution.py:144
  12.8 0.7 fusion.33
  13.5 1.2 convolution_compare_fusion
  14.8 2.0 convolution_convert_fusion
  16.8 1.9 copy.30
  18.7 2.0 reshape.73
  20.7 15.3 %all-to-all-start = ((bf16[32,18,320]{2,1,0:T(8,128)(2,1)}), bf16[32,18,320]{2,1,0:T(8,128)(2,1)}, u32[]{:S(2)}, u32[]{:S(2)}) async-start(bf16[32,18,320]{2,1,0:T(8,128)(2,1)} %reshape.73), calls=%async_computation | async-start | bytes 1179648 | tf_op jit(solution)/shard_map/all_to_all | solution.py:23
  36.1 1.7 pad_maximum_fusion.1
  37.8 3.1 %collective-permute-start.1 = (bf16[160,576]{1,0:T(8,128)(2,1)}, bf16[160,576]{1,0:T(8,128)(2,1)}, u32[]{:S(2)}, u32[]{:S(2)}) collective-permute-start(bf16[160,576]{1,0:T(8,128)(2,1)} %pad_maximum_fusion.1), channel_id=1, source_target_pairs={{0,256},{16,272},{32,288},{48,304},{64,320},{80,336},{96,352},{112... | collective-permute-start | bytes 552968 | tf_op jit(solution)/shard_map/ppermute | solution.py:142
  40.9 1.3 fusion.26
  42.2 1.2 pad_maximum_fusion.2
  43.4 1.4 concatenate.41
  44.9 1.3 concatenate.42
  46.2 1.9 concatenate.39
  48.2 1.1 concatenate.40
  49.3 2.4 %select_select_fusion.1 = (bf16[192,1280]{1,0:T(8,128)(2,1)S(1)}, bf16[192,1280]{1,0:T(8,128)(2,1)S(1)}, bf16[192,1280]{1,0:T(8,128)(2,1)}, bf16[192,1280]{1,0:T(8,128)(2,1)}) fusion(bf16[192,1280]{1,0:T(8,128)(2,1)S(1)} %concatenate.41, bf16[192,1280]{1,0:T(8,128)(2,1)S(1)} %concatenate.42, bf16[192,1280]{1,0:T(8,128)(2,1)} %concatenate.39, ...), kind=kLoop, calls=%fused_computation.60 | loop fusion | flops 2949120 | bytes 3932172 | tf_op jit(solution)/shard_map/jit(_where)/select_n | solution.py:135
  51.6 0.8 fusion.5
  52.5 3.6 %collective-permute-start.2 = (bf16[96,2560]{1,0:T(8,128)(2,1)}, bf16[96,2560]{1,0:T(8,128)(2,1)}, u32[]{:S(2)}, u32[]{:S(2)}) collective-permute-start(bf16[96,2560]{1,0:T(8,128)(2,1)} %fusion.5), channel_id=1, source_target_pairs={{0,2},{1,3},{2,0},{3,1},{4,6},{5,7},{6,4},{7,5},{8,10},{9,11},{10,... | collective-permute-start | bytes 1474568 | tf_op jit(solution)/shard_map/ppermute | solution.py:146
  56.1 1.4 slice_bitcast_fusion.4
  57.5 1.3 concatenate.45
  58.8 1.3 concatenate.44
  60.1 1.0 pad_maximum_fusion
  61.1 1.0 broadcast_select_fusion
  62.3 1.9 maximum_select_fusion
  64.2 5.6 %collective-permute-done.2 = bf16[96,2560]{1,0:T(8,128)(2,1)} collective-permute-done((bf16[96,2560]{1,0:T(8,128)(2,1)}, bf16[96,2560]{1,0:T(8,128)(2,1)}, u32[]{:S(2)}, u32[]{:S(2)}) %collective-permute-start.2) | collective-permute-done | bytes 491552 | tf_op jit(solution)/shard_map/ppermute | solution.py:146
  69.9 1.3 reshape.74
  71.2 0.9 maximum_bitcast_fusion
  72.4 1.5 broadcast_in_dim.69
  73.9 4.2 %all-to-all-start.1 = ((bf16[4,320,688]{2,1,0:T(8,128)(2,1)}), bf16[4,320,688]{2,1,0:T(8,128)(2,1)S(1)}, u32[]{:S(2)}, u32[]{:S(2)}) async-start(bf16[4,320,688]{2,1,0:T(8,128)(2,1)} %broadcast_in_dim.69), calls=%async_computation.1 | async-start | bytes 3932160 | tf_op jit(solution)/shard_map/all_to_all | solution.py:23
  78.0 1.1 slice.248
  79.1 3.1 %collective-permute-start.3 = (bf16[96,2560]{1,0:T(8,128)(2,1)S(1)}, bf16[96,2560]{1,0:T(8,128)(2,1)}, u32[]{:S(2)}, u32[]{:S(2)}) collective-permute-start(bf16[96,2560]{1,0:T(8,128)(2,1)S(1)} %slice.248), channel_id=1, source_target_pairs={{0,2},{1,3},{2,0},{3,1},{4,6},{5,7},{6,4},{7,5},{8,10},{9,11},{10,... | collective-permute-start | bytes 1474568 | tf_op jit(solution)/shard_map/ppermute | solution.py:150
  82.2 10.7 %collective-permute-done.3 = bf16[96,2560]{1,0:T(8,128)(2,1)} collective-permute-done((bf16[96,2560]{1,0:T(8,128)(2,1)S(1)}, bf16[96,2560]{1,0:T(8,128)(2,1)}, u32[]{:S(2)}, u32[]{:S(2)}) %collective-permute-start.3) | collective-permute-done | bytes 491552 | tf_op jit(solution)/shard_map/ppermute | solution.py:150
  92.9 7.7 %all-to-all-done.1.mine_ref.far_mine_ref = bf16[4,320,688]{2,1,0:T(8,128)(2,1)S(1)} async-done(((bf16[4,320,688]{2,1,0:T(8,128)(2,1)}), bf16[4,320,688]{2,1,0:T(8,128)(2,1)S(1)}, u32[]{:S(2)}, u32[]{:S(2)}) %all-to-all-start.1) | async-done | bytes 1761312 | tf_op jit(solution)/shard_map/all_to_all | solution.py:23
  100.6 5.2 %collective-permute-start.4 = (bf16[4,320,688]{2,1,0:T(8,128)(2,1)S(1)}, bf16[4,320,688]{2,1,0:T(8,128)(2,1)S(1)}, u32[]{:S(2)}, u32[]{:S(2)}) collective-permute-start(bf16[4,320,688]{2,1,0:T(8,128)(2,1)S(1)} %all-to-all-done.1.mine_ref.far_mine_ref), channel_id=1, source_target_pairs={{0,1},{1,0},{2,3},{3,2},{4,5},{5,4},{6,7},{7,6},{8,9},{9,8},{10,11... | collective-permute-start | bytes 5283848 | tf_op jit(solution)/shard_map/ppermute | solution.py:33
  105.8 1.1 constant_dynamic-update-slice_fusion.1
  106.9 1.6 fusion.64
  108.5 1.1 constant_dynamic-update-slice_fusion
  109.6 0.6 fusion.9
  110.2 0.6 fusion.7
  110.8 3.1 %collective-permute-start.5 = (bf16[192,576]{1,0:T(8,128)(2,1)S(1)}, bf16[192,576]{1,0:T(8,128)(2,1)S(1)}, u32[]{:S(2)}, u32[]{:S(2)}) collective-permute-start(bf16[192,576]{1,0:T(8,128)(2,1)S(1)} %fusion.6), channel_id=1, source_target_pairs={{0,2},{1,3},{2,0},{3,1},{4,6},{5,7},{6,4},{7,5},{8,10},{9,11},{10,... | collective-permute-start | bytes 663560 | tf_op jit(solution)/shard_map/ppermute | solution.py:161
  113.9 0.6 fusion.65
  114.5 7.3 %collective-permute-done.5 = bf16[192,576]{1,0:T(8,128)(2,1)S(1)} collective-permute-done((bf16[192,576]{1,0:T(8,128)(2,1)S(1)}, bf16[192,576]{1,0:T(8,128)(2,1)S(1)}, u32[]{:S(2)}, u32[]{:S(2)}) %collective-permute-start.5) | collective-permute-done | bytes 221216 | tf_op jit(solution)/shard_map/ppermute | solution.py:161
  122.0 18.4 %all_to_all.25 = bf16[8,96,576]{2,1,0:T(8,128)(2,1)S(1)} all-to-all(bf16[8,96,576]{2,1,0:T(8,128)(2,1)S(1)} %broadcast_in_dim.70), channel_id=1, replica_groups={{0,2,4,6,8,10,12,14},{1,3,5,7,9,11,13,15},{16,18,20,22,24,26,28,30},{17..., dimensions={0} | all-to-all | bytes 1769472 | tf_op jit(solution)/shard_map/all_to_all | solution.py:23
  140.5 4.1 %collective-permute-start.6 = (bf16[8,96,576]{2,1,0:T(8,128)(2,1)S(1)}, bf16[8,96,576]{2,1,0:T(8,128)(2,1)S(1)}, u32[]{:S(2)}, u32[]{:S(2)}) collective-permute-start(bf16[8,96,576]{2,1,0:T(8,128)(2,1)S(1)} %all_to_all.25), channel_id=1, source_target_pairs={{0,1},{1,0},{2,3},{3,2},{4,5},{5,4},{6,7},{7,6},{8,9},{9,8},{10,11... | collective-permute-start | bytes 2654216 | tf_op jit(solution)/shard_map/ppermute | solution.py:33
  144.5 2.2 collective-permute-done.6
  146.7 0.5 fusion.66
  147.3 0.6 fusion
  148.1 1.0 reshape.79
  149.1 11.5 %all-to-all-start.3 = ((bf16[32,18,320]{2,1,0:T(8,128)(2,1)}), bf16[32,18,320]{2,1,0:T(8,128)(2,1)S(1)}, u32[]{:S(2)}, u32[]{:S(2)}) async-start(bf16[32,18,320]{2,1,0:T(8,128)(2,1)} %reshape.79), calls=%async_computation.3 | async-start | bytes 1179648 | tf_op jit(solution)/shard_map/all_to_all | solution.py:23
  160.6 6.4 %shard_map.140 = bf16[4,4,48,320]{3,2,1,0:T(8,128)(2,1)} custom-call(s32[1]{0:T(128)} %bitcast.26.rank_ref, bf16[4,320,688]{2,1,0:T(8,128)(2,1)} %copy-done.1, bf16[4,320,688]{2,1,0:T(8,128)(2,1)} %copy-done.1, bf16[4,320,688]{2,1,0:T(8,128)(2,1)} %copy-done.2, bf16[4,320,688]{2,1,0:T(8,128)(2,1)} %copy-done.2, bf16[16,2,160,576]{3,2,1,0:T(8,128)(2,1)} %bitcast.92), custom_call_target="tpu_custom_call" | custom-call | flops 1000 | bytes 1000 | tf_op jit(solution)/shard_map/pallas_call | solution.py:70
  167.1 1.1 slice_bitcast_fusion.2
  168.2 3.0 %collective-permute-start.9 = (bf16[4,48,320]{2,1,0:T(8,128)(2,1)S(1)}, bf16[4,48,320]{2,1,0:T(8,128)(2,1)S(1)}, u32[]{:S(2)}, u32[]{:S(2)}) collective-permute-start(bf16[4,48,320]{2,1,0:T(8,128)(2,1)S(1)} %get-tuple-element.67), channel_id=1, source_target_pairs={{0,3},{1,2},{2,1},{3,0},{4,7},{5,6},{6,5},{7,4},{8,11},{9,10},{10,... | collective-permute-start | bytes 368648 | tf_op jit(solution)/shard_map/ppermute | solution.py:177
  171.2 4.3 %collective-permute-start.8 = (bf16[4,48,320]{2,1,0:T(8,128)(2,1)S(1)}, bf16[4,48,320]{2,1,0:T(8,128)(2,1)S(1)}, u32[]{:S(2)}, u32[]{:S(2)}) collective-permute-start(bf16[4,48,320]{2,1,0:T(8,128)(2,1)S(1)} %get-tuple-element.68), channel_id=1, source_target_pairs={{0,2},{1,3},{2,0},{3,1},{4,6},{5,7},{6,4},{7,5},{8,10},{9,11},{10,... | collective-permute-start | bytes 368648 | tf_op jit(solution)/shard_map/ppermute | solution.py:177
  175.5 2.2 collective-permute-start.7
  177.8 1.1 collective-permute-done.9
  178.9 4.1 %collective-permute-done.8 = bf16[4,48,320]{2,1,0:T(8,128)(2,1)S(1)} collective-permute-done((bf16[4,48,320]{2,1,0:T(8,128)(2,1)S(1)}, bf16[4,48,320]{2,1,0:T(8,128)(2,1)S(1)}, u32[]{:S(2)}, u32[]{:S(2)}) %collective-permute-start.8) | collective-permute-done | bytes 122912 | tf_op jit(solution)/shard_map/ppermute | solution.py:177
  183.0 1.0 fusion.16
  184.0 2.6 %collective-permute-start.12 = (bf16[48,320]{1,0:T(8,128)(2,1)S(1)}, bf16[48,320]{1,0:T(8,128)(2,1)S(1)}, u32[]{:S(2)}, u32[]{:S(2)}) collective-permute-start(bf16[48,320]{1,0:T(8,128)(2,1)S(1)} %get-tuple-element.70), channel_id=1, source_target_pairs={{0,12},{1,13},{2,14},{3,15},{4,8},{5,9},{6,10},{7,11},{8,4},{9,5},... | collective-permute-start | bytes 92168 | tf_op jit(solution)/shard_map/ppermute | solution.py:177
  186.7 3.1 %collective-permute-start.11 = (bf16[48,320]{1,0:T(8,128)(2,1)S(1)}, bf16[48,320]{1,0:T(8,128)(2,1)S(1)}, u32[]{:S(2)}, u32[]{:S(2)}) collective-permute-start(bf16[48,320]{1,0:T(8,128)(2,1)S(1)} %get-tuple-element.71), channel_id=1, source_target_pairs={{0,8},{1,9},{2,10},{3,11},{4,12},{5,13},{6,14},{7,15},{8,0},{9,1},... | collective-permute-start | bytes 92168 | tf_op jit(solution)/shard_map/ppermute | solution.py:177
  189.8 3.3 %collective-permute-start.10 = (bf16[48,320]{1,0:T(8,128)(2,1)S(1)}, bf16[48,320]{1,0:T(8,128)(2,1)S(1)}, u32[]{:S(2)}, u32[]{:S(2)}) collective-permute-start(bf16[48,320]{1,0:T(8,128)(2,1)S(1)} %get-tuple-element.69), channel_id=1, source_target_pairs={{0,4},{1,5},{2,6},{3,7},{4,0},{5,1},{6,2},{7,3},{8,12},{9,13},{10,... | collective-permute-start | bytes 92168 | tf_op jit(solution)/shard_map/ppermute | solution.py:177
  193.2 1.3 collective-permute-done.10
  195.3 18.3 %all_to_all.26 = bf16[16,48,320]{2,1,0:T(8,128)(2,1)S(1)} all-to-all(bf16[16,48,320]{2,1,0:T(8,128)(2,1)S(1)} %broadcast_in_dim.76), channel_id=1, replica_groups=mesh['expert'=32,'tensor'=16] {'tensor'}, dimensions={0} | all-to-all | bytes 983040 | tf_op jit(solution)/shard_map/all_to_all | solution.py:23
  214.1 1.3 reshape.84
  215.7 2.4 %convolution_convert_fusion.2 = bf16[48,132]{1,0:T(8,128)(2,1)} fusion(bf16[132,5120]{1,0:T(8,128)(2,1)S(1)} %copy-done, f32[48,5120]{1,0:T(8,128)} %reshape.84, f32[5120]{0:T(1024)S(1)} %copy-done.23, f32[48]{0:T(128)S(1)} %add_rsqrt_fusion), kind=kOutput, calls=%fused_computation.40 | convolution fusion | flops 65624256 | bytes 2368064 | tf_op jit(solution)/shard_map/dot_general | solution.py:17
  (86 shorter events, 2.8 us)
Async XLA Ops:
  7.2 208.5 %copy-start = (bf16[132,5120]{1,0:T(8,128)(2,1)S(1)}, bf16[132,5120]{1,0:T(8,128)(2,1)}, u32[]{:S(2)}) copy-start(bf16[132,5120]{1,0:T(8,128)(2,1)} %param.23) | copy-start | bytes 4055044
  7.2 29.0 %copy-start.16 = (bf16[192,160]{0,1:T(8,128)(2,1)S(1)}, bf16[192,160]{0,1:T(8,128)(2,1)}, u32[]{:S(2)}) copy-start(bf16[192,160]{0,1:T(8,128)(2,1)} %param.21) | copy-start | bytes 184324
  7.2 28.9 %copy-start.18 = (bf16[160,192]{1,0:T(8,128)(2,1)S(1)}, bf16[160,192]{1,0:T(8,128)(2,1)}, u32[]{:S(2)}) copy-start(bf16[160,192]{1,0:T(8,128)(2,1)} %param.20) | copy-start | bytes 184324
  7.2 57.0 %collective-permute-start = (bf16[48,320]{1,0:T(8,128)(2,1)}, bf16[48,320]{1,0:T(8,128)(2,1)}, u32[]{:S(2)}, u32[]{:S(2)}) collective-permute-start(bf16[48,320]{1,0:T(8,128)(2,1)} %param.13), channel_id=1, source_target_pairs={{0,2},{1,3},{2,0},{3,1},{4,6},{5,7},{6,4},{7,5},{8,10},{9,11},{10,... | collective-permute-start | bytes 92168 | tf_op jit(solution)/shard_map/ppermute | solution.py:144
  14.7 26.2 %copy-start.3 = (bf16[1,96,5120]{2,1,0:T(8,128)(2,1)S(1)}, bf16[1,96,5120]{2,1,0:T(8,128)(2,1)}, u32[]{:S(2)}) copy-start(bf16[1,96,5120]{2,1,0:T(8,128)(2,1)} %param.16) | copy-start | bytes 2949124
  14.7 26.2 %copy-start.4 = (bf16[1,96,5120]{2,1,0:T(8,128)(2,1)S(1)}, bf16[1,96,5120]{2,1,0:T(8,128)(2,1)}, u32[]{:S(2)}) copy-start(bf16[1,96,5120]{2,1,0:T(8,128)(2,1)} %param.17) | copy-start | bytes 2949124
  20.7 49.1 %all-to-all-start = ((bf16[32,18,320]{2,1,0:T(8,128)(2,1)}), bf16[32,18,320]{2,1,0:T(8,128)(2,1)}, u32[]{:S(2)}, u32[]{:S(2)}) async-start(bf16[32,18,320]{2,1,0:T(8,128)(2,1)} %reshape.73), calls=%async_computation | async-start | bytes 1179648 | tf_op jit(solution)/shard_map/all_to_all | solution.py:23
  36.1 124.5 %all-gather.3.cloned.1.call-start = ((), (), s32[]{:S(2)}) async-start(), calls=%async_computation.5 | async-start | bytes 6963200 | tf_op jit(solution)/shard_map/all_gather | solution.py:151
  37.8 24.5 %collective-permute-start.1 = (bf16[160,576]{1,0:T(8,128)(2,1)}, bf16[160,576]{1,0:T(8,128)(2,1)}, u32[]{:S(2)}, u32[]{:S(2)}) collective-permute-start(bf16[160,576]{1,0:T(8,128)(2,1)} %pad_maximum_fusion.1), channel_id=1, source_target_pairs={{0,256},{16,272},{32,288},{48,304},{64,320},{80,336},{96,352},{112... | collective-permute-start | bytes 552968 | tf_op jit(solution)/shard_map/ppermute | solution.py:142
  43.4 2.8 %copy-start.12 = (bf16[192,320]{1,0:T(8,128)(2,1)S(1)}, bf16[192,320]{1,0:T(8,128)(2,1)}, u32[]{:S(2)}) copy-start(bf16[192,320]{1,0:T(8,128)(2,1)} %get-tuple-element.33) | copy-start | bytes 368644
  43.4 2.8 %copy-start.13 = (bf16[192,320]{1,0:T(8,128)(2,1)S(1)}, bf16[192,320]{1,0:T(8,128)(2,1)}, u32[]{:S(2)}) copy-start(bf16[192,320]{1,0:T(8,128)(2,1)} %get-tuple-element.34) | copy-start | bytes 368644
  43.4 2.8 %copy-start.14 = (bf16[192,320]{1,0:T(8,128)(2,1)S(1)}, bf16[192,320]{1,0:T(8,128)(2,1)}, u32[]{:S(2)}) copy-start(bf16[192,320]{1,0:T(8,128)(2,1)} %get-tuple-element.35) | copy-start | bytes 368644
  43.4 4.8 %copy-start.9 = (bf16[192,320]{1,0:T(8,128)(2,1)S(1)}, bf16[192,320]{1,0:T(8,128)(2,1)}, u32[]{:S(2)}) copy-start(bf16[192,320]{1,0:T(8,128)(2,1)} %get-tuple-element.37) | copy-start | bytes 368644
  43.4 4.8 %copy-start.10 = (bf16[192,320]{1,0:T(8,128)(2,1)S(1)}, bf16[192,320]{1,0:T(8,128)(2,1)}, u32[]{:S(2)}) copy-start(bf16[192,320]{1,0:T(8,128)(2,1)} %get-tuple-element.38) | copy-start | bytes 368644
  43.4 4.8 %copy-start.11 = (bf16[192,320]{1,0:T(8,128)(2,1)S(1)}, bf16[192,320]{1,0:T(8,128)(2,1)}, u32[]{:S(2)}) copy-start(bf16[192,320]{1,0:T(8,128)(2,1)} %get-tuple-element.39) | copy-start | bytes 368644
  51.6 4.5 %copy-start.8 = (bf16[1,1536,320]{1,2,0:T(8,128)(2,1)S(1)}, bf16[1,1536,320]{1,2,0:T(8,128)(2,1)}, u32[]{:S(2)}) copy-start(bf16[1,1536,320]{1,2,0:T(8,128)(2,1)} %param.18) | copy-start | bytes 2949124
  52.5 17.3 %collective-permute-start.2 = (bf16[96,2560]{1,0:T(8,128)(2,1)}, bf16[96,2560]{1,0:T(8,128)(2,1)}, u32[]{:S(2)}, u32[]{:S(2)}) collective-permute-start(bf16[96,2560]{1,0:T(8,128)(2,1)} %fusion.5), channel_id=1, source_target_pairs={{0,2},{1,3},{2,0},{3,1},{4,6},{5,7},{6,4},{7,5},{8,10},{9,11},{10,... | collective-permute-start | bytes 1474568 | tf_op jit(solution)/shard_map/ppermute | solution.py:146
  60.1 2.0 copy-start.17
  61.1 1.0 copy-start.19
  61.1 1.0 copy-start.20
  61.1 10.1 %copy-start.15 = (bf16[48,320]{1,0:T(8,128)(2,1)S(1)}, bf16[48,320]{1,0:T(8,128)(2,1)}, u32[]{:S(2)}) copy-start(bf16[48,320]{1,0:T(8,128)(2,1)} %param.13) | copy-start | bytes 92164
  73.9 26.7 %all-to-all-start.1 = ((bf16[4,320,688]{2,1,0:T(8,128)(2,1)}), bf16[4,320,688]{2,1,0:T(8,128)(2,1)S(1)}, u32[]{:S(2)}, u32[]{:S(2)}) async-start(bf16[4,320,688]{2,1,0:T(8,128)(2,1)} %broadcast_in_dim.69), calls=%async_computation.1 | async-start | bytes 3932160 | tf_op jit(solution)/shard_map/all_to_all | solution.py:23
  79.1 13.8 %collective-permute-start.3 = (bf16[96,2560]{1,0:T(8,128)(2,1)S(1)}, bf16[96,2560]{1,0:T(8,128)(2,1)}, u32[]{:S(2)}, u32[]{:S(2)}) collective-permute-start(bf16[96,2560]{1,0:T(8,128)(2,1)S(1)} %slice.248), channel_id=1, source_target_pairs={{0,2},{1,3},{2,0},{3,1},{4,6},{5,7},{6,4},{7,5},{8,10},{9,11},{10,... | collective-permute-start | bytes 1474568 | tf_op jit(solution)/shard_map/ppermute | solution.py:150
  100.6 9.0 %copy-start.1 = (bf16[4,320,688]{2,1,0:T(8,128)(2,1)}, bf16[4,320,688]{2,1,0:T(8,128)(2,1)S(1)}, u32[]{:S(2)}) copy-start(bf16[4,320,688]{2,1,0:T(8,128)(2,1)S(1)} %all-to-all-done.1.mine_ref.far_mine_ref) | copy-start | bytes 5283844
  100.6 9.5 %collective-permute-start.4 = (bf16[4,320,688]{2,1,0:T(8,128)(2,1)S(1)}, bf16[4,320,688]{2,1,0:T(8,128)(2,1)S(1)}, u32[]{:S(2)}, u32[]{:S(2)}) collective-permute-start(bf16[4,320,688]{2,1,0:T(8,128)(2,1)S(1)} %all-to-all-done.1.mine_ref.far_mine_ref), channel_id=1, source_target_pairs={{0,1},{1,0},{2,3},{3,2},{4,5},{5,4},{6,7},{7,6},{8,9},{9,8},{10,11... | collective-permute-start | bytes 5283848 | tf_op jit(solution)/shard_map/ppermute | solution.py:33
  110.1 3.8 %copy-start.2 = (bf16[4,320,688]{2,1,0:T(8,128)(2,1)}, bf16[4,320,688]{2,1,0:T(8,128)(2,1)S(1)}, u32[]{:S(2)}) copy-start(bf16[4,320,688]{2,1,0:T(8,128)(2,1)S(1)} %collective-permute-done.4.theirs_ref.far_theirs_ref) | copy-start | bytes 5283844
  110.1 3.8 %copy-start.5 = (bf16[192,1280]{1,0:T(8,128)(2,1)S(1)}, bf16[192,1280]{1,0:T(8,128)(2,1)}, u32[]{:S(2)}) copy-start(bf16[192,1280]{1,0:T(8,128)(2,1)} %get-tuple-element.20) | copy-start | bytes 1474564
  110.8 11.0 %collective-permute-start.5 = (bf16[192,576]{1,0:T(8,128)(2,1)S(1)}, bf16[192,576]{1,0:T(8,128)(2,1)S(1)}, u32[]{:S(2)}, u32[]{:S(2)}) collective-permute-start(bf16[192,576]{1,0:T(8,128)(2,1)S(1)} %fusion.6), channel_id=1, source_target_pairs={{0,2},{1,3},{2,0},{3,1},{4,6},{5,7},{6,4},{7,5},{8,10},{9,11},{10,... | collective-permute-start | bytes 663560 | tf_op jit(solution)/shard_map/ppermute | solution.py:161
  121.8 24.9 %copy-start.7 = (bf16[768,320]{0,1:T(8,128)(2,1)S(1)}, bf16[768,320]{0,1:T(8,128)(2,1)}, u32[]{:S(2)}) copy-start(bf16[768,320]{0,1:T(8,128)(2,1)} %get-tuple-element.24) | copy-start | bytes 1474564
  122.0 25.3 %copy-start.6 = (bf16[768,320]{0,1:T(8,128)(2,1)S(1)}, bf16[768,320]{0,1:T(8,128)(2,1)}, u32[]{:S(2)}) copy-start(bf16[768,320]{0,1:T(8,128)(2,1)} %get-tuple-element.23) | copy-start | bytes 1474564
  140.5 6.2 %collective-permute-start.6 = (bf16[8,96,576]{2,1,0:T(8,128)(2,1)S(1)}, bf16[8,96,576]{2,1,0:T(8,128)(2,1)S(1)}, u32[]{:S(2)}, u32[]{:S(2)}) collective-permute-start(bf16[8,96,576]{2,1,0:T(8,128)(2,1)S(1)} %all_to_all.25), channel_id=1, source_target_pairs={{0,1},{1,0},{2,3},{3,2},{4,5},{5,4},{6,7},{7,6},{8,9},{9,8},{10,11... | collective-permute-start | bytes 2654216 | tf_op jit(solution)/shard_map/ppermute | solution.py:33
  149.1 45.4 %all-to-all-start.3 = ((bf16[32,18,320]{2,1,0:T(8,128)(2,1)}), bf16[32,18,320]{2,1,0:T(8,128)(2,1)S(1)}, u32[]{:S(2)}, u32[]{:S(2)}) async-start(bf16[32,18,320]{2,1,0:T(8,128)(2,1)} %reshape.79), calls=%async_computation.3 | async-start | bytes 1179648 | tf_op jit(solution)/shard_map/all_to_all | solution.py:23
  160.6 17.1 %copy-start.24 = (s32[48,6]{0,1:T(8,128)S(1)}, s32[48,6]{0,1:T(8,128)}, u32[]{:S(2)}) copy-start(s32[48,6]{0,1:T(8,128)} %param.14) | copy-start | bytes 3460
  160.6 17.1 %copy-start.25 = (f32[48,6]{0,1:T(8,128)S(1)}, f32[48,6]{0,1:T(8,128)}, u32[]{:S(2)}) copy-start(f32[48,6]{0,1:T(8,128)} %param.15) | copy-start | bytes 3460
  167.1 27.7 %copy-start.22 = (bf16[32,576]{1,0:T(8,128)(2,1)S(1)}, bf16[32,576]{1,0:T(8,128)(2,1)}, u32[]{:S(2)}) copy-start(bf16[32,576]{1,0:T(8,128)(2,1)} %constant.47.clone) | copy-start | bytes 110596
  168.2 10.8 %collective-permute-start.9 = (bf16[4,48,320]{2,1,0:T(8,128)(2,1)S(1)}, bf16[4,48,320]{2,1,0:T(8,128)(2,1)S(1)}, u32[]{:S(2)}, u32[]{:S(2)}) collective-permute-start(bf16[4,48,320]{2,1,0:T(8,128)(2,1)S(1)} %get-tuple-element.67), channel_id=1, source_target_pairs={{0,3},{1,2},{2,1},{3,0},{4,7},{5,6},{6,5},{7,4},{8,11},{9,10},{10,... | collective-permute-start | bytes 368648 | tf_op jit(solution)/shard_map/ppermute | solution.py:177
  171.2 11.9 %collective-permute-start.8 = (bf16[4,48,320]{2,1,0:T(8,128)(2,1)S(1)}, bf16[4,48,320]{2,1,0:T(8,128)(2,1)S(1)}, u32[]{:S(2)}, u32[]{:S(2)}) collective-permute-start(bf16[4,48,320]{2,1,0:T(8,128)(2,1)S(1)} %get-tuple-element.68), channel_id=1, source_target_pairs={{0,2},{1,3},{2,0},{3,1},{4,6},{5,7},{6,4},{7,5},{8,10},{9,11},{10,... | collective-permute-start | bytes 368648 | tf_op jit(solution)/shard_map/ppermute | solution.py:177
  175.5 7.5 %collective-permute-start.7 = (bf16[4,48,320]{2,1,0:T(8,128)(2,1)S(1)}, bf16[4,48,320]{2,1,0:T(8,128)(2,1)S(1)}, u32[]{:S(2)}, u32[]{:S(2)}) collective-permute-start(bf16[4,48,320]{2,1,0:T(8,128)(2,1)S(1)} %get-tuple-element.66), channel_id=1, source_target_pairs={{0,1},{1,0},{2,3},{3,2},{4,5},{5,4},{6,7},{7,6},{8,9},{9,8},{10,11... | collective-permute-start | bytes 368648 | tf_op jit(solution)/shard_map/ppermute | solution.py:177
  184.0 9.0 %collective-permute-start.12 = (bf16[48,320]{1,0:T(8,128)(2,1)S(1)}, bf16[48,320]{1,0:T(8,128)(2,1)S(1)}, u32[]{:S(2)}, u32[]{:S(2)}) collective-permute-start(bf16[48,320]{1,0:T(8,128)(2,1)S(1)} %get-tuple-element.70), channel_id=1, source_target_pairs={{0,12},{1,13},{2,14},{3,15},{4,8},{5,9},{6,10},{7,11},{8,4},{9,5},... | collective-permute-start | bytes 92168 | tf_op jit(solution)/shard_map/ppermute | solution.py:177
  186.7 6.5 %collective-permute-start.11 = (bf16[48,320]{1,0:T(8,128)(2,1)S(1)}, bf16[48,320]{1,0:T(8,128)(2,1)S(1)}, u32[]{:S(2)}, u32[]{:S(2)}) collective-permute-start(bf16[48,320]{1,0:T(8,128)(2,1)S(1)} %get-tuple-element.71), channel_id=1, source_target_pairs={{0,8},{1,9},{2,10},{3,11},{4,12},{5,13},{6,14},{7,15},{8,0},{9,1},... | collective-permute-start | bytes 92168 | tf_op jit(solution)/shard_map/ppermute | solution.py:177
  189.8 4.7 %collective-permute-start.10 = (bf16[48,320]{1,0:T(8,128)(2,1)S(1)}, bf16[48,320]{1,0:T(8,128)(2,1)S(1)}, u32[]{:S(2)}, u32[]{:S(2)}) collective-permute-start(bf16[48,320]{1,0:T(8,128)(2,1)S(1)} %get-tuple-element.69), channel_id=1, source_target_pairs={{0,4},{1,5},{2,6},{3,7},{4,0},{5,1},{6,2},{7,3},{8,12},{9,13},{10,... | collective-permute-start | bytes 92168 | tf_op jit(solution)/shard_map/ppermute | solution.py:177
  195.3 18.8 %copy-start.21 = (bf16[48,320]{1,0:T(8,128)(2,1)}, bf16[48,320]{1,0:T(8,128)(2,1)S(1)}, u32[]{:S(2)}) copy-start(bf16[48,320]{1,0:T(8,128)(2,1)S(1)} %fusion.35) | copy-start | bytes 92164
  214.1 1.6 copy-start.23
Sparse Core Ops, SparseCore 0:
  69.9 87.1 all-gather.2

commit v8 on v7

--- a/solution.py
+++ b/solution.py
@@ -83,6 +83,34 @@
         compiler_params=pltpu.CompilerParams(vmem_limit_bytes=56 * 2**20),
         cost_estimate=pl.CostEstimate(flops=1000, bytes_accessed=1000, transcendentals=0),
     )(rank.reshape(1), mine, mine, theirs, theirs, table)
+
+
+def norm_kernel(stream_ref, gain_ref, weight_ref, out_ref):
+    blocks, _, width = stream_ref.shape
+    squares = jnp.zeros(stream_ref.shape[1:], jnp.float32)
+    for k in range(blocks):
+        value = stream_ref[k].astype(jnp.float32)
+        squares = squares + value * value
+    mean = jnp.sum(squares, axis=1, keepdims=True) * (1.0 / (blocks * width))
+    scale = lax.rsqrt(mean + 1e-06)
+    total = jnp.zeros(out_ref.shape, jnp.float32)
+    for k in range(0, blocks, 2):
+        pair = [stream_ref[k + j].astype(jnp.float32) * scale for j in range(2)]
+        pair = [(pair[j] * gain_ref[k + j : k + j + 1]).astype(jnp.bfloat16) for j in range(2)]
+        total = total + dot(jnp.concatenate(pair, axis=1), weight_ref[:, k * width : (k + 2) * width], 1, 1)
+    out_ref[...] = total.astype(out_ref.dtype)
+
+
+def normed_product(copies, gain, weight):
+    blocks, tok, width = copies.shape
+    whole = pl.BlockSpec(memory_space=pltpu.VMEM)
+    return pl.pallas_call(
+        norm_kernel,
+        out_shape=jax.ShapeDtypeStruct((tok, weight.shape[0]), jnp.bfloat16),
+        in_specs=[whole, whole, whole],
+        out_specs=whole,
+        compiler_params=pltpu.CompilerParams(vmem_limit_bytes=24 * 2**20),
+    )(copies, gain.reshape(blocks, width), weight)
 
 
 def per_device(
@@ -141,19 +169,21 @@
     own = jnp.concatenate([shared_gate, shared_up, shared_down.T], axis=1)
     other = lax.ppermute(own, "expert", [(i, (i + ROWS) % (2 * ROWS)) for i in range(2 * ROWS)])
     pair = jnp.where(column == 0, jnp.stack([own, other]), jnp.stack([other, own]))
-    beside = lax.ppermute(tokens, "tensor", [(i, i ^ 2) for i in range(2 * CHIPS)])
     across = [(i, i ^ 2) for i in range(2 * CHIPS)]
-    far_gate = lax.ppermute(give[:hid], "tensor", across)
-    arrived, beside, pair, in_mine, in_theirs, give, far_gate, out_mine, out_theirs = lax.optimization_barrier(
-        (arrived, beside, pair, in_mine, in_theirs, give, far_gate, out_mine, out_theirs)
-    )
-    far_up = lax.ppermute(give[hid:], "tensor", across)
+    give, late = lax.optimization_barrier((give, tokens))
+    cut = give.shape[0] // 3
+    far_first = lax.ppermute(give[:cut], "tensor", across)
+    beside = lax.ppermute(late, "tensor", across)
+    arrived, beside, pair, in_mine, in_theirs, give, far_first, out_mine, out_theirs = lax.optimization_barrier(
+        (arrived, beside, pair, in_mine, in_theirs, give, far_first, out_mine, out_theirs)
+    )
+    far_rest = lax.ppermute(give[cut:], "tensor", across)
     gathered = lax.all_gather(pair, "expert", axis=0, axis_index_groups=LANES)
 
     blank = jnp.zeros((16, width), bf16)
     rows = jnp.concatenate([arrived.reshape(slots, width), tokens, blank, beside], axis=0)
-    mine, theirs, far_up = gather_halves(rows.T, RINGS, far_up)
-    far = jnp.concatenate([far_gate, far_up], axis=0)
+    mine, theirs, far_rest = gather_halves(rows.T, RINGS, far_rest)
+    far = jnp.concatenate([far_first, far_rest], axis=0)
     total = rows.shape[0]
     left, right = mine.reshape(-1, total), theirs.reshape(-1, total)
     middle = left.shape[0]
@@ -189,10 +219,7 @@
 
     stream = (tokens.astype(f32) + shared + routed).astype(bf16)
     copies = exchange(jnp.broadcast_to(stream[None], (2 * CHIPS,) + stream.shape), "tensor")
-    values = jnp.swapaxes(copies, 0, 1).reshape(tok, -1).astype(f32)
-    scale = lax.rsqrt(jnp.mean(values * values, axis=1, keepdims=True) + 1e-06)
-    normed = (values * scale * norm_gain[None, :]).astype(bf16)
-    projected = dot(normed, proj_weight, 1, 1).astype(bf16)
+    projected = normed_product(copies, norm_gain, proj_weight)
     return (stream, projected)
 
 

time: 227 us -> 216 us (0.952)
  blocking collectives: 36.7 us -> 19.5 us
  waiting for transfers between devices: 40.1 us -> 52.8 us
  starting transfers between devices: 77.4 us -> 85.9 us
  local copies, waits for them, and re-layouts: 24.5 us -> 16.8 us
  other arithmetic: 14.6 us -> 10.3 us
  matrix products: 10.4 us -> 7.09 us
    all_to_all x2 -> x1, blocking collectives: 36.7 us -> 19.5 us  [exchange(): lax.all_to_all(parts, axis, split_axis=0, concat_axis=0, tiled=True, axis...]
    all_to_all x3 -> x4, waiting for transfers between devices: 7.68 us -> 18.8 us  [exchange(): lax.all_to_all(parts, axis, split_axis=0, concat_axis=0, tiled=True, axis...]
    all_to_all x3 -> x4, starting transfers between devices: 31 us -> 37.1 us  [exchange(): lax.all_to_all(parts, axis, split_axis=0, concat_axis=0, tiled=True, axis...]
    dot_general x9 -> x8, matrix products: 9.26 us -> 5.91 us  [dot(): lax.dot_general(left, right, (((over_left,), (over_right,)), ((), ())), p...]
    concatenate x4, local copies, waits for them, and re-layouts: 5.78 us -> 3.49 us  [per_device(): jnp.concatenate([gate_up[:, k * width:(k + 1) * width] for k in range(low...]
  transfers between devices with their start and end apart: 17 -> 18, of which waited for: 9 -> 11; matrix products, arithmetic and copies ran while one was open for 20% -> 13% of each run, Pallas kernels for 3% -> 3%
where the time goes in v8:
time: 216 us; the launch traced here: 215 us
  starting transfers between devices  85.9 us (40%)
  waiting for transfers between devices  52.8 us (24%)
  blocking collectives  19.5 us (9%)
  local copies, waits for them, and re-layouts  16.8 us (8%)
  between operations  14.7 us (7%)
  other arithmetic  10.3 us (5%)
  Pallas kernels  7.84 us (4%)
  matrix products  7.09 us (3%)
    all_to_all x4, starting transfers between devices, exchange(): lax.all_to_all(parts, axis, split_axis=0, concat_axis=0, tiled=True, axis...  37.1 us
    ppermute x6, starting transfers between devices, summed(): total = total + lax.ppermute(parts[k], 'tensor', perm).astype(f32)  20.6 us
    all_to_all x1, blocking collectives, exchange(): lax.all_to_all(parts, axis, split_axis=0, concat_axis=0, tiled=True, axis...  19.5 us
    all_to_all x4, waiting for transfers between devices, exchange(): lax.all_to_all(parts, axis, split_axis=0, concat_axis=0, tiled=True, axis...  18.8 us
    ppermute x1, waiting for transfers between devices, per_device(): far_rest = lax.ppermute(give[cut:], 'tensor', across)  13.4 us
    ppermute x2, starting transfers between devices, gather_halves(): lax.ppermute(mine, 'tensor', [(i, i ^ 1) for i in range(2 * CHIPS)])  8.88 us
    ppermute x6, waiting for transfers between devices, summed(): total = total + lax.ppermute(parts[k], 'tensor', perm).astype(f32)  8.43 us
    pallas_call x1, Pallas kernels, shared_partial(): pl.pallas_call(shared_kernel, out_shape=out, grid=(1,), in_specs=[pl.Bloc...  6.41 us
  transfers between devices with their start and end apart: 18, of which 11 were waited for; matrix products, arithmetic and copies ran while one was open for 13% of the time, Pallas kernels for 3%

profile of v8, /device:TPU:1, one launch (start us, length us, event | category | flops | bytes accessed | tf_op | source)
XLA Modules:
  0.0 214.9 jit_solution(2798254712319590834)
XLA Ops:
  7.2 0.8 fusion.29
  8.0 1.2 convolution_compare_fusion
  9.2 1.1 convolution_convert_fusion
  10.6 1.0 reshape.64
  11.6 17.0 %all-to-all-start = ((bf16[32,18,320]{2,1,0:T(8,128)(2,1)}), bf16[32,18,320]{2,1,0:T(8,128)(2,1)S(1)}, u32[]{:S(2)}, u32[]{:S(2)}) async-start(bf16[32,18,320]{2,1,0:T(8,128)(2,1)} %reshape.64), calls=%async_computation | async-start | bytes 1179648 | tf_op jit(solution)/shard_map/all_to_all | solution.py:23
  28.6 1.0 fusion.22
  29.6 1.2 pad_maximum_fusion.2
  30.8 1.4 concatenate.40
  32.1 1.3 concatenate.41
  33.5 0.4 concatenate.38
  33.9 0.4 concatenate.39
  34.3 1.0 select_select_fusion
  35.4 0.7 copy-done.10
  36.1 4.3 %collective-permute-start = (bf16[48,320]{1,0:T(8,128)(2,1)S(1)}, bf16[48,320]{1,0:T(8,128)(2,1)S(1)}, u32[]{:S(2)}, u32[]{:S(2)}) collective-permute-start(bf16[48,320]{1,0:T(8,128)(2,1)S(1)} %copy-done.10), channel_id=1, source_target_pairs={{0,2},{1,3},{2,0},{3,1},{4,6},{5,7},{6,4},{7,5},{8,10},{9,11},{10,... | collective-permute-start | bytes 92168 | tf_op jit(solution)/shard_map/ppermute | solution.py:176
  40.5 0.8 pad_maximum_fusion.1
  41.3 2.5 %collective-permute-start.1 = (bf16[160,576]{1,0:T(8,128)(2,1)}, bf16[160,576]{1,0:T(8,128)(2,1)}, u32[]{:S(2)}, u32[]{:S(2)}) collective-permute-start(bf16[160,576]{1,0:T(8,128)(2,1)} %pad_maximum_fusion.1), channel_id=1, source_target_pairs={{0,256},{16,272},{32,288},{48,304},{64,320},{80,336},{96,352},{112... | collective-permute-start | bytes 552968 | tf_op jit(solution)/shard_map/ppermute | solution.py:170
  43.8 0.7 slice.215
  44.6 3.6 %collective-permute-start.2 = (bf16[64,2560]{1,0:T(8,128)(2,1)}, bf16[64,2560]{1,0:T(8,128)(2,1)}, u32[]{:S(2)}, u32[]{:S(2)}) collective-permute-start(bf16[64,2560]{1,0:T(8,128)(2,1)} %slice.215), channel_id=1, source_target_pairs={{0,2},{1,3},{2,0},{3,1},{4,6},{5,7},{6,4},{7,5},{8,10},{9,11},{10,... | collective-permute-start | bytes 983048 | tf_op jit(solution)/shard_map/ppermute | solution.py:175
  48.2 1.3 slice_bitcast_fusion.4
  49.6 1.3 concatenate.45
  50.9 1.2 concatenate.44
  52.1 1.0 broadcast_select_fusion
  53.1 1.1 fusion.79
  54.2 1.9 maximum_select_fusion
  56.1 4.0 %collective-permute-done.2 = bf16[64,2560]{1,0:T(8,128)(2,1)} collective-permute-done((bf16[64,2560]{1,0:T(8,128)(2,1)}, bf16[64,2560]{1,0:T(8,128)(2,1)}, u32[]{:S(2)}, u32[]{:S(2)}) %collective-permute-start.2) | collective-permute-done | bytes 327712 | tf_op jit(solution)/shard_map/ppermute | solution.py:175
  60.0 1.6 all-to-all-done
  62.4 1.5 broadcast_in_dim.67
  63.8 4.2 %all-to-all-start.1 = ((bf16[4,320,688]{2,1,0:T(8,128)(2,1)}), bf16[4,320,688]{2,1,0:T(8,128)(2,1)S(1)}, u32[]{:S(2)}, u32[]{:S(2)}) async-start(bf16[4,320,688]{2,1,0:T(8,128)(2,1)} %broadcast_in_dim.67), calls=%async_computation.1 | async-start | bytes 3932160 | tf_op jit(solution)/shard_map/all_to_all | solution.py:23
  68.1 4.4 %collective-permute-start.3 = (bf16[128,2560]{1,0:T(8,128)(2,1)S(1)}, bf16[128,2560]{1,0:T(8,128)(2,1)S(1)}, u32[]{:S(2)}, u32[]{:S(2)}) collective-permute-start(bf16[128,2560]{1,0:T(8,128)(2,1)S(1)} %slice.248), channel_id=1, source_target_pairs={{0,2},{1,3},{2,0},{3,1},{4,6},{5,7},{6,4},{7,5},{8,10},{9,11},{10,... | collective-permute-start | bytes 1966088 | tf_op jit(solution)/shard_map/ppermute | solution.py:180
  72.4 13.4 %collective-permute-done.3 = bf16[128,2560]{1,0:T(8,128)(2,1)S(1)} collective-permute-done((bf16[128,2560]{1,0:T(8,128)(2,1)S(1)}, bf16[128,2560]{1,0:T(8,128)(2,1)S(1)}, u32[]{:S(2)}, u32[]{:S(2)}) %collective-permute-start.3) | collective-permute-done | bytes 655392 | tf_op jit(solution)/shard_map/ppermute | solution.py:180
  85.9 5.3 %all-to-all-done.1.mine_ref.far_mine_ref = bf16[4,320,688]{2,1,0:T(8,128)(2,1)S(1)} async-done(((bf16[4,320,688]{2,1,0:T(8,128)(2,1)}), bf16[4,320,688]{2,1,0:T(8,128)(2,1)S(1)}, u32[]{:S(2)}, u32[]{:S(2)}) %all-to-all-start.1) | async-done | bytes 1761312 | tf_op jit(solution)/shard_map/all_to_all | solution.py:23
  91.2 4.7 %collective-permute-start.4 = (bf16[4,320,688]{2,1,0:T(8,128)(2,1)S(1)}, bf16[4,320,688]{2,1,0:T(8,128)(2,1)S(1)}, u32[]{:S(2)}, u32[]{:S(2)}) collective-permute-start(bf16[4,320,688]{2,1,0:T(8,128)(2,1)S(1)} %all-to-all-done.1.mine_ref.far_mine_ref), channel_id=1, source_target_pairs={{0,1},{1,0},{2,3},{3,2},{4,5},{5,4},{6,7},{7,6},{8,9},{9,8},{10,11... | collective-permute-start | bytes 5283848 | tf_op jit(solution)/shard_map/ppermute | solution.py:33
  95.8 1.0 constant_dynamic-update-slice_fusion.1
  96.8 1.6 fusion.60
  98.5 0.6 fusion.7
  99.0 0.4 collective-permute-done.4.theirs_ref.far_theirs_ref
  99.4 0.6 fusion.5
  100.0 4.4 %collective-permute-start.5 = (bf16[192,576]{1,0:T(8,128)(2,1)S(1)}, bf16[192,576]{1,0:T(8,128)(2,1)S(1)}, u32[]{:S(2)}, u32[]{:S(2)}) collective-permute-start(bf16[192,576]{1,0:T(8,128)(2,1)S(1)} %fusion.4), channel_id=1, source_target_pairs={{0,2},{1,3},{2,0},{3,1},{4,6},{5,7},{6,4},{7,5},{8,10},{9,11},{10,... | collective-permute-start | bytes 663560 | tf_op jit(solution)/shard_map/ppermute | solution.py:191
  104.4 0.6 fusion.61
  105.0 5.6 %collective-permute-done.5 = bf16[192,576]{1,0:T(8,128)(2,1)S(1)} collective-permute-done((bf16[192,576]{1,0:T(8,128)(2,1)S(1)}, bf16[192,576]{1,0:T(8,128)(2,1)S(1)}, u32[]{:S(2)}, u32[]{:S(2)}) %collective-permute-start.5) | collective-permute-done | bytes 221216 | tf_op jit(solution)/shard_map/ppermute | solution.py:191
  110.8 19.5 %all_to_all.25 = bf16[8,96,576]{2,1,0:T(8,128)(2,1)S(1)} all-to-all(bf16[8,96,576]{2,1,0:T(8,128)(2,1)S(1)} %broadcast_in_dim.68), channel_id=1, replica_groups={{0,2,4,6,8,10,12,14},{1,3,5,7,9,11,13,15},{16,18,20,22,24,26,28,30},{17..., dimensions={0} | all-to-all | bytes 1769472 | tf_op jit(solution)/shard_map/all_to_all | solution.py:23
  130.4 4.2 %collective-permute-start.6 = (bf16[8,96,576]{2,1,0:T(8,128)(2,1)S(1)}, bf16[8,96,576]{2,1,0:T(8,128)(2,1)S(1)}, u32[]{:S(2)}, u32[]{:S(2)}) collective-permute-start(bf16[8,96,576]{2,1,0:T(8,128)(2,1)S(1)} %all_to_all.25), channel_id=1, source_target_pairs={{0,1},{1,0},{2,3},{3,2},{4,5},{5,4},{6,7},{7,6},{8,9},{9,8},{10,11... | collective-permute-start | bytes 2654216 | tf_op jit(solution)/shard_map/ppermute | solution.py:33
  134.6 2.2 %collective-permute-done.6 = bf16[8,96,576]{2,1,0:T(8,128)(2,1)S(1)} collective-permute-done((bf16[8,96,576]{2,1,0:T(8,128)(2,1)S(1)}, bf16[8,96,576]{2,1,0:T(8,128)(2,1)S(1)}, u32[]{:S(2)}, u32[]{:S(2)}) %collective-permute-start.6) | collective-permute-done | bytes 884768 | tf_op jit(solution)/shard_map/ppermute | solution.py:33
  136.8 0.6 fusion.62
  137.3 0.6 fusion
  138.2 1.0 reshape.70
  139.1 8.5 %all-to-all-start.3 = ((bf16[32,18,320]{2,1,0:T(8,128)(2,1)}), bf16[32,18,320]{2,1,0:T(8,128)(2,1)S(1)}, u32[]{:S(2)}, u32[]{:S(2)}) async-start(bf16[32,18,320]{2,1,0:T(8,128)(2,1)} %reshape.70), calls=%async_computation.3 | async-start | bytes 1179648 | tf_op jit(solution)/shard_map/all_to_all | solution.py:23
  147.7 6.4 %shard_map.140 = bf16[4,4,48,320]{3,2,1,0:T(8,128)(2,1)} custom-call(s32[1]{0:T(128)} %bitcast.26.rank_ref, bf16[4,320,688]{2,1,0:T(8,128)(2,1)} %copy-done.1, bf16[4,320,688]{2,1,0:T(8,128)(2,1)} %copy-done.1, bf16[4,320,688]{2,1,0:T(8,128)(2,1)} %copy-done.2, bf16[4,320,688]{2,1,0:T(8,128)(2,1)} %copy-done.2, bf16[16,2,160,576]{3,2,1,0:T(8,128)(2,1)} %bitcast.89), custom_call_target="tpu_custom_call" | custom-call | flops 1000 | bytes 1000 | tf_op jit(solution)/shard_map/pallas_call | solution.py:70
  154.1 1.1 slice_bitcast_fusion.2
  155.2 5.8 %collective-permute-start.9 = (bf16[4,48,320]{2,1,0:T(8,128)(2,1)S(1)}, bf16[4,48,320]{2,1,0:T(8,128)(2,1)S(1)}, u32[]{:S(2)}, u32[]{:S(2)}) collective-permute-start(bf16[4,48,320]{2,1,0:T(8,128)(2,1)S(1)} %get-tuple-element.71), channel_id=1, source_target_pairs={{0,3},{1,2},{2,1},{3,0},{4,7},{5,6},{6,5},{7,4},{8,11},{9,10},{10,... | collective-permute-start | bytes 368648 | tf_op jit(solution)/shard_map/ppermute | solution.py:207
  161.1 1.9 collective-permute-start.8
  163.0 2.3 %collective-permute-start.7 = (bf16[4,48,320]{2,1,0:T(8,128)(2,1)S(1)}, bf16[4,48,320]{2,1,0:T(8,128)(2,1)S(1)}, u32[]{:S(2)}, u32[]{:S(2)}) collective-permute-start(bf16[4,48,320]{2,1,0:T(8,128)(2,1)S(1)} %get-tuple-element.70), channel_id=1, source_target_pairs={{0,1},{1,0},{2,3},{3,2},{4,5},{5,4},{6,7},{7,6},{8,9},{9,8},{10,11... | collective-permute-start | bytes 368648 | tf_op jit(solution)/shard_map/ppermute | solution.py:207
  165.3 0.9 collective-permute-done.9
  166.3 4.1 %collective-permute-done.8 = bf16[4,48,320]{2,1,0:T(8,128)(2,1)S(1)} collective-permute-done((bf16[4,48,320]{2,1,0:T(8,128)(2,1)S(1)}, bf16[4,48,320]{2,1,0:T(8,128)(2,1)S(1)}, u32[]{:S(2)}, u32[]{:S(2)}) %collective-permute-start.8) | collective-permute-done | bytes 122912 | tf_op jit(solution)/shard_map/ppermute | solution.py:207
  170.4 1.0 fusion.12
  171.4 4.2 %collective-permute-start.12 = (bf16[48,320]{1,0:T(8,128)(2,1)S(1)}, bf16[48,320]{1,0:T(8,128)(2,1)S(1)}, u32[]{:S(2)}, u32[]{:S(2)}) collective-permute-start(bf16[48,320]{1,0:T(8,128)(2,1)S(1)} %get-tuple-element.74), channel_id=1, source_target_pairs={{0,12},{1,13},{2,14},{3,15},{4,8},{5,9},{6,10},{7,11},{8,4},{9,5},... | collective-permute-start | bytes 92168 | tf_op jit(solution)/shard_map/ppermute | solution.py:207
  175.6 4.5 %collective-permute-start.11 = (bf16[48,320]{1,0:T(8,128)(2,1)S(1)}, bf16[48,320]{1,0:T(8,128)(2,1)S(1)}, u32[]{:S(2)}, u32[]{:S(2)}) collective-permute-start(bf16[48,320]{1,0:T(8,128)(2,1)S(1)} %get-tuple-element.75), channel_id=1, source_target_pairs={{0,8},{1,9},{2,10},{3,11},{4,12},{5,13},{6,14},{7,15},{8,0},{9,1},... | collective-permute-start | bytes 92168 | tf_op jit(solution)/shard_map/ppermute | solution.py:207
  180.1 1.9 collective-permute-start.10
  182.1 3.4 %collective-permute-done.10 = bf16[48,320]{1,0:T(8,128)(2,1)S(1)} collective-permute-done((bf16[48,320]{1,0:T(8,128)(2,1)S(1)}, bf16[48,320]{1,0:T(8,128)(2,1)S(1)}, u32[]{:S(2)}, u32[]{:S(2)}) %collective-permute-start.10) | collective-permute-done | bytes 30752 | tf_op jit(solution)/shard_map/ppermute | solution.py:207
  185.7 0.5 fusion.2
  186.2 0.9 broadcast_in_dim.74
  187.1 7.5 %all-to-all-start.4 = ((bf16[16,48,320]{2,1,0:T(8,128)(2,1)}), bf16[16,48,320]{2,1,0:T(8,128)(2,1)S(1)}, u32[]{:S(2)}, u32[]{:S(2)}) async-start(bf16[16,48,320]{2,1,0:T(8,128)(2,1)} %broadcast_in_dim.74), calls=%async_computation.4 | async-start | bytes 1179648 | tf_op jit(solution)/shard_map/all_to_all | solution.py:23
  194.7 11.9 %all-to-all-done.4.stream_ref = bf16[16,48,320]{2,1,0:T(8,128)(2,1)S(1)} async-done(((bf16[16,48,320]{2,1,0:T(8,128)(2,1)}), bf16[16,48,320]{2,1,0:T(8,128)(2,1)S(1)}, u32[]{:S(2)}, u32[]{:S(2)}) %all-to-all-start.4) | async-done | bytes 491552 | tf_op jit(solution)/shard_map/all_to_all | solution.py:23
  206.6 1.4 shard_map.141
  (69 shorter events, 2.2 us)
Async XLA Ops:
  7.2 21.4 %copy-start.3 = (bf16[1,96,5120]{2,1,0:T(8,128)(2,1)S(1)}, bf16[1,96,5120]{2,1,0:T(8,128)(2,1)}, u32[]{:S(2)}) copy-start(bf16[1,96,5120]{2,1,0:T(8,128)(2,1)} %param.16) | copy-start | bytes 2949124
  7.2 21.4 %copy-start.4 = (bf16[1,96,5120]{2,1,0:T(8,128)(2,1)S(1)}, bf16[1,96,5120]{2,1,0:T(8,128)(2,1)}, u32[]{:S(2)}) copy-start(bf16[1,96,5120]{2,1,0:T(8,128)(2,1)} %param.17) | copy-start | bytes 2949124
  11.6 50.0 %all-to-all-start = ((bf16[32,18,320]{2,1,0:T(8,128)(2,1)}), bf16[32,18,320]{2,1,0:T(8,128)(2,1)S(1)}, u32[]{:S(2)}, u32[]{:S(2)}) async-start(bf16[32,18,320]{2,1,0:T(8,128)(2,1)} %reshape.64), calls=%async_computation | async-start | bytes 1179648 | tf_op jit(solution)/shard_map/all_to_all | solution.py:23
  28.5 119.2 %all-gather.3.cloned.1.call-start = ((), (), s32[]{:S(2)}) async-start(), calls=%async_computation.5 | async-start | bytes 6963200 | tf_op jit(solution)/shard_map/all_gather | solution.py:181
  30.8 2.7 %copy-start.8 = (bf16[192,320]{1,0:T(8,128)(2,1)S(1)}, bf16[192,320]{1,0:T(8,128)(2,1)}, u32[]{:S(2)}) copy-start(bf16[192,320]{1,0:T(8,128)(2,1)} %get-tuple-element.39) | copy-start | bytes 368644
  30.8 2.7 %copy-start.9 = (bf16[192,320]{1,0:T(8,128)(2,1)S(1)}, bf16[192,320]{1,0:T(8,128)(2,1)}, u32[]{:S(2)}) copy-start(bf16[192,320]{1,0:T(8,128)(2,1)} %get-tuple-element.40) | copy-start | bytes 368644
  35.3 0.8 copy-start.10
  35.3 5.1 %copy-start.11 = (bf16[192,160]{0,1:T(8,128)(2,1)S(1)}, bf16[192,160]{0,1:T(8,128)(2,1)}, u32[]{:S(2)}) copy-start(bf16[192,160]{0,1:T(8,128)(2,1)} %param.21) | copy-start | bytes 184324
  35.3 5.1 %copy-start.12 = (bf16[160,192]{1,0:T(8,128)(2,1)S(1)}, bf16[160,192]{1,0:T(8,128)(2,1)}, u32[]{:S(2)}) copy-start(bf16[160,192]{1,0:T(8,128)(2,1)} %param.20) | copy-start | bytes 184324
  35.3 5.1 %copy-start.13 = (bf16[160,192]{1,0:T(8,128)(2,1)S(1)}, bf16[160,192]{1,0:T(8,128)(2,1)}, u32[]{:S(2)}) copy-start(bf16[160,192]{1,0:T(8,128)(2,1)} %param.19) | copy-start | bytes 184324
  35.3 12.9 %copy-start.7 = (bf16[1,1536,320]{1,2,0:T(8,128)(2,1)S(1)}, bf16[1,1536,320]{1,2,0:T(8,128)(2,1)}, u32[]{:S(2)}) copy-start(bf16[1,1536,320]{1,2,0:T(8,128)(2,1)} %param.18) | copy-start | bytes 2949124
  36.1 20.0 %collective-permute-start = (bf16[48,320]{1,0:T(8,128)(2,1)S(1)}, bf16[48,320]{1,0:T(8,128)(2,1)S(1)}, u32[]{:S(2)}, u32[]{:S(2)}) collective-permute-start(bf16[48,320]{1,0:T(8,128)(2,1)S(1)} %copy-done.10), channel_id=1, source_target_pairs={{0,2},{1,3},{2,0},{3,1},{4,6},{5,7},{6,4},{7,5},{8,10},{9,11},{10,... | collective-permute-start | bytes 92168 | tf_op jit(solution)/shard_map/ppermute | solution.py:176
  41.3 12.9 %collective-permute-start.1 = (bf16[160,576]{1,0:T(8,128)(2,1)}, bf16[160,576]{1,0:T(8,128)(2,1)}, u32[]{:S(2)}, u32[]{:S(2)}) collective-permute-start(bf16[160,576]{1,0:T(8,128)(2,1)} %pad_maximum_fusion.1), channel_id=1, source_target_pairs={{0,256},{16,272},{32,288},{48,304},{64,320},{80,336},{96,352},{112... | collective-permute-start | bytes 552968 | tf_op jit(solution)/shard_map/ppermute | solution.py:170
  44.6 15.5 %collective-permute-start.2 = (bf16[64,2560]{1,0:T(8,128)(2,1)}, bf16[64,2560]{1,0:T(8,128)(2,1)}, u32[]{:S(2)}, u32[]{:S(2)}) collective-permute-start(bf16[64,2560]{1,0:T(8,128)(2,1)} %slice.215), channel_id=1, source_target_pairs={{0,2},{1,3},{2,0},{3,1},{4,6},{5,7},{6,4},{7,5},{8,10},{9,11},{10,... | collective-permute-start | bytes 983048 | tf_op jit(solution)/shard_map/ppermute | solution.py:175
  63.8 27.3 %all-to-all-start.1 = ((bf16[4,320,688]{2,1,0:T(8,128)(2,1)}), bf16[4,320,688]{2,1,0:T(8,128)(2,1)S(1)}, u32[]{:S(2)}, u32[]{:S(2)}) async-start(bf16[4,320,688]{2,1,0:T(8,128)(2,1)} %broadcast_in_dim.67), calls=%async_computation.1 | async-start | bytes 3932160 | tf_op jit(solution)/shard_map/all_to_all | solution.py:23
  68.1 17.8 %collective-permute-start.3 = (bf16[128,2560]{1,0:T(8,128)(2,1)S(1)}, bf16[128,2560]{1,0:T(8,128)(2,1)S(1)}, u32[]{:S(2)}, u32[]{:S(2)}) collective-permute-start(bf16[128,2560]{1,0:T(8,128)(2,1)S(1)} %slice.248), channel_id=1, source_target_pairs={{0,2},{1,3},{2,0},{3,1},{4,6},{5,7},{6,4},{7,5},{8,10},{9,11},{10,... | collective-permute-start | bytes 1966088 | tf_op jit(solution)/shard_map/ppermute | solution.py:180
  91.2 7.3 %copy-start.1 = (bf16[4,320,688]{2,1,0:T(8,128)(2,1)}, bf16[4,320,688]{2,1,0:T(8,128)(2,1)S(1)}, u32[]{:S(2)}) copy-start(bf16[4,320,688]{2,1,0:T(8,128)(2,1)S(1)} %all-to-all-done.1.mine_ref.far_mine_ref) | copy-start | bytes 5283844
  91.2 8.2 %collective-permute-start.4 = (bf16[4,320,688]{2,1,0:T(8,128)(2,1)S(1)}, bf16[4,320,688]{2,1,0:T(8,128)(2,1)S(1)}, u32[]{:S(2)}, u32[]{:S(2)}) collective-permute-start(bf16[4,320,688]{2,1,0:T(8,128)(2,1)S(1)} %all-to-all-done.1.mine_ref.far_mine_ref), channel_id=1, source_target_pairs={{0,1},{1,0},{2,3},{3,2},{4,5},{5,4},{6,7},{7,6},{8,9},{9,8},{10,11... | collective-permute-start | bytes 5283848 | tf_op jit(solution)/shard_map/ppermute | solution.py:33
  99.4 5.0 %copy-start.2 = (bf16[4,320,688]{2,1,0:T(8,128)(2,1)}, bf16[4,320,688]{2,1,0:T(8,128)(2,1)S(1)}, u32[]{:S(2)}) copy-start(bf16[4,320,688]{2,1,0:T(8,128)(2,1)S(1)} %collective-permute-done.4.theirs_ref.far_theirs_ref) | copy-start | bytes 5283844
  100.0 10.6 %collective-permute-start.5 = (bf16[192,576]{1,0:T(8,128)(2,1)S(1)}, bf16[192,576]{1,0:T(8,128)(2,1)S(1)}, u32[]{:S(2)}, u32[]{:S(2)}) collective-permute-start(bf16[192,576]{1,0:T(8,128)(2,1)S(1)} %fusion.4), channel_id=1, source_target_pairs={{0,2},{1,3},{2,0},{3,1},{4,6},{5,7},{6,4},{7,5},{8,10},{9,11},{10,... | collective-permute-start | bytes 663560 | tf_op jit(solution)/shard_map/ppermute | solution.py:191
  110.7 26.1 %copy-start.6 = (bf16[768,320]{0,1:T(8,128)(2,1)S(1)}, bf16[768,320]{0,1:T(8,128)(2,1)}, u32[]{:S(2)}) copy-start(bf16[768,320]{0,1:T(8,128)(2,1)} %get-tuple-element.28) | copy-start | bytes 1474564
  110.8 26.5 %copy-start.5 = (bf16[768,320]{0,1:T(8,128)(2,1)S(1)}, bf16[768,320]{0,1:T(8,128)(2,1)}, u32[]{:S(2)}) copy-start(bf16[768,320]{0,1:T(8,128)(2,1)} %get-tuple-element.27) | copy-start | bytes 1474564
  130.4 6.4 %collective-permute-start.6 = (bf16[8,96,576]{2,1,0:T(8,128)(2,1)S(1)}, bf16[8,96,576]{2,1,0:T(8,128)(2,1)S(1)}, u32[]{:S(2)}, u32[]{:S(2)}) collective-permute-start(bf16[8,96,576]{2,1,0:T(8,128)(2,1)S(1)} %all_to_all.25), channel_id=1, source_target_pairs={{0,1},{1,0},{2,3},{3,2},{4,5},{5,4},{6,7},{7,6},{8,9},{9,8},{10,11... | collective-permute-start | bytes 2654216 | tf_op jit(solution)/shard_map/ppermute | solution.py:33
  139.1 46.3 %all-to-all-start.3 = ((bf16[32,18,320]{2,1,0:T(8,128)(2,1)}), bf16[32,18,320]{2,1,0:T(8,128)(2,1)S(1)}, u32[]{:S(2)}, u32[]{:S(2)}) async-start(bf16[32,18,320]{2,1,0:T(8,128)(2,1)} %reshape.70), calls=%async_computation.3 | async-start | bytes 1179648 | tf_op jit(solution)/shard_map/all_to_all | solution.py:23
  147.7 17.6 %copy-start.17 = (s32[48,6]{0,1:T(8,128)S(1)}, s32[48,6]{0,1:T(8,128)}, u32[]{:S(2)}) copy-start(s32[48,6]{0,1:T(8,128)} %param.14) | copy-start | bytes 3460
  147.7 17.6 %copy-start.18 = (f32[48,6]{0,1:T(8,128)S(1)}, f32[48,6]{0,1:T(8,128)}, u32[]{:S(2)}) copy-start(f32[48,6]{0,1:T(8,128)} %param.15) | copy-start | bytes 3460
  154.1 31.6 %copy-start.15 = (bf16[32,576]{1,0:T(8,128)(2,1)S(1)}, bf16[32,576]{1,0:T(8,128)(2,1)}, u32[]{:S(2)}) copy-start(bf16[32,576]{1,0:T(8,128)(2,1)} %constant.42.clone) | copy-start | bytes 110596
  155.2 11.0 %collective-permute-start.9 = (bf16[4,48,320]{2,1,0:T(8,128)(2,1)S(1)}, bf16[4,48,320]{2,1,0:T(8,128)(2,1)S(1)}, u32[]{:S(2)}, u32[]{:S(2)}) collective-permute-start(bf16[4,48,320]{2,1,0:T(8,128)(2,1)S(1)} %get-tuple-element.71), channel_id=1, source_target_pairs={{0,3},{1,2},{2,1},{3,0},{4,7},{5,6},{6,5},{7,4},{8,11},{9,10},{10,... | collective-permute-start | bytes 368648 | tf_op jit(solution)/shard_map/ppermute | solution.py:207
  161.1 9.3 %collective-permute-start.8 = (bf16[4,48,320]{2,1,0:T(8,128)(2,1)S(1)}, bf16[4,48,320]{2,1,0:T(8,128)(2,1)S(1)}, u32[]{:S(2)}, u32[]{:S(2)}) collective-permute-start(bf16[4,48,320]{2,1,0:T(8,128)(2,1)S(1)} %get-tuple-element.72), channel_id=1, source_target_pairs={{0,2},{1,3},{2,0},{3,1},{4,6},{5,7},{6,4},{7,5},{8,10},{9,11},{10,... | collective-permute-start | bytes 368648 | tf_op jit(solution)/shard_map/ppermute | solution.py:207
  163.0 7.4 %collective-permute-start.7 = (bf16[4,48,320]{2,1,0:T(8,128)(2,1)S(1)}, bf16[4,48,320]{2,1,0:T(8,128)(2,1)S(1)}, u32[]{:S(2)}, u32[]{:S(2)}) collective-permute-start(bf16[4,48,320]{2,1,0:T(8,128)(2,1)S(1)} %get-tuple-element.70), channel_id=1, source_target_pairs={{0,1},{1,0},{2,3},{3,2},{4,5},{5,4},{6,7},{7,6},{8,9},{9,8},{10,11... | collective-permute-start | bytes 368648 | tf_op jit(solution)/shard_map/ppermute | solution.py:207
  171.4 10.6 %collective-permute-start.12 = (bf16[48,320]{1,0:T(8,128)(2,1)S(1)}, bf16[48,320]{1,0:T(8,128)(2,1)S(1)}, u32[]{:S(2)}, u32[]{:S(2)}) collective-permute-start(bf16[48,320]{1,0:T(8,128)(2,1)S(1)} %get-tuple-element.74), channel_id=1, source_target_pairs={{0,12},{1,13},{2,14},{3,15},{4,8},{5,9},{6,10},{7,11},{8,4},{9,5},... | collective-permute-start | bytes 92168 | tf_op jit(solution)/shard_map/ppermute | solution.py:207
  175.6 6.5 %collective-permute-start.11 = (bf16[48,320]{1,0:T(8,128)(2,1)S(1)}, bf16[48,320]{1,0:T(8,128)(2,1)S(1)}, u32[]{:S(2)}, u32[]{:S(2)}) collective-permute-start(bf16[48,320]{1,0:T(8,128)(2,1)S(1)} %get-tuple-element.75), channel_id=1, source_target_pairs={{0,8},{1,9},{2,10},{3,11},{4,12},{5,13},{6,14},{7,15},{8,0},{9,1},... | collective-permute-start | bytes 92168 | tf_op jit(solution)/shard_map/ppermute | solution.py:207
  180.1 5.3 %collective-permute-start.10 = (bf16[48,320]{1,0:T(8,128)(2,1)S(1)}, bf16[48,320]{1,0:T(8,128)(2,1)S(1)}, u32[]{:S(2)}, u32[]{:S(2)}) collective-permute-start(bf16[48,320]{1,0:T(8,128)(2,1)S(1)} %get-tuple-element.73), channel_id=1, source_target_pairs={{0,4},{1,5},{2,6},{3,7},{4,0},{5,1},{6,2},{7,3},{8,12},{9,13},{10,... | collective-permute-start | bytes 92168 | tf_op jit(solution)/shard_map/ppermute | solution.py:207
  185.4 9.1 %copy-start.16 = (f32[5120]{0:T(1024)S(1)}, f32[5120]{0:T(1024)}, u32[]{:S(2)}) copy-start(f32[5120]{0:T(1024)} %param.22) | copy-start | bytes 61444
  185.5 21.1 %copy-start = (bf16[132,5120]{1,0:T(8,128)(2,1)S(1)}, bf16[132,5120]{1,0:T(8,128)(2,1)}, u32[]{:S(2)}) copy-start(bf16[132,5120]{1,0:T(8,128)(2,1)} %weight_ref.1) | copy-start | bytes 4055044
  186.2 21.8 %copy-start.14 = (bf16[48,320]{1,0:T(8,128)(2,1)}, bf16[48,320]{1,0:T(8,128)(2,1)S(1)}, u32[]{:S(2)}) copy-start(bf16[48,320]{1,0:T(8,128)(2,1)S(1)} %fusion.31) | copy-start | bytes 92164
  187.1 19.4 %all-to-all-start.4 = ((bf16[16,48,320]{2,1,0:T(8,128)(2,1)}), bf16[16,48,320]{2,1,0:T(8,128)(2,1)S(1)}, u32[]{:S(2)}, u32[]{:S(2)}) async-start(bf16[16,48,320]{2,1,0:T(8,128)(2,1)} %broadcast_in_dim.74), calls=%async_computation.4 | async-start | bytes 1179648 | tf_op jit(solution)/shard_map/all_to_all | solution.py:23
Sparse Core Ops, SparseCore 0:
  61.7 85.4 all-gather.2

commit v9 on v8

--- a/solution.py
+++ b/solution.py
@@ -34,9 +34,9 @@
     return mine, theirs, held
 
 
-def shared_kernel(rank_ref, mine_ref, far_mine_ref, theirs_ref, far_theirs_ref, table_ref, out_ref):
+def shared_kernel(rank_ref, mine_ref, far_mine_ref, theirs_ref, far_theirs_ref, table_ref, out_ref, hidden_ref):
     rank = rank_ref[0]
-    inner = table_ref.shape[3] // 3
+    inner = table_ref.shape[3] // 2
     size = table_ref.shape[2]
     tok = out_ref.shape[2]
 
@@ -48,38 +48,46 @@
         for y in range(4):
             for core in range(2):
                 device = 4 * y + (((rank & 3) ^ (2 * across)) ^ core)
-                block = weights(device)[:, :, : 2 * inner].reshape(2 * size, 2 * inner)
+                block = weights(device)[...].reshape(2 * size, 2 * inner)
                 total = total + dot(refs[core][y], block, 0, 0)
         return total
 
-    sums = product((mine_ref, theirs_ref), 0)[64 : 64 + tok]
-    sums = sums + product((far_mine_ref, far_theirs_ref), 1)[:tok]
-    gate, up = sums[:, :inner], sums[:, inner:]
-    hidden = (gate * (1.0 / (1.0 + jnp.exp(-gate))) * up).astype(jnp.bfloat16)
-    for near in range(4):
-        for far in range(4):
-            block = weights(rank ^ (near + 4 * far))[:, :, 2 * inner :].reshape(2 * size, inner)
-            out_ref[near, far] = dot(hidden, block, 1, 1).astype(out_ref.dtype)
+    @pl.when(pl.program_id(0) == 0)
+    def _():
+        sums = product((mine_ref, theirs_ref), 0)[64 : 64 + tok]
+        sums = sums + product((far_mine_ref, far_theirs_ref), 1)[:tok]
+        gate, up = sums[:, :inner], sums[:, inner:]
+        hidden_ref[...] = (gate * (1.0 / (1.0 + jnp.exp(-gate))) * up).astype(jnp.bfloat16)
+
+    @pl.when(pl.program_id(0) == 1)
+    def _():
+        hidden = hidden_ref[...]
+        for near in range(4):
+            for far in range(4):
+                block = weights(rank ^ (near + 4 * far))[:, :, :inner].reshape(2 * size, inner)
+                out_ref[far, near] = dot(hidden, block, 1, 1).astype(out_ref.dtype)
 
 
 def shared_partial(rank, mine, theirs, table, tok):
     width = mine.shape[1]
+    columns = 2 * table.shape[3] // 3
     out = jax.ShapeDtypeStruct((4, 4, tok, width), jnp.bfloat16)
     near = pl.BlockSpec((4, width, 128), lambda i: (0, 0, 4))
     far = pl.BlockSpec((4, width, 128), lambda i: (0, 0, 5))
     return pl.pallas_call(
         shared_kernel,
         out_shape=out,
-        grid=(1,),
+        grid=(2,),
         in_specs=[
             pl.BlockSpec(memory_space=pltpu.SMEM),
             near,
             far,
             near,
             far,
-            pl.BlockSpec(table.shape, lambda i: (0, 0, 0, 0), pipeline_mode=pl.Buffered(1)),
+            pl.BlockSpec(table.shape[:3] + (columns,), lambda i: (0, 0, 0, i)),
         ],
         out_specs=pl.BlockSpec(out.shape, lambda i: (0, 0, 0, 0)),
+        scratch_shapes=[pltpu.VMEM((tok, columns // 2), jnp.bfloat16)],
         compiler_params=pltpu.CompilerParams(vmem_limit_bytes=56 * 2**20),
         cost_estimate=pl.CostEstimate(flops=1000, bytes_accessed=1000, transcendentals=0),
     )(rank.reshape(1), mine, mine, theirs, theirs, table)
@@ -207,7 +215,7 @@
             total = total + lax.ppermute(parts[k], "tensor", perm).astype(f32)
         return total
 
-    shared = summed(summed(partial, 1).astype(bf16), 4)
+    shared = summed(summed(partial, 4).astype(bf16), 1)
 
     returned, shared = lax.optimization_barrier((returned, shared))
     high = lax.reduce_precision(weight, 8, 7)

time: 216 us -> 214 us (level)
  waiting for transfers between devices: 52.8 us -> 50.3 us
    ppermute x6, starting transfers between devices: 20.6 us -> 23.5 us  [summed(): total = total + lax.ppermute(parts[k], 'tensor', perm).astype(f32)]
    ppermute x6, waiting for transfers between devices: 8.43 us -> 6.01 us  [summed(): total = total + lax.ppermute(parts[k], 'tensor', perm).astype(f32)]
where the time goes in v9:
time: 214 us; the launch traced here: 212 us
  starting transfers between devices  86.9 us (41%)
  waiting for transfers between devices  50.3 us (24%)
  blocking collectives  19.5 us (9%)
  local copies, waits for them, and re-layouts  16.8 us (8%)
  between operations  14.7 us (7%)
  other arithmetic  10.3 us (5%)
  matrix products  7.09 us (3%)
  Pallas kernels  6.85 us (3%)
    all_to_all x4, starting transfers between devices, exchange(): lax.all_to_all(parts, axis, split_axis=0, concat_axis=0, tiled=True, axis...  35.2 us
    ppermute x6, starting transfers between devices, summed(): total = total + lax.ppermute(parts[k], 'tensor', perm).astype(f32)  23.5 us
    all_to_all x1, blocking collectives, exchange(): lax.all_to_all(parts, axis, split_axis=0, concat_axis=0, tiled=True, axis...  19.5 us
    all_to_all x4, waiting for transfers between devices, exchange(): lax.all_to_all(parts, axis, split_axis=0, concat_axis=0, tiled=True, axis...  18.8 us
    ppermute x1, waiting for transfers between devices, per_device(): far_rest = lax.ppermute(give[cut:], 'tensor', across)  13.4 us
    ppermute x2, starting transfers between devices, gather_halves(): lax.ppermute(mine, 'tensor', [(i, i ^ 1) for i in range(2 * CHIPS)])  8.88 us
    ppermute x6, waiting for transfers between devices, summed(): total = total + lax.ppermute(parts[k], 'tensor', perm).astype(f32)  6.01 us
    dot_general x8, matrix products, dot(): lax.dot_general(left, right, (((over_left,), (over_right,)), ((), ())), p...  5.91 us
  transfers between devices with their start and end apart: 18, of which 11 were waited for; matrix products, arithmetic and copies ran while one was open for 13% of the time, Pallas kernels for 3%

profile of v9, /device:TPU:1, one launch (start us, length us, event | category | flops | bytes accessed | tf_op | source)
XLA Modules:
  0.0 212.5 jit_solution(189142331467551597)
XLA Ops:
  7.2 0.8 fusion.29
  8.0 1.2 convolution_compare_fusion
  9.2 1.1 convolution_convert_fusion
  10.6 1.0 reshape.64
  11.6 17.0 %all-to-all-start = ((bf16[32,18,320]{2,1,0:T(8,128)(2,1)}), bf16[32,18,320]{2,1,0:T(8,128)(2,1)S(1)}, u32[]{:S(2)}, u32[]{:S(2)}) async-start(bf16[32,18,320]{2,1,0:T(8,128)(2,1)} %reshape.64), calls=%async_computation | async-start | bytes 1179648 | tf_op jit(solution)/shard_map/all_to_all | solution.py:23
  28.6 1.0 fusion.22
  29.6 1.2 pad_maximum_fusion.2
  30.8 1.4 concatenate.40
  32.1 1.3 concatenate.41
  33.5 0.4 concatenate.38
  33.9 0.4 concatenate.39
  34.3 1.0 select_select_fusion
  35.4 0.7 copy-done.10
  36.1 4.3 %collective-permute-start = (bf16[48,320]{1,0:T(8,128)(2,1)S(1)}, bf16[48,320]{1,0:T(8,128)(2,1)S(1)}, u32[]{:S(2)}, u32[]{:S(2)}) collective-permute-start(bf16[48,320]{1,0:T(8,128)(2,1)S(1)} %copy-done.10), channel_id=1, source_target_pairs={{0,2},{1,3},{2,0},{3,1},{4,6},{5,7},{6,4},{7,5},{8,10},{9,11},{10,... | collective-permute-start | bytes 92168 | tf_op jit(solution)/shard_map/ppermute | solution.py:184
  40.5 0.8 pad_maximum_fusion.1
  41.3 2.5 %collective-permute-start.1 = (bf16[160,576]{1,0:T(8,128)(2,1)}, bf16[160,576]{1,0:T(8,128)(2,1)}, u32[]{:S(2)}, u32[]{:S(2)}) collective-permute-start(bf16[160,576]{1,0:T(8,128)(2,1)} %pad_maximum_fusion.1), channel_id=1, source_target_pairs={{0,256},{16,272},{32,288},{48,304},{64,320},{80,336},{96,352},{112... | collective-permute-start | bytes 552968 | tf_op jit(solution)/shard_map/ppermute | solution.py:178
  43.8 0.7 slice.215
  44.6 3.6 %collective-permute-start.2 = (bf16[64,2560]{1,0:T(8,128)(2,1)}, bf16[64,2560]{1,0:T(8,128)(2,1)}, u32[]{:S(2)}, u32[]{:S(2)}) collective-permute-start(bf16[64,2560]{1,0:T(8,128)(2,1)} %slice.215), channel_id=1, source_target_pairs={{0,2},{1,3},{2,0},{3,1},{4,6},{5,7},{6,4},{7,5},{8,10},{9,11},{10,... | collective-permute-start | bytes 983048 | tf_op jit(solution)/shard_map/ppermute | solution.py:183
  48.2 1.3 slice_bitcast_fusion.4
  49.6 1.3 concatenate.45
  50.9 1.2 concatenate.44
  52.1 1.0 broadcast_select_fusion
  53.1 1.1 fusion.79
  54.2 1.9 maximum_select_fusion
  56.1 4.0 %collective-permute-done.2 = bf16[64,2560]{1,0:T(8,128)(2,1)} collective-permute-done((bf16[64,2560]{1,0:T(8,128)(2,1)}, bf16[64,2560]{1,0:T(8,128)(2,1)}, u32[]{:S(2)}, u32[]{:S(2)}) %collective-permute-start.2) | collective-permute-done | bytes 327712 | tf_op jit(solution)/shard_map/ppermute | solution.py:183
  60.0 1.6 all-to-all-done
  62.4 1.5 broadcast_in_dim.67
  63.8 4.2 %all-to-all-start.1 = ((bf16[4,320,688]{2,1,0:T(8,128)(2,1)}), bf16[4,320,688]{2,1,0:T(8,128)(2,1)S(1)}, u32[]{:S(2)}, u32[]{:S(2)}) async-start(bf16[4,320,688]{2,1,0:T(8,128)(2,1)} %broadcast_in_dim.67), calls=%async_computation.1 | async-start | bytes 3932160 | tf_op jit(solution)/shard_map/all_to_all | solution.py:23
  68.1 4.4 %collective-permute-start.3 = (bf16[128,2560]{1,0:T(8,128)(2,1)S(1)}, bf16[128,2560]{1,0:T(8,128)(2,1)S(1)}, u32[]{:S(2)}, u32[]{:S(2)}) collective-permute-start(bf16[128,2560]{1,0:T(8,128)(2,1)S(1)} %slice.248), channel_id=1, source_target_pairs={{0,2},{1,3},{2,0},{3,1},{4,6},{5,7},{6,4},{7,5},{8,10},{9,11},{10,... | collective-permute-start | bytes 1966088 | tf_op jit(solution)/shard_map/ppermute | solution.py:188
  72.4 13.4 %collective-permute-done.3 = bf16[128,2560]{1,0:T(8,128)(2,1)S(1)} collective-permute-done((bf16[128,2560]{1,0:T(8,128)(2,1)S(1)}, bf16[128,2560]{1,0:T(8,128)(2,1)S(1)}, u32[]{:S(2)}, u32[]{:S(2)}) %collective-permute-start.3) | collective-permute-done | bytes 655392 | tf_op jit(solution)/shard_map/ppermute | solution.py:188
  85.9 5.3 %all-to-all-done.1.mine_ref.far_mine_ref = bf16[4,320,688]{2,1,0:T(8,128)(2,1)S(1)} async-done(((bf16[4,320,688]{2,1,0:T(8,128)(2,1)}), bf16[4,320,688]{2,1,0:T(8,128)(2,1)S(1)}, u32[]{:S(2)}, u32[]{:S(2)}) %all-to-all-start.1) | async-done | bytes 1761312 | tf_op jit(solution)/shard_map/all_to_all | solution.py:23
  91.2 4.7 %collective-permute-start.4 = (bf16[4,320,688]{2,1,0:T(8,128)(2,1)S(1)}, bf16[4,320,688]{2,1,0:T(8,128)(2,1)S(1)}, u32[]{:S(2)}, u32[]{:S(2)}) collective-permute-start(bf16[4,320,688]{2,1,0:T(8,128)(2,1)S(1)} %all-to-all-done.1.mine_ref.far_mine_ref), channel_id=1, source_target_pairs={{0,1},{1,0},{2,3},{3,2},{4,5},{5,4},{6,7},{7,6},{8,9},{9,8},{10,11... | collective-permute-start | bytes 5283848 | tf_op jit(solution)/shard_map/ppermute | solution.py:33
  95.8 1.0 constant_dynamic-update-slice_fusion.1
  96.8 1.6 fusion.60
  98.5 0.6 fusion.7
  99.0 0.4 collective-permute-done.4.theirs_ref.far_theirs_ref
  99.4 0.6 fusion.5
  100.0 4.4 %collective-permute-start.5 = (bf16[192,576]{1,0:T(8,128)(2,1)S(1)}, bf16[192,576]{1,0:T(8,128)(2,1)S(1)}, u32[]{:S(2)}, u32[]{:S(2)}) collective-permute-start(bf16[192,576]{1,0:T(8,128)(2,1)S(1)} %fusion.4), channel_id=1, source_target_pairs={{0,2},{1,3},{2,0},{3,1},{4,6},{5,7},{6,4},{7,5},{8,10},{9,11},{10,... | collective-permute-start | bytes 663560 | tf_op jit(solution)/shard_map/ppermute | solution.py:199
  104.4 0.6 fusion.61
  105.0 5.6 %collective-permute-done.5 = bf16[192,576]{1,0:T(8,128)(2,1)S(1)} collective-permute-done((bf16[192,576]{1,0:T(8,128)(2,1)S(1)}, bf16[192,576]{1,0:T(8,128)(2,1)S(1)}, u32[]{:S(2)}, u32[]{:S(2)}) %collective-permute-start.5) | collective-permute-done | bytes 221216 | tf_op jit(solution)/shard_map/ppermute | solution.py:199
  110.8 19.5 %all_to_all.25 = bf16[8,96,576]{2,1,0:T(8,128)(2,1)S(1)} all-to-all(bf16[8,96,576]{2,1,0:T(8,128)(2,1)S(1)} %broadcast_in_dim.68), channel_id=1, replica_groups={{0,2,4,6,8,10,12,14},{1,3,5,7,9,11,13,15},{16,18,20,22,24,26,28,30},{17..., dimensions={0} | all-to-all | bytes 1769472 | tf_op jit(solution)/shard_map/all_to_all | solution.py:23
  130.4 4.2 %collective-permute-start.6 = (bf16[8,96,576]{2,1,0:T(8,128)(2,1)S(1)}, bf16[8,96,576]{2,1,0:T(8,128)(2,1)S(1)}, u32[]{:S(2)}, u32[]{:S(2)}) collective-permute-start(bf16[8,96,576]{2,1,0:T(8,128)(2,1)S(1)} %all_to_all.25), channel_id=1, source_target_pairs={{0,1},{1,0},{2,3},{3,2},{4,5},{5,4},{6,7},{7,6},{8,9},{9,8},{10,11... | collective-permute-start | bytes 2654216 | tf_op jit(solution)/shard_map/ppermute | solution.py:33
  134.6 2.2 %collective-permute-done.6 = bf16[8,96,576]{2,1,0:T(8,128)(2,1)S(1)} collective-permute-done((bf16[8,96,576]{2,1,0:T(8,128)(2,1)S(1)}, bf16[8,96,576]{2,1,0:T(8,128)(2,1)S(1)}, u32[]{:S(2)}, u32[]{:S(2)}) %collective-permute-start.6) | collective-permute-done | bytes 884768 | tf_op jit(solution)/shard_map/ppermute | solution.py:33
  136.8 0.6 fusion.62
  137.3 0.6 fusion
  138.2 1.0 reshape.70
  139.1 8.5 %all-to-all-start.3 = ((bf16[32,18,320]{2,1,0:T(8,128)(2,1)}), bf16[32,18,320]{2,1,0:T(8,128)(2,1)S(1)}, u32[]{:S(2)}, u32[]{:S(2)}) async-start(bf16[32,18,320]{2,1,0:T(8,128)(2,1)} %reshape.70), calls=%async_computation.3 | async-start | bytes 1179648 | tf_op jit(solution)/shard_map/all_to_all | solution.py:23
  147.7 5.4 %shard_map.140 = bf16[4,4,48,320]{3,2,1,0:T(8,128)(2,1)} custom-call(s32[1]{0:T(128)} %bitcast.26.rank_ref, bf16[4,320,688]{2,1,0:T(8,128)(2,1)} %copy-done.1, bf16[4,320,688]{2,1,0:T(8,128)(2,1)} %copy-done.1, bf16[4,320,688]{2,1,0:T(8,128)(2,1)} %copy-done.2, bf16[4,320,688]{2,1,0:T(8,128)(2,1)} %copy-done.2, bf16[16,2,160,576]{3,2,1,0:T(8,128)(2,1)} %bitcast.89), custom_call_target="tpu_custom_call" | custom-call | flops 1000 | bytes 1000 | tf_op jit(solution)/shard_map/pallas_call | solution.py:77
  153.1 1.1 slice_bitcast_fusion.2
  154.3 4.0 %collective-permute-start.9 = (bf16[4,48,320]{2,1,0:T(8,128)(2,1)S(1)}, bf16[4,48,320]{2,1,0:T(8,128)(2,1)S(1)}, u32[]{:S(2)}, u32[]{:S(2)}) collective-permute-start(bf16[4,48,320]{2,1,0:T(8,128)(2,1)S(1)} %get-tuple-element.71), channel_id=1, source_target_pairs={{0,12},{1,13},{2,14},{3,15},{4,8},{5,9},{6,10},{7,11},{8,4},{9,5},... | collective-permute-start | bytes 368648 | tf_op jit(solution)/shard_map/ppermute | solution.py:215
  158.2 2.0 collective-permute-start.8
  160.3 3.0 %collective-permute-start.7 = (bf16[4,48,320]{2,1,0:T(8,128)(2,1)S(1)}, bf16[4,48,320]{2,1,0:T(8,128)(2,1)S(1)}, u32[]{:S(2)}, u32[]{:S(2)}) collective-permute-start(bf16[4,48,320]{2,1,0:T(8,128)(2,1)S(1)} %get-tuple-element.70), channel_id=1, source_target_pairs={{0,4},{1,5},{2,6},{3,7},{4,0},{5,1},{6,2},{7,3},{8,12},{9,13},{10,... | collective-permute-start | bytes 368648 | tf_op jit(solution)/shard_map/ppermute | solution.py:215
  163.3 2.6 %collective-permute-done.8 = bf16[4,48,320]{2,1,0:T(8,128)(2,1)S(1)} collective-permute-done((bf16[4,48,320]{2,1,0:T(8,128)(2,1)S(1)}, bf16[4,48,320]{2,1,0:T(8,128)(2,1)S(1)}, u32[]{:S(2)}, u32[]{:S(2)}) %collective-permute-start.8) | collective-permute-done | bytes 122912 | tf_op jit(solution)/shard_map/ppermute | solution.py:215
  165.9 1.5 collective-permute-done.7
  167.4 1.0 fusion.12
  168.4 10.3 %collective-permute-start.12 = (bf16[48,320]{1,0:T(8,128)(2,1)S(1)}, bf16[48,320]{1,0:T(8,128)(2,1)S(1)}, u32[]{:S(2)}, u32[]{:S(2)}) collective-permute-start(bf16[48,320]{1,0:T(8,128)(2,1)S(1)} %get-tuple-element.74), channel_id=1, source_target_pairs={{0,3},{1,2},{2,1},{3,0},{4,7},{5,6},{6,5},{7,4},{8,11},{9,10},{10,... | collective-permute-start | bytes 92168 | tf_op jit(solution)/shard_map/ppermute | solution.py:215
  178.7 1.9 collective-permute-start.11
  180.7 2.3 %collective-permute-start.10 = (bf16[48,320]{1,0:T(8,128)(2,1)S(1)}, bf16[48,320]{1,0:T(8,128)(2,1)S(1)}, u32[]{:S(2)}, u32[]{:S(2)}) collective-permute-start(bf16[48,320]{1,0:T(8,128)(2,1)S(1)} %get-tuple-element.73), channel_id=1, source_target_pairs={{0,1},{1,0},{2,3},{3,2},{4,5},{5,4},{6,7},{7,6},{8,9},{9,8},{10,11... | collective-permute-start | bytes 92168 | tf_op jit(solution)/shard_map/ppermute | solution.py:215
  183.0 1.9 collective-permute-done.11
  185.3 0.5 fusion.2
  185.8 0.9 broadcast_in_dim.74
  186.7 5.6 %all-to-all-start.4 = ((bf16[16,48,320]{2,1,0:T(8,128)(2,1)}), bf16[16,48,320]{2,1,0:T(8,128)(2,1)S(1)}, u32[]{:S(2)}, u32[]{:S(2)}) async-start(bf16[16,48,320]{2,1,0:T(8,128)(2,1)} %broadcast_in_dim.74), calls=%async_computation.4 | async-start | bytes 1179648 | tf_op jit(solution)/shard_map/all_to_all | solution.py:23
  192.3 11.9 %all-to-all-done.4.stream_ref = bf16[16,48,320]{2,1,0:T(8,128)(2,1)S(1)} async-done(((bf16[16,48,320]{2,1,0:T(8,128)(2,1)}), bf16[16,48,320]{2,1,0:T(8,128)(2,1)S(1)}, u32[]{:S(2)}, u32[]{:S(2)}) %all-to-all-start.4) | async-done | bytes 491552 | tf_op jit(solution)/shard_map/all_to_all | solution.py:23
  204.2 1.4 shard_map.141
  (69 shorter events, 2.2 us)
Async XLA Ops:
  7.2 21.4 %copy-start.3 = (bf16[1,96,5120]{2,1,0:T(8,128)(2,1)S(1)}, bf16[1,96,5120]{2,1,0:T(8,128)(2,1)}, u32[]{:S(2)}) copy-start(bf16[1,96,5120]{2,1,0:T(8,128)(2,1)} %param.16) | copy-start | bytes 2949124
  7.2 21.4 %copy-start.4 = (bf16[1,96,5120]{2,1,0:T(8,128)(2,1)S(1)}, bf16[1,96,5120]{2,1,0:T(8,128)(2,1)}, u32[]{:S(2)}) copy-start(bf16[1,96,5120]{2,1,0:T(8,128)(2,1)} %param.17) | copy-start | bytes 2949124
  11.6 50.0 %all-to-all-start = ((bf16[32,18,320]{2,1,0:T(8,128)(2,1)}), bf16[32,18,320]{2,1,0:T(8,128)(2,1)S(1)}, u32[]{:S(2)}, u32[]{:S(2)}) async-start(bf16[32,18,320]{2,1,0:T(8,128)(2,1)} %reshape.64), calls=%async_computation | async-start | bytes 1179648 | tf_op jit(solution)/shard_map/all_to_all | solution.py:23
  28.5 119.2 %all-gather.3.cloned.1.call-start = ((), (), s32[]{:S(2)}) async-start(), calls=%async_computation.5 | async-start | bytes 6963200 | tf_op jit(solution)/shard_map/all_gather | solution.py:189
  30.8 2.7 %copy-start.8 = (bf16[192,320]{1,0:T(8,128)(2,1)S(1)}, bf16[192,320]{1,0:T(8,128)(2,1)}, u32[]{:S(2)}) copy-start(bf16[192,320]{1,0:T(8,128)(2,1)} %get-tuple-element.39) | copy-start | bytes 368644
  30.8 2.7 %copy-start.9 = (bf16[192,320]{1,0:T(8,128)(2,1)S(1)}, bf16[192,320]{1,0:T(8,128)(2,1)}, u32[]{:S(2)}) copy-start(bf16[192,320]{1,0:T(8,128)(2,1)} %get-tuple-element.40) | copy-start | bytes 368644
  35.3 0.8 copy-start.10
  35.3 5.1 %copy-start.11 = (bf16[192,160]{0,1:T(8,128)(2,1)S(1)}, bf16[192,160]{0,1:T(8,128)(2,1)}, u32[]{:S(2)}) copy-start(bf16[192,160]{0,1:T(8,128)(2,1)} %param.21) | copy-start | bytes 184324
  35.3 5.1 %copy-start.12 = (bf16[160,192]{1,0:T(8,128)(2,1)S(1)}, bf16[160,192]{1,0:T(8,128)(2,1)}, u32[]{:S(2)}) copy-start(bf16[160,192]{1,0:T(8,128)(2,1)} %param.20) | copy-start | bytes 184324
  35.3 5.1 %copy-start.13 = (bf16[160,192]{1,0:T(8,128)(2,1)S(1)}, bf16[160,192]{1,0:T(8,128)(2,1)}, u32[]{:S(2)}) copy-start(bf16[160,192]{1,0:T(8,128)(2,1)} %param.19) | copy-start | bytes 184324
  35.3 12.9 %copy-start.7 = (bf16[1,1536,320]{1,2,0:T(8,128)(2,1)S(1)}, bf16[1,1536,320]{1,2,0:T(8,128)(2,1)}, u32[]{:S(2)}) copy-start(bf16[1,1536,320]{1,2,0:T(8,128)(2,1)} %param.18) | copy-start | bytes 2949124
  36.1 20.0 %collective-permute-start = (bf16[48,320]{1,0:T(8,128)(2,1)S(1)}, bf16[48,320]{1,0:T(8,128)(2,1)S(1)}, u32[]{:S(2)}, u32[]{:S(2)}) collective-permute-start(bf16[48,320]{1,0:T(8,128)(2,1)S(1)} %copy-done.10), channel_id=1, source_target_pairs={{0,2},{1,3},{2,0},{3,1},{4,6},{5,7},{6,4},{7,5},{8,10},{9,11},{10,... | collective-permute-start | bytes 92168 | tf_op jit(solution)/shard_map/ppermute | solution.py:184
  41.3 12.9 %collective-permute-start.1 = (bf16[160,576]{1,0:T(8,128)(2,1)}, bf16[160,576]{1,0:T(8,128)(2,1)}, u32[]{:S(2)}, u32[]{:S(2)}) collective-permute-start(bf16[160,576]{1,0:T(8,128)(2,1)} %pad_maximum_fusion.1), channel_id=1, source_target_pairs={{0,256},{16,272},{32,288},{48,304},{64,320},{80,336},{96,352},{112... | collective-permute-start | bytes 552968 | tf_op jit(solution)/shard_map/ppermute | solution.py:178
  44.6 15.5 %collective-permute-start.2 = (bf16[64,2560]{1,0:T(8,128)(2,1)}, bf16[64,2560]{1,0:T(8,128)(2,1)}, u32[]{:S(2)}, u32[]{:S(2)}) collective-permute-start(bf16[64,2560]{1,0:T(8,128)(2,1)} %slice.215), channel_id=1, source_target_pairs={{0,2},{1,3},{2,0},{3,1},{4,6},{5,7},{6,4},{7,5},{8,10},{9,11},{10,... | collective-permute-start | bytes 983048 | tf_op jit(solution)/shard_map/ppermute | solution.py:183
  63.8 27.3 %all-to-all-start.1 = ((bf16[4,320,688]{2,1,0:T(8,128)(2,1)}), bf16[4,320,688]{2,1,0:T(8,128)(2,1)S(1)}, u32[]{:S(2)}, u32[]{:S(2)}) async-start(bf16[4,320,688]{2,1,0:T(8,128)(2,1)} %broadcast_in_dim.67), calls=%async_computation.1 | async-start | bytes 3932160 | tf_op jit(solution)/shard_map/all_to_all | solution.py:23
  68.1 17.8 %collective-permute-start.3 = (bf16[128,2560]{1,0:T(8,128)(2,1)S(1)}, bf16[128,2560]{1,0:T(8,128)(2,1)S(1)}, u32[]{:S(2)}, u32[]{:S(2)}) collective-permute-start(bf16[128,2560]{1,0:T(8,128)(2,1)S(1)} %slice.248), channel_id=1, source_target_pairs={{0,2},{1,3},{2,0},{3,1},{4,6},{5,7},{6,4},{7,5},{8,10},{9,11},{10,... | collective-permute-start | bytes 1966088 | tf_op jit(solution)/shard_map/ppermute | solution.py:188
  91.2 7.3 %copy-start.1 = (bf16[4,320,688]{2,1,0:T(8,128)(2,1)}, bf16[4,320,688]{2,1,0:T(8,128)(2,1)S(1)}, u32[]{:S(2)}) copy-start(bf16[4,320,688]{2,1,0:T(8,128)(2,1)S(1)} %all-to-all-done.1.mine_ref.far_mine_ref) | copy-start | bytes 5283844
  91.2 8.2 %collective-permute-start.4 = (bf16[4,320,688]{2,1,0:T(8,128)(2,1)S(1)}, bf16[4,320,688]{2,1,0:T(8,128)(2,1)S(1)}, u32[]{:S(2)}, u32[]{:S(2)}) collective-permute-start(bf16[4,320,688]{2,1,0:T(8,128)(2,1)S(1)} %all-to-all-done.1.mine_ref.far_mine_ref), channel_id=1, source_target_pairs={{0,1},{1,0},{2,3},{3,2},{4,5},{5,4},{6,7},{7,6},{8,9},{9,8},{10,11... | collective-permute-start | bytes 5283848 | tf_op jit(solution)/shard_map/ppermute | solution.py:33
  99.4 5.0 %copy-start.2 = (bf16[4,320,688]{2,1,0:T(8,128)(2,1)}, bf16[4,320,688]{2,1,0:T(8,128)(2,1)S(1)}, u32[]{:S(2)}) copy-start(bf16[4,320,688]{2,1,0:T(8,128)(2,1)S(1)} %collective-permute-done.4.theirs_ref.far_theirs_ref) | copy-start | bytes 5283844
  100.0 10.6 %collective-permute-start.5 = (bf16[192,576]{1,0:T(8,128)(2,1)S(1)}, bf16[192,576]{1,0:T(8,128)(2,1)S(1)}, u32[]{:S(2)}, u32[]{:S(2)}) collective-permute-start(bf16[192,576]{1,0:T(8,128)(2,1)S(1)} %fusion.4), channel_id=1, source_target_pairs={{0,2},{1,3},{2,0},{3,1},{4,6},{5,7},{6,4},{7,5},{8,10},{9,11},{10,... | collective-permute-start | bytes 663560 | tf_op jit(solution)/shard_map/ppermute | solution.py:199
  110.7 26.1 %copy-start.6 = (bf16[768,320]{0,1:T(8,128)(2,1)S(1)}, bf16[768,320]{0,1:T(8,128)(2,1)}, u32[]{:S(2)}) copy-start(bf16[768,320]{0,1:T(8,128)(2,1)} %get-tuple-element.28) | copy-start | bytes 1474564
  110.8 26.5 %copy-start.5 = (bf16[768,320]{0,1:T(8,128)(2,1)S(1)}, bf16[768,320]{0,1:T(8,128)(2,1)}, u32[]{:S(2)}) copy-start(bf16[768,320]{0,1:T(8,128)(2,1)} %get-tuple-element.27) | copy-start | bytes 1474564
  130.4 6.4 %collective-permute-start.6 = (bf16[8,96,576]{2,1,0:T(8,128)(2,1)S(1)}, bf16[8,96,576]{2,1,0:T(8,128)(2,1)S(1)}, u32[]{:S(2)}, u32[]{:S(2)}) collective-permute-start(bf16[8,96,576]{2,1,0:T(8,128)(2,1)S(1)} %all_to_all.25), channel_id=1, source_target_pairs={{0,1},{1,0},{2,3},{3,2},{4,5},{5,4},{6,7},{7,6},{8,9},{9,8},{10,11... | collective-permute-start | bytes 2654216 | tf_op jit(solution)/shard_map/ppermute | solution.py:33
  139.1 45.8 %all-to-all-start.3 = ((bf16[32,18,320]{2,1,0:T(8,128)(2,1)}), bf16[32,18,320]{2,1,0:T(8,128)(2,1)S(1)}, u32[]{:S(2)}, u32[]{:S(2)}) async-start(bf16[32,18,320]{2,1,0:T(8,128)(2,1)} %reshape.70), calls=%async_computation.3 | async-start | bytes 1179648 | tf_op jit(solution)/shard_map/all_to_all | solution.py:23
  147.7 15.6 %copy-start.17 = (s32[48,6]{0,1:T(8,128)S(1)}, s32[48,6]{0,1:T(8,128)}, u32[]{:S(2)}) copy-start(s32[48,6]{0,1:T(8,128)} %param.14) | copy-start | bytes 3460
  147.7 15.6 %copy-start.18 = (f32[48,6]{0,1:T(8,128)S(1)}, f32[48,6]{0,1:T(8,128)}, u32[]{:S(2)}) copy-start(f32[48,6]{0,1:T(8,128)} %param.15) | copy-start | bytes 3460
  153.1 32.1 %copy-start.15 = (bf16[32,576]{1,0:T(8,128)(2,1)S(1)}, bf16[32,576]{1,0:T(8,128)(2,1)}, u32[]{:S(2)}) copy-start(bf16[32,576]{1,0:T(8,128)(2,1)} %constant.42.clone) | copy-start | bytes 110596
  154.3 9.1 %collective-permute-start.9 = (bf16[4,48,320]{2,1,0:T(8,128)(2,1)S(1)}, bf16[4,48,320]{2,1,0:T(8,128)(2,1)S(1)}, u32[]{:S(2)}, u32[]{:S(2)}) collective-permute-start(bf16[4,48,320]{2,1,0:T(8,128)(2,1)S(1)} %get-tuple-element.71), channel_id=1, source_target_pairs={{0,12},{1,13},{2,14},{3,15},{4,8},{5,9},{6,10},{7,11},{8,4},{9,5},... | collective-permute-start | bytes 368648 | tf_op jit(solution)/shard_map/ppermute | solution.py:215
  158.2 7.7 %collective-permute-start.8 = (bf16[4,48,320]{2,1,0:T(8,128)(2,1)S(1)}, bf16[4,48,320]{2,1,0:T(8,128)(2,1)S(1)}, u32[]{:S(2)}, u32[]{:S(2)}) collective-permute-start(bf16[4,48,320]{2,1,0:T(8,128)(2,1)S(1)} %get-tuple-element.72), channel_id=1, source_target_pairs={{0,8},{1,9},{2,10},{3,11},{4,12},{5,13},{6,14},{7,15},{8,0},{9,1},... | collective-permute-start | bytes 368648 | tf_op jit(solution)/shard_map/ppermute | solution.py:215
  160.3 7.1 %collective-permute-start.7 = (bf16[4,48,320]{2,1,0:T(8,128)(2,1)S(1)}, bf16[4,48,320]{2,1,0:T(8,128)(2,1)S(1)}, u32[]{:S(2)}, u32[]{:S(2)}) collective-permute-start(bf16[4,48,320]{2,1,0:T(8,128)(2,1)S(1)} %get-tuple-element.70), channel_id=1, source_target_pairs={{0,4},{1,5},{2,6},{3,7},{4,0},{5,1},{6,2},{7,3},{8,12},{9,13},{10,... | collective-permute-start | bytes 368648 | tf_op jit(solution)/shard_map/ppermute | solution.py:215
  168.4 14.6 %collective-permute-start.12 = (bf16[48,320]{1,0:T(8,128)(2,1)S(1)}, bf16[48,320]{1,0:T(8,128)(2,1)S(1)}, u32[]{:S(2)}, u32[]{:S(2)}) collective-permute-start(bf16[48,320]{1,0:T(8,128)(2,1)S(1)} %get-tuple-element.74), channel_id=1, source_target_pairs={{0,3},{1,2},{2,1},{3,0},{4,7},{5,6},{6,5},{7,4},{8,11},{9,10},{10,... | collective-permute-start | bytes 92168 | tf_op jit(solution)/shard_map/ppermute | solution.py:215
  178.7 6.2 %collective-permute-start.11 = (bf16[48,320]{1,0:T(8,128)(2,1)S(1)}, bf16[48,320]{1,0:T(8,128)(2,1)S(1)}, u32[]{:S(2)}, u32[]{:S(2)}) collective-permute-start(bf16[48,320]{1,0:T(8,128)(2,1)S(1)} %get-tuple-element.75), channel_id=1, source_target_pairs={{0,2},{1,3},{2,0},{3,1},{4,6},{5,7},{6,4},{7,5},{8,10},{9,11},{10,... | collective-permute-start | bytes 92168 | tf_op jit(solution)/shard_map/ppermute | solution.py:215
  180.7 4.3 %collective-permute-start.10 = (bf16[48,320]{1,0:T(8,128)(2,1)S(1)}, bf16[48,320]{1,0:T(8,128)(2,1)S(1)}, u32[]{:S(2)}, u32[]{:S(2)}) collective-permute-start(bf16[48,320]{1,0:T(8,128)(2,1)S(1)} %get-tuple-element.73), channel_id=1, source_target_pairs={{0,1},{1,0},{2,3},{3,2},{4,5},{5,4},{6,7},{7,6},{8,9},{9,8},{10,11... | collective-permute-start | bytes 92168 | tf_op jit(solution)/shard_map/ppermute | solution.py:215
  185.0 7.3 %copy-start.16 = (f32[5120]{0:T(1024)S(1)}, f32[5120]{0:T(1024)}, u32[]{:S(2)}) copy-start(f32[5120]{0:T(1024)} %param.22) | copy-start | bytes 61444
  185.0 19.2 %copy-start = (bf16[132,5120]{1,0:T(8,128)(2,1)S(1)}, bf16[132,5120]{1,0:T(8,128)(2,1)}, u32[]{:S(2)}) copy-start(bf16[132,5120]{1,0:T(8,128)(2,1)} %weight_ref.1) | copy-start | bytes 4055044
  185.8 19.9 %copy-start.14 = (bf16[48,320]{1,0:T(8,128)(2,1)}, bf16[48,320]{1,0:T(8,128)(2,1)S(1)}, u32[]{:S(2)}) copy-start(bf16[48,320]{1,0:T(8,128)(2,1)S(1)} %fusion.31) | copy-start | bytes 92164
  186.7 17.6 %all-to-all-start.4 = ((bf16[16,48,320]{2,1,0:T(8,128)(2,1)}), bf16[16,48,320]{2,1,0:T(8,128)(2,1)S(1)}, u32[]{:S(2)}, u32[]{:S(2)}) async-start(bf16[16,48,320]{2,1,0:T(8,128)(2,1)} %broadcast_in_dim.74), calls=%async_computation.4 | async-start | bytes 1179648 | tf_op jit(solution)/shard_map/all_to_all | solution.py:23
Sparse Core Ops, SparseCore 0:
  61.7 85.4 all-gather.2

commit v10 on v9

--- a/solution.py
+++ b/solution.py
@@ -34,11 +34,12 @@
     return mine, theirs, held
 
 
-def shared_kernel(rank_ref, mine_ref, far_mine_ref, theirs_ref, far_theirs_ref, table_ref, out_ref, hidden_ref):
+def shared_kernel(rank_ref, mine_ref, far_mine_ref, theirs_ref, far_theirs_ref, table_ref, *out_refs):
     rank = rank_ref[0]
     inner = table_ref.shape[3] // 2
     size = table_ref.shape[2]
-    tok = out_ref.shape[2]
+    *out_refs, hidden_ref = out_refs
+    tok = out_refs[0].shape[1]
 
     def weights(device):
         return table_ref.at[pl.ds(2 * (device & 7), 2), device >> 3]
@@ -65,18 +66,18 @@
         for near in range(4):
             for far in range(4):
                 block = weights(rank ^ (near + 4 * far))[:, :, :inner].reshape(2 * size, inner)
-                out_ref[far, near] = dot(hidden, block, 1, 1).astype(out_ref.dtype)
+                out_refs[far][near] = dot(hidden, block, 1, 1).astype(jnp.bfloat16)
 
 
 def shared_partial(rank, mine, theirs, table, tok):
     width = mine.shape[1]
     columns = 2 * table.shape[3] // 3
-    out = jax.ShapeDtypeStruct((4, 4, tok, width), jnp.bfloat16)
+    out = jax.ShapeDtypeStruct((4, tok, width), jnp.bfloat16)
     near = pl.BlockSpec((4, width, 128), lambda i: (0, 0, 4))
     far = pl.BlockSpec((4, width, 128), lambda i: (0, 0, 5))
     return pl.pallas_call(
         shared_kernel,
-        out_shape=out,
+        out_shape=(out,) * 4,
         grid=(2,),
         in_specs=[
             pl.BlockSpec(memory_space=pltpu.SMEM),
@@ -86,7 +87,7 @@
             far,
             pl.BlockSpec(table.shape[:3] + (columns,), lambda i: (0, 0, 0, i)),
         ],
-        out_specs=pl.BlockSpec(out.shape, lambda i: (0, 0, 0, 0)),
+        out_specs=(pl.BlockSpec(out.shape, lambda i: (0, 0, 0)),) * 4,
         scratch_shapes=[pltpu.VMEM((tok, columns // 2), jnp.bfloat16)],
         compiler_params=pltpu.CompilerParams(vmem_limit_bytes=56 * 2**20),
         cost_estimate=pl.CostEstimate(flops=1000, bytes_accessed=1000, transcendentals=0),
@@ -190,8 +191,8 @@
 
     blank = jnp.zeros((16, width), bf16)
     rows = jnp.concatenate([arrived.reshape(slots, width), tokens, blank, beside], axis=0)
-    mine, theirs, far_rest = gather_halves(rows.T, RINGS, far_rest)
     far = jnp.concatenate([far_first, far_rest], axis=0)
+    mine, theirs, far = gather_halves(rows.T, RINGS, far)
     total = rows.shape[0]
     left, right = mine.reshape(-1, total), theirs.reshape(-1, total)
     middle = left.shape[0]

time: 214 us -> 215 us (level)
  waiting for transfers between devices: 50.3 us -> 53.4 us
  local copies, waits for them, and re-layouts: 16.8 us -> 14.2 us
  transfers between devices with their start and end apart: 18 -> 18, of which waited for: 11 -> 11; matrix products, arithmetic and copies ran while one was open for 13% -> 11% of each run, Pallas kernels for 3% -> 3%
where the time goes in v10:
time: 215 us; the launch traced here: 213 us
  starting transfers between devices  87.9 us (41%)
  waiting for transfers between devices  53.4 us (25%)
  blocking collectives  19.5 us (9%)
  between operations  14.7 us (7%)
  local copies, waits for them, and re-layouts  14.2 us (7%)
  other arithmetic  10.6 us (5%)
  Pallas kernels  6.9 us (3%)
  matrix products  6.05 us (3%)
    all_to_all x4, starting transfers between devices, exchange(): lax.all_to_all(parts, axis, split_axis=0, concat_axis=0, tiled=True, axis...  35.4 us
    ppermute x6, starting transfers between devices, summed(): total = total + lax.ppermute(parts[k], 'tensor', perm).astype(f32)  24.2 us
    all_to_all x1, blocking collectives, exchange(): lax.all_to_all(parts, axis, split_axis=0, concat_axis=0, tiled=True, axis...  19.5 us
    all_to_all x4, waiting for transfers between devices, exchange(): lax.all_to_all(parts, axis, split_axis=0, concat_axis=0, tiled=True, axis...  17.5 us
    ppermute x1, waiting for transfers between devices, per_device(): far_rest = lax.ppermute(give[cut:], 'tensor', across)  13.4 us
    ppermute x2, starting transfers between devices, gather_halves(): lax.ppermute(mine, 'tensor', [(i, i ^ 1) for i in range(2 * CHIPS)])  8.88 us
    ppermute x6, waiting for transfers between devices, summed(): total = total + lax.ppermute(parts[k], 'tensor', perm).astype(f32)  6.36 us
    ppermute x1, waiting for transfers between devices, per_device(): far_first = lax.ppermute(give[:cut], 'tensor', across)  5.83 us
  transfers between devices with their start and end apart: 18, of which 11 were waited for; matrix products, arithmetic and copies ran while one was open for 11% of the time, Pallas kernels for 3%

profile of v10, /device:TPU:1, one launch (start us, length us, event | category | flops | bytes accessed | tf_op | source)
XLA Modules:
  0.0 213.3 jit_solution(11886812203230519789)
XLA Ops:
  7.2 0.8 fusion.26
  8.0 1.2 convolution_compare_fusion
  9.2 0.6 copy-done.21
  9.8 1.1 convolution_convert_fusion
  11.2 1.0 reshape.62
  12.2 17.0 %all-to-all-start = ((bf16[32,18,320]{2,1,0:T(8,128)(2,1)}), bf16[32,18,320]{2,1,0:T(8,128)(2,1)S(1)}, u32[]{:S(2)}, u32[]{:S(2)}) async-start(bf16[32,18,320]{2,1,0:T(8,128)(2,1)} %reshape.62), calls=%async_computation | async-start | bytes 1179648 | tf_op jit(solution)/shard_map/all_to_all | solution.py:23
  29.2 1.0 fusion.19
  30.2 1.2 pad_maximum_fusion.3
  31.4 1.4 concatenate.40
  32.8 1.3 concatenate.41
  34.1 0.4 concatenate.38
  34.5 0.4 concatenate.39
  34.9 1.2 select_select_fusion
  36.2 0.7 copy-done.12
  36.9 4.3 %collective-permute-start = (bf16[48,320]{1,0:T(8,128)(2,1)S(1)}, bf16[48,320]{1,0:T(8,128)(2,1)S(1)}, u32[]{:S(2)}, u32[]{:S(2)}) collective-permute-start(bf16[48,320]{1,0:T(8,128)(2,1)S(1)} %copy-done.12), channel_id=1, source_target_pairs={{0,2},{1,3},{2,0},{3,1},{4,6},{5,7},{6,4},{7,5},{8,10},{9,11},{10,... | collective-permute-start | bytes 92168 | tf_op jit(solution)/shard_map/ppermute | solution.py:185
  41.3 0.8 pad_maximum_fusion.2
  42.1 2.5 %collective-permute-start.1 = (bf16[160,576]{1,0:T(8,128)(2,1)}, bf16[160,576]{1,0:T(8,128)(2,1)}, u32[]{:S(2)}, u32[]{:S(2)}) collective-permute-start(bf16[160,576]{1,0:T(8,128)(2,1)} %pad_maximum_fusion.2), channel_id=1, source_target_pairs={{0,256},{16,272},{32,288},{48,304},{64,320},{80,336},{96,352},{112... | collective-permute-start | bytes 552968 | tf_op jit(solution)/shard_map/ppermute | solution.py:179
  44.6 0.7 slice.203
  45.3 3.6 %collective-permute-start.2 = (bf16[64,2560]{1,0:T(8,128)(2,1)}, bf16[64,2560]{1,0:T(8,128)(2,1)}, u32[]{:S(2)}, u32[]{:S(2)}) collective-permute-start(bf16[64,2560]{1,0:T(8,128)(2,1)} %slice.203), channel_id=1, source_target_pairs={{0,2},{1,3},{2,0},{3,1},{4,6},{5,7},{6,4},{7,5},{8,10},{9,11},{10,... | collective-permute-start | bytes 983048 | tf_op jit(solution)/shard_map/ppermute | solution.py:184
  49.0 1.1 slice_bitcast_fusion
  50.1 1.2 concatenate.45
  51.4 0.4 concatenate.44
  51.8 1.0 broadcast_select_fusion
  53.0 1.9 maximum_select_fusion
  54.9 5.8 %collective-permute-done.2 = bf16[64,2560]{1,0:T(8,128)(2,1)} collective-permute-done((bf16[64,2560]{1,0:T(8,128)(2,1)}, bf16[64,2560]{1,0:T(8,128)(2,1)}, u32[]{:S(2)}, u32[]{:S(2)}) %collective-permute-start.2) | collective-permute-done | bytes 327712 | tf_op jit(solution)/shard_map/ppermute | solution.py:184
  60.8 1.4 all-to-all-done
  63.0 1.5 broadcast_in_dim.67
  64.4 4.2 %all-to-all-start.1 = ((bf16[4,320,688]{2,1,0:T(8,128)(2,1)}), bf16[4,320,688]{2,1,0:T(8,128)(2,1)S(1)}, u32[]{:S(2)}, u32[]{:S(2)}) async-start(bf16[4,320,688]{2,1,0:T(8,128)(2,1)} %broadcast_in_dim.67), calls=%async_computation.1 | async-start | bytes 3932160 | tf_op jit(solution)/shard_map/all_to_all | solution.py:23
  68.7 4.5 %collective-permute-start.3 = (bf16[128,2560]{1,0:T(8,128)(2,1)S(1)}, bf16[128,2560]{1,0:T(8,128)(2,1)S(1)}, u32[]{:S(2)}, u32[]{:S(2)}) collective-permute-start(bf16[128,2560]{1,0:T(8,128)(2,1)S(1)} %slice.236), channel_id=1, source_target_pairs={{0,2},{1,3},{2,0},{3,1},{4,6},{5,7},{6,4},{7,5},{8,10},{9,11},{10,... | collective-permute-start | bytes 1966088 | tf_op jit(solution)/shard_map/ppermute | solution.py:189
  73.2 13.4 %collective-permute-done.3 = bf16[128,2560]{1,0:T(8,128)(2,1)S(1)} collective-permute-done((bf16[128,2560]{1,0:T(8,128)(2,1)S(1)}, bf16[128,2560]{1,0:T(8,128)(2,1)S(1)}, u32[]{:S(2)}, u32[]{:S(2)}) %collective-permute-start.3) | collective-permute-done | bytes 655392 | tf_op jit(solution)/shard_map/ppermute | solution.py:189
  86.6 1.0 pad_maximum_fusion.1
  87.6 4.1 %all-to-all-done.1.mine_ref.far_mine_ref = bf16[4,320,688]{2,1,0:T(8,128)(2,1)S(1)} async-done(((bf16[4,320,688]{2,1,0:T(8,128)(2,1)}), bf16[4,320,688]{2,1,0:T(8,128)(2,1)S(1)}, u32[]{:S(2)}, u32[]{:S(2)}) %all-to-all-start.1) | async-done | bytes 1761312 | tf_op jit(solution)/shard_map/all_to_all | solution.py:23
  91.8 4.7 %collective-permute-start.4 = (bf16[4,320,688]{2,1,0:T(8,128)(2,1)S(1)}, bf16[4,320,688]{2,1,0:T(8,128)(2,1)S(1)}, u32[]{:S(2)}, u32[]{:S(2)}) collective-permute-start(bf16[4,320,688]{2,1,0:T(8,128)(2,1)S(1)} %all-to-all-done.1.mine_ref.far_mine_ref), channel_id=1, source_target_pairs={{0,1},{1,0},{2,3},{3,2},{4,5},{5,4},{6,7},{7,6},{8,9},{9,8},{10,11... | collective-permute-start | bytes 5283848 | tf_op jit(solution)/shard_map/ppermute | solution.py:33
  96.4 0.6 fusion.57
  97.0 0.6 fusion.8
  97.6 2.4 %collective-permute-done.4.theirs_ref.far_theirs_ref = bf16[4,320,688]{2,1,0:T(8,128)(2,1)S(1)} collective-permute-done((bf16[4,320,688]{2,1,0:T(8,128)(2,1)S(1)}, bf16[4,320,688]{2,1,0:T(8,128)(2,1)S(1)}, u32[]{:S(2)}, u32[]{:S(2)}) %collective-permute-start.4) | collective-permute-done | bytes 1761312 | tf_op jit(solution)/shard_map/ppermute | solution.py:33
  100.0 0.5 fusion.6
  100.6 4.4 %collective-permute-start.5 = (bf16[192,576]{1,0:T(8,128)(2,1)S(1)}, bf16[192,576]{1,0:T(8,128)(2,1)S(1)}, u32[]{:S(2)}, u32[]{:S(2)}) collective-permute-start(bf16[192,576]{1,0:T(8,128)(2,1)S(1)} %fusion.4), channel_id=1, source_target_pairs={{0,2},{1,3},{2,0},{3,1},{4,6},{5,7},{6,4},{7,5},{8,10},{9,11},{10,... | collective-permute-start | bytes 663560 | tf_op jit(solution)/shard_map/ppermute | solution.py:200
  105.0 0.6 fusion.58
  105.6 5.6 %collective-permute-done.5 = bf16[192,576]{1,0:T(8,128)(2,1)S(1)} collective-permute-done((bf16[192,576]{1,0:T(8,128)(2,1)S(1)}, bf16[192,576]{1,0:T(8,128)(2,1)S(1)}, u32[]{:S(2)}, u32[]{:S(2)}) %collective-permute-start.5) | collective-permute-done | bytes 221216 | tf_op jit(solution)/shard_map/ppermute | solution.py:200
  111.4 19.5 %all_to_all.25 = bf16[8,96,576]{2,1,0:T(8,128)(2,1)S(1)} all-to-all(bf16[8,96,576]{2,1,0:T(8,128)(2,1)S(1)} %broadcast_in_dim.68), channel_id=1, replica_groups={{0,2,4,6,8,10,12,14},{1,3,5,7,9,11,13,15},{16,18,20,22,24,26,28,30},{17..., dimensions={0} | all-to-all | bytes 1769472 | tf_op jit(solution)/shard_map/all_to_all | solution.py:23
  131.0 4.2 %collective-permute-start.6 = (bf16[8,96,576]{2,1,0:T(8,128)(2,1)S(1)}, bf16[8,96,576]{2,1,0:T(8,128)(2,1)S(1)}, u32[]{:S(2)}, u32[]{:S(2)}) collective-permute-start(bf16[8,96,576]{2,1,0:T(8,128)(2,1)S(1)} %all_to_all.25), channel_id=1, source_target_pairs={{0,1},{1,0},{2,3},{3,2},{4,5},{5,4},{6,7},{7,6},{8,9},{9,8},{10,11... | collective-permute-start | bytes 2654216 | tf_op jit(solution)/shard_map/ppermute | solution.py:33
  135.2 2.2 %collective-permute-done.6 = bf16[8,96,576]{2,1,0:T(8,128)(2,1)S(1)} collective-permute-done((bf16[8,96,576]{2,1,0:T(8,128)(2,1)S(1)}, bf16[8,96,576]{2,1,0:T(8,128)(2,1)S(1)}, u32[]{:S(2)}, u32[]{:S(2)}) %collective-permute-start.6) | collective-permute-done | bytes 884768 | tf_op jit(solution)/shard_map/ppermute | solution.py:33
  137.4 0.5 fusion.59
  137.9 0.6 fusion
  138.5 0.2 copy.31
  138.8 1.0 reshape.68
  139.7 8.7 %all-to-all-start.3 = ((bf16[32,18,320]{2,1,0:T(8,128)(2,1)}), bf16[32,18,320]{2,1,0:T(8,128)(2,1)S(1)}, u32[]{:S(2)}, u32[]{:S(2)}) async-start(bf16[32,18,320]{2,1,0:T(8,128)(2,1)} %reshape.68), calls=%async_computation.3 | async-start | bytes 1179648 | tf_op jit(solution)/shard_map/all_to_all | solution.py:23
  148.5 5.5 %shard_map.140 = (bf16[4,48,320]{2,1,0:T(8,128)(2,1)}, bf16[4,48,320]{2,1,0:T(8,128)(2,1)}, bf16[4,48,320]{2,1,0:T(8,128)(2,1)}, bf16[4,48,320]{2,1,0:T(8,128)(2,1)}) custom-call(s32[1]{0:T(128)} %bitcast.26.rank_ref, bf16[4,320,688]{2,1,0:T(8,128)(2,1)} %copy-done.1, bf16[4,320,688]{2,1,0:T(8,128)(2,1)} %copy-done.1, bf16[4,320,688]{2,1,0:T(8,128)(2,1)} %copy-done.2, ...), custom_call_target="tpu_custom_call" | custom-call | flops 1000 | bytes 1000 | tf_op jit(solution)/shard_map/pallas_call | solution.py:78
  154.0 4.1 %collective-permute-start.9 = (bf16[4,48,320]{2,1,0:T(8,128)(2,1)}, bf16[4,48,320]{2,1,0:T(8,128)(2,1)S(1)}, u32[]{:S(2)}, u32[]{:S(2)}) collective-permute-start(bf16[4,48,320]{2,1,0:T(8,128)(2,1)} %get-tuple-element.37), channel_id=1, source_target_pairs={{0,12},{1,13},{2,14},{3,15},{4,8},{5,9},{6,10},{7,11},{8,4},{9,5},... | collective-permute-start | bytes 368648 | tf_op jit(solution)/shard_map/ppermute | solution.py:216
  158.0 2.4 %collective-permute-start.8 = (bf16[4,48,320]{2,1,0:T(8,128)(2,1)}, bf16[4,48,320]{2,1,0:T(8,128)(2,1)S(1)}, u32[]{:S(2)}, u32[]{:S(2)}) collective-permute-start(bf16[4,48,320]{2,1,0:T(8,128)(2,1)} %get-tuple-element.36), channel_id=1, source_target_pairs={{0,8},{1,9},{2,10},{3,11},{4,12},{5,13},{6,14},{7,15},{8,0},{9,1},... | collective-permute-start | bytes 368648 | tf_op jit(solution)/shard_map/ppermute | solution.py:216
  160.4 2.7 %collective-permute-start.7 = (bf16[4,48,320]{2,1,0:T(8,128)(2,1)}, bf16[4,48,320]{2,1,0:T(8,128)(2,1)S(1)}, u32[]{:S(2)}, u32[]{:S(2)}) collective-permute-start(bf16[4,48,320]{2,1,0:T(8,128)(2,1)} %get-tuple-element.35), channel_id=1, source_target_pairs={{0,4},{1,5},{2,6},{3,7},{4,0},{5,1},{6,2},{7,3},{8,12},{9,13},{10,... | collective-permute-start | bytes 368648 | tf_op jit(solution)/shard_map/ppermute | solution.py:216
  163.2 2.8 %collective-permute-done.8 = bf16[4,48,320]{2,1,0:T(8,128)(2,1)S(1)} collective-permute-done((bf16[4,48,320]{2,1,0:T(8,128)(2,1)}, bf16[4,48,320]{2,1,0:T(8,128)(2,1)S(1)}, u32[]{:S(2)}, u32[]{:S(2)}) %collective-permute-start.8) | collective-permute-done | bytes 122912 | tf_op jit(solution)/shard_map/ppermute | solution.py:216
  165.9 1.6 collective-permute-done.7
  167.6 1.0 add_convert_fusion
  168.6 10.9 %collective-permute-start.12 = (bf16[48,320]{1,0:T(8,128)(2,1)S(1)}, bf16[48,320]{1,0:T(8,128)(2,1)S(1)}, u32[]{:S(2)}, u32[]{:S(2)}) collective-permute-start(bf16[48,320]{1,0:T(8,128)(2,1)S(1)} %get-tuple-element.79), channel_id=1, source_target_pairs={{0,3},{1,2},{2,1},{3,0},{4,7},{5,6},{6,5},{7,4},{8,11},{9,10},{10,... | collective-permute-start | bytes 92168 | tf_op jit(solution)/shard_map/ppermute | solution.py:216
  179.5 1.9 collective-permute-start.11
  181.4 2.3 %collective-permute-start.10 = (bf16[48,320]{1,0:T(8,128)(2,1)S(1)}, bf16[48,320]{1,0:T(8,128)(2,1)S(1)}, u32[]{:S(2)}, u32[]{:S(2)}) collective-permute-start(bf16[48,320]{1,0:T(8,128)(2,1)S(1)} %get-tuple-element.78), channel_id=1, source_target_pairs={{0,1},{1,0},{2,3},{3,2},{4,5},{5,4},{6,7},{7,6},{8,9},{9,8},{10,11... | collective-permute-start | bytes 92168 | tf_op jit(solution)/shard_map/ppermute | solution.py:216
  183.8 1.9 collective-permute-done.11
  186.0 0.5 fusion.2
  186.6 0.9 broadcast_in_dim.74
  187.4 5.6 %all-to-all-start.4 = ((bf16[16,48,320]{2,1,0:T(8,128)(2,1)}), bf16[16,48,320]{2,1,0:T(8,128)(2,1)S(1)}, u32[]{:S(2)}, u32[]{:S(2)}) async-start(bf16[16,48,320]{2,1,0:T(8,128)(2,1)} %broadcast_in_dim.74), calls=%async_computation.4 | async-start | bytes 1179648 | tf_op jit(solution)/shard_map/all_to_all | solution.py:23
  193.1 11.9 %all-to-all-done.4.stream_ref = bf16[16,48,320]{2,1,0:T(8,128)(2,1)S(1)} async-done(((bf16[16,48,320]{2,1,0:T(8,128)(2,1)}), bf16[16,48,320]{2,1,0:T(8,128)(2,1)S(1)}, u32[]{:S(2)}, u32[]{:S(2)}) %all-to-all-start.4) | async-done | bytes 491552 | tf_op jit(solution)/shard_map/all_to_all | solution.py:23
  205.0 1.4 shard_map.141
  (83 shorter events, 2.1 us)
Async XLA Ops:
  7.2 22.0 %copy-start.3 = (bf16[1,96,5120]{2,1,0:T(8,128)(2,1)S(1)}, bf16[1,96,5120]{2,1,0:T(8,128)(2,1)}, u32[]{:S(2)}) copy-start(bf16[1,96,5120]{2,1,0:T(8,128)(2,1)} %param.16) | copy-start | bytes 2949124
  7.2 22.0 %copy-start.4 = (bf16[1,96,5120]{2,1,0:T(8,128)(2,1)S(1)}, bf16[1,96,5120]{2,1,0:T(8,128)(2,1)}, u32[]{:S(2)}) copy-start(bf16[1,96,5120]{2,1,0:T(8,128)(2,1)} %param.17) | copy-start | bytes 2949124
  9.2 0.6 copy-start.21
  12.2 50.0 %all-to-all-start = ((bf16[32,18,320]{2,1,0:T(8,128)(2,1)}), bf16[32,18,320]{2,1,0:T(8,128)(2,1)S(1)}, u32[]{:S(2)}, u32[]{:S(2)}) async-start(bf16[32,18,320]{2,1,0:T(8,128)(2,1)} %reshape.62), calls=%async_computation | async-start | bytes 1179648 | tf_op jit(solution)/shard_map/all_to_all | solution.py:23
  29.1 119.3 %all-gather.3.cloned.1.call-start = ((), (), s32[]{:S(2)}) async-start(), calls=%async_computation.5 | async-start | bytes 6963200 | tf_op jit(solution)/shard_map/all_gather | solution.py:190
  31.4 2.7 %copy-start.10 = (bf16[192,320]{1,0:T(8,128)(2,1)S(1)}, bf16[192,320]{1,0:T(8,128)(2,1)}, u32[]{:S(2)}) copy-start(bf16[192,320]{1,0:T(8,128)(2,1)} %get-tuple-element.47) | copy-start | bytes 368644
  31.4 2.7 %copy-start.11 = (bf16[192,320]{1,0:T(8,128)(2,1)S(1)}, bf16[192,320]{1,0:T(8,128)(2,1)}, u32[]{:S(2)}) copy-start(bf16[192,320]{1,0:T(8,128)(2,1)} %get-tuple-element.48) | copy-start | bytes 368644
  36.1 0.8 copy-start.12
  36.1 5.1 %copy-start.14 = (bf16[192,160]{0,1:T(8,128)(2,1)S(1)}, bf16[192,160]{0,1:T(8,128)(2,1)}, u32[]{:S(2)}) copy-start(bf16[192,160]{0,1:T(8,128)(2,1)} %param.21) | copy-start | bytes 184324
  36.1 5.1 %copy-start.16 = (bf16[160,192]{1,0:T(8,128)(2,1)S(1)}, bf16[160,192]{1,0:T(8,128)(2,1)}, u32[]{:S(2)}) copy-start(bf16[160,192]{1,0:T(8,128)(2,1)} %param.20) | copy-start | bytes 184324
  36.1 5.1 %copy-start.18 = (bf16[160,192]{1,0:T(8,128)(2,1)S(1)}, bf16[160,192]{1,0:T(8,128)(2,1)}, u32[]{:S(2)}) copy-start(bf16[160,192]{1,0:T(8,128)(2,1)} %param.19) | copy-start | bytes 184324
  36.1 12.9 %copy-start.9 = (bf16[1,1536,320]{1,2,0:T(8,128)(2,1)S(1)}, bf16[1,1536,320]{1,2,0:T(8,128)(2,1)}, u32[]{:S(2)}) copy-start(bf16[1,1536,320]{1,2,0:T(8,128)(2,1)} %param.18) | copy-start | bytes 2949124
  36.9 18.1 %collective-permute-start = (bf16[48,320]{1,0:T(8,128)(2,1)S(1)}, bf16[48,320]{1,0:T(8,128)(2,1)S(1)}, u32[]{:S(2)}, u32[]{:S(2)}) collective-permute-start(bf16[48,320]{1,0:T(8,128)(2,1)S(1)} %copy-done.12), channel_id=1, source_target_pairs={{0,2},{1,3},{2,0},{3,1},{4,6},{5,7},{6,4},{7,5},{8,10},{9,11},{10,... | collective-permute-start | bytes 92168 | tf_op jit(solution)/shard_map/ppermute | solution.py:185
  42.1 10.9 %collective-permute-start.1 = (bf16[160,576]{1,0:T(8,128)(2,1)}, bf16[160,576]{1,0:T(8,128)(2,1)}, u32[]{:S(2)}, u32[]{:S(2)}) collective-permute-start(bf16[160,576]{1,0:T(8,128)(2,1)} %pad_maximum_fusion.2), channel_id=1, source_target_pairs={{0,256},{16,272},{32,288},{48,304},{64,320},{80,336},{96,352},{112... | collective-permute-start | bytes 552968 | tf_op jit(solution)/shard_map/ppermute | solution.py:179
  45.3 15.4 %collective-permute-start.2 = (bf16[64,2560]{1,0:T(8,128)(2,1)}, bf16[64,2560]{1,0:T(8,128)(2,1)}, u32[]{:S(2)}, u32[]{:S(2)}) collective-permute-start(bf16[64,2560]{1,0:T(8,128)(2,1)} %slice.203), channel_id=1, source_target_pairs={{0,2},{1,3},{2,0},{3,1},{4,6},{5,7},{6,4},{7,5},{8,10},{9,11},{10,... | collective-permute-start | bytes 983048 | tf_op jit(solution)/shard_map/ppermute | solution.py:184
  51.4 1.5 copy-start.15
  51.4 1.5 copy-start.17
  51.4 1.5 copy-start.19
  64.4 27.3 %all-to-all-start.1 = ((bf16[4,320,688]{2,1,0:T(8,128)(2,1)}), bf16[4,320,688]{2,1,0:T(8,128)(2,1)S(1)}, u32[]{:S(2)}, u32[]{:S(2)}) async-start(bf16[4,320,688]{2,1,0:T(8,128)(2,1)} %broadcast_in_dim.67), calls=%async_computation.1 | async-start | bytes 3932160 | tf_op jit(solution)/shard_map/all_to_all | solution.py:23
  68.6 27.8 %copy-start.6 = (bf16[192,1280]{1,0:T(8,128)(2,1)S(1)}, bf16[192,1280]{1,0:T(8,128)(2,1)}, u32[]{:S(2)}) copy-start(bf16[192,1280]{1,0:T(8,128)(2,1)} %get-tuple-element.23) | copy-start | bytes 1474564
  68.7 17.9 %collective-permute-start.3 = (bf16[128,2560]{1,0:T(8,128)(2,1)S(1)}, bf16[128,2560]{1,0:T(8,128)(2,1)S(1)}, u32[]{:S(2)}, u32[]{:S(2)}) collective-permute-start(bf16[128,2560]{1,0:T(8,128)(2,1)S(1)} %slice.236), channel_id=1, source_target_pairs={{0,2},{1,3},{2,0},{3,1},{4,6},{5,7},{6,4},{7,5},{8,10},{9,11},{10,... | collective-permute-start | bytes 1966088 | tf_op jit(solution)/shard_map/ppermute | solution.py:189
  91.8 5.8 %copy-start.1 = (bf16[4,320,688]{2,1,0:T(8,128)(2,1)}, bf16[4,320,688]{2,1,0:T(8,128)(2,1)S(1)}, u32[]{:S(2)}) copy-start(bf16[4,320,688]{2,1,0:T(8,128)(2,1)S(1)} %all-to-all-done.1.mine_ref.far_mine_ref) | copy-start | bytes 5283844
  91.8 8.2 %collective-permute-start.4 = (bf16[4,320,688]{2,1,0:T(8,128)(2,1)S(1)}, bf16[4,320,688]{2,1,0:T(8,128)(2,1)S(1)}, u32[]{:S(2)}, u32[]{:S(2)}) collective-permute-start(bf16[4,320,688]{2,1,0:T(8,128)(2,1)S(1)} %all-to-all-done.1.mine_ref.far_mine_ref), channel_id=1, source_target_pairs={{0,1},{1,0},{2,3},{3,2},{4,5},{5,4},{6,7},{7,6},{8,9},{9,8},{10,11... | collective-permute-start | bytes 5283848 | tf_op jit(solution)/shard_map/ppermute | solution.py:33
  100.0 5.0 %copy-start.2 = (bf16[4,320,688]{2,1,0:T(8,128)(2,1)}, bf16[4,320,688]{2,1,0:T(8,128)(2,1)S(1)}, u32[]{:S(2)}) copy-start(bf16[4,320,688]{2,1,0:T(8,128)(2,1)S(1)} %collective-permute-done.4.theirs_ref.far_theirs_ref) | copy-start | bytes 5283844
  100.0 5.0 %copy-start.5 = (bf16[192,1280]{1,0:T(8,128)(2,1)S(1)}, bf16[192,1280]{1,0:T(8,128)(2,1)}, u32[]{:S(2)}) copy-start(bf16[192,1280]{1,0:T(8,128)(2,1)} %get-tuple-element.29) | copy-start | bytes 1474564
  100.6 10.6 %collective-permute-start.5 = (bf16[192,576]{1,0:T(8,128)(2,1)S(1)}, bf16[192,576]{1,0:T(8,128)(2,1)S(1)}, u32[]{:S(2)}, u32[]{:S(2)}) collective-permute-start(bf16[192,576]{1,0:T(8,128)(2,1)S(1)} %fusion.4), channel_id=1, source_target_pairs={{0,2},{1,3},{2,0},{3,1},{4,6},{5,7},{6,4},{7,5},{8,10},{9,11},{10,... | collective-permute-start | bytes 663560 | tf_op jit(solution)/shard_map/ppermute | solution.py:200
  111.2 26.1 %copy-start.8 = (bf16[768,320]{0,1:T(8,128)(2,1)S(1)}, bf16[768,320]{0,1:T(8,128)(2,1)}, u32[]{:S(2)}) copy-start(bf16[768,320]{0,1:T(8,128)(2,1)} %get-tuple-element.32) | copy-start | bytes 1474564
  111.4 26.5 %copy-start.7 = (bf16[768,320]{0,1:T(8,128)(2,1)S(1)}, bf16[768,320]{0,1:T(8,128)(2,1)}, u32[]{:S(2)}) copy-start(bf16[768,320]{0,1:T(8,128)(2,1)} %get-tuple-element.31) | copy-start | bytes 1474564
  131.0 6.4 %collective-permute-start.6 = (bf16[8,96,576]{2,1,0:T(8,128)(2,1)S(1)}, bf16[8,96,576]{2,1,0:T(8,128)(2,1)S(1)}, u32[]{:S(2)}, u32[]{:S(2)}) collective-permute-start(bf16[8,96,576]{2,1,0:T(8,128)(2,1)S(1)} %all_to_all.25), channel_id=1, source_target_pairs={{0,1},{1,0},{2,3},{3,2},{4,5},{5,4},{6,7},{7,6},{8,9},{9,8},{10,11... | collective-permute-start | bytes 2654216 | tf_op jit(solution)/shard_map/ppermute | solution.py:33
  139.7 46.0 %all-to-all-start.3 = ((bf16[32,18,320]{2,1,0:T(8,128)(2,1)}), bf16[32,18,320]{2,1,0:T(8,128)(2,1)S(1)}, u32[]{:S(2)}, u32[]{:S(2)}) async-start(bf16[32,18,320]{2,1,0:T(8,128)(2,1)} %reshape.68), calls=%async_computation.3 | async-start | bytes 1179648 | tf_op jit(solution)/shard_map/all_to_all | solution.py:23
  148.5 14.6 %copy-start.25 = (s32[48,6]{0,1:T(8,128)S(1)}, s32[48,6]{0,1:T(8,128)}, u32[]{:S(2)}) copy-start(s32[48,6]{0,1:T(8,128)} %param.14) | copy-start | bytes 3460
  148.5 14.6 %copy-start.26 = (f32[48,6]{0,1:T(8,128)S(1)}, f32[48,6]{0,1:T(8,128)}, u32[]{:S(2)}) copy-start(f32[48,6]{0,1:T(8,128)} %param.15) | copy-start | bytes 3460
  154.0 32.0 %copy-start.22 = (pred[48,576]{1,0:T(8,128)(4,1)S(1)}, pred[48,576]{1,0:T(8,128)(4,1)}, u32[]{:S(2)}) copy-start(pred[48,576]{1,0:T(8,128)(4,1)} %copy-done.21) | copy-start | bytes 82948
  154.0 32.1 %copy-start.23 = (bf16[32,576]{1,0:T(8,128)(2,1)S(1)}, bf16[32,576]{1,0:T(8,128)(2,1)}, u32[]{:S(2)}) copy-start(bf16[32,576]{1,0:T(8,128)(2,1)} %constant.42.clone) | copy-start | bytes 110596
  154.0 32.5 %copy-start.13 = (bf16[48,320]{1,0:T(8,128)(2,1)S(1)}, bf16[48,320]{1,0:T(8,128)(2,1)}, u32[]{:S(2)}) copy-start(bf16[48,320]{1,0:T(8,128)(2,1)} %param.13) | copy-start | bytes 92164
  154.0 9.2 %collective-permute-start.9 = (bf16[4,48,320]{2,1,0:T(8,128)(2,1)}, bf16[4,48,320]{2,1,0:T(8,128)(2,1)S(1)}, u32[]{:S(2)}, u32[]{:S(2)}) collective-permute-start(bf16[4,48,320]{2,1,0:T(8,128)(2,1)} %get-tuple-element.37), channel_id=1, source_target_pairs={{0,12},{1,13},{2,14},{3,15},{4,8},{5,9},{6,10},{7,11},{8,4},{9,5},... | collective-permute-start | bytes 368648 | tf_op jit(solution)/shard_map/ppermute | solution.py:216
  158.0 7.9 %collective-permute-start.8 = (bf16[4,48,320]{2,1,0:T(8,128)(2,1)}, bf16[4,48,320]{2,1,0:T(8,128)(2,1)S(1)}, u32[]{:S(2)}, u32[]{:S(2)}) collective-permute-start(bf16[4,48,320]{2,1,0:T(8,128)(2,1)} %get-tuple-element.36), channel_id=1, source_target_pairs={{0,8},{1,9},{2,10},{3,11},{4,12},{5,13},{6,14},{7,15},{8,0},{9,1},... | collective-permute-start | bytes 368648 | tf_op jit(solution)/shard_map/ppermute | solution.py:216
  160.4 7.1 %collective-permute-start.7 = (bf16[4,48,320]{2,1,0:T(8,128)(2,1)}, bf16[4,48,320]{2,1,0:T(8,128)(2,1)S(1)}, u32[]{:S(2)}, u32[]{:S(2)}) collective-permute-start(bf16[4,48,320]{2,1,0:T(8,128)(2,1)} %get-tuple-element.35), channel_id=1, source_target_pairs={{0,4},{1,5},{2,6},{3,7},{4,0},{5,1},{6,2},{7,3},{8,12},{9,13},{10,... | collective-permute-start | bytes 368648 | tf_op jit(solution)/shard_map/ppermute | solution.py:216
  168.6 15.2 %collective-permute-start.12 = (bf16[48,320]{1,0:T(8,128)(2,1)S(1)}, bf16[48,320]{1,0:T(8,128)(2,1)S(1)}, u32[]{:S(2)}, u32[]{:S(2)}) collective-permute-start(bf16[48,320]{1,0:T(8,128)(2,1)S(1)} %get-tuple-element.79), channel_id=1, source_target_pairs={{0,3},{1,2},{2,1},{3,0},{4,7},{5,6},{6,5},{7,4},{8,11},{9,10},{10,... | collective-permute-start | bytes 92168 | tf_op jit(solution)/shard_map/ppermute | solution.py:216
  179.5 6.2 %collective-permute-start.11 = (bf16[48,320]{1,0:T(8,128)(2,1)S(1)}, bf16[48,320]{1,0:T(8,128)(2,1)S(1)}, u32[]{:S(2)}, u32[]{:S(2)}) collective-permute-start(bf16[48,320]{1,0:T(8,128)(2,1)S(1)} %get-tuple-element.80), channel_id=1, source_target_pairs={{0,2},{1,3},{2,0},{3,1},{4,6},{5,7},{6,4},{7,5},{8,10},{9,11},{10,... | collective-permute-start | bytes 92168 | tf_op jit(solution)/shard_map/ppermute | solution.py:216
  181.4 4.3 %collective-permute-start.10 = (bf16[48,320]{1,0:T(8,128)(2,1)S(1)}, bf16[48,320]{1,0:T(8,128)(2,1)S(1)}, u32[]{:S(2)}, u32[]{:S(2)}) collective-permute-start(bf16[48,320]{1,0:T(8,128)(2,1)S(1)} %get-tuple-element.78), channel_id=1, source_target_pairs={{0,1},{1,0},{2,3},{3,2},{4,5},{5,4},{6,7},{7,6},{8,9},{9,8},{10,11... | collective-permute-start | bytes 92168 | tf_op jit(solution)/shard_map/ppermute | solution.py:216
  185.7 7.3 %copy-start.24 = (f32[5120]{0:T(1024)S(1)}, f32[5120]{0:T(1024)}, u32[]{:S(2)}) copy-start(f32[5120]{0:T(1024)} %param.22) | copy-start | bytes 61444
  185.7 19.3 %copy-start = (bf16[132,5120]{1,0:T(8,128)(2,1)S(1)}, bf16[132,5120]{1,0:T(8,128)(2,1)}, u32[]{:S(2)}) copy-start(bf16[132,5120]{1,0:T(8,128)(2,1)} %weight_ref.1) | copy-start | bytes 4055044
  186.5 19.9 %copy-start.20 = (bf16[48,320]{1,0:T(8,128)(2,1)}, bf16[48,320]{1,0:T(8,128)(2,1)S(1)}, u32[]{:S(2)}) copy-start(bf16[48,320]{1,0:T(8,128)(2,1)S(1)} %fusion.28) | copy-start | bytes 92164
  187.4 17.6 %all-to-all-start.4 = ((bf16[16,48,320]{2,1,0:T(8,128)(2,1)}), bf16[16,48,320]{2,1,0:T(8,128)(2,1)S(1)}, u32[]{:S(2)}, u32[]{:S(2)}) async-start(bf16[16,48,320]{2,1,0:T(8,128)(2,1)} %broadcast_in_dim.74), calls=%async_computation.4 | async-start | bytes 1179648 | tf_op jit(solution)/shard_map/all_to_all | solution.py:23
Sparse Core Ops, SparseCore 0:
  62.4 85.4 all-gather.2
